TPU v7x, 32 devices: a whole 2x2x4 slice. The times are simulated.
32 devices in a mesh: space: 16 (over z, x, core), ch: 2 (over y).
Axes of the slice: x: 2, y: 2, z: 4, core: 2. Of those that a mesh axis runs over, the one named last changes fastest.
Arguments:
- inputs: bfloat16 [256, 1, 128, 128], P('ch', None, 'space'), may hold values from -6 to 6
- w_up: bfloat16 [64, 128, 256], P(None, 'ch'), may hold values from -0.125 to 0.125
- b_up: float32 [128], replicated, may hold values from -4 to 4
- w_conv: bfloat16 [27, 128, 128], replicated, may hold values from -0.109375 to 0.109375
- b_conv: float32 [128], replicated, may hold values from -4 to 4
Outputs:
- result: bfloat16 [128, 2, 256, 256], P(None, None, ('space', 'ch'))
All inputs are finite; a program needn't handle non-finite values.
Results may differ from a plain program's by a relative error of at most 0.0036.
Values may be sent and summed in bfloat16 or wider, within the bound.
No kernel may reach another device: no remote copies, remote signals or barrier semaphores. Data moves between devices by JAX's collectives and lax.ppermute only.
A program may use at most 128 MiB of HBM per device.

v0:
```python
import jax
import jax.numpy as jnp
from jax import lax
from jax.experimental import pallas as pl
from jax.experimental.pallas import tpu as pltpu
from jax.sharding import PartitionSpec as P

AXES = ("space", "ch")
PHASES = (((1, 0), (3, -1)), ((2, 0), (0, 1)))
COLUMNS = ((3, 0, 1), (0, 1, 2))


def column_of(bias):
    lanes = bias.shape[-1]
    return jnp.transpose(jnp.broadcast_to(bias, (lanes, lanes)))


def shifted(value, step):
    cols = value.shape[1]
    place = lax.broadcasted_iota(jnp.int32, value.shape, 1)
    edge = 0 if step == 1 else cols - 1
    return jnp.where(place == edge, 0.0, pltpu.roll(value, step % cols, 1))


def compute(x_ref, w_ref, b_up_ref, w_conv_ref, b_conv_ref, out_ref, u_ref, total_ref, first, last):
    rows = out_ref.shape[2]
    cout = out_ref.shape[0]
    cols = x_ref.shape[3]
    held = rows + 2
    bias = column_of(b_up_ref[...])
    bias = jnp.concatenate([bias, bias], axis=0)
    for row_phase in (0, 1):
        for col_phase in (0, 1):
            taps = []
            for row_tap, row_shift in PHASES[row_phase]:
                for col_tap, col_shift in PHASES[col_phase]:
                    slot = row_shift + 1 - row_phase
                    taps.append((row_tap * 4 + col_tap, slot, col_shift % 3))
            kernel = jnp.concatenate([w_ref[tap] for tap, _, _ in taps], axis=1)
            for start in range(0, held // 2, 2):
                places = range(start, min(start + 2, held // 2))
                cells = jnp.concatenate(
                    [
                        jnp.concatenate([x_ref[copy, slot + place] for place in places], axis=1)
                        for _, slot, copy in taps
                    ],
                    axis=0,
                )
                summed = jnp.dot(kernel, cells, preferred_element_type=jnp.float32)
                for number, place in enumerate(places):
                    row = 2 * place + 1 - row_phase
                    value = summed[:, number * cols : (number + 1) * cols] + bias
                    value = jnp.where(value > 0, value, 0.2 * value)
                    if row == 0:
                        value = jnp.where(first, 0.0, value)
                    if row == held - 1:
                        value = jnp.where(last, 0.0, value)
                    u_ref[col_phase, row] = value.astype(jnp.bfloat16)
                    moved = shifted(value, -1 if col_phase == 0 else 1)
                    u_ref[2 + col_phase, row] = moved.astype(jnp.bfloat16)

    bias = column_of(b_conv_ref[...])
    bias = jnp.concatenate([bias, bias], axis=0)
    source = lax.broadcasted_iota(jnp.int32, (2 * cols, 2 * cols), 0)
    target = lax.broadcasted_iota(jnp.int32, (2 * cols, 2 * cols), 1)
    wanted = jnp.where(source < cols, 2 * source, 2 * (source - cols) + 1)
    interleave = jnp.where(wanted == target, 1.0, 0.0).astype(jnp.bfloat16)
    kernels = []
    for row_tap in range(3):
        for col_tap in range(3):
            below, here, above = [w_conv_ref[a * 9 + row_tap * 3 + col_tap] for a in range(3)]
            kernels.append(
                jnp.concatenate(
                    [jnp.concatenate([here, above], 1), jnp.concatenate([below, here], 1)], 0
                )
            )
    kernel = jnp.concatenate(kernels, axis=1)
    for start in range(0, rows, 2):
        halves = []
        for col_phase in (0, 1):
            cells = jnp.concatenate(
                [
                    jnp.concatenate([u_ref[copy, start + row_tap], u_ref[copy, start + row_tap + 1]], 1)
                    for row_tap in range(3)
                    for copy in COLUMNS[col_phase]
                ],
                axis=0,
            )
            halves.append(jnp.dot(kernel, cells, preferred_element_type=jnp.float32))
        for number in (0, 1):
            pair = [
                (half[:, number * cols : (number + 1) * cols] + bias).astype(jnp.bfloat16)
                for half in halves
            ]
            pair = jnp.concatenate(pair, axis=1)
            mixed = jnp.dot(pair, interleave, preferred_element_type=jnp.float32)
            for side in (0, 1):
                total_ref[side, pl.ds(start + number, 2 * cout, stride=rows), :] = mixed[
                    :, side * cols : (side + 1) * cols
                ]
    for plane in (0, 1):
        for side in (0, 1):
            block = total_ref[side, pl.ds(plane * cout * rows, cout * rows), :]
            out_ref[:, plane, :, side * cols : (side + 1) * cols] = block.reshape(
                cout, rows, cols
            ).astype(jnp.bfloat16)


def store_row(x_ref, slot, offset, value):
    chans = value.shape[0]
    where = pl.ds(pl.multiple_of(offset, 16), chans)
    wide = value.astype(jnp.float32)
    x_ref[0, slot, where] = value
    x_ref[1, slot, where] = shifted(wide, -1).astype(jnp.bfloat16)
    x_ref[2, slot, where] = shifted(wide, 1).astype(jnp.bfloat16)


def position():
    s, c = lax.axis_index("space"), lax.axis_index("ch")
    return s, c


def paired_kernel(
    own_ref, peer_ref, near_ref, far_ref, w_own_ref, w_peer_ref, w_core_ref,
    b_up_ref, w_conv_ref, b_conv_ref, out_ref, x_ref, w_ref, u_ref, total_ref, sems,
):
    s, c = position()
    core = lax.rem(s, 2)
    part, cout = w_own_ref.shape[1], out_ref.shape[0]

    def rows_of(plane, half):
        return pl.ds(pl.multiple_of(plane * cout + half * part, part), part)

    copies = [
        pltpu.make_async_copy(w_own_ref.at[pl.ds(16, 16)], w_ref.at[:, rows_of(0, c)], sems.at[0]),
        pltpu.make_async_copy(w_own_ref.at[pl.ds(32, 16)], w_ref.at[:, rows_of(1, c)], sems.at[1]),
        pltpu.make_async_copy(w_peer_ref, w_ref.at[:, rows_of(core, 1 - c)], sems.at[2]),
        pltpu.make_async_copy(w_core_ref, w_ref.at[:, rows_of(1 - core, 1 - c)], sems.at[3]),
    ]
    for copy in copies:
        copy.start()
    chans = own_ref.shape[1]
    share = peer_ref.shape[0]
    own, other = c * chans, (1 - c) * chans
    for place in range(share):
        store_row(x_ref, place + 1 - c, own, own_ref[place + c * (own_ref.shape[0] - share)])
        store_row(x_ref, place + 1 - c, other, peer_ref[place])
    store_row(x_ref, c * share, own, near_ref[0])
    store_row(x_ref, c * share, other, far_ref[0])
    for copy in copies:
        copy.wait()
    first = (s == 0) & (c == 0)
    last = (s == lax.axis_size("space") - 1) & (c == 1)
    compute(x_ref, w_ref, b_up_ref, w_conv_ref, b_conv_ref, out_ref, u_ref, total_ref, first, last)


def gathered_kernel(
    rows_ref, w_all_ref, b_up_ref, w_conv_ref, b_conv_ref, out_ref, x_ref, w_ref, u_ref, total_ref, sems
):
    s, c = position()
    cout = out_ref.shape[0]
    copies = [
        pltpu.make_async_copy(
            w_all_ref.at[pl.ds(16 * plane, 16)], w_ref.at[:, pl.ds(plane * cout, cout)], sems.at[plane]
        )
        for plane in (0, 1)
    ]
    for copy in copies:
        copy.start()
    for slot in range(rows_ref.shape[0]):
        store_row(x_ref, slot, 0, rows_ref[slot])
    for copy in copies:
        copy.wait()
    first = (s == 0) & (c == 0)
    last = (s == lax.axis_size("space") - 1) & (c == lax.axis_size("ch") - 1)
    compute(x_ref, w_ref, b_up_ref, w_conv_ref, b_conv_ref, out_ref, u_ref, total_ref, first, last)


def run(kernel, spaces, operands, sizes):
    cin, cout, rows, cols = sizes
    spec = {"vmem": pl.BlockSpec(memory_space=pltpu.VMEM), "any": pl.BlockSpec(memory_space=pl.ANY)}
    return pl.pallas_call(
        kernel,
        out_shape=jax.ShapeDtypeStruct((cout, 2, rows, 2 * cols), jnp.bfloat16),
        in_specs=[spec[space] for space in spaces],
        out_specs=spec["vmem"],
        scratch_shapes=[
            pltpu.VMEM((3, rows // 2 + 2, cin, cols), jnp.bfloat16),
            pltpu.VMEM((16, 2 * cout, cin), jnp.bfloat16),
            pltpu.VMEM((4, rows + 2, 2 * cout, cols), jnp.bfloat16),
            pltpu.VMEM((2, 2 * cout * rows, cols), jnp.float32),
            pltpu.SemaphoreType.DMA((4,)),
        ],
        compiler_params=pltpu.CompilerParams(vmem_limit_bytes=48 * 2**20),
    )(*operands)


def paired(inputs, w_up, b_up, w_conv, b_conv, sizes):
    spaces = lax.axis_size("space")
    s, c = position()
    core = lax.rem(s, 2)
    held = inputs.shape[2]
    share = held // 2 + 1

    def at(space, ch):
        return space * 2 + ch

    across = [(at(i, j), at(i, 1 - j)) for i in range(spaces) for j in (0, 1)]
    cores = [(at(i, j), at(i ^ 1, j)) for i in range(spaces) for j in (0, 1)]
    down = [(at(i - 1, 0), at(i, 0)) for i in range(1, spaces)]
    up = [(at(i + 1, 1), at(i, 1)) for i in range(spaces - 1)]
    down_far = [(at(i - 1, 1), at(i, 0)) for i in range(1, spaces)]
    up_far = [(at(i + 1, 0), at(i, 1)) for i in range(spaces - 1)]

    w_mine = lax.dynamic_slice_in_dim(w_up, 16 + 16 * core, 16, 0)
    w_peer = lax.ppermute(w_mine, AXES, across)
    w_core = lax.ppermute(w_peer, AXES, cores)

    rows = inputs[:, 0].transpose(1, 0, 2)
    wanted = lax.dynamic_slice_in_dim(rows, (1 - c) * (held - share), share, 0)
    peer = lax.ppermute(wanted, AXES, across)
    edge_near = lax.dynamic_slice_in_dim(rows, (1 - c) * (held - 1), 1, 0)
    edge_far = lax.dynamic_slice_in_dim(rows, c * (held - 1), 1, 0)
    near = lax.ppermute(edge_near, AXES, down + up)
    far = lax.ppermute(edge_far, AXES, down_far + up_far)
    operands = (rows, peer, near, far, w_up, w_peer, w_core, b_up[None], w_conv, b_conv[None])
    places = ("vmem",) * 4 + ("any",) * 3 + ("vmem",) * 3
    return run(paired_kernel, places, operands, sizes)


def gathered(inputs, w_up, b_up, w_conv, b_conv, sizes):
    spaces, chs = lax.axis_size("space"), lax.axis_size("ch")
    c = lax.axis_index("ch")
    w_all = lax.all_gather(w_up[16:48], "ch", axis=1, tiled=True)
    rows = lax.all_gather(inputs[:, 0], "ch", axis=0, tiled=True).transpose(1, 0, 2)
    forward = [(i, i + 1) for i in range(spaces - 1)]
    backward = [(j, i) for i, j in forward]
    low = lax.ppermute(rows[-1:], "space", forward)
    high = lax.ppermute(rows[:1], "space", backward)
    rows = jnp.concatenate([low, rows, high], axis=0)
    share = inputs.shape[2] // chs
    rows = lax.dynamic_slice_in_dim(rows, c * share, share + 2, 0)
    operands = (rows, w_all, b_up[None], w_conv, b_conv[None])
    return run(gathered_kernel, ("vmem", "any", "vmem", "vmem", "vmem"), operands, sizes)


def local(inputs, w_up, b_up, w_conv, b_conv):
    chs = lax.axis_size("ch")
    sizes = (w_up.shape[2], w_conv.shape[1], 2 * inputs.shape[2] // chs, inputs.shape[3])
    plan = paired if chs == 2 and lax.axis_size("space") % 2 == 0 else gathered
    return plan(inputs, w_up, b_up, w_conv, b_conv, sizes)


def solution(mesh):
    return jax.shard_map(
        local,
        mesh=mesh,
        in_specs=(P("ch", None, "space", None), P(None, "ch", None), P(), P(), P()),
        out_specs=P(None, None, ("space", "ch"), None),
        check_vma=False,
    )
```

profile of v0, /device:TPU:23, one launch (start us, length us, event | category | flops | bytes accessed | tf_op | source)
XLA Modules:
  0.0 37.8 jit_solution(10318753633938317042)
XLA Ops:
  0.0 0.0 copy-start
  0.0 0.0 copy-start.3
  0.0 0.0 copy-start.2
  0.0 1.2 %constant_dynamic-slice_fusion = bf16[16,64,256]{2,1,0:T(8,128)(2,1)S(1)} fusion(bf16[64,64,256]{2,1,0:T(8,128)(2,1)} %w_own_ref.1, s32[]{:T(128)S(6)} %select_n.15), kind=kLoop, calls=%fused_computation.3 | loop fusion | bytes 1048580 | tf_op jit(solution)/shard_map/dynamic_slice | solution.py:215
  1.3 0.3 collective-permute-start.3
  1.5 12.6 %collective-permute-done.3.w_peer_ref = bf16[16,64,256]{2,1,0:T(8,128)(2,1)S(1)} collective-permute-done((bf16[16,64,256]{2,1,0:T(8,128)(2,1)S(1)}, bf16[16,64,256]{2,1,0:T(8,128)(2,1)S(1)}, u32[]{:S(2)}, u32[]{:S(2)}) %collective-permute-start.3) | collective-permute-done | bytes 524320 | tf_op jit(solution)/shard_map/ppermute | solution.py:216
  14.1 1.5 %collective-permute-start.4 = (bf16[16,64,256]{2,1,0:T(8,128)(2,1)S(1)}, bf16[16,64,256]{2,1,0:T(8,128)(2,1)S(1)}, u32[]{:S(2)}, u32[]{:S(2)}) collective-permute-start(bf16[16,64,256]{2,1,0:T(8,128)(2,1)S(1)} %collective-permute-done.3.w_peer_ref), channel_id=1, source_target_pairs={{0,2},{1,3},{2,0},{3,1},{4,6},{5,7},{6,4},{7,5},{8,10},{9,11},{10,... | collective-permute-start | bytes 1572872 | tf_op jit(solution)/shard_map/ppermute | solution.py:217
  15.7 1.0 %constant_dynamic-slice_fusion.1 = bf16[128,1,5,128]{3,2,1,0:T(8,128)(2,1)S(1)} fusion(bf16[128,1,8,128]{3,2,1,0:T(8,128)(2,1)} %param.5, s32[]{:T(128)S(6)} %select_n.12), kind=kLoop, calls=%fused_computation.4 | loop fusion | bytes 327684 | tf_op jit(solution)/shard_map/dynamic-slice.3
  16.7 0.7 %copy.15 = bf16[128,1,5,128]{3,0,2,1:T(8,128)(2,1)} copy(bf16[128,1,5,128]{3,2,1,0:T(8,128)(2,1)S(1)} %constant_dynamic-slice_fusion.1) | data formatting | bytes 327680 | tf_op jit(solution)/shard_map/dynamic-slice.3
  17.4 0.2 collective-permute-start
  17.6 1.0 %copy.16 = bf16[128,1,8,128]{3,0,2,1:T(8,128)(2,1)S(1)} copy(bf16[128,1,8,128]{3,2,1,0:T(8,128)(2,1)} %param.5) | data formatting | bytes 524288 | tf_op args[0]
  18.6 4.3 %collective-permute-start.2 = (bf16[1,128,128]{2,1,0:T(8,128)(2,1)S(1)}, bf16[1,128,128]{2,1,0:T(8,128)(2,1)S(1)}, u32[]{:S(2)}, u32[]{:S(2)}) collective-permute-start(bf16[1,128,128]{2,1,0:T(8,128)(2,1)S(1)} %get-tuple-element.5), channel_id=1, source_target_pairs={{1,2},{3,4},{5,6},{7,8},{9,10},{11,12},{13,14},{15,16},{17,18},{19... | collective-permute-start | bytes 98312 | tf_op jit(solution)/shard_map/ppermute | solution.py:225
  22.9 1.9 %collective-permute-start.1 = (bf16[1,128,128]{2,1,0:T(8,128)(2,1)S(1)}, bf16[1,128,128]{2,1,0:T(8,128)(2,1)S(1)}, u32[]{:S(2)}, u32[]{:S(2)}) collective-permute-start(bf16[1,128,128]{2,1,0:T(8,128)(2,1)S(1)} %get-tuple-element.6), channel_id=1, source_target_pairs={{0,2},{2,4},{4,6},{6,8},{8,10},{10,12},{12,14},{14,16},{16,18},{18... | collective-permute-start | bytes 98312 | tf_op jit(solution)/shard_map/ppermute | solution.py:224
  24.8 0.8 %collective-permute-done.2.far_ref = bf16[1,128,128]{2,1,0:T(8,128)(2,1)S(1)} collective-permute-done((bf16[1,128,128]{2,1,0:T(8,128)(2,1)S(1)}, bf16[1,128,128]{2,1,0:T(8,128)(2,1)S(1)}, u32[]{:S(2)}, u32[]{:S(2)}) %collective-permute-start.2) | collective-permute-done | bytes 32800 | tf_op jit(solution)/shard_map/ppermute | solution.py:225
  25.6 3.4 %collective-permute-done.1.near_ref = bf16[1,128,128]{2,1,0:T(8,128)(2,1)S(1)} collective-permute-done((bf16[1,128,128]{2,1,0:T(8,128)(2,1)S(1)}, bf16[1,128,128]{2,1,0:T(8,128)(2,1)S(1)}, u32[]{:S(2)}, u32[]{:S(2)}) %collective-permute-start.1) | collective-permute-done | bytes 32800 | tf_op jit(solution)/shard_map/ppermute | solution.py:224
  29.1 0.0 collective-permute-done.peer_ref
  29.1 0.0 collective-permute-done.4.w_core_ref
  29.1 0.0 copy-done
  29.1 0.0 copy-done.3
  29.1 0.0 copy-done.2
  29.1 0.0 copy-start.1
  29.1 1.2 %copy-done.1 = bf16[27,128,128]{2,1,0:T(8,128)(2,1)S(1)} copy-done((bf16[27,128,128]{2,1,0:T(8,128)(2,1)S(1)}, bf16[27,128,128]{2,1,0:T(8,128)(2,1)}, u32[]{:S(2)}) %copy-start.1) | copy-done | bytes 884760
  30.3 7.5 %shard_map.55 = bf16[128,2,8,256]{3,2,1,0:T(8,128)(2,1)} custom-call(bf16[8,128,128]{2,1,0:T(8,128)(2,1)S(1)} %bitcast.15, bf16[5,128,128]{2,1,0:T(8,128)(2,1)} %collective-permute-done.peer_ref, bf16[1,128,128]{2,1,0:T(8,128)(2,1)S(1)} %collective-permute-done.1.near_ref, bf16[1,128,128]{2,1,0:T(8,128)(2,1)S(1)} %collective-permute-done.2.far_ref, ...), custom_call_target="tpu_custom_call" | custom-call | tf_op jit(solution)/shard_map/pallas_call | solution.py:182
  (1 shorter events, 0.0 us)
Async XLA Ops:
  0.0 29.1 %copy-start = (bf16[64,64,256]{2,1,0:T(8,128)(2,1)S(1)}, bf16[64,64,256]{2,1,0:T(8,128)(2,1)}, u32[]{:S(2)}) copy-start(bf16[64,64,256]{2,1,0:T(8,128)(2,1)} %w_own_ref.1) | copy-start | bytes 6291460
  0.0 29.1 %copy-start.3 = (f32[128]{0:T(128)S(1)}, f32[128]{0:T(128)}, u32[]{:S(2)}) copy-start(f32[128]{0:T(128)} %param.9) | copy-start | bytes 1540
  0.0 29.1 %copy-start.2 = (f32[128]{0:T(128)S(1)}, f32[128]{0:T(128)}, u32[]{:S(2)}) copy-start(f32[128]{0:T(128)} %param.7) | copy-start | bytes 1540
  1.3 12.9 %collective-permute-start.3 = (bf16[16,64,256]{2,1,0:T(8,128)(2,1)S(1)}, bf16[16,64,256]{2,1,0:T(8,128)(2,1)S(1)}, u32[]{:S(2)}, u32[]{:S(2)}) collective-permute-start(bf16[16,64,256]{2,1,0:T(8,128)(2,1)S(1)} %constant_dynamic-slice_fusion), channel_id=1, source_target_pairs={{0,1},{1,0},{2,3},{3,2},{4,5},{5,4},{6,7},{7,6},{8,9},{9,8},{10,11... | collective-permute-start | bytes 1572872 | tf_op jit(solution)/shard_map/ppermute | solution.py:216
  14.1 14.9 %collective-permute-start.4 = (bf16[16,64,256]{2,1,0:T(8,128)(2,1)S(1)}, bf16[16,64,256]{2,1,0:T(8,128)(2,1)S(1)}, u32[]{:S(2)}, u32[]{:S(2)}) collective-permute-start(bf16[16,64,256]{2,1,0:T(8,128)(2,1)S(1)} %collective-permute-done.3.w_peer_ref), channel_id=1, source_target_pairs={{0,2},{1,3},{2,0},{3,1},{4,6},{5,7},{6,4},{7,5},{8,10},{9,11},{10,... | collective-permute-start | bytes 1572872 | tf_op jit(solution)/shard_map/ppermute | solution.py:217
  17.4 11.7 %collective-permute-start = (bf16[5,128,128]{2,1,0:T(8,128)(2,1)}, bf16[5,128,128]{2,1,0:T(8,128)(2,1)}, u32[]{:S(2)}, u32[]{:S(2)}) collective-permute-start(bf16[5,128,128]{2,1,0:T(8,128)(2,1)} %bitcast.14), channel_id=1, source_target_pairs={{0,1},{1,0},{2,3},{3,2},{4,5},{5,4},{6,7},{7,6},{8,9},{9,8},{10,11... | collective-permute-start | bytes 491528 | tf_op jit(solution)/shard_map/ppermute | solution.py:221
  18.6 7.0 %collective-permute-start.2 = (bf16[1,128,128]{2,1,0:T(8,128)(2,1)S(1)}, bf16[1,128,128]{2,1,0:T(8,128)(2,1)S(1)}, u32[]{:S(2)}, u32[]{:S(2)}) collective-permute-start(bf16[1,128,128]{2,1,0:T(8,128)(2,1)S(1)} %get-tuple-element.5), channel_id=1, source_target_pairs={{1,2},{3,4},{5,6},{7,8},{9,10},{11,12},{13,14},{15,16},{17,18},{19... | collective-permute-start | bytes 98312 | tf_op jit(solution)/shard_map/ppermute | solution.py:225
  22.9 6.1 %collective-permute-start.1 = (bf16[1,128,128]{2,1,0:T(8,128)(2,1)S(1)}, bf16[1,128,128]{2,1,0:T(8,128)(2,1)S(1)}, u32[]{:S(2)}, u32[]{:S(2)}) collective-permute-start(bf16[1,128,128]{2,1,0:T(8,128)(2,1)S(1)} %get-tuple-element.6), channel_id=1, source_target_pairs={{0,2},{2,4},{4,6},{6,8},{8,10},{10,12},{12,14},{14,16},{16,18},{18... | collective-permute-start | bytes 98312 | tf_op jit(solution)/shard_map/ppermute | solution.py:224
  29.1 1.2 %copy-start.1 = (bf16[27,128,128]{2,1,0:T(8,128)(2,1)S(1)}, bf16[27,128,128]{2,1,0:T(8,128)(2,1)}, u32[]{:S(2)}) copy-start(bf16[27,128,128]{2,1,0:T(8,128)(2,1)} %w_conv_ref.1) | copy-start | bytes 2654212
where the time goes:
time: 38.1 us; the launch traced here: 37.8 us
  waiting for transfers between devices  16.8 us (44%)
  starting transfers between devices  8.29 us (22%)
  Pallas kernels  7.53 us (20%)
  local copies, waits for them, and re-layouts  5.11 us (13%)
    ppermute x1, waiting for transfers between devices, paired(): w_peer = lax.ppermute(w_mine, AXES, across)  12.6 us
    pallas_call x1, Pallas kernels, run(): pl.pallas_call(kernel, out_shape=jax.ShapeDtypeStruct((cout, 2, rows, 2 *...  7.53 us
    ppermute x1, starting transfers between devices, paired(): far = lax.ppermute(edge_far, AXES, down_far + up_far)  4.3 us
    ppermute x1, waiting for transfers between devices, paired(): near = lax.ppermute(edge_near, AXES, down + up)  3.41 us
    unnamed x9, local copies, waits for them, and re-layouts  2.16 us
    ppermute x1, starting transfers between devices, paired(): near = lax.ppermute(edge_near, AXES, down + up)  1.92 us
    another operation x2, local copies, waits for them, and re-layouts  1.71 us
    ppermute x1, starting transfers between devices, paired(): w_core = lax.ppermute(w_peer, AXES, cores)  1.55 us
  transfers between devices with their start and end apart: 5, of which 3 were waited for; matrix products, arithmetic and copies ran while one was open for 7% of the time, Pallas kernels for 0%

commit v1 on v0

--- a/solution.py
+++ b/solution.py
@@ -121,22 +121,29 @@
 
 
 def paired_kernel(
-    own_ref, peer_ref, near_ref, far_ref, w_own_ref, w_peer_ref, w_core_ref,
+    own_ref, peer_ref, near_ref, far_ref, w_own_ref, w_y_ref, w_y_core_ref, w_x_ref, w_x_core_ref,
     b_up_ref, w_conv_ref, b_conv_ref, out_ref, x_ref, w_ref, u_ref, total_ref, sems,
 ):
     s, c = position()
-    core = lax.rem(s, 2)
     part, cout = w_own_ref.shape[1], out_ref.shape[0]
 
-    def rows_of(plane, half):
-        return pl.ds(pl.multiple_of(plane * cout + half * part, part), part)
+    def taps_of(plane, half, first, count):
+        place = pl.multiple_of(plane * cout + half * part, part)
+        return w_ref.at[pl.ds(first, count), pl.ds(place, part)]
 
     copies = [
-        pltpu.make_async_copy(w_own_ref.at[pl.ds(16, 16)], w_ref.at[:, rows_of(0, c)], sems.at[0]),
-        pltpu.make_async_copy(w_own_ref.at[pl.ds(32, 16)], w_ref.at[:, rows_of(1, c)], sems.at[1]),
-        pltpu.make_async_copy(w_peer_ref, w_ref.at[:, rows_of(core, 1 - c)], sems.at[2]),
-        pltpu.make_async_copy(w_core_ref, w_ref.at[:, rows_of(1 - core, 1 - c)], sems.at[3]),
+        pltpu.make_async_copy(
+            w_own_ref.at[pl.ds(16 + 16 * plane, 16)], taps_of(plane, c, 0, 16), sems.at[plane]
+        )
+        for plane in (0, 1)
     ]
+    me = lax.rem(s, 4)
+    x, core = me // 2, lax.rem(me, 2)
+    parts = ((w_y_ref, x, core), (w_y_core_ref, x, 1 - core), (w_x_ref, 1 - x, core), (w_x_core_ref, 1 - x, 1 - core))
+    for number, (part_ref, plane, side) in enumerate(parts):
+        copies.append(
+            pltpu.make_async_copy(part_ref, taps_of(plane, 1 - c, 8 * side, 8), sems.at[2 + number])
+        )
     for copy in copies:
         copy.start()
     chans = own_ref.shape[1]
@@ -189,7 +196,7 @@
             pltpu.VMEM((16, 2 * cout, cin), jnp.bfloat16),
             pltpu.VMEM((4, rows + 2, 2 * cout, cols), jnp.bfloat16),
             pltpu.VMEM((2, 2 * cout * rows, cols), jnp.float32),
-            pltpu.SemaphoreType.DMA((4,)),
+            pltpu.SemaphoreType.DMA((6,)),
         ],
         compiler_params=pltpu.CompilerParams(vmem_limit_bytes=48 * 2**20),
     )(*operands)
@@ -198,7 +205,6 @@
 def paired(inputs, w_up, b_up, w_conv, b_conv, sizes):
     spaces = lax.axis_size("space")
     s, c = position()
-    core = lax.rem(s, 2)
     held = inputs.shape[2]
     share = held // 2 + 1
 
@@ -207,24 +213,30 @@
 
     across = [(at(i, j), at(i, 1 - j)) for i in range(spaces) for j in (0, 1)]
     cores = [(at(i, j), at(i ^ 1, j)) for i in range(spaces) for j in (0, 1)]
+    pairs = [(at(i, j), at(i ^ 2, j)) for i in range(spaces) for j in (0, 1)]
     down = [(at(i - 1, 0), at(i, 0)) for i in range(1, spaces)]
     up = [(at(i + 1, 1), at(i, 1)) for i in range(spaces - 1)]
     down_far = [(at(i - 1, 1), at(i, 0)) for i in range(1, spaces)]
     up_far = [(at(i + 1, 0), at(i, 1)) for i in range(spaces - 1)]
 
-    w_mine = lax.dynamic_slice_in_dim(w_up, 16 + 16 * core, 16, 0)
-    w_peer = lax.ppermute(w_mine, AXES, across)
-    w_core = lax.ppermute(w_peer, AXES, cores)
+    quarter = 8 * lax.rem(s, 4)
+    w_y = lax.ppermute(lax.dynamic_slice_in_dim(w_up, 16 + quarter, 8, 0), AXES, across)
 
     rows = inputs[:, 0].transpose(1, 0, 2)
     wanted = lax.dynamic_slice_in_dim(rows, (1 - c) * (held - share), share, 0)
-    peer = lax.ppermute(wanted, AXES, across)
     edge_near = lax.dynamic_slice_in_dim(rows, (1 - c) * (held - 1), 1, 0)
     edge_far = lax.dynamic_slice_in_dim(rows, c * (held - 1), 1, 0)
+    w_y, wanted, edge_near, edge_far = lax.optimization_barrier((w_y, wanted, edge_near, edge_far))
+    w_x = lax.ppermute(w_y, AXES, pairs)
+    peer = lax.ppermute(wanted, AXES, across)
     near = lax.ppermute(edge_near, AXES, down + up)
     far = lax.ppermute(edge_far, AXES, down_far + up_far)
-    operands = (rows, peer, near, far, w_up, w_peer, w_core, b_up[None], w_conv, b_conv[None])
-    places = ("vmem",) * 4 + ("any",) * 3 + ("vmem",) * 3
+    w_y_core = lax.ppermute(w_y, AXES, cores)
+    w_x, w_y_core, peer, near, far = lax.optimization_barrier((w_x, w_y_core, peer, near, far))
+    w_x_core = lax.ppermute(w_x, AXES, cores)
+    w_parts = (w_y, w_y_core, w_x, w_x_core)
+    operands = (rows, peer, near, far, w_up, *w_parts, b_up[None], w_conv, b_conv[None])
+    places = ("vmem",) * 4 + ("any",) * 5 + ("vmem",) * 3
     return run(paired_kernel, places, operands, sizes)
 
 
@@ -247,7 +259,7 @@
 def local(inputs, w_up, b_up, w_conv, b_conv):
     chs = lax.axis_size("ch")
     sizes = (w_up.shape[2], w_conv.shape[1], 2 * inputs.shape[2] // chs, inputs.shape[3])
-    plan = paired if chs == 2 and lax.axis_size("space") % 2 == 0 else gathered
+    plan = paired if chs == 2 and lax.axis_size("space") % 4 == 0 else gathered
     return plan(inputs, w_up, b_up, w_conv, b_conv, sizes)
 
 

time: 38.1 us -> 31.2 us (0.82)
  the two profiles are of different devices: /device:TPU:23 before, /device:TPU:9 now
where the time goes in v1:
time: 31.2 us; the launch traced here: 31 us
  starting transfers between devices  11.6 us (37%)
  waiting for transfers between devices  8.33 us (27%)
  Pallas kernels  6.67 us (21%)
  local copies, waits for them, and re-layouts  4.34 us (14%)
    pallas_call x1, Pallas kernels, run(): pl.pallas_call(kernel, out_shape=jax.ShapeDtypeStruct((cout, 2, rows, 2 *...  6.67 us
    ppermute x1, waiting for transfers between devices, paired(): lax.ppermute(lax.dynamic_slice_in_dim(w_up, 16 + quarter, 8, 0), AXES, ac...  3.86 us
    ppermute x1, waiting for transfers between devices, paired(): far = lax.ppermute(edge_far, AXES, down_far + up_far)  2.64 us
    ppermute x1, starting transfers between devices, paired(): near = lax.ppermute(edge_near, AXES, down + up)  2.6 us
    unnamed x9, local copies, waits for them, and re-layouts  2.16 us
    ppermute x1, starting transfers between devices, paired(): far = lax.ppermute(edge_far, AXES, down_far + up_far)  1.92 us
    ppermute x1, starting transfers between devices, paired(): w_x_core = lax.ppermute(w_x, AXES, cores)  1.74 us
    ppermute x1, starting transfers between devices, paired(): w_y_core = lax.ppermute(w_y, AXES, cores)  1.55 us
  transfers between devices with their start and end apart: 7, of which 4 were waited for; matrix products, arithmetic and copies ran while one was open for 7% of the time, Pallas kernels for 0%

profile of v1, /device:TPU:9, one launch (start us, length us, event | category | flops | bytes accessed | tf_op | source)
XLA Modules:
  0.0 31.0 jit_solution(10126536990798932376)
XLA Ops:
  0.0 0.0 copy-start
  0.0 0.0 copy-start.3
  0.0 0.0 copy-start.2
  0.0 1.1 %constant_dynamic-slice_fusion.1 = bf16[8,64,256]{2,1,0:T(8,128)(2,1)S(1)} fusion(bf16[64,64,256]{2,1,0:T(8,128)(2,1)} %w_own_ref.1, s32[]{:T(128)S(6)} %select_n.12), kind=kLoop, calls=%fused_computation.4 | loop fusion | bytes 524292 | tf_op jit(solution)/shard_map/dynamic_slice | solution.py:223
  1.1 1.3 %collective-permute-start = (bf16[8,64,256]{2,1,0:T(8,128)(2,1)S(1)}, bf16[8,64,256]{2,1,0:T(8,128)(2,1)S(1)}, u32[]{:S(2)}, u32[]{:S(2)}) collective-permute-start(bf16[8,64,256]{2,1,0:T(8,128)(2,1)S(1)} %constant_dynamic-slice_fusion.1), channel_id=1, source_target_pairs={{0,1},{1,0},{2,3},{3,2},{4,5},{5,4},{6,7},{7,6},{8,9},{9,8},{10,11... | collective-permute-start | bytes 786440 | tf_op jit(solution)/shard_map/ppermute | solution.py:223
  2.4 1.0 %copy.16 = bf16[128,1,8,128]{3,0,2,1:T(8,128)(2,1)S(1)} copy(bf16[128,1,8,128]{3,2,1,0:T(8,128)(2,1)} %param.5) | data formatting | bytes 524288 | tf_op args[0]
  3.4 1.0 %constant_dynamic-slice_fusion = bf16[128,1,5,128]{3,2,1,0:T(8,128)(2,1)S(1)} fusion(bf16[128,1,8,128]{3,2,1,0:T(8,128)(2,1)} %param.5, s32[]{:T(128)S(6)} %select_n.13), kind=kLoop, calls=%fused_computation.3 | loop fusion | bytes 327684 | tf_op jit(solution)/shard_map/dynamic-slice.3
  4.5 3.9 %collective-permute-done.w_y_ref = bf16[8,64,256]{2,1,0:T(8,128)(2,1)S(1)} collective-permute-done((bf16[8,64,256]{2,1,0:T(8,128)(2,1)S(1)}, bf16[8,64,256]{2,1,0:T(8,128)(2,1)S(1)}, u32[]{:S(2)}, u32[]{:S(2)}) %collective-permute-start) | collective-permute-done | bytes 262176 | tf_op jit(solution)/shard_map/ppermute | solution.py:223
  8.4 1.5 %collective-permute-start.2 = (bf16[8,64,256]{2,1,0:T(8,128)(2,1)S(1)}, bf16[8,64,256]{2,1,0:T(8,128)(2,1)S(1)}, u32[]{:S(2)}, u32[]{:S(2)}) collective-permute-start(bf16[8,64,256]{2,1,0:T(8,128)(2,1)S(1)} %collective-permute-done.w_y_ref), channel_id=1, source_target_pairs={{0,2},{1,3},{2,0},{3,1},{4,6},{5,7},{6,4},{7,5},{8,10},{9,11},{10,... | collective-permute-start | bytes 786440 | tf_op jit(solution)/shard_map/ppermute | solution.py:234
  9.9 1.2 %collective-permute-start.1 = (bf16[8,64,256]{2,1,0:T(8,128)(2,1)S(1)}, bf16[8,64,256]{2,1,0:T(8,128)(2,1)S(1)}, u32[]{:S(2)}, u32[]{:S(2)}) collective-permute-start(bf16[8,64,256]{2,1,0:T(8,128)(2,1)S(1)} %collective-permute-done.w_y_ref), channel_id=1, source_target_pairs={{0,4},{1,5},{2,6},{3,7},{4,0},{5,1},{6,2},{7,3},{8,12},{9,13},{10,... | collective-permute-start | bytes 786440 | tf_op jit(solution)/shard_map/ppermute | solution.py:230
  11.1 1.2 %collective-permute-start.3 = (bf16[5,128,128]{2,1,0:T(8,128)(2,1)S(1)}, bf16[5,128,128]{2,1,0:T(8,128)(2,1)S(1)}, u32[]{:S(2)}, u32[]{:S(2)}) collective-permute-start(bf16[5,128,128]{2,1,0:T(8,128)(2,1)S(1)} %bitcast.18), channel_id=1, source_target_pairs={{0,1},{1,0},{2,3},{3,2},{4,5},{5,4},{6,7},{7,6},{8,9},{9,8},{10,11... | collective-permute-start | bytes 491528 | tf_op jit(solution)/shard_map/ppermute | solution.py:231
  12.4 2.6 %collective-permute-start.4 = (bf16[1,128,128]{2,1,0:T(8,128)(2,1)S(1)}, bf16[1,128,128]{2,1,0:T(8,128)(2,1)S(1)}, u32[]{:S(2)}, u32[]{:S(2)}) collective-permute-start(bf16[1,128,128]{2,1,0:T(8,128)(2,1)S(1)} %get-tuple-element.16), channel_id=1, source_target_pairs={{0,2},{2,4},{4,6},{6,8},{8,10},{10,12},{12,14},{14,16},{16,18},{18... | collective-permute-start | bytes 98312 | tf_op jit(solution)/shard_map/ppermute | solution.py:232
  15.0 1.9 %collective-permute-start.5 = (bf16[1,128,128]{2,1,0:T(8,128)(2,1)S(1)}, bf16[1,128,128]{2,1,0:T(8,128)(2,1)S(1)}, u32[]{:S(2)}, u32[]{:S(2)}) collective-permute-start(bf16[1,128,128]{2,1,0:T(8,128)(2,1)S(1)} %get-tuple-element.17), channel_id=1, source_target_pairs={{1,2},{3,4},{5,6},{7,8},{9,10},{11,12},{13,14},{15,16},{17,18},{19... | collective-permute-start | bytes 98312 | tf_op jit(solution)/shard_map/ppermute | solution.py:233
  16.9 0.7 %collective-permute-done.4.near_ref = bf16[1,128,128]{2,1,0:T(8,128)(2,1)S(1)} collective-permute-done((bf16[1,128,128]{2,1,0:T(8,128)(2,1)S(1)}, bf16[1,128,128]{2,1,0:T(8,128)(2,1)S(1)}, u32[]{:S(2)}, u32[]{:S(2)}) %collective-permute-start.4) | collective-permute-done | bytes 32800 | tf_op jit(solution)/shard_map/ppermute | solution.py:232
  17.6 2.6 %collective-permute-done.5.far_ref = bf16[1,128,128]{2,1,0:T(8,128)(2,1)S(1)} collective-permute-done((bf16[1,128,128]{2,1,0:T(8,128)(2,1)S(1)}, bf16[1,128,128]{2,1,0:T(8,128)(2,1)S(1)}, u32[]{:S(2)}, u32[]{:S(2)}) %collective-permute-start.5) | collective-permute-done | bytes 32800 | tf_op jit(solution)/shard_map/ppermute | solution.py:233
  20.2 0.0 collective-permute-done.3.peer_ref
  20.2 0.0 collective-permute-done.2.w_y_core_ref
  20.2 0.0 collective-permute-done.1.w_x_ref
  20.2 1.7 %collective-permute-start.6 = (bf16[8,64,256]{2,1,0:T(8,128)(2,1)S(1)}, bf16[8,64,256]{2,1,0:T(8,128)(2,1)S(1)}, u32[]{:S(2)}, u32[]{:S(2)}) collective-permute-start(bf16[8,64,256]{2,1,0:T(8,128)(2,1)S(1)} %collective-permute-done.1.w_x_ref), channel_id=1, source_target_pairs={{0,2},{1,3},{2,0},{3,1},{4,6},{5,7},{6,4},{7,5},{8,10},{9,11},{10,... | collective-permute-start | bytes 786440 | tf_op jit(solution)/shard_map/ppermute | solution.py:236
  22.0 1.2 %collective-permute-done.6.w_x_core_ref = bf16[8,64,256]{2,1,0:T(8,128)(2,1)S(1)} collective-permute-done((bf16[8,64,256]{2,1,0:T(8,128)(2,1)S(1)}, bf16[8,64,256]{2,1,0:T(8,128)(2,1)S(1)}, u32[]{:S(2)}, u32[]{:S(2)}) %collective-permute-start.6) | collective-permute-done | bytes 262176 | tf_op jit(solution)/shard_map/ppermute | solution.py:236
  23.1 0.0 copy-done
  23.1 0.0 copy-done.3
  23.1 0.0 copy-done.2
  23.1 0.0 copy-start.1
  23.1 1.2 %copy-done.1 = bf16[27,128,128]{2,1,0:T(8,128)(2,1)S(1)} copy-done((bf16[27,128,128]{2,1,0:T(8,128)(2,1)S(1)}, bf16[27,128,128]{2,1,0:T(8,128)(2,1)}, u32[]{:S(2)}) %copy-start.1) | copy-done | bytes 884760
  24.3 6.7 %shard_map.55 = bf16[128,2,8,256]{3,2,1,0:T(8,128)(2,1)} custom-call(bf16[8,128,128]{2,1,0:T(8,128)(2,1)S(1)} %bitcast.15, bf16[5,128,128]{2,1,0:T(8,128)(2,1)S(1)} %collective-permute-done.3.peer_ref, bf16[1,128,128]{2,1,0:T(8,128)(2,1)S(1)} %collective-permute-done.4.near_ref, bf16[1,128,128]{2,1,0:T(8,128)(2,1)S(1)} %collective-permute-done.5.far_ref, ...), custom_call_target="tpu_custom_call" | custom-call | tf_op jit(solution)/shard_map/pallas_call | solution.py:189
  (2 shorter events, 0.0 us)
Async XLA Ops:
  0.0 23.1 %copy-start = (bf16[64,64,256]{2,1,0:T(8,128)(2,1)S(1)}, bf16[64,64,256]{2,1,0:T(8,128)(2,1)}, u32[]{:S(2)}) copy-start(bf16[64,64,256]{2,1,0:T(8,128)(2,1)} %w_own_ref.1) | copy-start | bytes 6291460
  0.0 23.1 %copy-start.3 = (f32[128]{0:T(128)S(1)}, f32[128]{0:T(128)}, u32[]{:S(2)}) copy-start(f32[128]{0:T(128)} %param.9) | copy-start | bytes 1540
  0.0 23.1 %copy-start.2 = (f32[128]{0:T(128)S(1)}, f32[128]{0:T(128)}, u32[]{:S(2)}) copy-start(f32[128]{0:T(128)} %param.7) | copy-start | bytes 1540
  1.1 7.2 %collective-permute-start = (bf16[8,64,256]{2,1,0:T(8,128)(2,1)S(1)}, bf16[8,64,256]{2,1,0:T(8,128)(2,1)S(1)}, u32[]{:S(2)}, u32[]{:S(2)}) collective-permute-start(bf16[8,64,256]{2,1,0:T(8,128)(2,1)S(1)} %constant_dynamic-slice_fusion.1), channel_id=1, source_target_pairs={{0,1},{1,0},{2,3},{3,2},{4,5},{5,4},{6,7},{7,6},{8,9},{9,8},{10,11... | collective-permute-start | bytes 786440 | tf_op jit(solution)/shard_map/ppermute | solution.py:223
  8.4 11.8 %collective-permute-start.2 = (bf16[8,64,256]{2,1,0:T(8,128)(2,1)S(1)}, bf16[8,64,256]{2,1,0:T(8,128)(2,1)S(1)}, u32[]{:S(2)}, u32[]{:S(2)}) collective-permute-start(bf16[8,64,256]{2,1,0:T(8,128)(2,1)S(1)} %collective-permute-done.w_y_ref), channel_id=1, source_target_pairs={{0,2},{1,3},{2,0},{3,1},{4,6},{5,7},{6,4},{7,5},{8,10},{9,11},{10,... | collective-permute-start | bytes 786440 | tf_op jit(solution)/shard_map/ppermute | solution.py:234
  9.9 10.3 %collective-permute-start.1 = (bf16[8,64,256]{2,1,0:T(8,128)(2,1)S(1)}, bf16[8,64,256]{2,1,0:T(8,128)(2,1)S(1)}, u32[]{:S(2)}, u32[]{:S(2)}) collective-permute-start(bf16[8,64,256]{2,1,0:T(8,128)(2,1)S(1)} %collective-permute-done.w_y_ref), channel_id=1, source_target_pairs={{0,4},{1,5},{2,6},{3,7},{4,0},{5,1},{6,2},{7,3},{8,12},{9,13},{10,... | collective-permute-start | bytes 786440 | tf_op jit(solution)/shard_map/ppermute | solution.py:230
  11.1 9.1 %collective-permute-start.3 = (bf16[5,128,128]{2,1,0:T(8,128)(2,1)S(1)}, bf16[5,128,128]{2,1,0:T(8,128)(2,1)S(1)}, u32[]{:S(2)}, u32[]{:S(2)}) collective-permute-start(bf16[5,128,128]{2,1,0:T(8,128)(2,1)S(1)} %bitcast.18), channel_id=1, source_target_pairs={{0,1},{1,0},{2,3},{3,2},{4,5},{5,4},{6,7},{7,6},{8,9},{9,8},{10,11... | collective-permute-start | bytes 491528 | tf_op jit(solution)/shard_map/ppermute | solution.py:231
  12.4 5.2 %collective-permute-start.4 = (bf16[1,128,128]{2,1,0:T(8,128)(2,1)S(1)}, bf16[1,128,128]{2,1,0:T(8,128)(2,1)S(1)}, u32[]{:S(2)}, u32[]{:S(2)}) collective-permute-start(bf16[1,128,128]{2,1,0:T(8,128)(2,1)S(1)} %get-tuple-element.16), channel_id=1, source_target_pairs={{0,2},{2,4},{4,6},{6,8},{8,10},{10,12},{12,14},{14,16},{16,18},{18... | collective-permute-start | bytes 98312 | tf_op jit(solution)/shard_map/ppermute | solution.py:232
  15.0 5.2 %collective-permute-start.5 = (bf16[1,128,128]{2,1,0:T(8,128)(2,1)S(1)}, bf16[1,128,128]{2,1,0:T(8,128)(2,1)S(1)}, u32[]{:S(2)}, u32[]{:S(2)}) collective-permute-start(bf16[1,128,128]{2,1,0:T(8,128)(2,1)S(1)} %get-tuple-element.17), channel_id=1, source_target_pairs={{1,2},{3,4},{5,6},{7,8},{9,10},{11,12},{13,14},{15,16},{17,18},{19... | collective-permute-start | bytes 98312 | tf_op jit(solution)/shard_map/ppermute | solution.py:233
  20.2 2.9 %collective-permute-start.6 = (bf16[8,64,256]{2,1,0:T(8,128)(2,1)S(1)}, bf16[8,64,256]{2,1,0:T(8,128)(2,1)S(1)}, u32[]{:S(2)}, u32[]{:S(2)}) collective-permute-start(bf16[8,64,256]{2,1,0:T(8,128)(2,1)S(1)} %collective-permute-done.1.w_x_ref), channel_id=1, source_target_pairs={{0,2},{1,3},{2,0},{3,1},{4,6},{5,7},{6,4},{7,5},{8,10},{9,11},{10,... | collective-permute-start | bytes 786440 | tf_op jit(solution)/shard_map/ppermute | solution.py:236
  23.1 1.2 %copy-start.1 = (bf16[27,128,128]{2,1,0:T(8,128)(2,1)S(1)}, bf16[27,128,128]{2,1,0:T(8,128)(2,1)}, u32[]{:S(2)}) copy-start(bf16[27,128,128]{2,1,0:T(8,128)(2,1)} %w_conv_ref.1) | copy-start | bytes 2654212

commit v2 on v1

--- a/solution.py
+++ b/solution.py
@@ -22,7 +22,7 @@
     return jnp.where(place == edge, 0.0, pltpu.roll(value, step % cols, 1))
 
 
-def compute(x_ref, w_ref, b_up_ref, w_conv_ref, b_conv_ref, out_ref, u_ref, total_ref, first, last):
+def compute(x_ref, w_ref, b_up_ref, late, w_conv_ref, b_conv_ref, out_ref, u_ref, total_ref, first, last):
     rows = out_ref.shape[2]
     cout = out_ref.shape[0]
     cols = x_ref.shape[3]
@@ -59,6 +59,7 @@
                     moved = shifted(value, -1 if col_phase == 0 else 1)
                     u_ref[2 + col_phase, row] = moved.astype(jnp.bfloat16)
 
+    late.wait()
     bias = column_of(b_conv_ref[...])
     bias = jnp.concatenate([bias, bias], axis=0)
     source = lax.broadcasted_iota(jnp.int32, (2 * cols, 2 * cols), 0)
@@ -121,9 +122,9 @@
 
 
 def paired_kernel(
-    own_ref, peer_ref, near_ref, far_ref, w_own_ref, w_y_ref, w_y_core_ref, w_x_ref, w_x_core_ref,
-    b_up_ref, w_conv_ref, b_conv_ref, out_ref, x_ref, w_ref, u_ref, total_ref, sems,
+    own_ref, peer_ref, near_ref, far_ref, w_own_ref, *refs,
 ):
+    *part_refs, b_up_ref, w_conv_ref, b_conv_ref, out_ref, x_ref, w_ref, v_ref, u_ref, total_ref, sems = refs
     s, c = position()
     part, cout = w_own_ref.shape[1], out_ref.shape[0]
 
@@ -139,12 +140,13 @@
     ]
     me = lax.rem(s, 4)
     x, core = me // 2, lax.rem(me, 2)
-    parts = ((w_y_ref, x, core), (w_y_core_ref, x, 1 - core), (w_x_ref, 1 - x, core), (w_x_core_ref, 1 - x, 1 - core))
-    for number, (part_ref, plane, side) in enumerate(parts):
-        copies.append(
-            pltpu.make_async_copy(part_ref, taps_of(plane, 1 - c, 8 * side, 8), sems.at[2 + number])
-        )
-    for copy in copies:
+    sources = ((x, core), (x, 1 - core), (1 - x, core), (1 - x, 1 - core))
+    for number, part_ref in enumerate(part_refs):
+        plane, side = sources[number // 2]
+        place = taps_of(plane, 1 - c, 8 * side + 4 * (number % 2), 4)
+        copies.append(pltpu.make_async_copy(part_ref, place, sems.at[2 + number]))
+    late = pltpu.make_async_copy(w_conv_ref, v_ref, sems.at[10])
+    for copy in copies + [late]:
         copy.start()
     chans = own_ref.shape[1]
     share = peer_ref.shape[0]
@@ -158,11 +160,11 @@
         copy.wait()
     first = (s == 0) & (c == 0)
     last = (s == lax.axis_size("space") - 1) & (c == 1)
-    compute(x_ref, w_ref, b_up_ref, w_conv_ref, b_conv_ref, out_ref, u_ref, total_ref, first, last)
+    compute(x_ref, w_ref, b_up_ref, late, v_ref, b_conv_ref, out_ref, u_ref, total_ref, first, last)
 
 
 def gathered_kernel(
-    rows_ref, w_all_ref, b_up_ref, w_conv_ref, b_conv_ref, out_ref, x_ref, w_ref, u_ref, total_ref, sems
+    rows_ref, w_all_ref, b_up_ref, w_conv_ref, b_conv_ref, out_ref, x_ref, w_ref, v_ref, u_ref, total_ref, sems
 ):
     s, c = position()
     cout = out_ref.shape[0]
@@ -172,7 +174,8 @@
         )
         for plane in (0, 1)
     ]
-    for copy in copies:
+    late = pltpu.make_async_copy(w_conv_ref, v_ref, sems.at[10])
+    for copy in copies + [late]:
         copy.start()
     for slot in range(rows_ref.shape[0]):
         store_row(x_ref, slot, 0, rows_ref[slot])
@@ -180,12 +183,12 @@
         copy.wait()
     first = (s == 0) & (c == 0)
     last = (s == lax.axis_size("space") - 1) & (c == lax.axis_size("ch") - 1)
-    compute(x_ref, w_ref, b_up_ref, w_conv_ref, b_conv_ref, out_ref, u_ref, total_ref, first, last)
+    compute(x_ref, w_ref, b_up_ref, late, v_ref, b_conv_ref, out_ref, u_ref, total_ref, first, last)
 
 
 def run(kernel, spaces, operands, sizes):
     cin, cout, rows, cols = sizes
-    spec = {"vmem": pl.BlockSpec(memory_space=pltpu.VMEM), "any": pl.BlockSpec(memory_space=pl.ANY)}
+    spec = {"vmem": pl.BlockSpec(memory_space=pltpu.VMEM), "any": pl.BlockSpec(memory_space=pl.ANY), "hbm": pl.BlockSpec(memory_space=pltpu.HBM)}
     return pl.pallas_call(
         kernel,
         out_shape=jax.ShapeDtypeStruct((cout, 2, rows, 2 * cols), jnp.bfloat16),
@@ -194,9 +197,10 @@
         scratch_shapes=[
             pltpu.VMEM((3, rows // 2 + 2, cin, cols), jnp.bfloat16),
             pltpu.VMEM((16, 2 * cout, cin), jnp.bfloat16),
+            pltpu.VMEM((27, cout, cout), jnp.bfloat16),
             pltpu.VMEM((4, rows + 2, 2 * cout, cols), jnp.bfloat16),
             pltpu.VMEM((2, 2 * cout * rows, cols), jnp.float32),
-            pltpu.SemaphoreType.DMA((6,)),
+            pltpu.SemaphoreType.DMA((11,)),
         ],
         compiler_params=pltpu.CompilerParams(vmem_limit_bytes=48 * 2**20),
     )(*operands)
@@ -214,29 +218,36 @@
     across = [(at(i, j), at(i, 1 - j)) for i in range(spaces) for j in (0, 1)]
     cores = [(at(i, j), at(i ^ 1, j)) for i in range(spaces) for j in (0, 1)]
     pairs = [(at(i, j), at(i ^ 2, j)) for i in range(spaces) for j in (0, 1)]
-    down = [(at(i - 1, 0), at(i, 0)) for i in range(1, spaces)]
-    up = [(at(i + 1, 1), at(i, 1)) for i in range(spaces - 1)]
-    down_far = [(at(i - 1, 1), at(i, 0)) for i in range(1, spaces)]
-    up_far = [(at(i + 1, 0), at(i, 1)) for i in range(spaces - 1)]
-
-    quarter = 8 * lax.rem(s, 4)
-    w_y = lax.ppermute(lax.dynamic_slice_in_dim(w_up, 16 + quarter, 8, 0), AXES, across)
+    steps = [(at(i - 1, 0), at(i, 0)) for i in range(1, spaces)]
+    steps += [(at(i + 1, 1), at(i, 1)) for i in range(spaces - 1)]
+
+    quarter = 16 + 8 * lax.rem(s, 4)
+    mine = [lax.dynamic_slice_in_dim(w_up, quarter + 4 * piece, 4, 0) for piece in (0, 1)]
+    mine = lax.optimization_barrier(mine)
+    w_y = [lax.ppermute(piece, AXES, across) for piece in mine]
 
     rows = inputs[:, 0].transpose(1, 0, 2)
     wanted = lax.dynamic_slice_in_dim(rows, (1 - c) * (held - share), share, 0)
-    edge_near = lax.dynamic_slice_in_dim(rows, (1 - c) * (held - 1), 1, 0)
-    edge_far = lax.dynamic_slice_in_dim(rows, c * (held - 1), 1, 0)
-    w_y, wanted, edge_near, edge_far = lax.optimization_barrier((w_y, wanted, edge_near, edge_far))
-    w_x = lax.ppermute(w_y, AXES, pairs)
+    edge = lax.dynamic_slice_in_dim(rows, (1 - c) * (held - 1), 1, 0)
+    edge_other = lax.dynamic_slice_in_dim(rows, c * (held - 1), 1, 0)
+    w_y[0], wanted, edge, edge_other = lax.optimization_barrier((w_y[0], wanted, edge, edge_other))
+    w_x, w_y_core = [None, None], [None, None]
+    w_x[0] = lax.ppermute(w_y[0], AXES, pairs)
+    far = lax.ppermute(edge_other, AXES, across)
     peer = lax.ppermute(wanted, AXES, across)
-    near = lax.ppermute(edge_near, AXES, down + up)
-    far = lax.ppermute(edge_far, AXES, down_far + up_far)
-    w_y_core = lax.ppermute(w_y, AXES, cores)
-    w_x, w_y_core, peer, near, far = lax.optimization_barrier((w_x, w_y_core, peer, near, far))
-    w_x_core = lax.ppermute(w_x, AXES, cores)
-    w_parts = (w_y, w_y_core, w_x, w_x_core)
+    w_y_core[0] = lax.ppermute(w_y[0], AXES, cores)
+    near = lax.ppermute(edge, AXES, steps)
+    w_y[1], w_y_core[0] = lax.optimization_barrier((w_y[1], w_y_core[0]))
+    w_x[1] = lax.ppermute(w_y[1], AXES, pairs)
+    w_y_core[1] = lax.ppermute(w_y[1], AXES, cores)
+    far, near, w_x[0], w_y_core[1] = lax.optimization_barrier((far, near, w_x[0], w_y_core[1]))
+    far = lax.ppermute(far, AXES, steps)
+    w_x_core = [lax.ppermute(w_x[0], AXES, cores), None]
+    far, peer, w_x[1] = lax.optimization_barrier((far, peer, w_x[1]))
+    w_x_core[1] = lax.ppermute(w_x[1], AXES, cores)
+    w_parts = (*w_y, *w_y_core, *w_x, *w_x_core)
     operands = (rows, peer, near, far, w_up, *w_parts, b_up[None], w_conv, b_conv[None])
-    places = ("vmem",) * 4 + ("any",) * 5 + ("vmem",) * 3
+    places = ("vmem",) * 4 + ("any",) * 9 + ("vmem", "hbm", "vmem")
     return run(paired_kernel, places, operands, sizes)
 
 
@@ -253,7 +264,7 @@
     share = inputs.shape[2] // chs
     rows = lax.dynamic_slice_in_dim(rows, c * share, share + 2, 0)
     operands = (rows, w_all, b_up[None], w_conv, b_conv[None])
-    return run(gathered_kernel, ("vmem", "any", "vmem", "vmem", "vmem"), operands, sizes)
+    return run(gathered_kernel, ("vmem", "any", "vmem", "hbm", "vmem"), operands, sizes)
 
 
 def local(inputs, w_up, b_up, w_conv, b_conv):

time: 31.2 us -> 39.3 us (1.26)
  the two profiles are of different devices: /device:TPU:9 before, /device:TPU:25 now
where the time goes in v2:
time: 39.3 us; the launch traced here: 39 us
  starting transfers between devices  19.7 us (50%)
  waiting for transfers between devices  7.52 us (19%)
  Pallas kernels  7.3 us (19%)
  local copies, waits for them, and re-layouts  4.36 us (11%)
    pallas_call x1, Pallas kernels, run(): pl.pallas_call(kernel, out_shape=jax.ShapeDtypeStruct((cout, 2, rows, 2 *...  7.3 us
    ppermute x1, starting transfers between devices, paired(): far = lax.ppermute(far, AXES, steps)  4.21 us
    ppermute x1, starting transfers between devices, paired(): near = lax.ppermute(edge, AXES, steps)  3.84 us
    ppermute x1, waiting for transfers between devices, paired(): far = lax.ppermute(edge_other, AXES, across)  3.79 us
    ppermute x1, starting transfers between devices, paired(): w_x_core[1] = lax.ppermute(w_x[1], AXES, cores)  3.02 us
    ppermute x1, starting transfers between devices, paired(): w_y_core[0] = lax.ppermute(w_y[0], AXES, cores)  2.69 us
    unnamed x9, local copies, waits for them, and re-layouts  2.16 us
    ppermute x2, starting transfers between devices, paired(): w_y = [lax.ppermute(piece, AXES, across) for piece in mine]  1.53 us
  transfers between devices with their start and end apart: 12, of which 5 were waited for; matrix products, arithmetic and copies ran while one was open for 5% of the time, Pallas kernels for 0%

profile of v2, /device:TPU:25, one launch (start us, length us, event | category | flops | bytes accessed | tf_op | source)
XLA Modules:
  0.0 39.0 jit_solution(1342363365903989964)
XLA Ops:
  0.0 0.0 copy-start
  0.0 0.0 copy-start.3
  0.0 0.0 copy-start.2
  0.0 1.1 %constant_dynamic-slice_fusion.1 = (bf16[4,64,256]{2,1,0:T(8,128)(2,1)S(1)}, bf16[4,64,256]{2,1,0:T(8,128)(2,1)S(1)}) fusion(bf16[64,64,256]{2,1,0:T(8,128)(2,1)} %w_own_ref.1, s32[]{:T(128)S(6)} %select_n.16, s32[]{:T(128)S(6)} %select_n.15), kind=kLoop, calls=%fused_computation.4 | loop fusion | bytes 524296 | tf_op jit(solution)/shard_map/dynamic_slice | solution.py:225
  1.2 1.3 %collective-permute-start = (bf16[4,64,256]{2,1,0:T(8,128)(2,1)S(1)}, bf16[4,64,256]{2,1,0:T(8,128)(2,1)S(1)}, u32[]{:S(2)}, u32[]{:S(2)}) collective-permute-start(bf16[4,64,256]{2,1,0:T(8,128)(2,1)S(1)} %get-tuple-element.20), channel_id=1, source_target_pairs={{0,1},{1,0},{2,3},{3,2},{4,5},{5,4},{6,7},{7,6},{8,9},{9,8},{10,11... | collective-permute-start | bytes 393224 | tf_op jit(solution)/shard_map/ppermute | solution.py:227
  2.5 0.2 collective-permute-start.4
  2.7 1.0 %constant_dynamic-slice_fusion = bf16[128,1,5,128]{3,2,1,0:T(8,128)(2,1)S(1)} fusion(bf16[128,1,8,128]{3,2,1,0:T(8,128)(2,1)} %param.5, s32[]{:T(128)S(6)} %select_n.17), kind=kLoop, calls=%fused_computation.3 | loop fusion | bytes 327684 | tf_op jit(solution)/shard_map/dynamic-slice.3
  3.7 1.0 %copy.16 = bf16[128,1,8,128]{3,0,2,1:T(8,128)(2,1)S(1)} copy(bf16[128,1,8,128]{3,2,1,0:T(8,128)(2,1)} %param.5) | data formatting | bytes 524288 | tf_op args[0]
  4.8 0.8 %collective-permute-done.refs_0_ = bf16[4,64,256]{2,1,0:T(8,128)(2,1)S(1)} collective-permute-done((bf16[4,64,256]{2,1,0:T(8,128)(2,1)S(1)}, bf16[4,64,256]{2,1,0:T(8,128)(2,1)S(1)}, u32[]{:S(2)}, u32[]{:S(2)}) %collective-permute-start) | collective-permute-done | bytes 131104 | tf_op jit(solution)/shard_map/ppermute | solution.py:227
  5.6 2.7 %collective-permute-start.5 = (bf16[4,64,256]{2,1,0:T(8,128)(2,1)S(1)}, bf16[4,64,256]{2,1,0:T(8,128)(2,1)S(1)}, u32[]{:S(2)}, u32[]{:S(2)}) collective-permute-start(bf16[4,64,256]{2,1,0:T(8,128)(2,1)S(1)} %collective-permute-done.refs_0_), channel_id=1, source_target_pairs={{0,2},{1,3},{2,0},{3,1},{4,6},{5,7},{6,4},{7,5},{8,10},{9,11},{10,... | collective-permute-start | bytes 393224 | tf_op jit(solution)/shard_map/ppermute | solution.py:238
  8.3 1.2 %collective-permute-start.3 = (bf16[4,64,256]{2,1,0:T(8,128)(2,1)S(1)}, bf16[4,64,256]{2,1,0:T(8,128)(2,1)S(1)}, u32[]{:S(2)}, u32[]{:S(2)}) collective-permute-start(bf16[4,64,256]{2,1,0:T(8,128)(2,1)S(1)} %collective-permute-done.refs_0_), channel_id=1, source_target_pairs={{0,4},{1,5},{2,6},{3,7},{4,0},{5,1},{6,2},{7,3},{8,12},{9,13},{10,... | collective-permute-start | bytes 393224 | tf_op jit(solution)/shard_map/ppermute | solution.py:235
  9.5 0.0 collective-permute-done.4.refs_1_
  9.5 0.0 collective-permute-done.5.refs_2_
  9.5 0.4 %collective-permute-start.6 = (bf16[4,64,256]{2,1,0:T(8,128)(2,1)S(1)}, bf16[4,64,256]{2,1,0:T(8,128)(2,1)S(1)}, u32[]{:S(2)}, u32[]{:S(2)}) collective-permute-start(bf16[4,64,256]{2,1,0:T(8,128)(2,1)S(1)} %collective-permute-done.4.refs_1_), channel_id=1, source_target_pairs={{0,2},{1,3},{2,0},{3,1},{4,6},{5,7},{6,4},{7,5},{8,10},{9,11},{10,... | collective-permute-start | bytes 393224 | tf_op jit(solution)/shard_map/ppermute | solution.py:242
  10.0 1.2 %collective-permute-start.8 = (bf16[5,128,128]{2,1,0:T(8,128)(2,1)S(1)}, bf16[5,128,128]{2,1,0:T(8,128)(2,1)S(1)}, u32[]{:S(2)}, u32[]{:S(2)}) collective-permute-start(bf16[5,128,128]{2,1,0:T(8,128)(2,1)S(1)} %bitcast.18), channel_id=1, source_target_pairs={{0,1},{1,0},{2,3},{3,2},{4,5},{5,4},{6,7},{7,6},{8,9},{9,8},{10,11... | collective-permute-start | bytes 491528 | tf_op jit(solution)/shard_map/ppermute | solution.py:237
  11.2 1.2 %collective-permute-start.9 = (bf16[4,64,256]{2,1,0:T(8,128)(2,1)S(1)}, bf16[4,64,256]{2,1,0:T(8,128)(2,1)S(1)}, u32[]{:S(2)}, u32[]{:S(2)}) collective-permute-start(bf16[4,64,256]{2,1,0:T(8,128)(2,1)S(1)} %collective-permute-done.4.refs_1_), channel_id=1, source_target_pairs={{0,4},{1,5},{2,6},{3,7},{4,0},{5,1},{6,2},{7,3},{8,12},{9,13},{10,... | collective-permute-start | bytes 393224 | tf_op jit(solution)/shard_map/ppermute | solution.py:241
  12.4 0.2 collective-permute-start.1
  12.6 3.8 %collective-permute-done.1 = bf16[1,128,128]{2,1,0:T(8,128)(2,1)S(1)} collective-permute-done((bf16[1,128,128]{2,1,0:T(8,128)(2,1)S(1)}, bf16[1,128,128]{2,1,0:T(8,128)(2,1)S(1)}, u32[]{:S(2)}, u32[]{:S(2)}) %collective-permute-start.1) | collective-permute-done | bytes 32800 | tf_op jit(solution)/shard_map/ppermute | solution.py:236
  16.4 3.8 %collective-permute-start.2 = (bf16[1,128,128]{2,1,0:T(8,128)(2,1)S(1)}, bf16[1,128,128]{2,1,0:T(8,128)(2,1)S(1)}, u32[]{:S(2)}, u32[]{:S(2)}) collective-permute-start(bf16[1,128,128]{2,1,0:T(8,128)(2,1)S(1)} %get-tuple-element.22), channel_id=1, source_target_pairs={{0,2},{2,4},{4,6},{6,8},{8,10},{10,12},{12,14},{14,16},{16,18},{18... | collective-permute-start | bytes 98312 | tf_op jit(solution)/shard_map/ppermute | solution.py:239
  20.3 1.0 %collective-permute-done.2.near_ref = bf16[1,128,128]{2,1,0:T(8,128)(2,1)S(1)} collective-permute-done((bf16[1,128,128]{2,1,0:T(8,128)(2,1)S(1)}, bf16[1,128,128]{2,1,0:T(8,128)(2,1)S(1)}, u32[]{:S(2)}, u32[]{:S(2)}) %collective-permute-start.2) | collective-permute-done | bytes 32800 | tf_op jit(solution)/shard_map/ppermute | solution.py:239
  21.3 0.0 collective-permute-done.3.refs_4_
  21.3 0.0 collective-permute-done.6.refs_3_
  21.3 4.2 %collective-permute-start.7 = (bf16[1,128,128]{2,1,0:T(8,128)(2,1)S(1)}, bf16[1,128,128]{2,1,0:T(8,128)(2,1)S(1)}, u32[]{:S(2)}, u32[]{:S(2)}) collective-permute-start(bf16[1,128,128]{2,1,0:T(8,128)(2,1)S(1)} %collective-permute-done.1), channel_id=1, source_target_pairs={{0,2},{2,4},{4,6},{6,8},{8,10},{10,12},{12,14},{14,16},{16,18},{18... | collective-permute-start | bytes 98312 | tf_op jit(solution)/shard_map/ppermute | solution.py:244
  25.5 0.1 collective-permute-start.10
  25.6 0.0 collective-permute-done.8.peer_ref
  25.6 0.0 collective-permute-done.9.refs_5_
  25.6 0.9 %collective-permute-done.7.far_ref = bf16[1,128,128]{2,1,0:T(8,128)(2,1)S(1)} collective-permute-done((bf16[1,128,128]{2,1,0:T(8,128)(2,1)S(1)}, bf16[1,128,128]{2,1,0:T(8,128)(2,1)S(1)}, u32[]{:S(2)}, u32[]{:S(2)}) %collective-permute-start.7) | collective-permute-done | bytes 32800 | tf_op jit(solution)/shard_map/ppermute | solution.py:244
  26.5 3.0 %collective-permute-start.11 = (bf16[4,64,256]{2,1,0:T(8,128)(2,1)S(1)}, bf16[4,64,256]{2,1,0:T(8,128)(2,1)S(1)}, u32[]{:S(2)}, u32[]{:S(2)}) collective-permute-start(bf16[4,64,256]{2,1,0:T(8,128)(2,1)S(1)} %collective-permute-done.9.refs_5_), channel_id=1, source_target_pairs={{0,2},{1,3},{2,0},{3,1},{4,6},{5,7},{6,4},{7,5},{8,10},{9,11},{10,... | collective-permute-start | bytes 393224 | tf_op jit(solution)/shard_map/ppermute | solution.py:247
  29.5 0.0 collective-permute-done.10.refs_6_
  29.5 1.0 %collective-permute-done.11.refs_7_ = bf16[4,64,256]{2,1,0:T(8,128)(2,1)S(1)} collective-permute-done((bf16[4,64,256]{2,1,0:T(8,128)(2,1)S(1)}, bf16[4,64,256]{2,1,0:T(8,128)(2,1)S(1)}, u32[]{:S(2)}, u32[]{:S(2)}) %collective-permute-start.11) | collective-permute-done | bytes 131104 | tf_op jit(solution)/shard_map/ppermute | solution.py:247
  30.5 0.0 copy-done
  30.5 0.0 copy-done.3
  30.5 0.0 copy-done.2
  30.5 0.0 copy-start.1
  30.5 1.2 %copy-done.1 = bf16[27,128,128]{2,1,0:T(8,128)(2,1)S(1)} copy-done((bf16[27,128,128]{2,1,0:T(8,128)(2,1)S(1)}, bf16[27,128,128]{2,1,0:T(8,128)(2,1)}, u32[]{:S(2)}) %copy-start.1) | copy-done | bytes 884760
  31.7 7.3 %shard_map.55 = bf16[128,2,8,256]{3,2,1,0:T(8,128)(2,1)} custom-call(bf16[8,128,128]{2,1,0:T(8,128)(2,1)S(1)} %bitcast.15, bf16[5,128,128]{2,1,0:T(8,128)(2,1)S(1)} %collective-permute-done.8.peer_ref, bf16[1,128,128]{2,1,0:T(8,128)(2,1)S(1)} %collective-permute-done.2.near_ref, bf16[1,128,128]{2,1,0:T(8,128)(2,1)S(1)} %collective-permute-done.7.far_ref, ...), custom_call_target="tpu_custom_call" | custom-call | tf_op jit(solution)/shard_map/pallas_call | solution.py:192
  (2 shorter events, 0.0 us)
Async XLA Ops:
  0.0 30.5 %copy-start = (bf16[64,64,256]{2,1,0:T(8,128)(2,1)S(1)}, bf16[64,64,256]{2,1,0:T(8,128)(2,1)}, u32[]{:S(2)}) copy-start(bf16[64,64,256]{2,1,0:T(8,128)(2,1)} %w_own_ref.1) | copy-start | bytes 6291460
  0.0 30.5 %copy-start.3 = (f32[128]{0:T(128)S(1)}, f32[128]{0:T(128)}, u32[]{:S(2)}) copy-start(f32[128]{0:T(128)} %param.9) | copy-start | bytes 1540
  0.0 30.5 %copy-start.2 = (f32[128]{0:T(128)S(1)}, f32[128]{0:T(128)}, u32[]{:S(2)}) copy-start(f32[128]{0:T(128)} %param.7) | copy-start | bytes 1540
  1.2 4.4 %collective-permute-start = (bf16[4,64,256]{2,1,0:T(8,128)(2,1)S(1)}, bf16[4,64,256]{2,1,0:T(8,128)(2,1)S(1)}, u32[]{:S(2)}, u32[]{:S(2)}) collective-permute-start(bf16[4,64,256]{2,1,0:T(8,128)(2,1)S(1)} %get-tuple-element.20), channel_id=1, source_target_pairs={{0,1},{1,0},{2,3},{3,2},{4,5},{5,4},{6,7},{7,6},{8,9},{9,8},{10,11... | collective-permute-start | bytes 393224 | tf_op jit(solution)/shard_map/ppermute | solution.py:227
  2.5 7.0 %collective-permute-start.4 = (bf16[4,64,256]{2,1,0:T(8,128)(2,1)S(1)}, bf16[4,64,256]{2,1,0:T(8,128)(2,1)S(1)}, u32[]{:S(2)}, u32[]{:S(2)}) collective-permute-start(bf16[4,64,256]{2,1,0:T(8,128)(2,1)S(1)} %get-tuple-element.24), channel_id=1, source_target_pairs={{0,1},{1,0},{2,3},{3,2},{4,5},{5,4},{6,7},{7,6},{8,9},{9,8},{10,11... | collective-permute-start | bytes 393224 | tf_op jit(solution)/shard_map/ppermute | solution.py:227
  5.6 3.9 %collective-permute-start.5 = (bf16[4,64,256]{2,1,0:T(8,128)(2,1)S(1)}, bf16[4,64,256]{2,1,0:T(8,128)(2,1)S(1)}, u32[]{:S(2)}, u32[]{:S(2)}) collective-permute-start(bf16[4,64,256]{2,1,0:T(8,128)(2,1)S(1)} %collective-permute-done.refs_0_), channel_id=1, source_target_pairs={{0,2},{1,3},{2,0},{3,1},{4,6},{5,7},{6,4},{7,5},{8,10},{9,11},{10,... | collective-permute-start | bytes 393224 | tf_op jit(solution)/shard_map/ppermute | solution.py:238
  8.3 13.0 %collective-permute-start.3 = (bf16[4,64,256]{2,1,0:T(8,128)(2,1)S(1)}, bf16[4,64,256]{2,1,0:T(8,128)(2,1)S(1)}, u32[]{:S(2)}, u32[]{:S(2)}) collective-permute-start(bf16[4,64,256]{2,1,0:T(8,128)(2,1)S(1)} %collective-permute-done.refs_0_), channel_id=1, source_target_pairs={{0,4},{1,5},{2,6},{3,7},{4,0},{5,1},{6,2},{7,3},{8,12},{9,13},{10,... | collective-permute-start | bytes 393224 | tf_op jit(solution)/shard_map/ppermute | solution.py:235
  9.5 11.8 %collective-permute-start.6 = (bf16[4,64,256]{2,1,0:T(8,128)(2,1)S(1)}, bf16[4,64,256]{2,1,0:T(8,128)(2,1)S(1)}, u32[]{:S(2)}, u32[]{:S(2)}) collective-permute-start(bf16[4,64,256]{2,1,0:T(8,128)(2,1)S(1)} %collective-permute-done.4.refs_1_), channel_id=1, source_target_pairs={{0,2},{1,3},{2,0},{3,1},{4,6},{5,7},{6,4},{7,5},{8,10},{9,11},{10,... | collective-permute-start | bytes 393224 | tf_op jit(solution)/shard_map/ppermute | solution.py:242
  10.0 15.6 %collective-permute-start.8 = (bf16[5,128,128]{2,1,0:T(8,128)(2,1)S(1)}, bf16[5,128,128]{2,1,0:T(8,128)(2,1)S(1)}, u32[]{:S(2)}, u32[]{:S(2)}) collective-permute-start(bf16[5,128,128]{2,1,0:T(8,128)(2,1)S(1)} %bitcast.18), channel_id=1, source_target_pairs={{0,1},{1,0},{2,3},{3,2},{4,5},{5,4},{6,7},{7,6},{8,9},{9,8},{10,11... | collective-permute-start | bytes 491528 | tf_op jit(solution)/shard_map/ppermute | solution.py:237
  11.2 14.4 %collective-permute-start.9 = (bf16[4,64,256]{2,1,0:T(8,128)(2,1)S(1)}, bf16[4,64,256]{2,1,0:T(8,128)(2,1)S(1)}, u32[]{:S(2)}, u32[]{:S(2)}) collective-permute-start(bf16[4,64,256]{2,1,0:T(8,128)(2,1)S(1)} %collective-permute-done.4.refs_1_), channel_id=1, source_target_pairs={{0,4},{1,5},{2,6},{3,7},{4,0},{5,1},{6,2},{7,3},{8,12},{9,13},{10,... | collective-permute-start | bytes 393224 | tf_op jit(solution)/shard_map/ppermute | solution.py:241
  12.4 4.0 %collective-permute-start.1 = (bf16[1,128,128]{2,1,0:T(8,128)(2,1)S(1)}, bf16[1,128,128]{2,1,0:T(8,128)(2,1)S(1)}, u32[]{:S(2)}, u32[]{:S(2)}) collective-permute-start(bf16[1,128,128]{2,1,0:T(8,128)(2,1)S(1)} %get-tuple-element.21), channel_id=1, source_target_pairs={{0,1},{1,0},{2,3},{3,2},{4,5},{5,4},{6,7},{7,6},{8,9},{9,8},{10,11... | collective-permute-start | bytes 98312 | tf_op jit(solution)/shard_map/ppermute | solution.py:236
  16.4 4.9 %collective-permute-start.2 = (bf16[1,128,128]{2,1,0:T(8,128)(2,1)S(1)}, bf16[1,128,128]{2,1,0:T(8,128)(2,1)S(1)}, u32[]{:S(2)}, u32[]{:S(2)}) collective-permute-start(bf16[1,128,128]{2,1,0:T(8,128)(2,1)S(1)} %get-tuple-element.22), channel_id=1, source_target_pairs={{0,2},{2,4},{4,6},{6,8},{8,10},{10,12},{12,14},{14,16},{16,18},{18... | collective-permute-start | bytes 98312 | tf_op jit(solution)/shard_map/ppermute | solution.py:239
  21.3 5.2 %collective-permute-start.7 = (bf16[1,128,128]{2,1,0:T(8,128)(2,1)S(1)}, bf16[1,128,128]{2,1,0:T(8,128)(2,1)S(1)}, u32[]{:S(2)}, u32[]{:S(2)}) collective-permute-start(bf16[1,128,128]{2,1,0:T(8,128)(2,1)S(1)} %collective-permute-done.1), channel_id=1, source_target_pairs={{0,2},{2,4},{4,6},{6,8},{8,10},{10,12},{12,14},{14,16},{16,18},{18... | collective-permute-start | bytes 98312 | tf_op jit(solution)/shard_map/ppermute | solution.py:244
  25.5 4.0 %collective-permute-start.10 = (bf16[4,64,256]{2,1,0:T(8,128)(2,1)S(1)}, bf16[4,64,256]{2,1,0:T(8,128)(2,1)S(1)}, u32[]{:S(2)}, u32[]{:S(2)}) collective-permute-start(bf16[4,64,256]{2,1,0:T(8,128)(2,1)S(1)} %collective-permute-done.3.refs_4_), channel_id=1, source_target_pairs={{0,2},{1,3},{2,0},{3,1},{4,6},{5,7},{6,4},{7,5},{8,10},{9,11},{10,... | collective-permute-start | bytes 393224 | tf_op jit(solution)/shard_map/ppermute | solution.py:245
  26.5 4.0 %collective-permute-start.11 = (bf16[4,64,256]{2,1,0:T(8,128)(2,1)S(1)}, bf16[4,64,256]{2,1,0:T(8,128)(2,1)S(1)}, u32[]{:S(2)}, u32[]{:S(2)}) collective-permute-start(bf16[4,64,256]{2,1,0:T(8,128)(2,1)S(1)} %collective-permute-done.9.refs_5_), channel_id=1, source_target_pairs={{0,2},{1,3},{2,0},{3,1},{4,6},{5,7},{6,4},{7,5},{8,10},{9,11},{10,... | collective-permute-start | bytes 393224 | tf_op jit(solution)/shard_map/ppermute | solution.py:247
  30.5 1.2 %copy-start.1 = (bf16[27,128,128]{2,1,0:T(8,128)(2,1)S(1)}, bf16[27,128,128]{2,1,0:T(8,128)(2,1)}, u32[]{:S(2)}) copy-start(bf16[27,128,128]{2,1,0:T(8,128)(2,1)} %refs_9_.1) | copy-start | bytes 2654212

commit v3 on v1

--- a/solution.py
+++ b/solution.py
@@ -121,7 +121,7 @@
 
 
 def paired_kernel(
-    own_ref, peer_ref, near_ref, far_ref, w_own_ref, w_y_ref, w_y_core_ref, w_x_ref, w_x_core_ref,
+    own_ref, edge_ref, peer_ref, near_ref, far_ref, w_own_ref, w_y_ref, w_y_core_ref, w_x_ref, w_x_core_ref,
     b_up_ref, w_conv_ref, b_conv_ref, out_ref, x_ref, w_ref, u_ref, total_ref, sems,
 ):
     s, c = position()
@@ -149,11 +149,13 @@
     chans = own_ref.shape[1]
     share = peer_ref.shape[0]
     own, other = c * chans, (1 - c) * chans
+    for place in range(share + 1):
+        store_row(x_ref, place + 1 - c, own, own_ref[place + c * (own_ref.shape[0] - share - 1)])
     for place in range(share):
-        store_row(x_ref, place + 1 - c, own, own_ref[place + c * (own_ref.shape[0] - share)])
-        store_row(x_ref, place + 1 - c, other, peer_ref[place])
-    store_row(x_ref, c * share, own, near_ref[0])
-    store_row(x_ref, c * share, other, far_ref[0])
+        store_row(x_ref, place + 2 - 2 * c, other, peer_ref[place])
+    store_row(x_ref, 1 + c * (share - 1), other, edge_ref[0])
+    store_row(x_ref, c * (share + 1), own, far_ref[0])
+    store_row(x_ref, c * (share + 1), other, near_ref[0])
     for copy in copies:
         copy.wait()
     first = (s == 0) & (c == 0)
@@ -214,29 +216,30 @@
     across = [(at(i, j), at(i, 1 - j)) for i in range(spaces) for j in (0, 1)]
     cores = [(at(i, j), at(i ^ 1, j)) for i in range(spaces) for j in (0, 1)]
     pairs = [(at(i, j), at(i ^ 2, j)) for i in range(spaces) for j in (0, 1)]
-    down = [(at(i - 1, 0), at(i, 0)) for i in range(1, spaces)]
-    up = [(at(i + 1, 1), at(i, 1)) for i in range(spaces - 1)]
-    down_far = [(at(i - 1, 1), at(i, 0)) for i in range(1, spaces)]
-    up_far = [(at(i + 1, 0), at(i, 1)) for i in range(spaces - 1)]
+    outer = [(t, t + 1) for t in range(1, 2 * spaces - 1, 2)]
+    outer += [(j, i) for i, j in outer]
 
     quarter = 8 * lax.rem(s, 4)
     w_y = lax.ppermute(lax.dynamic_slice_in_dim(w_up, 16 + quarter, 8, 0), AXES, across)
 
     rows = inputs[:, 0].transpose(1, 0, 2)
-    wanted = lax.dynamic_slice_in_dim(rows, (1 - c) * (held - share), share, 0)
-    edge_near = lax.dynamic_slice_in_dim(rows, (1 - c) * (held - 1), 1, 0)
-    edge_far = lax.dynamic_slice_in_dim(rows, c * (held - 1), 1, 0)
-    w_y, wanted, edge_near, edge_far = lax.optimization_barrier((w_y, wanted, edge_near, edge_far))
+    last = held - 1
+    edge_own = lax.dynamic_slice_in_dim(rows, c * last, 1, 0)
+    edge_other = lax.dynamic_slice_in_dim(rows, (1 - c) * last, 1, 0)
+    wanted = lax.dynamic_slice_in_dim(rows, 1 + (1 - c) * (held - share - 1), share - 1, 0)
+    edge_own, edge_other, wanted = lax.optimization_barrier((edge_own, edge_other, wanted))
+    edge = lax.ppermute(edge_other, AXES, across)
+    peer = lax.ppermute(wanted, AXES, across)
+    w_y, edge = lax.optimization_barrier((w_y, edge))
     w_x = lax.ppermute(w_y, AXES, pairs)
-    peer = lax.ppermute(wanted, AXES, across)
-    near = lax.ppermute(edge_near, AXES, down + up)
-    far = lax.ppermute(edge_far, AXES, down_far + up_far)
     w_y_core = lax.ppermute(w_y, AXES, cores)
+    near = lax.ppermute(edge_own, AXES, outer)
+    far = lax.ppermute(edge, AXES, outer)
     w_x, w_y_core, peer, near, far = lax.optimization_barrier((w_x, w_y_core, peer, near, far))
     w_x_core = lax.ppermute(w_x, AXES, cores)
     w_parts = (w_y, w_y_core, w_x, w_x_core)
-    operands = (rows, peer, near, far, w_up, *w_parts, b_up[None], w_conv, b_conv[None])
-    places = ("vmem",) * 4 + ("any",) * 5 + ("vmem",) * 3
+    operands = (rows, edge, peer, near, far, w_up, *w_parts, b_up[None], w_conv, b_conv[None])
+    places = ("vmem",) * 5 + ("any",) * 5 + ("vmem",) * 3
     return run(paired_kernel, places, operands, sizes)
 
 

time: 31.2 us -> 34.9 us (1.12)
  the two profiles are of different devices: /device:TPU:9 before, /device:TPU:23 now
where the time goes in v3:
time: 34.9 us; the launch traced here: 34.6 us
  starting transfers between devices  11.1 us (32%)
  waiting for transfers between devices  10.9 us (31%)
  Pallas kernels  6.57 us (19%)
  local copies, waits for them, and re-layouts  6 us (17%)
    pallas_call x1, Pallas kernels, run(): pl.pallas_call(kernel, out_shape=jax.ShapeDtypeStruct((cout, 2, rows, 2 *...  6.57 us
    ppermute x1, starting transfers between devices, paired(): near = lax.ppermute(edge_own, AXES, outer)  5.53 us
    ppermute x1, waiting for transfers between devices, paired(): far = lax.ppermute(edge, AXES, outer)  5.08 us
    ppermute x1, waiting for transfers between devices, paired(): edge = lax.ppermute(edge_other, AXES, across)  4.27 us
    unnamed x9, local copies, waits for them, and re-layouts  3.89 us
    ppermute x1, starting transfers between devices, paired(): far = lax.ppermute(edge, AXES, outer)  1.92 us
    ppermute x1, starting transfers between devices, paired(): w_y_core = lax.ppermute(w_y, AXES, cores)  1.55 us
    ppermute x1, waiting for transfers between devices, paired(): w_x_core = lax.ppermute(w_x, AXES, cores)  1.53 us
  transfers between devices with their start and end apart: 8, of which 3 were waited for; matrix products, arithmetic and copies ran while one was open for 6% of the time, Pallas kernels for 0%

profile of v3, /device:TPU:23, one launch (start us, length us, event | category | flops | bytes accessed | tf_op | source)
XLA Modules:
  0.0 34.6 jit_solution(122015739745763460)
XLA Ops:
  0.0 0.0 copy-start.1
  0.0 1.0 %constant_dynamic-slice_fusion.1 = bf16[8,64,256]{2,1,0:T(8,128)(2,1)S(1)} fusion(bf16[64,64,256]{2,1,0:T(8,128)(2,1)} %w_own_ref.1, s32[]{:T(128)S(6)} %select_n.12), kind=kLoop, calls=%fused_computation.4 | loop fusion | bytes 524292 | tf_op jit(solution)/shard_map/dynamic_slice | solution.py:223
  1.1 0.3 collective-permute-start
  1.3 1.0 %copy.16 = bf16[128,1,8,128]{3,0,2,1:T(8,128)(2,1)S(1)} copy(bf16[128,1,8,128]{3,2,1,0:T(8,128)(2,1)} %param.5) | data formatting | bytes 524288 | tf_op args[0]
  2.3 1.0 %constant_dynamic-slice_fusion = bf16[128,1,4,128]{3,2,1,0:T(4,128)(2,1)S(1)} fusion(bf16[128,1,8,128]{3,2,1,0:T(8,128)(2,1)} %param.5, s32[]{:T(128)S(6)} %select_n.15), kind=kLoop, calls=%fused_computation.3 | loop fusion | bytes 262148 | tf_op jit(solution)/shard_map/dynamic-slice.5
  3.4 1.3 %collective-permute-start.1 = (bf16[1,128,128]{2,1,0:T(8,128)(2,1)S(1)}, bf16[1,128,128]{2,1,0:T(8,128)(2,1)S(1)}, u32[]{:S(2)}, u32[]{:S(2)}) collective-permute-start(bf16[1,128,128]{2,1,0:T(8,128)(2,1)S(1)} %get-tuple-element.15), channel_id=1, source_target_pairs={{0,1},{1,0},{2,3},{3,2},{4,5},{5,4},{6,7},{7,6},{8,9},{9,8},{10,11... | collective-permute-start | bytes 98312 | tf_op jit(solution)/shard_map/ppermute | solution.py:231
  4.7 4.3 %collective-permute-done.1.edge_ref = bf16[1,128,128]{2,1,0:T(8,128)(2,1)S(1)} collective-permute-done((bf16[1,128,128]{2,1,0:T(8,128)(2,1)S(1)}, bf16[1,128,128]{2,1,0:T(8,128)(2,1)S(1)}, u32[]{:S(2)}, u32[]{:S(2)}) %collective-permute-start.1) | collective-permute-done | bytes 32800 | tf_op jit(solution)/shard_map/ppermute | solution.py:231
  9.0 0.0 collective-permute-done.w_y_ref
  9.0 1.5 %collective-permute-start.3 = (bf16[8,64,256]{2,1,0:T(8,128)(2,1)S(1)}, bf16[8,64,256]{2,1,0:T(8,128)(2,1)S(1)}, u32[]{:S(2)}, u32[]{:S(2)}) collective-permute-start(bf16[8,64,256]{2,1,0:T(8,128)(2,1)S(1)} %collective-permute-done.w_y_ref), channel_id=1, source_target_pairs={{0,2},{1,3},{2,0},{3,1},{4,6},{5,7},{6,4},{7,5},{8,10},{9,11},{10,... | collective-permute-start | bytes 786440 | tf_op jit(solution)/shard_map/ppermute | solution.py:235
  10.5 0.3 collective-permute-start.2
  10.8 0.2 collective-permute-start.4
  11.0 5.5 %collective-permute-start.5 = (bf16[1,128,128]{2,1,0:T(8,128)(2,1)S(1)}, bf16[1,128,128]{2,1,0:T(8,128)(2,1)S(1)}, u32[]{:S(2)}, u32[]{:S(2)}) collective-permute-start(bf16[1,128,128]{2,1,0:T(8,128)(2,1)S(1)} %get-tuple-element.19), channel_id=1, source_target_pairs={{1,2},{3,4},{5,6},{7,8},{9,10},{11,12},{13,14},{15,16},{17,18},{19... | collective-permute-start | bytes 98312 | tf_op jit(solution)/shard_map/ppermute | solution.py:236
  16.6 1.9 %collective-permute-start.6 = (bf16[1,128,128]{2,1,0:T(8,128)(2,1)S(1)}, bf16[1,128,128]{2,1,0:T(8,128)(2,1)S(1)}, u32[]{:S(2)}, u32[]{:S(2)}) collective-permute-start(bf16[1,128,128]{2,1,0:T(8,128)(2,1)S(1)} %collective-permute-done.1.edge_ref), channel_id=1, source_target_pairs={{1,2},{3,4},{5,6},{7,8},{9,10},{11,12},{13,14},{15,16},{17,18},{19... | collective-permute-start | bytes 98312 | tf_op jit(solution)/shard_map/ppermute | solution.py:237
  18.5 0.0 collective-permute-done.5.near_ref
  18.5 0.0 collective-permute-done.4.peer_ref
  18.5 5.1 %collective-permute-done.6.far_ref = bf16[1,128,128]{2,1,0:T(8,128)(2,1)S(1)} collective-permute-done((bf16[1,128,128]{2,1,0:T(8,128)(2,1)S(1)}, bf16[1,128,128]{2,1,0:T(8,128)(2,1)S(1)}, u32[]{:S(2)}, u32[]{:S(2)}) %collective-permute-start.6) | collective-permute-done | bytes 32800 | tf_op jit(solution)/shard_map/ppermute | solution.py:237
  23.6 0.0 collective-permute-done.3.w_y_core_ref
  23.6 0.0 collective-permute-done.2.w_x_ref
  23.6 0.0 collective-permute-start.7
  23.6 1.5 %collective-permute-done.7.w_x_core_ref = bf16[8,64,256]{2,1,0:T(8,128)(2,1)S(1)} collective-permute-done((bf16[8,64,256]{2,1,0:T(8,128)(2,1)S(1)}, bf16[8,64,256]{2,1,0:T(8,128)(2,1)S(1)}, u32[]{:S(2)}, u32[]{:S(2)}) %collective-permute-start.7) | collective-permute-done | bytes 262176 | tf_op jit(solution)/shard_map/ppermute | solution.py:239
  25.1 0.0 copy-done.1
  25.1 0.0 copy-start
  25.1 1.6 %copy-done = bf16[64,64,256]{2,1,0:T(8,128)(2,1)S(1)} copy-done((bf16[64,64,256]{2,1,0:T(8,128)(2,1)S(1)}, bf16[64,64,256]{2,1,0:T(8,128)(2,1)}, u32[]{:S(2)}) %copy-start) | copy-done | bytes 2097176
  26.7 0.0 copy-start.2
  26.7 0.7 %copy-done.2 = f32[128]{0:T(128)S(1)} copy-done((f32[128]{0:T(128)S(1)}, f32[128]{0:T(128)}, u32[]{:S(2)}) %copy-start.2) | copy-done | bytes 536
  27.4 0.0 copy-start.3
  27.4 0.7 %copy-done.3 = f32[128]{0:T(128)S(1)} copy-done((f32[128]{0:T(128)S(1)}, f32[128]{0:T(128)}, u32[]{:S(2)}) %copy-start.3) | copy-done | bytes 536
  28.0 6.6 %shard_map.55 = bf16[128,2,8,256]{3,2,1,0:T(8,128)(2,1)} custom-call(bf16[8,128,128]{2,1,0:T(8,128)(2,1)S(1)} %bitcast.15, bf16[1,128,128]{2,1,0:T(8,128)(2,1)S(1)} %collective-permute-done.1.edge_ref, bf16[4,128,128]{2,1,0:T(8,128)(2,1)S(1)} %collective-permute-done.4.peer_ref, bf16[1,128,128]{2,1,0:T(8,128)(2,1)S(1)} %collective-permute-done.5.near_ref, ...), custom_call_target="tpu_custom_call" | custom-call | tf_op jit(solution)/shard_map/pallas_call | solution.py:191
  (2 shorter events, 0.0 us)
Async XLA Ops:
  0.0 25.1 %copy-start.1 = (bf16[27,128,128]{2,1,0:T(8,128)(2,1)S(1)}, bf16[27,128,128]{2,1,0:T(8,128)(2,1)}, u32[]{:S(2)}) copy-start(bf16[27,128,128]{2,1,0:T(8,128)(2,1)} %w_conv_ref.1) | copy-start | bytes 2654212
  1.1 7.9 %collective-permute-start = (bf16[8,64,256]{2,1,0:T(8,128)(2,1)S(1)}, bf16[8,64,256]{2,1,0:T(8,128)(2,1)S(1)}, u32[]{:S(2)}, u32[]{:S(2)}) collective-permute-start(bf16[8,64,256]{2,1,0:T(8,128)(2,1)S(1)} %constant_dynamic-slice_fusion.1), channel_id=1, source_target_pairs={{0,1},{1,0},{2,3},{3,2},{4,5},{5,4},{6,7},{7,6},{8,9},{9,8},{10,11... | collective-permute-start | bytes 786440 | tf_op jit(solution)/shard_map/ppermute | solution.py:223
  3.4 5.6 %collective-permute-start.1 = (bf16[1,128,128]{2,1,0:T(8,128)(2,1)S(1)}, bf16[1,128,128]{2,1,0:T(8,128)(2,1)S(1)}, u32[]{:S(2)}, u32[]{:S(2)}) collective-permute-start(bf16[1,128,128]{2,1,0:T(8,128)(2,1)S(1)} %get-tuple-element.15), channel_id=1, source_target_pairs={{0,1},{1,0},{2,3},{3,2},{4,5},{5,4},{6,7},{7,6},{8,9},{9,8},{10,11... | collective-permute-start | bytes 98312 | tf_op jit(solution)/shard_map/ppermute | solution.py:231
  9.0 14.6 %collective-permute-start.3 = (bf16[8,64,256]{2,1,0:T(8,128)(2,1)S(1)}, bf16[8,64,256]{2,1,0:T(8,128)(2,1)S(1)}, u32[]{:S(2)}, u32[]{:S(2)}) collective-permute-start(bf16[8,64,256]{2,1,0:T(8,128)(2,1)S(1)} %collective-permute-done.w_y_ref), channel_id=1, source_target_pairs={{0,2},{1,3},{2,0},{3,1},{4,6},{5,7},{6,4},{7,5},{8,10},{9,11},{10,... | collective-permute-start | bytes 786440 | tf_op jit(solution)/shard_map/ppermute | solution.py:235
  10.5 13.1 %collective-permute-start.2 = (bf16[8,64,256]{2,1,0:T(8,128)(2,1)S(1)}, bf16[8,64,256]{2,1,0:T(8,128)(2,1)S(1)}, u32[]{:S(2)}, u32[]{:S(2)}) collective-permute-start(bf16[8,64,256]{2,1,0:T(8,128)(2,1)S(1)} %collective-permute-done.w_y_ref), channel_id=1, source_target_pairs={{0,4},{1,5},{2,6},{3,7},{4,0},{5,1},{6,2},{7,3},{8,12},{9,13},{10,... | collective-permute-start | bytes 786440 | tf_op jit(solution)/shard_map/ppermute | solution.py:234
  10.8 7.7 %collective-permute-start.4 = (bf16[4,128,128]{2,1,0:T(8,128)(2,1)S(1)}, bf16[4,128,128]{2,1,0:T(8,128)(2,1)S(1)}, u32[]{:S(2)}, u32[]{:S(2)}) collective-permute-start(bf16[4,128,128]{2,1,0:T(8,128)(2,1)S(1)} %bitcast.18), channel_id=1, source_target_pairs={{0,1},{1,0},{2,3},{3,2},{4,5},{5,4},{6,7},{7,6},{8,9},{9,8},{10,11... | collective-permute-start | bytes 393224 | tf_op jit(solution)/shard_map/ppermute | solution.py:232
  11.0 7.5 %collective-permute-start.5 = (bf16[1,128,128]{2,1,0:T(8,128)(2,1)S(1)}, bf16[1,128,128]{2,1,0:T(8,128)(2,1)S(1)}, u32[]{:S(2)}, u32[]{:S(2)}) collective-permute-start(bf16[1,128,128]{2,1,0:T(8,128)(2,1)S(1)} %get-tuple-element.19), channel_id=1, source_target_pairs={{1,2},{3,4},{5,6},{7,8},{9,10},{11,12},{13,14},{15,16},{17,18},{19... | collective-permute-start | bytes 98312 | tf_op jit(solution)/shard_map/ppermute | solution.py:236
  16.6 7.0 %collective-permute-start.6 = (bf16[1,128,128]{2,1,0:T(8,128)(2,1)S(1)}, bf16[1,128,128]{2,1,0:T(8,128)(2,1)S(1)}, u32[]{:S(2)}, u32[]{:S(2)}) collective-permute-start(bf16[1,128,128]{2,1,0:T(8,128)(2,1)S(1)} %collective-permute-done.1.edge_ref), channel_id=1, source_target_pairs={{1,2},{3,4},{5,6},{7,8},{9,10},{11,12},{13,14},{15,16},{17,18},{19... | collective-permute-start | bytes 98312 | tf_op jit(solution)/shard_map/ppermute | solution.py:237
  23.6 1.5 %collective-permute-start.7 = (bf16[8,64,256]{2,1,0:T(8,128)(2,1)S(1)}, bf16[8,64,256]{2,1,0:T(8,128)(2,1)S(1)}, u32[]{:S(2)}, u32[]{:S(2)}) collective-permute-start(bf16[8,64,256]{2,1,0:T(8,128)(2,1)S(1)} %collective-permute-done.2.w_x_ref), channel_id=1, source_target_pairs={{0,2},{1,3},{2,0},{3,1},{4,6},{5,7},{6,4},{7,5},{8,10},{9,11},{10,... | collective-permute-start | bytes 786440 | tf_op jit(solution)/shard_map/ppermute | solution.py:239
  25.1 1.6 %copy-start = (bf16[64,64,256]{2,1,0:T(8,128)(2,1)S(1)}, bf16[64,64,256]{2,1,0:T(8,128)(2,1)}, u32[]{:S(2)}) copy-start(bf16[64,64,256]{2,1,0:T(8,128)(2,1)} %w_own_ref.1) | copy-start | bytes 6291460
  26.7 0.7 %copy-start.2 = (f32[128]{0:T(128)S(1)}, f32[128]{0:T(128)}, u32[]{:S(2)}) copy-start(f32[128]{0:T(128)} %param.7) | copy-start | bytes 1540
  27.4 0.7 %copy-start.3 = (f32[128]{0:T(128)S(1)}, f32[128]{0:T(128)}, u32[]{:S(2)}) copy-start(f32[128]{0:T(128)} %param.9) | copy-start | bytes 1540

commit v4 on v1

--- a/solution.py
+++ b/solution.py
@@ -22,12 +22,13 @@
     return jnp.where(place == edge, 0.0, pltpu.roll(value, step % cols, 1))
 
 
-def compute(x_ref, w_ref, b_up_ref, w_conv_ref, b_conv_ref, out_ref, u_ref, total_ref, first, last):
+def compute(x_ref, w_ref, w_conv_ref, b_ref, kept, out_ref, u_ref, total_ref, first, last):
     rows = out_ref.shape[2]
     cout = out_ref.shape[0]
     cols = x_ref.shape[3]
     held = rows + 2
-    bias = column_of(b_up_ref[...])
+    kept[0].wait()
+    bias = column_of(b_ref[0])
     bias = jnp.concatenate([bias, bias], axis=0)
     for row_phase in (0, 1):
         for col_phase in (0, 1):
@@ -59,7 +60,9 @@
                     moved = shifted(value, -1 if col_phase == 0 else 1)
                     u_ref[2 + col_phase, row] = moved.astype(jnp.bfloat16)
 
-    bias = column_of(b_conv_ref[...])
+    kept[1].wait()
+    kept[2].wait()
+    bias = column_of(b_ref[1])
     bias = jnp.concatenate([bias, bias], axis=0)
     source = lax.broadcasted_iota(jnp.int32, (2 * cols, 2 * cols), 0)
     target = lax.broadcasted_iota(jnp.int32, (2 * cols, 2 * cols), 1)
@@ -120,12 +123,11 @@
     return s, c
 
 
-def paired_kernel(
-    own_ref, peer_ref, near_ref, far_ref, w_own_ref, w_y_ref, w_y_core_ref, w_x_ref, w_x_core_ref,
-    b_up_ref, w_conv_ref, b_conv_ref, out_ref, x_ref, w_ref, u_ref, total_ref, sems,
-):
+def paired_kernel(own_ref, peer_ref, near_ref, far_ref, w_own_ref, *refs):
+    *part_refs, b_up_ref, w_conv_ref, b_conv_ref, out_ref, x_ref, w_ref, v_ref, b_ref, u_ref, total_ref, sems = refs
     s, c = position()
     part, cout = w_own_ref.shape[1], out_ref.shape[0]
+    kept = keep(b_up_ref, w_conv_ref, b_conv_ref, b_ref, v_ref, sems)
 
     def taps_of(plane, half, first, count):
         place = pl.multiple_of(plane * cout + half * part, part)
@@ -133,17 +135,16 @@
 
     copies = [
         pltpu.make_async_copy(
-            w_own_ref.at[pl.ds(16 + 16 * plane, 16)], taps_of(plane, c, 0, 16), sems.at[plane]
+            w_own_ref.at[pl.ds(16 + 16 * plane, 16)], taps_of(plane, c, 0, 16), sems.at[3 + plane]
         )
         for plane in (0, 1)
     ]
     me = lax.rem(s, 4)
     x, core = me // 2, lax.rem(me, 2)
-    parts = ((w_y_ref, x, core), (w_y_core_ref, x, 1 - core), (w_x_ref, 1 - x, core), (w_x_core_ref, 1 - x, 1 - core))
-    for number, (part_ref, plane, side) in enumerate(parts):
-        copies.append(
-            pltpu.make_async_copy(part_ref, taps_of(plane, 1 - c, 8 * side, 8), sems.at[2 + number])
-        )
+    firsts = [4 * (2 * i + j) for i in (x, 1 - x) for j in (core, 1 - core)] + [8 * core, 8 - 8 * core]
+    for number, part_ref in enumerate(part_refs):
+        place = taps_of(number // 4, 1 - c, firsts[number], part_ref.shape[0])
+        copies.append(pltpu.make_async_copy(part_ref, place, sems.at[5 + number]))
     for copy in copies:
         copy.start()
     chans = own_ref.shape[1]
@@ -158,17 +159,17 @@
         copy.wait()
     first = (s == 0) & (c == 0)
     last = (s == lax.axis_size("space") - 1) & (c == 1)
-    compute(x_ref, w_ref, b_up_ref, w_conv_ref, b_conv_ref, out_ref, u_ref, total_ref, first, last)
-
-
-def gathered_kernel(
-    rows_ref, w_all_ref, b_up_ref, w_conv_ref, b_conv_ref, out_ref, x_ref, w_ref, u_ref, total_ref, sems
-):
+    compute(x_ref, w_ref, v_ref, b_ref, kept, out_ref, u_ref, total_ref, first, last)
+
+
+def gathered_kernel(rows_ref, w_all_ref, *refs):
+    b_up_ref, w_conv_ref, b_conv_ref, out_ref, x_ref, w_ref, v_ref, b_ref, u_ref, total_ref, sems = refs
     s, c = position()
     cout = out_ref.shape[0]
+    kept = keep(b_up_ref, w_conv_ref, b_conv_ref, b_ref, v_ref, sems)
     copies = [
         pltpu.make_async_copy(
-            w_all_ref.at[pl.ds(16 * plane, 16)], w_ref.at[:, pl.ds(plane * cout, cout)], sems.at[plane]
+            w_all_ref.at[pl.ds(16 * plane, 16)], w_ref.at[:, pl.ds(plane * cout, cout)], sems.at[3 + plane]
         )
         for plane in (0, 1)
     ]
@@ -180,12 +181,28 @@
         copy.wait()
     first = (s == 0) & (c == 0)
     last = (s == lax.axis_size("space") - 1) & (c == lax.axis_size("ch") - 1)
-    compute(x_ref, w_ref, b_up_ref, w_conv_ref, b_conv_ref, out_ref, u_ref, total_ref, first, last)
+    compute(x_ref, w_ref, v_ref, b_ref, kept, out_ref, u_ref, total_ref, first, last)
+
+
+def keep(b_up_ref, w_conv_ref, b_conv_ref, b_ref, v_ref, sems):
+    kept = [
+        pltpu.make_async_copy(b_up_ref, b_ref.at[0], sems.at[0]),
+        pltpu.make_async_copy(w_conv_ref, v_ref, sems.at[1]),
+        pltpu.make_async_copy(b_conv_ref, b_ref.at[1], sems.at[2]),
+    ]
+    for copy in kept:
+        copy.start()
+    return kept
 
 
 def run(kernel, spaces, operands, sizes):
     cin, cout, rows, cols = sizes
     spec = {"vmem": pl.BlockSpec(memory_space=pltpu.VMEM), "any": pl.BlockSpec(memory_space=pl.ANY)}
+    spec["hbm"] = spec["any"]
+    operands = [
+        pltpu.with_memory_space_constraint(operand, pltpu.HBM) if space == "hbm" else operand
+        for operand, space in zip(operands, spaces)
+    ]
     return pl.pallas_call(
         kernel,
         out_shape=jax.ShapeDtypeStruct((cout, 2, rows, 2 * cols), jnp.bfloat16),
@@ -194,9 +211,11 @@
         scratch_shapes=[
             pltpu.VMEM((3, rows // 2 + 2, cin, cols), jnp.bfloat16),
             pltpu.VMEM((16, 2 * cout, cin), jnp.bfloat16),
+            pltpu.VMEM((27, cout, cout), jnp.bfloat16),
+            pltpu.VMEM((2, 1, cout), jnp.float32),
             pltpu.VMEM((4, rows + 2, 2 * cout, cols), jnp.bfloat16),
             pltpu.VMEM((2, 2 * cout * rows, cols), jnp.float32),
-            pltpu.SemaphoreType.DMA((6,)),
+            pltpu.SemaphoreType.DMA((11,)),
         ],
         compiler_params=pltpu.CompilerParams(vmem_limit_bytes=48 * 2**20),
     )(*operands)
@@ -216,27 +235,32 @@
     pairs = [(at(i, j), at(i ^ 2, j)) for i in range(spaces) for j in (0, 1)]
     down = [(at(i - 1, 0), at(i, 0)) for i in range(1, spaces)]
     up = [(at(i + 1, 1), at(i, 1)) for i in range(spaces - 1)]
-    down_far = [(at(i - 1, 1), at(i, 0)) for i in range(1, spaces)]
-    up_far = [(at(i + 1, 0), at(i, 1)) for i in range(spaces - 1)]
-
-    quarter = 8 * lax.rem(s, 4)
-    w_y = lax.ppermute(lax.dynamic_slice_in_dim(w_up, 16 + quarter, 8, 0), AXES, across)
+    outer = [(t, t + 1) for t in range(1, 2 * spaces - 1, 2)]
+    outer += [(j, i) for i, j in outer]
+
+    w_a = lax.dynamic_slice_in_dim(w_up, 16 + 4 * lax.rem(s, 4), 4, 0)
+    w_b = lax.dynamic_slice_in_dim(w_up, 32 + 8 * lax.rem(s, 2), 8, 0)
+    w_a, w_b = lax.optimization_barrier((w_a, w_b))
+    w_a = lax.ppermute(w_a, AXES, across)
+    w_b = lax.ppermute(w_b, AXES, across)
 
     rows = inputs[:, 0].transpose(1, 0, 2)
+    last = held - 1
+    edge_outer = lax.dynamic_slice_in_dim(rows, c * last, 1, 0)
+    edge_inner = lax.dynamic_slice_in_dim(rows, (1 - c) * last, 1, 0)
     wanted = lax.dynamic_slice_in_dim(rows, (1 - c) * (held - share), share, 0)
-    edge_near = lax.dynamic_slice_in_dim(rows, (1 - c) * (held - 1), 1, 0)
-    edge_far = lax.dynamic_slice_in_dim(rows, c * (held - 1), 1, 0)
-    w_y, wanted, edge_near, edge_far = lax.optimization_barrier((w_y, wanted, edge_near, edge_far))
-    w_x = lax.ppermute(w_y, AXES, pairs)
+    w_a, edge_outer, edge_inner, wanted = lax.optimization_barrier((w_a, edge_outer, edge_inner, wanted))
+    w_ax = lax.ppermute(w_a, AXES, pairs)
     peer = lax.ppermute(wanted, AXES, across)
-    near = lax.ppermute(edge_near, AXES, down + up)
-    far = lax.ppermute(edge_far, AXES, down_far + up_far)
-    w_y_core = lax.ppermute(w_y, AXES, cores)
-    w_x, w_y_core, peer, near, far = lax.optimization_barrier((w_x, w_y_core, peer, near, far))
-    w_x_core = lax.ppermute(w_x, AXES, cores)
-    w_parts = (w_y, w_y_core, w_x, w_x_core)
+    w_ac = lax.ppermute(w_a, AXES, cores)
+    near = lax.ppermute(edge_inner, AXES, down + up)
+    far = lax.ppermute(edge_outer, AXES, outer)
+    w_b, w_ax, w_ac = lax.optimization_barrier((w_b, w_ax, w_ac))
+    w_bc = lax.ppermute(w_b, AXES, cores)
+    w_axc = lax.ppermute(w_ax, AXES, cores)
+    w_parts = (w_a, w_ac, w_ax, w_axc, w_b, w_bc)
     operands = (rows, peer, near, far, w_up, *w_parts, b_up[None], w_conv, b_conv[None])
-    places = ("vmem",) * 4 + ("any",) * 5 + ("vmem",) * 3
+    places = ("vmem",) * 4 + ("any",) * 7 + ("hbm",) * 3
     return run(paired_kernel, places, operands, sizes)
 
 
@@ -253,7 +277,7 @@
     share = inputs.shape[2] // chs
     rows = lax.dynamic_slice_in_dim(rows, c * share, share + 2, 0)
     operands = (rows, w_all, b_up[None], w_conv, b_conv[None])
-    return run(gathered_kernel, ("vmem", "any", "vmem", "vmem", "vmem"), operands, sizes)
+    return run(gathered_kernel, ("vmem", "any", "hbm", "hbm", "hbm"), operands, sizes)
 
 
 def local(inputs, w_up, b_up, w_conv, b_conv):

time: 31.2 us -> 34.1 us (1.093)
  the two profiles are of different devices: /device:TPU:9 before, /device:TPU:1 now
where the time goes in v4:
time: 34.1 us; the launch traced here: 33.8 us
  starting transfers between devices  13.5 us (40%)
  waiting for transfers between devices  8.45 us (25%)
  Pallas kernels  7.01 us (21%)
  local copies, waits for them, and re-layouts  4.74 us (14%)
    pallas_call x1, Pallas kernels, run(): pl.pallas_call(kernel, out_shape=jax.ShapeDtypeStruct((cout, 2, rows, 2 *...  7.01 us
    ppermute x1, waiting for transfers between devices, paired(): w_ax = lax.ppermute(w_a, AXES, pairs)  3.86 us
    ppermute x1, waiting for transfers between devices, paired(): far = lax.ppermute(edge_outer, AXES, outer)  3.29 us
    ppermute x1, starting transfers between devices, paired(): near = lax.ppermute(edge_inner, AXES, down + up)  3.22 us
    ppermute x1, starting transfers between devices, paired(): w_a = lax.ppermute(w_a, AXES, across)  2.13 us
    ppermute x1, starting transfers between devices, paired(): w_ac = lax.ppermute(w_a, AXES, cores)  2.06 us
    ppermute x1, starting transfers between devices, paired(): far = lax.ppermute(edge_outer, AXES, outer)  1.92 us
    ppermute x1, starting transfers between devices, paired(): w_ax = lax.ppermute(w_a, AXES, pairs)  1.75 us
  transfers between devices with their start and end apart: 9, of which 3 were waited for; matrix products, arithmetic and copies ran while one was open for 6% of the time, Pallas kernels for 0%

profile of v4, /device:TPU:1, one launch (start us, length us, event | category | flops | bytes accessed | tf_op | source)
XLA Modules:
  0.0 33.8 jit_solution(9873324164706731524)
XLA Ops:
  0.0 0.0 copy-start
  0.0 1.7 %constant_dynamic-slice_fusion.2 = bf16[4,64,256]{2,1,0:T(8,128)(2,1)} fusion(bf16[64,64,256]{2,1,0:T(8,128)(2,1)} %w_own_ref.1, s32[]{:T(128)S(6)} %select_n.15), kind=kLoop, calls=%fused_computation.5 | loop fusion | bytes 262148 | tf_op jit(solution)/shard_map/dynamic_slice | solution.py:241
  1.7 1.0 %constant_dynamic-slice_fusion.1 = bf16[8,64,256]{2,1,0:T(8,128)(2,1)S(1)} fusion(bf16[64,64,256]{2,1,0:T(8,128)(2,1)} %w_own_ref.1, s32[]{:T(128)S(6)} %select_n.16), kind=kLoop, calls=%fused_computation.4 | loop fusion | bytes 524292 | tf_op jit(solution)/shard_map/dynamic_slice | solution.py:242
  2.7 2.1 %collective-permute-start = (bf16[4,64,256]{2,1,0:T(8,128)(2,1)}, bf16[4,64,256]{2,1,0:T(8,128)(2,1)S(1)}, u32[]{:S(2)}, u32[]{:S(2)}) collective-permute-start(bf16[4,64,256]{2,1,0:T(8,128)(2,1)} %constant_dynamic-slice_fusion.2), channel_id=1, source_target_pairs={{0,1},{1,0},{2,3},{3,2},{4,5},{5,4},{6,7},{7,6},{8,9},{9,8},{10,11... | collective-permute-start | bytes 393224 | tf_op jit(solution)/shard_map/ppermute | solution.py:244
  4.8 0.1 collective-permute-start.4
  4.9 1.0 %constant_dynamic-slice_fusion = bf16[128,1,5,128]{3,2,1,0:T(8,128)(2,1)S(1)} fusion(bf16[128,1,8,128]{3,2,1,0:T(8,128)(2,1)} %param.5, s32[]{:T(128)S(6)} %select_n.19), kind=kLoop, calls=%fused_computation.3 | loop fusion | bytes 327684 | tf_op jit(solution)/shard_map/dynamic-slice.5
  5.9 1.0 %copy.16 = bf16[128,1,8,128]{3,0,2,1:T(8,128)(2,1)S(1)} copy(bf16[128,1,8,128]{3,2,1,0:T(8,128)(2,1)} %param.5) | data formatting | bytes 524288 | tf_op args[0]
  7.0 1.3 %collective-permute-done.refs_0_ = bf16[4,64,256]{2,1,0:T(8,128)(2,1)S(1)} collective-permute-done((bf16[4,64,256]{2,1,0:T(8,128)(2,1)}, bf16[4,64,256]{2,1,0:T(8,128)(2,1)S(1)}, u32[]{:S(2)}, u32[]{:S(2)}) %collective-permute-start) | collective-permute-done | bytes 131104 | tf_op jit(solution)/shard_map/ppermute | solution.py:244
  8.3 2.1 %collective-permute-start.6 = (bf16[4,64,256]{2,1,0:T(8,128)(2,1)S(1)}, bf16[4,64,256]{2,1,0:T(8,128)(2,1)S(1)}, u32[]{:S(2)}, u32[]{:S(2)}) collective-permute-start(bf16[4,64,256]{2,1,0:T(8,128)(2,1)S(1)} %collective-permute-done.refs_0_), channel_id=1, source_target_pairs={{0,2},{1,3},{2,0},{3,1},{4,6},{5,7},{6,4},{7,5},{8,10},{9,11},{10,... | collective-permute-start | bytes 393224 | tf_op jit(solution)/shard_map/ppermute | solution.py:255
  10.3 1.8 %collective-permute-start.5 = (bf16[4,64,256]{2,1,0:T(8,128)(2,1)S(1)}, bf16[4,64,256]{2,1,0:T(8,128)(2,1)S(1)}, u32[]{:S(2)}, u32[]{:S(2)}) collective-permute-start(bf16[4,64,256]{2,1,0:T(8,128)(2,1)S(1)} %collective-permute-done.refs_0_), channel_id=1, source_target_pairs={{0,4},{1,5},{2,6},{3,7},{4,0},{5,1},{6,2},{7,3},{8,12},{9,13},{10,... | collective-permute-start | bytes 393224 | tf_op jit(solution)/shard_map/ppermute | solution.py:253
  12.1 0.0 collective-permute-done.6.refs_1_
  12.1 3.9 %collective-permute-done.5.refs_2_ = bf16[4,64,256]{2,1,0:T(8,128)(2,1)S(1)} collective-permute-done((bf16[4,64,256]{2,1,0:T(8,128)(2,1)S(1)}, bf16[4,64,256]{2,1,0:T(8,128)(2,1)S(1)}, u32[]{:S(2)}, u32[]{:S(2)}) %collective-permute-start.5) | collective-permute-done | bytes 131104 | tf_op jit(solution)/shard_map/ppermute | solution.py:253
  15.9 0.0 collective-permute-done.4.refs_4_
  15.9 0.6 %collective-permute-start.8 = (bf16[8,64,256]{2,1,0:T(8,128)(2,1)S(1)}, bf16[8,64,256]{2,1,0:T(8,128)(2,1)S(1)}, u32[]{:S(2)}, u32[]{:S(2)}) collective-permute-start(bf16[8,64,256]{2,1,0:T(8,128)(2,1)S(1)} %collective-permute-done.4.refs_4_), channel_id=1, source_target_pairs={{0,2},{1,3},{2,0},{3,1},{4,6},{5,7},{6,4},{7,5},{8,10},{9,11},{10,... | collective-permute-start | bytes 786440 | tf_op jit(solution)/shard_map/ppermute | solution.py:259
  16.5 1.5 %collective-permute-start.1 = (bf16[5,128,128]{2,1,0:T(8,128)(2,1)S(1)}, bf16[5,128,128]{2,1,0:T(8,128)(2,1)S(1)}, u32[]{:S(2)}, u32[]{:S(2)}) collective-permute-start(bf16[5,128,128]{2,1,0:T(8,128)(2,1)S(1)} %bitcast.16), channel_id=1, source_target_pairs={{0,1},{1,0},{2,3},{3,2},{4,5},{5,4},{6,7},{7,6},{8,9},{9,8},{10,11... | collective-permute-start | bytes 491528 | tf_op jit(solution)/shard_map/ppermute | solution.py:254
  18.0 0.3 collective-permute-start.7
  18.3 3.2 %collective-permute-start.2 = (bf16[1,128,128]{2,1,0:T(8,128)(2,1)S(1)}, bf16[1,128,128]{2,1,0:T(8,128)(2,1)S(1)}, u32[]{:S(2)}, u32[]{:S(2)}) collective-permute-start(bf16[1,128,128]{2,1,0:T(8,128)(2,1)S(1)} %get-tuple-element.16), channel_id=1, source_target_pairs={{0,2},{2,4},{4,6},{6,8},{8,10},{10,12},{12,14},{14,16},{16,18},{18... | collective-permute-start | bytes 98312 | tf_op jit(solution)/shard_map/ppermute | solution.py:256
  21.5 1.9 %collective-permute-start.3 = (bf16[1,128,128]{2,1,0:T(8,128)(2,1)S(1)}, bf16[1,128,128]{2,1,0:T(8,128)(2,1)S(1)}, u32[]{:S(2)}, u32[]{:S(2)}) collective-permute-start(bf16[1,128,128]{2,1,0:T(8,128)(2,1)S(1)} %get-tuple-element.17), channel_id=1, source_target_pairs={{1,2},{3,4},{5,6},{7,8},{9,10},{11,12},{13,14},{15,16},{17,18},{19... | collective-permute-start | bytes 98312 | tf_op jit(solution)/shard_map/ppermute | solution.py:257
  23.5 0.0 collective-permute-done.2.near_ref
  23.5 3.3 %collective-permute-done.3.far_ref = bf16[1,128,128]{2,1,0:T(8,128)(2,1)S(1)} collective-permute-done((bf16[1,128,128]{2,1,0:T(8,128)(2,1)S(1)}, bf16[1,128,128]{2,1,0:T(8,128)(2,1)S(1)}, u32[]{:S(2)}, u32[]{:S(2)}) %collective-permute-start.3) | collective-permute-done | bytes 32800 | tf_op jit(solution)/shard_map/ppermute | solution.py:257
  26.8 0.0 collective-permute-done.1.peer_ref
  26.8 0.0 collective-permute-done.7.refs_3_
  26.8 0.0 collective-permute-done.8.refs_5_
  26.8 0.0 copy-done
  26.8 7.0 %shard_map.55 = bf16[128,2,8,256]{3,2,1,0:T(8,128)(2,1)} custom-call(bf16[8,128,128]{2,1,0:T(8,128)(2,1)S(1)} %bitcast.15, bf16[5,128,128]{2,1,0:T(8,128)(2,1)S(1)} %collective-permute-done.1.peer_ref, bf16[1,128,128]{2,1,0:T(8,128)(2,1)S(1)} %collective-permute-done.2.near_ref, bf16[1,128,128]{2,1,0:T(8,128)(2,1)S(1)} %collective-permute-done.3.far_ref, ...), custom_call_target="tpu_custom_call" | custom-call | tf_op jit(solution)/shard_map/pallas_call | solution.py:206
  (2 shorter events, 0.0 us)
Async XLA Ops:
  0.0 26.8 %copy-start = (bf16[64,64,256]{2,1,0:T(8,128)(2,1)S(1)}, bf16[64,64,256]{2,1,0:T(8,128)(2,1)}, u32[]{:S(2)}) copy-start(bf16[64,64,256]{2,1,0:T(8,128)(2,1)} %w_own_ref.1) | copy-start | bytes 6291460
  2.7 5.6 %collective-permute-start = (bf16[4,64,256]{2,1,0:T(8,128)(2,1)}, bf16[4,64,256]{2,1,0:T(8,128)(2,1)S(1)}, u32[]{:S(2)}, u32[]{:S(2)}) collective-permute-start(bf16[4,64,256]{2,1,0:T(8,128)(2,1)} %constant_dynamic-slice_fusion.2), channel_id=1, source_target_pairs={{0,1},{1,0},{2,3},{3,2},{4,5},{5,4},{6,7},{7,6},{8,9},{9,8},{10,11... | collective-permute-start | bytes 393224 | tf_op jit(solution)/shard_map/ppermute | solution.py:244
  4.8 11.1 %collective-permute-start.4 = (bf16[8,64,256]{2,1,0:T(8,128)(2,1)S(1)}, bf16[8,64,256]{2,1,0:T(8,128)(2,1)S(1)}, u32[]{:S(2)}, u32[]{:S(2)}) collective-permute-start(bf16[8,64,256]{2,1,0:T(8,128)(2,1)S(1)} %constant_dynamic-slice_fusion.1), channel_id=1, source_target_pairs={{0,1},{1,0},{2,3},{3,2},{4,5},{5,4},{6,7},{7,6},{8,9},{9,8},{10,11... | collective-permute-start | bytes 786440 | tf_op jit(solution)/shard_map/ppermute | solution.py:245
  8.3 3.8 %collective-permute-start.6 = (bf16[4,64,256]{2,1,0:T(8,128)(2,1)S(1)}, bf16[4,64,256]{2,1,0:T(8,128)(2,1)S(1)}, u32[]{:S(2)}, u32[]{:S(2)}) collective-permute-start(bf16[4,64,256]{2,1,0:T(8,128)(2,1)S(1)} %collective-permute-done.refs_0_), channel_id=1, source_target_pairs={{0,2},{1,3},{2,0},{3,1},{4,6},{5,7},{6,4},{7,5},{8,10},{9,11},{10,... | collective-permute-start | bytes 393224 | tf_op jit(solution)/shard_map/ppermute | solution.py:255
  10.3 5.6 %collective-permute-start.5 = (bf16[4,64,256]{2,1,0:T(8,128)(2,1)S(1)}, bf16[4,64,256]{2,1,0:T(8,128)(2,1)S(1)}, u32[]{:S(2)}, u32[]{:S(2)}) collective-permute-start(bf16[4,64,256]{2,1,0:T(8,128)(2,1)S(1)} %collective-permute-done.refs_0_), channel_id=1, source_target_pairs={{0,4},{1,5},{2,6},{3,7},{4,0},{5,1},{6,2},{7,3},{8,12},{9,13},{10,... | collective-permute-start | bytes 393224 | tf_op jit(solution)/shard_map/ppermute | solution.py:253
  15.9 10.8 %collective-permute-start.8 = (bf16[8,64,256]{2,1,0:T(8,128)(2,1)S(1)}, bf16[8,64,256]{2,1,0:T(8,128)(2,1)S(1)}, u32[]{:S(2)}, u32[]{:S(2)}) collective-permute-start(bf16[8,64,256]{2,1,0:T(8,128)(2,1)S(1)} %collective-permute-done.4.refs_4_), channel_id=1, source_target_pairs={{0,2},{1,3},{2,0},{3,1},{4,6},{5,7},{6,4},{7,5},{8,10},{9,11},{10,... | collective-permute-start | bytes 786440 | tf_op jit(solution)/shard_map/ppermute | solution.py:259
  16.5 10.2 %collective-permute-start.1 = (bf16[5,128,128]{2,1,0:T(8,128)(2,1)S(1)}, bf16[5,128,128]{2,1,0:T(8,128)(2,1)S(1)}, u32[]{:S(2)}, u32[]{:S(2)}) collective-permute-start(bf16[5,128,128]{2,1,0:T(8,128)(2,1)S(1)} %bitcast.16), channel_id=1, source_target_pairs={{0,1},{1,0},{2,3},{3,2},{4,5},{5,4},{6,7},{7,6},{8,9},{9,8},{10,11... | collective-permute-start | bytes 491528 | tf_op jit(solution)/shard_map/ppermute | solution.py:254
  18.0 8.8 %collective-permute-start.7 = (bf16[4,64,256]{2,1,0:T(8,128)(2,1)S(1)}, bf16[4,64,256]{2,1,0:T(8,128)(2,1)S(1)}, u32[]{:S(2)}, u32[]{:S(2)}) collective-permute-start(bf16[4,64,256]{2,1,0:T(8,128)(2,1)S(1)} %collective-permute-done.5.refs_2_), channel_id=1, source_target_pairs={{0,2},{1,3},{2,0},{3,1},{4,6},{5,7},{6,4},{7,5},{8,10},{9,11},{10,... | collective-permute-start | bytes 393224 | tf_op jit(solution)/shard_map/ppermute | solution.py:260
  18.3 5.2 %collective-permute-start.2 = (bf16[1,128,128]{2,1,0:T(8,128)(2,1)S(1)}, bf16[1,128,128]{2,1,0:T(8,128)(2,1)S(1)}, u32[]{:S(2)}, u32[]{:S(2)}) collective-permute-start(bf16[1,128,128]{2,1,0:T(8,128)(2,1)S(1)} %get-tuple-element.16), channel_id=1, source_target_pairs={{0,2},{2,4},{4,6},{6,8},{8,10},{10,12},{12,14},{14,16},{16,18},{18... | collective-permute-start | bytes 98312 | tf_op jit(solution)/shard_map/ppermute | solution.py:256
  21.5 5.2 %collective-permute-start.3 = (bf16[1,128,128]{2,1,0:T(8,128)(2,1)S(1)}, bf16[1,128,128]{2,1,0:T(8,128)(2,1)S(1)}, u32[]{:S(2)}, u32[]{:S(2)}) collective-permute-start(bf16[1,128,128]{2,1,0:T(8,128)(2,1)S(1)} %get-tuple-element.17), channel_id=1, source_target_pairs={{1,2},{3,4},{5,6},{7,8},{9,10},{11,12},{13,14},{15,16},{17,18},{19... | collective-permute-start | bytes 98312 | tf_op jit(solution)/shard_map/ppermute | solution.py:257

commit v5 on v0

v5 whole, which is shorter than its diff:
```python
import functools

import jax
import jax.numpy as jnp
from jax import lax
from jax.experimental import pallas as pl
from jax.experimental.pallas import tpu as pltpu
from jax.sharding import PartitionSpec as P

AXES = ("space", "ch")
PHASES = (((1, 0), (3, -1)), ((2, 0), (0, 1)))
COLUMNS = ((3, 0, 1), (0, 1, 2))
VMEM = pl.BlockSpec(memory_space=pltpu.VMEM)
ANY = pl.BlockSpec(memory_space=pl.ANY)
LIMIT = 40 * 2**20


def column_of(bias):
    lanes = bias.shape[-1]
    return jnp.transpose(jnp.broadcast_to(bias, (lanes, lanes)))


def shifted(value, step):
    cols = value.shape[1]
    place = lax.broadcasted_iota(jnp.int32, value.shape, 1)
    edge = 0 if step == 1 else cols - 1
    return jnp.where(place == edge, 0.0, pltpu.roll(value, step % cols, 1))


def upsample(x_ref, tap_of, bias, u_ref, first, last):
    held, cols = u_ref.shape[1], u_ref.shape[3]
    for row_phase in (0, 1):
        for col_phase in (0, 1):
            taps = []
            for row_tap, row_shift in PHASES[row_phase]:
                for col_tap, col_shift in PHASES[col_phase]:
                    slot = row_shift + 1 - row_phase
                    taps.append((row_tap * 4 + col_tap, slot, col_shift % 3))
            kernel = jnp.concatenate([tap_of(tap) for tap, _, _ in taps], axis=1)
            for start in range(0, held // 2, 2):
                places = range(start, min(start + 2, held // 2))
                cells = jnp.concatenate(
                    [
                        jnp.concatenate([x_ref[copy, slot + place] for place in places], axis=1)
                        for _, slot, copy in taps
                    ],
                    axis=0,
                )
                summed = jnp.dot(kernel, cells, preferred_element_type=jnp.float32)
                for number, place in enumerate(places):
                    row = 2 * place + 1 - row_phase
                    value = summed[:, number * cols : (number + 1) * cols] + bias
                    value = jnp.where(value > 0, value, 0.2 * value)
                    if row == 0:
                        value = jnp.where(first, 0.0, value)
                    if row == held - 1:
                        value = jnp.where(last, 0.0, value)
                    u_ref[col_phase, row] = value.astype(jnp.bfloat16)
                    moved = shifted(value, -1 if col_phase == 0 else 1)
                    u_ref[2 + col_phase, row] = moved.astype(jnp.bfloat16)


def convolve(kernel, u_ref, start, col_phase):
    cells = jnp.concatenate(
        [
            jnp.concatenate([u_ref[copy, start + row_tap], u_ref[copy, start + row_tap + 1]], 1)
            for row_tap in range(3)
            for copy in COLUMNS[col_phase]
        ],
        axis=0,
    )
    return jnp.dot(kernel, cells, preferred_element_type=jnp.float32)


def split_kernels(w_conv_ref, halves_ref):
    cout = w_conv_ref.shape[1]
    part = cout // 2
    low = lax.broadcasted_iota(jnp.int32, (cout, cout), 1) < part
    for row_tap in range(3):
        for col_tap in range(3):
            taps = [w_conv_ref[a * 9 + row_tap * 3 + col_tap].astype(jnp.float32) for a in range(3)]
            turned = [pltpu.roll(tap, part, 1) for tap in taps]
            columns = pl.ds((row_tap * 3 + col_tap) * cout, cout)
            for plane in (0, 1):
                near, far = 1 - plane, 2 - plane
                rows = pl.ds(plane * cout, cout)
                halves_ref[0, rows, columns] = jnp.where(low, taps[near], turned[far]).astype(jnp.bfloat16)
                halves_ref[1, rows, columns] = jnp.where(low, turned[near], taps[far]).astype(jnp.bfloat16)


def bias_of(bias_ref, column_ref, half):
    column_ref[...] = column_of(bias_ref[...])
    part = column_ref.shape[0] // 2
    bias = column_ref[pl.ds(pl.multiple_of(half * part, part), part)]
    return jnp.concatenate([bias, bias], axis=0)


def ends(s, c):
    first = (s == 0) & (c == 0)
    last = (s == lax.axis_size("space") - 1) & (c == lax.axis_size("ch") - 1)
    return first, last


def store_row(x_ref, slot, offset, value):
    where = pl.ds(pl.multiple_of(offset, 16), value.shape[0])
    x_ref[0, slot, where] = value.astype(jnp.bfloat16)
    x_ref[1, slot, where] = shifted(value, -1).astype(jnp.bfloat16)
    x_ref[2, slot, where] = shifted(value, 1).astype(jnp.bfloat16)


def own_part(half, first, last, w_half_ref, b_up_ref, w_conv_ref, x_ref, sum_ref, other_ref, halves_ref, column_ref, u_ref):
    planes = (w_half_ref.shape[0] - 32) // 2
    split_kernels(w_conv_ref, halves_ref)
    other_ref[...] = halves_ref[1 - half]

    def tap_of(tap):
        return jnp.concatenate([w_half_ref[planes + tap], w_half_ref[planes + 16 + tap]], axis=0)

    upsample(x_ref, tap_of, bias_of(b_up_ref, column_ref, half), u_ref, first, last)
    kernel = halves_ref[half]
    cols = u_ref.shape[3]
    for start in range(0, u_ref.shape[1] - 2, 2):
        for col_phase in (0, 1):
            sum_ref[col_phase, :, start * cols : (start + 2) * cols] = convolve(kernel, u_ref, start, col_phase)


def paired_first(own_ref, peer_ref, halo_ref, w_half_ref, b_up_ref, w_conv_ref, x_ref, sum_ref, other_ref, *scratch):
    *rest, wide_ref = scratch
    s, c = lax.axis_index("space"), lax.axis_index("ch")
    chans, rows, cols = own_ref.shape
    share = rows // 2 + 1
    for number, source in enumerate((own_ref, peer_ref)):
        wide_ref[number] = source[...].astype(jnp.float32).reshape(chans * rows, cols)
    for number in (0, 1):
        offset = (c if number == 0 else 1 - c) * chans
        for place in range(share):
            value = wide_ref[number, pl.ds(place + c * (rows - share), chans, stride=rows), :]
            store_row(x_ref, place + 1 - c, offset, value)
        store_row(x_ref, c * share, offset, halo_ref[number].astype(jnp.float32))
    own_part(c, *ends(s, c), w_half_ref, b_up_ref, w_conv_ref, x_ref, sum_ref, other_ref, *rest)


def gathered_first(rows_ref, w_half_ref, b_up_ref, w_conv_ref, x_ref, sum_ref, other_ref, *scratch):
    s, c = lax.axis_index("space"), lax.axis_index("ch")
    for slot in range(rows_ref.shape[0]):
        store_row(x_ref, slot, 0, rows_ref[slot].astype(jnp.float32))
    own_part(0, *ends(s, c), w_half_ref, b_up_ref, w_conv_ref, x_ref, sum_ref, other_ref, *scratch)


def second(paired, count, *refs):
    parts, refs = refs[:count], refs[count:]
    x_ref, sum_ref, other_ref, b_up_ref, b_conv_ref, out_ref, w_ref, column_ref, u_ref, total_ref, sems = refs
    s, c = lax.axis_index("space"), lax.axis_index("ch")
    half = 1 - c if paired else 1
    copies = []
    if paired:
        me, core = lax.rem(s, 4), lax.rem(s, 2)
        x = me // 2
        taps = [4 * (2 * i + j) for i in (x, 1 - x) for j in (core, 1 - core)] + [8 * core, 8 - 8 * core]
        for number, part_ref in enumerate(parts):
            place = w_ref.at[number // 4, pl.ds(taps[number], part_ref.shape[0])]
            copies.append(pltpu.make_async_copy(part_ref, place, sems.at[number]))
    else:
        for plane in (0, 1):
            source = parts[0].at[pl.ds(16 * plane, 16)]
            copies.append(pltpu.make_async_copy(source, w_ref.at[plane], sems.at[plane]))
    for copy in copies:
        copy.start()
    cout, _, rows, _ = out_ref.shape
    cols = x_ref.shape[3]
    source = lax.broadcasted_iota(jnp.int32, (2 * cols, 2 * cols), 0)
    target = lax.broadcasted_iota(jnp.int32, (2 * cols, 2 * cols), 1)
    wanted = jnp.where(source < cols, 2 * source, 2 * (source - cols) + 1)
    interleave = jnp.where(wanted == target, 1.0, 0.0).astype(jnp.bfloat16)
    bias = bias_of(b_up_ref, column_ref, half)
    for copy in copies:
        copy.wait()

    def tap_of(tap):
        return jnp.concatenate([w_ref[0, tap], w_ref[1, tap]], axis=0)

    upsample(x_ref, tap_of, bias, u_ref, *ends(s, c))
    kernel = other_ref[...]
    bias = column_of(b_conv_ref[...])
    bias = jnp.concatenate([bias, bias], axis=0)
    for start in range(0, rows, 2):
        halves = [
            convolve(kernel, u_ref, start, col_phase) + sum_ref[col_phase, :, start * cols : (start + 2) * cols]
            for col_phase in (0, 1)
        ]
        for number in (0, 1):
            pair = [
                (half[:, number * cols : (number + 1) * cols] + bias).astype(jnp.bfloat16) for half in halves
            ]
            mixed = jnp.dot(jnp.concatenate(pair, axis=1), interleave, preferred_element_type=jnp.float32)
            for side in (0, 1):
                total_ref[side, pl.ds(start + number, 2 * cout, stride=rows), :] = mixed[
                    :, side * cols : (side + 1) * cols
                ]
    for plane in (0, 1):
        for side in (0, 1):
            block = total_ref[side, pl.ds(plane * cout * rows, cout * rows), :]
            out_ref[:, plane, :, side * cols : (side + 1) * cols] = block.reshape(cout, rows, cols).astype(
                jnp.bfloat16
            )


def cost(sizes, read):
    cin, cout, rows, cols = sizes
    flops = 2 * cout * 4 * cin * 2 * cols * (rows + 2) + 2 * 2 * cout * 9 * cout * 2 * cols * rows
    return pl.CostEstimate(flops=flops, bytes_accessed=read, transcendentals=0)


def call_first(body, operands, wide, sizes):
    cin, cout, rows, cols = sizes
    return pl.pallas_call(
        body,
        out_shape=(
            jax.ShapeDtypeStruct((3, rows // 2 + 2, cin, cols), jnp.bfloat16),
            jax.ShapeDtypeStruct((2, 2 * cout, rows * cols), jnp.float32),
            jax.ShapeDtypeStruct((2 * cout, 9 * cout), jnp.bfloat16),
        ),
        in_specs=[VMEM] * len(operands),
        out_specs=(VMEM,) * 3,
        scratch_shapes=[
            pltpu.VMEM((2, 2 * cout, 9 * cout), jnp.bfloat16),
            pltpu.VMEM((cout, cout), jnp.float32),
            pltpu.VMEM((4, rows + 2, cout, cols), jnp.bfloat16),
        ]
        + wide,
        cost_estimate=cost(sizes, 8 * 2**20),
        compiler_params=pltpu.CompilerParams(vmem_limit_bytes=LIMIT),
    )(*operands)


def call_second(paired, parts, results, biases, sizes):
    cin, cout, rows, cols = sizes
    return pl.pallas_call(
        functools.partial(second, paired, len(parts)),
        out_shape=jax.ShapeDtypeStruct((cout, 2, rows, 2 * cols), jnp.bfloat16),
        in_specs=[ANY] * len(parts) + [VMEM] * 5,
        out_specs=VMEM,
        scratch_shapes=[
            pltpu.VMEM((2, 16, cout // 2, cin), jnp.bfloat16),
            pltpu.VMEM((cout, cout), jnp.float32),
            pltpu.VMEM((4, rows + 2, cout, cols), jnp.bfloat16),
            pltpu.VMEM((2, 2 * cout * rows, cols), jnp.float32),
            pltpu.SemaphoreType.DMA((6,)),
        ],
        cost_estimate=cost(sizes, 8 * 2**20),
        compiler_params=pltpu.CompilerParams(vmem_limit_bytes=LIMIT),
    )(*parts, *results, *biases)


def paired(inputs, w_up, b_up, w_conv, b_conv, sizes):
    spaces = lax.axis_size("space")
    s, c = lax.axis_index("space"), lax.axis_index("ch")
    chans, _, held, cols = inputs.shape

    def at(space, ch):
        return space * 2 + ch

    across = [(at(i, j), at(i, 1 - j)) for i in range(spaces) for j in (0, 1)]
    cores = [(at(i, j), at(i ^ 1, j)) for i in range(spaces) for j in (0, 1)]
    pairs = [(at(i, j), at(i ^ 2, j)) for i in range(spaces) for j in (0, 1)]
    chain = [(at(i - 1, 0), at(i, 0)) for i in range(1, spaces)]
    chain += [(at(i + 1, 1), at(i, 1)) for i in range(spaces - 1)]

    peer = lax.ppermute(inputs, AXES, across)
    w_a = lax.dynamic_slice_in_dim(w_up, 16 + 4 * lax.rem(s, 4), 4, 0)
    w_b = lax.dynamic_slice_in_dim(w_up, 32 + 8 * lax.rem(s, 2), 8, 0)
    w_a, w_b = lax.optimization_barrier((w_a, w_b))
    w_a = lax.ppermute(w_a, AXES, across)
    w_b = lax.ppermute(w_b, AXES, across)

    own, peer = inputs.reshape(chans, held, cols), peer.reshape(chans, held, cols)
    edges = [lax.dynamic_slice_in_dim(rows, (1 - c) * (held - 1), 1, 1)[:, 0] for rows in (own, peer)]
    halo = lax.ppermute(jnp.stack(edges), AXES, chain)
    w_a, halo = lax.optimization_barrier((w_a, halo))
    w_ax = lax.ppermute(w_a, AXES, pairs)
    w_ac = lax.ppermute(w_a, AXES, cores)
    biases = (b_up[None], b_conv[None])
    wide = [pltpu.VMEM((2, chans * held, cols), jnp.float32)]
    results = call_first(paired_first, (own, peer, halo, w_up, biases[0], w_conv), wide, sizes)
    w_b, w_ax, w_ac, *results = lax.optimization_barrier((w_b, w_ax, w_ac, *results))
    w_bc = lax.ppermute(w_b, AXES, cores)
    w_axc = lax.ppermute(w_ax, AXES, cores)
    return call_second(True, (w_a, w_ac, w_ax, w_axc, w_b, w_bc), results, biases, sizes)


def gathered(inputs, w_up, b_up, w_conv, b_conv, sizes):
    spaces, chs = lax.axis_size("space"), lax.axis_size("ch")
    c = lax.axis_index("ch")
    w_all = lax.all_gather(w_up[16:48], "ch", axis=1, tiled=True)
    part = w_all.shape[1] // 2
    rows = lax.all_gather(inputs[:, 0], "ch", axis=0, tiled=True).transpose(1, 0, 2)
    forward = [(i, i + 1) for i in range(spaces - 1)]
    backward = [(j, i) for i, j in forward]
    low = lax.ppermute(rows[-1:], "space", forward)
    high = lax.ppermute(rows[:1], "space", backward)
    rows = jnp.concatenate([low, rows, high], axis=0)
    share = inputs.shape[2] // chs
    rows = lax.dynamic_slice_in_dim(rows, c * share, share + 2, 0)
    biases = (b_up[None], b_conv[None])
    results = call_first(gathered_first, (rows, w_all[:, :part], biases[0], w_conv), [], sizes)
    return call_second(False, (w_all[:, part:],), results, biases, sizes)


def local(inputs, w_up, b_up, w_conv, b_conv):
    chs = lax.axis_size("ch")
    sizes = (w_up.shape[2], w_conv.shape[1], 2 * inputs.shape[2] // chs, inputs.shape[3])
    plan = paired if chs == 2 and lax.axis_size("space") % 4 == 0 else gathered
    return plan(inputs, w_up, b_up, w_conv, b_conv, sizes)


def solution(mesh):
    return jax.shard_map(
        local,
        mesh=mesh,
        in_specs=(P("ch", None, "space", None), P(None, "ch", None), P(), P(), P()),
        out_specs=P(None, None, ("space", "ch"), None),
        check_vma=False,
    )
```

time: 38.1 us -> 33.3 us (0.87)
  the two profiles are of different devices: /device:TPU:23 before, /device:TPU:0 now
where the time goes in v5:
time: 33.3 us; the launch traced here: 33 us
  starting transfers between devices  11.8 us (35%)
  Pallas kernels  8.77 us (26%)
  local copies, waits for them, and re-layouts  7.36 us (22%)
  waiting for transfers between devices  4.94 us (15%)
    pallas_call x1, Pallas kernels, call_second(): pl.pallas_call(functools.partial(second, paired, len(parts)), out_shape=j...  5.32 us
    unnamed x14, local copies, waits for them, and re-layouts  4.38 us
    pallas_call x1, Pallas kernels, call_first(): pl.pallas_call(body, out_shape=(jax.ShapeDtypeStruct((3, rows // 2 + 2, c...  3.45 us
    ppermute x1, starting transfers between devices, paired(): peer = lax.ppermute(inputs, AXES, across)  2.97 us
    ppermute x1, starting transfers between devices, paired(): w_ac = lax.ppermute(w_a, AXES, cores)  2.67 us
    ppermute x1, waiting for transfers between devices, paired(): peer = lax.ppermute(inputs, AXES, across)  2.32 us
    ppermute x1, starting transfers between devices, paired(): w_ax = lax.ppermute(w_a, AXES, pairs)  2.25 us
    ppermute x1, starting transfers between devices, paired(): w_b = lax.ppermute(w_b, AXES, across)  2.01 us
  transfers between devices with their start and end apart: 8, of which 3 were waited for; matrix products, arithmetic and copies ran while one was open for 9% of the time, Pallas kernels for 10%

profile of v5, /device:TPU:0, one launch (start us, length us, event | category | flops | bytes accessed | tf_op | source)
XLA Modules:
  0.0 33.0 jit_solution(3716650881632983070)
XLA Ops:
  0.0 3.0 %collective-permute-start.1 = (bf16[128,1,8,128]{3,2,0,1:T(8,128)(2,1)}, bf16[128,1,8,128]{3,2,0,1:T(8,128)(2,1)S(1)}, u32[]{:S(2)}, u32[]{:S(2)}) collective-permute-start(bf16[128,1,8,128]{3,2,0,1:T(8,128)(2,1)} %bitcast.11), channel_id=1, source_target_pairs={{0,1},{1,0},{2,3},{3,2},{4,5},{5,4},{6,7},{7,6},{8,9},{9,8},{10,11... | collective-permute-start | bytes 786440 | tf_op jit(solution)/shard_map/ppermute | solution.py:269
  3.0 0.9 %constant_dynamic-slice_fusion.3 = bf16[4,64,256]{2,1,0:T(8,128)(2,1)S(1)} fusion(bf16[64,64,256]{2,1,0:T(8,128)(2,1)} %w_half_ref.1, s32[]{:T(128)S(6)} %select_n.10), kind=kLoop, calls=%fused_computation.6 | loop fusion | bytes 262148 | tf_op jit(solution)/shard_map/dynamic_slice | solution.py:270
  3.9 1.0 %constant_dynamic-slice_fusion.2 = bf16[8,64,256]{2,1,0:T(8,128)(2,1)S(1)} fusion(bf16[64,64,256]{2,1,0:T(8,128)(2,1)} %w_half_ref.1, s32[]{:T(128)S(6)} %select_n.11), kind=kLoop, calls=%fused_computation.5 | loop fusion | bytes 524292 | tf_op jit(solution)/shard_map/dynamic_slice | solution.py:271
  4.9 0.1 collective-permute-start
  4.9 2.0 %collective-permute-start.3 = (bf16[8,64,256]{2,1,0:T(8,128)(2,1)S(1)}, bf16[8,64,256]{2,1,0:T(8,128)(2,1)S(1)}, u32[]{:S(2)}, u32[]{:S(2)}) collective-permute-start(bf16[8,64,256]{2,1,0:T(8,128)(2,1)S(1)} %constant_dynamic-slice_fusion.2), channel_id=1, source_target_pairs={{0,1},{1,0},{2,3},{3,2},{4,5},{5,4},{6,7},{7,6},{8,9},{9,8},{10,11... | collective-permute-start | bytes 786440 | tf_op jit(solution)/shard_map/ppermute | solution.py:274
  7.0 1.0 %constant_dynamic-slice_fusion.1 = bf16[128,1,1,128]{3,2,1,0:T(2,128)(2,1)S(1)} fusion(bf16[128,1,8,128]{3,2,1,0:T(8,128)(2,1)} %param.5, s32[]{:T(128)S(6)} %select_n.12), kind=kLoop, calls=%fused_computation.4 | loop fusion | bytes 65540 | tf_op jit(solution)/shard_map/dynamic_slice | solution.py:277
  8.0 2.3 %collective-permute-done.1 = bf16[128,1,8,128]{3,2,0,1:T(8,128)(2,1)S(1)} collective-permute-done((bf16[128,1,8,128]{3,2,0,1:T(8,128)(2,1)}, bf16[128,1,8,128]{3,2,0,1:T(8,128)(2,1)S(1)}, u32[]{:S(2)}, u32[]{:S(2)}) %collective-permute-start.1) | collective-permute-done | bytes 262176 | tf_op jit(solution)/shard_map/ppermute | solution.py:269
  10.3 0.1 constant_dynamic-slice_fusion
  10.4 1.3 %collective-permute-start.2 = (bf16[2,128,128]{2,1,0:T(8,128)(2,1)S(1)}, bf16[2,128,128]{2,1,0:T(8,128)(2,1)S(1)}, u32[]{:S(2)}, u32[]{:S(2)}) collective-permute-start(bf16[2,128,128]{2,1,0:T(8,128)(2,1)S(1)} %pad_maximum_fusion), channel_id=1, source_target_pairs={{0,2},{2,4},{4,6},{6,8},{8,10},{10,12},{12,14},{14,16},{16,18},{18... | collective-permute-start | bytes 196616 | tf_op jit(solution)/shard_map/ppermute | solution.py:278
  11.7 1.4 %collective-permute-done.refs_0_ = bf16[4,64,256]{2,1,0:T(8,128)(2,1)S(1)} collective-permute-done((bf16[4,64,256]{2,1,0:T(8,128)(2,1)S(1)}, bf16[4,64,256]{2,1,0:T(8,128)(2,1)S(1)}, u32[]{:S(2)}, u32[]{:S(2)}) %collective-permute-start) | collective-permute-done | bytes 131104 | tf_op jit(solution)/shard_map/ppermute | solution.py:273
  13.1 0.0 collective-permute-done.2.halo_ref
  13.1 2.7 %collective-permute-start.5 = (bf16[4,64,256]{2,1,0:T(8,128)(2,1)S(1)}, bf16[4,64,256]{2,1,0:T(8,128)(2,1)S(1)}, u32[]{:S(2)}, u32[]{:S(2)}) collective-permute-start(bf16[4,64,256]{2,1,0:T(8,128)(2,1)S(1)} %collective-permute-done.refs_0_), channel_id=1, source_target_pairs={{0,2},{1,3},{2,0},{3,1},{4,6},{5,7},{6,4},{7,5},{8,10},{9,11},{10,... | collective-permute-start | bytes 393224 | tf_op jit(solution)/shard_map/ppermute | solution.py:281
  15.8 2.2 %collective-permute-start.4 = (bf16[4,64,256]{2,1,0:T(8,128)(2,1)S(1)}, bf16[4,64,256]{2,1,0:T(8,128)(2,1)S(1)}, u32[]{:S(2)}, u32[]{:S(2)}) collective-permute-start(bf16[4,64,256]{2,1,0:T(8,128)(2,1)S(1)} %collective-permute-done.refs_0_), channel_id=1, source_target_pairs={{0,4},{1,5},{2,6},{3,7},{4,0},{5,1},{6,2},{7,3},{8,12},{9,13},{10,... | collective-permute-start | bytes 393224 | tf_op jit(solution)/shard_map/ppermute | solution.py:280
  18.0 0.0 copy-start
  18.0 1.6 %copy-done = bf16[64,64,256]{2,1,0:T(8,128)(2,1)S(1)} copy-done((bf16[64,64,256]{2,1,0:T(8,128)(2,1)S(1)}, bf16[64,64,256]{2,1,0:T(8,128)(2,1)}, u32[]{:S(2)}) %copy-start) | copy-done | bytes 2097176
  19.6 0.0 copy-start.1
  19.6 0.9 %copy-done.1 = bf16[128,1,8,128]{3,2,1,0:T(8,128)(2,1)S(1)} copy-done((bf16[128,1,8,128]{3,2,1,0:T(8,128)(2,1)S(1)}, bf16[128,1,8,128]{3,2,1,0:T(8,128)(2,1)}, u32[]{:S(2)}) %copy-start.1) | copy-done | bytes 262168
  20.6 0.0 copy-start.2
  20.6 1.2 %copy-done.2 = bf16[27,128,128]{2,1,0:T(8,128)(2,1)S(1)} copy-done((bf16[27,128,128]{2,1,0:T(8,128)(2,1)S(1)}, bf16[27,128,128]{2,1,0:T(8,128)(2,1)}, u32[]{:S(2)}) %copy-start.2) | copy-done | bytes 884760
  21.8 0.0 copy-start.3
  21.8 0.7 %copy-done.3 = f32[128]{0:T(128)S(1)} copy-done((f32[128]{0:T(128)S(1)}, f32[128]{0:T(128)}, u32[]{:S(2)}) %copy-start.3) | copy-done | bytes 536
  22.4 0.0 copy-start.4
  22.4 0.0 copy-start.5
  22.4 3.4 %shard_map.55 = (bf16[3,6,256,128]{3,2,1,0:T(8,128)(2,1)S(1)}, f32[2,256,1024]{2,1,0:T(8,128)S(1)}, bf16[256,1152]{1,0:T(8,128)(2,1)S(1)}) custom-call(bf16[128,8,128]{2,1,0:T(8,128)(2,1)S(1)} %bitcast.12, bf16[128,8,128]{2,1,0:T(8,128)(2,1)S(1)} %bitcast.13, bf16[2,128,128]{2,1,0:T(8,128)(2,1)S(1)} %collective-permute-done.2.halo_ref, ...), custom_call_target="tpu_custom_call" | custom-call | flops 1879048192 | bytes 8388608 | tf_op jit(solution)/shard_map/pallas_call | solution.py:216
  25.9 0.0 collective-permute-done.3.refs_4_
  25.9 0.0 collective-permute-done.5.refs_1_
  25.9 0.0 collective-permute-done.4.refs_2_
  25.9 0.3 collective-permute-start.7
  26.2 0.3 collective-permute-start.6
  26.5 1.2 %collective-permute-done.6.refs_3_ = bf16[4,64,256]{2,1,0:T(8,128)(2,1)S(1)} collective-permute-done((bf16[4,64,256]{2,1,0:T(8,128)(2,1)S(1)}, bf16[4,64,256]{2,1,0:T(8,128)(2,1)S(1)}, u32[]{:S(2)}, u32[]{:S(2)}) %collective-permute-start.6) | collective-permute-done | bytes 131104 | tf_op jit(solution)/shard_map/ppermute | solution.py:287
  27.7 0.0 collective-permute-done.7.refs_5_
  27.7 0.0 copy-done.4
  27.7 0.0 copy-done.5
  27.7 5.3 %shard_map.56 = bf16[128,2,8,256]{3,2,1,0:T(8,128)(2,1)} custom-call(bf16[4,64,256]{2,1,0:T(8,128)(2,1)S(1)} %collective-permute-done.refs_0_, bf16[4,64,256]{2,1,0:T(8,128)(2,1)S(1)} %collective-permute-done.5.refs_1_, bf16[4,64,256]{2,1,0:T(8,128)(2,1)S(1)} %collective-permute-done.4.refs_2_, bf16[4,64,256]{2,1,0:T(8,128)(2,1)S(1)} %collective-permute-done.6.refs_3_, ...), custom_call_target="tpu_custom_call" | custom-call | flops 1879048192 | bytes 8388608 | tf_op jit(solution)/shard_map/pallas_call | solution.py:238
  (3 shorter events, 0.0 us)
Async XLA Ops:
  0.0 10.3 %collective-permute-start.1 = (bf16[128,1,8,128]{3,2,0,1:T(8,128)(2,1)}, bf16[128,1,8,128]{3,2,0,1:T(8,128)(2,1)S(1)}, u32[]{:S(2)}, u32[]{:S(2)}) collective-permute-start(bf16[128,1,8,128]{3,2,0,1:T(8,128)(2,1)} %bitcast.11), channel_id=1, source_target_pairs={{0,1},{1,0},{2,3},{3,2},{4,5},{5,4},{6,7},{7,6},{8,9},{9,8},{10,11... | collective-permute-start | bytes 786440 | tf_op jit(solution)/shard_map/ppermute | solution.py:269
  4.9 8.3 %collective-permute-start = (bf16[4,64,256]{2,1,0:T(8,128)(2,1)S(1)}, bf16[4,64,256]{2,1,0:T(8,128)(2,1)S(1)}, u32[]{:S(2)}, u32[]{:S(2)}) collective-permute-start(bf16[4,64,256]{2,1,0:T(8,128)(2,1)S(1)} %constant_dynamic-slice_fusion.3), channel_id=1, source_target_pairs={{0,1},{1,0},{2,3},{3,2},{4,5},{5,4},{6,7},{7,6},{8,9},{9,8},{10,11... | collective-permute-start | bytes 393224 | tf_op jit(solution)/shard_map/ppermute | solution.py:273
  4.9 20.9 %collective-permute-start.3 = (bf16[8,64,256]{2,1,0:T(8,128)(2,1)S(1)}, bf16[8,64,256]{2,1,0:T(8,128)(2,1)S(1)}, u32[]{:S(2)}, u32[]{:S(2)}) collective-permute-start(bf16[8,64,256]{2,1,0:T(8,128)(2,1)S(1)} %constant_dynamic-slice_fusion.2), channel_id=1, source_target_pairs={{0,1},{1,0},{2,3},{3,2},{4,5},{5,4},{6,7},{7,6},{8,9},{9,8},{10,11... | collective-permute-start | bytes 786440 | tf_op jit(solution)/shard_map/ppermute | solution.py:274
  10.4 2.7 %collective-permute-start.2 = (bf16[2,128,128]{2,1,0:T(8,128)(2,1)S(1)}, bf16[2,128,128]{2,1,0:T(8,128)(2,1)S(1)}, u32[]{:S(2)}, u32[]{:S(2)}) collective-permute-start(bf16[2,128,128]{2,1,0:T(8,128)(2,1)S(1)} %pad_maximum_fusion), channel_id=1, source_target_pairs={{0,2},{2,4},{4,6},{6,8},{8,10},{10,12},{12,14},{14,16},{16,18},{18... | collective-permute-start | bytes 196616 | tf_op jit(solution)/shard_map/ppermute | solution.py:278
  13.1 12.8 %collective-permute-start.5 = (bf16[4,64,256]{2,1,0:T(8,128)(2,1)S(1)}, bf16[4,64,256]{2,1,0:T(8,128)(2,1)S(1)}, u32[]{:S(2)}, u32[]{:S(2)}) collective-permute-start(bf16[4,64,256]{2,1,0:T(8,128)(2,1)S(1)} %collective-permute-done.refs_0_), channel_id=1, source_target_pairs={{0,2},{1,3},{2,0},{3,1},{4,6},{5,7},{6,4},{7,5},{8,10},{9,11},{10,... | collective-permute-start | bytes 393224 | tf_op jit(solution)/shard_map/ppermute | solution.py:281
  15.8 10.1 %collective-permute-start.4 = (bf16[4,64,256]{2,1,0:T(8,128)(2,1)S(1)}, bf16[4,64,256]{2,1,0:T(8,128)(2,1)S(1)}, u32[]{:S(2)}, u32[]{:S(2)}) collective-permute-start(bf16[4,64,256]{2,1,0:T(8,128)(2,1)S(1)} %collective-permute-done.refs_0_), channel_id=1, source_target_pairs={{0,4},{1,5},{2,6},{3,7},{4,0},{5,1},{6,2},{7,3},{8,12},{9,13},{10,... | collective-permute-start | bytes 393224 | tf_op jit(solution)/shard_map/ppermute | solution.py:280
  18.0 1.6 %copy-start = (bf16[64,64,256]{2,1,0:T(8,128)(2,1)S(1)}, bf16[64,64,256]{2,1,0:T(8,128)(2,1)}, u32[]{:S(2)}) copy-start(bf16[64,64,256]{2,1,0:T(8,128)(2,1)} %w_half_ref.1) | copy-start | bytes 6291460
  19.6 0.9 %copy-start.1 = (bf16[128,1,8,128]{3,2,1,0:T(8,128)(2,1)S(1)}, bf16[128,1,8,128]{3,2,1,0:T(8,128)(2,1)}, u32[]{:S(2)}) copy-start(bf16[128,1,8,128]{3,2,1,0:T(8,128)(2,1)} %param.5) | copy-start | bytes 786436
  20.6 1.2 %copy-start.2 = (bf16[27,128,128]{2,1,0:T(8,128)(2,1)S(1)}, bf16[27,128,128]{2,1,0:T(8,128)(2,1)}, u32[]{:S(2)}) copy-start(bf16[27,128,128]{2,1,0:T(8,128)(2,1)} %w_conv_ref.1) | copy-start | bytes 2654212
  21.8 0.7 %copy-start.3 = (f32[128]{0:T(128)S(1)}, f32[128]{0:T(128)}, u32[]{:S(2)}) copy-start(f32[128]{0:T(128)} %param.7) | copy-start | bytes 1540
  22.4 5.3 %copy-start.4 = (f32[128]{0:T(128)S(1)}, f32[128]{0:T(128)}, u32[]{:S(2)}) copy-start(f32[128]{0:T(128)} %param.7) | copy-start | bytes 1540
  22.4 5.3 %copy-start.5 = (f32[128]{0:T(128)S(1)}, f32[128]{0:T(128)}, u32[]{:S(2)}) copy-start(f32[128]{0:T(128)} %param.9) | copy-start | bytes 1540
  25.9 1.8 %collective-permute-start.7 = (bf16[8,64,256]{2,1,0:T(8,128)(2,1)S(1)}, bf16[8,64,256]{2,1,0:T(8,128)(2,1)S(1)}, u32[]{:S(2)}, u32[]{:S(2)}) collective-permute-start(bf16[8,64,256]{2,1,0:T(8,128)(2,1)S(1)} %collective-permute-done.3.refs_4_), channel_id=1, source_target_pairs={{0,2},{1,3},{2,0},{3,1},{4,6},{5,7},{6,4},{7,5},{8,10},{9,11},{10,... | collective-permute-start | bytes 786440 | tf_op jit(solution)/shard_map/ppermute | solution.py:286
  26.2 1.5 %collective-permute-start.6 = (bf16[4,64,256]{2,1,0:T(8,128)(2,1)S(1)}, bf16[4,64,256]{2,1,0:T(8,128)(2,1)S(1)}, u32[]{:S(2)}, u32[]{:S(2)}) collective-permute-start(bf16[4,64,256]{2,1,0:T(8,128)(2,1)S(1)} %collective-permute-done.4.refs_2_), channel_id=1, source_target_pairs={{0,2},{1,3},{2,0},{3,1},{4,6},{5,7},{6,4},{7,5},{8,10},{9,11},{10,... | collective-permute-start | bytes 393224 | tf_op jit(solution)/shard_map/ppermute | solution.py:287

commit v6 on v5

--- a/solution.py
+++ b/solution.py
@@ -50,7 +50,7 @@
                 for number, place in enumerate(places):
                     row = 2 * place + 1 - row_phase
                     value = summed[:, number * cols : (number + 1) * cols] + bias
-                    value = jnp.where(value > 0, value, 0.2 * value)
+                    value = jnp.maximum(value, 0.2 * value)
                     if row == 0:
                         value = jnp.where(first, 0.0, value)
                     if row == held - 1:
@@ -88,11 +88,9 @@
                 halves_ref[1, rows, columns] = jnp.where(low, turned[near], taps[far]).astype(jnp.bfloat16)
 
 
-def bias_of(bias_ref, column_ref, half):
+def bias_of(bias_ref, column_ref, blocks):
     column_ref[...] = column_of(bias_ref[...])
-    part = column_ref.shape[0] // 2
-    bias = column_ref[pl.ds(pl.multiple_of(half * part, part), part)]
-    return jnp.concatenate([bias, bias], axis=0)
+    return jnp.concatenate([column_ref[pl.ds(pl.multiple_of(at, 16), size)] for at, size in blocks], axis=0)
 
 
 def ends(s, c):
@@ -108,78 +106,116 @@
     x_ref[2, slot, where] = shifted(value, 1).astype(jnp.bfloat16)
 
 
-def own_part(half, first, last, w_half_ref, b_up_ref, w_conv_ref, x_ref, sum_ref, other_ref, halves_ref, column_ref, u_ref):
-    planes = (w_half_ref.shape[0] - 32) // 2
-    split_kernels(w_conv_ref, halves_ref)
-    other_ref[...] = halves_ref[1 - half]
+def arrival(x_core, part):
+    if x_core is None:
+        return [[(0, part)], [(0, part)]]
+    quarter, half = part // 4, part // 2
+    return [
+        [((x_core ^ number) * quarter, quarter) for number in range(4)],
+        [((lax.rem(x_core, 2) ^ number) * half, half) for number in (0, 1)],
+    ]
+
+
+def arrange(x_core, part):
+    source = lax.broadcasted_iota(jnp.int32, (2 * part, 2 * part), 0)
+    target = lax.broadcasted_iota(jnp.int32, (2 * part, 2 * part), 1)
+    wanted = jnp.zeros_like(target)
+    for plane, blocks in enumerate(arrival(x_core, part)):
+        place = plane * part
+        for first, size in blocks:
+            inside = (target >= place) & (target < place + size)
+            wanted = jnp.where(inside, target - place + plane * part + first, wanted)
+            place += size
+    return jnp.where(source == wanted, 1.0, 0.0).astype(jnp.bfloat16)
+
+
+def own_part(half, x_core, refs, results, scratch):
+    w_half_ref, b_up_ref, w_conv_ref = refs
+    x_ref, sum_ref, other_ref = results
+    halves_ref, column_ref, u_ref, w_ref, v_ref, sems = scratch
+    s, c = lax.axis_index("space"), lax.axis_index("ch")
+    skipped = (w_half_ref.shape[0] - 32) // 2
+    copies = [
+        pltpu.make_async_copy(w_conv_ref, v_ref, sems.at[0]),
+        pltpu.make_async_copy(w_half_ref.at[pl.ds(skipped, 32)], w_ref, sems.at[1]),
+    ]
+    for copy in copies:
+        copy.start()
+    yield
+    cout, part, cols = w_conv_ref.shape[1], w_half_ref.shape[1], u_ref.shape[3]
 
     def tap_of(tap):
-        return jnp.concatenate([w_half_ref[planes + tap], w_half_ref[planes + 16 + tap]], axis=0)
-
-    upsample(x_ref, tap_of, bias_of(b_up_ref, column_ref, half), u_ref, first, last)
+        return jnp.concatenate([w_ref[tap], w_ref[16 + tap]], axis=0)
+
+    copies[1].wait()
+    bias = bias_of(b_up_ref, column_ref, [(half * part, part)] * 2)
+    upsample(x_ref, tap_of, bias, u_ref, *ends(s, c))
+    copies[0].wait()
+    split_kernels(v_ref, halves_ref)
+    matrix = arrange(x_core, part)
+    for number in range(9):
+        columns = pl.ds(number * cout, cout)
+        moved = jnp.dot(halves_ref[1 - half, :, columns], matrix, preferred_element_type=jnp.float32)
+        other_ref[:, columns] = moved.astype(jnp.bfloat16)
     kernel = halves_ref[half]
-    cols = u_ref.shape[3]
     for start in range(0, u_ref.shape[1] - 2, 2):
         for col_phase in (0, 1):
             sum_ref[col_phase, :, start * cols : (start + 2) * cols] = convolve(kernel, u_ref, start, col_phase)
 
 
-def paired_first(own_ref, peer_ref, halo_ref, w_half_ref, b_up_ref, w_conv_ref, x_ref, sum_ref, other_ref, *scratch):
-    *rest, wide_ref = scratch
+def paired_first(own_ref, peer_ref, near_ref, far_ref, *refs):
+    refs, results, scratch = refs[:3], refs[3:6], refs[6:]
+    *scratch, wide_ref, raw_ref, raw_sem = scratch
+    x_ref = results[0]
+    copy = pltpu.make_async_copy(own_ref, raw_ref, raw_sem)
+    copy.start()
     s, c = lax.axis_index("space"), lax.axis_index("ch")
+    steps = own_part(c, lax.rem(s, 4), refs, results, scratch)
+    next(steps)
     chans, rows, cols = own_ref.shape
     share = rows // 2 + 1
-    for number, source in enumerate((own_ref, peer_ref)):
+    for number, (source, halo_ref) in enumerate(((peer_ref, far_ref), (raw_ref, near_ref))):
+        if number == 1:
+            copy.wait()
         wide_ref[number] = source[...].astype(jnp.float32).reshape(chans * rows, cols)
-    for number in (0, 1):
-        offset = (c if number == 0 else 1 - c) * chans
+        offset = (1 - c if number == 0 else c) * chans
         for place in range(share):
             value = wide_ref[number, pl.ds(place + c * (rows - share), chans, stride=rows), :]
             store_row(x_ref, place + 1 - c, offset, value)
-        store_row(x_ref, c * share, offset, halo_ref[number].astype(jnp.float32))
-    own_part(c, *ends(s, c), w_half_ref, b_up_ref, w_conv_ref, x_ref, sum_ref, other_ref, *rest)
-
-
-def gathered_first(rows_ref, w_half_ref, b_up_ref, w_conv_ref, x_ref, sum_ref, other_ref, *scratch):
-    s, c = lax.axis_index("space"), lax.axis_index("ch")
+        store_row(x_ref, c * share, offset, halo_ref[...].astype(jnp.float32))
+    for _ in steps:
+        pass
+
+
+def gathered_first(rows_ref, *refs):
+    refs, results, scratch = refs[:3], refs[3:6], refs[6:]
+    steps = own_part(0, None, refs, results, scratch)
+    next(steps)
     for slot in range(rows_ref.shape[0]):
-        store_row(x_ref, slot, 0, rows_ref[slot].astype(jnp.float32))
-    own_part(0, *ends(s, c), w_half_ref, b_up_ref, w_conv_ref, x_ref, sum_ref, other_ref, *scratch)
+        store_row(results[0], slot, 0, rows_ref[slot].astype(jnp.float32))
+    for _ in steps:
+        pass
 
 
 def second(paired, count, *refs):
     parts, refs = refs[:count], refs[count:]
-    x_ref, sum_ref, other_ref, b_up_ref, b_conv_ref, out_ref, w_ref, column_ref, u_ref, total_ref, sems = refs
+    x_ref, sum_ref, other_ref, b_up_ref, b_conv_ref, out_ref, column_ref, u_ref, total_ref, made_ref, sems = refs
     s, c = lax.axis_index("space"), lax.axis_index("ch")
-    half = 1 - c if paired else 1
-    copies = []
-    if paired:
-        me, core = lax.rem(s, 4), lax.rem(s, 2)
-        x = me // 2
-        taps = [4 * (2 * i + j) for i in (x, 1 - x) for j in (core, 1 - core)] + [8 * core, 8 - 8 * core]
-        for number, part_ref in enumerate(parts):
-            place = w_ref.at[number // 4, pl.ds(taps[number], part_ref.shape[0])]
-            copies.append(pltpu.make_async_copy(part_ref, place, sems.at[number]))
-    else:
-        for plane in (0, 1):
-            source = parts[0].at[pl.ds(16 * plane, 16)]
-            copies.append(pltpu.make_async_copy(source, w_ref.at[plane], sems.at[plane]))
-    for copy in copies:
-        copy.start()
     cout, _, rows, _ = out_ref.shape
+    part = cout // 2
+    half, x_core = (1 - c, lax.rem(s, 4)) if paired else (1, None)
     cols = x_ref.shape[3]
+
+    def tap_of(tap):
+        return jnp.concatenate([part_ref[tap] for part_ref in parts], axis=0)
+
+    blocks = [(half * part + at, size) for plane in arrival(x_core, part) for at, size in plane]
+    bias = bias_of(b_up_ref, column_ref, blocks)
+    upsample(x_ref, tap_of, bias, u_ref, *ends(s, c))
     source = lax.broadcasted_iota(jnp.int32, (2 * cols, 2 * cols), 0)
     target = lax.broadcasted_iota(jnp.int32, (2 * cols, 2 * cols), 1)
     wanted = jnp.where(source < cols, 2 * source, 2 * (source - cols) + 1)
     interleave = jnp.where(wanted == target, 1.0, 0.0).astype(jnp.bfloat16)
-    bias = bias_of(b_up_ref, column_ref, half)
-    for copy in copies:
-        copy.wait()
-
-    def tap_of(tap):
-        return jnp.concatenate([w_ref[0, tap], w_ref[1, tap]], axis=0)
-
-    upsample(x_ref, tap_of, bias, u_ref, *ends(s, c))
     kernel = other_ref[...]
     bias = column_of(b_conv_ref[...])
     bias = jnp.concatenate([bias, bias], axis=0)
@@ -197,22 +233,75 @@
                 total_ref[side, pl.ds(start + number, 2 * cout, stride=rows), :] = mixed[
                     :, side * cols : (side + 1) * cols
                 ]
+    copies = []
     for plane in (0, 1):
         for side in (0, 1):
+            number = 2 * plane + side
             block = total_ref[side, pl.ds(plane * cout * rows, cout * rows), :]
-            out_ref[:, plane, :, side * cols : (side + 1) * cols] = block.reshape(cout, rows, cols).astype(
-                jnp.bfloat16
-            )
-
-
-def cost(sizes, read):
+            made_ref[number] = block.reshape(cout, rows, cols).astype(jnp.bfloat16)
+            place = out_ref.at[:, plane, :, pl.ds(side * cols, cols)]
+            copies.append(pltpu.make_async_copy(made_ref.at[number], place, sems.at[number]))
+            copies[-1].start()
+    for copy in copies:
+        copy.wait()
+
+
+def pieces(own_ref, w_up_ref, near_ref, far_ref, w_a_ref, w_b_ref, wide_ref, raw_ref, sems):
+    s, c = lax.axis_index("space"), lax.axis_index("ch")
+    raw = pltpu.make_async_copy(own_ref, raw_ref, sems.at[2])
+    raw.start()
+    firsts = [block[0] for plane in arrival(lax.rem(s, 4), w_up_ref.shape[1]) for block in plane[:1]]
+    copies = []
+    for plane, piece_ref in enumerate((w_a_ref, w_b_ref)):
+        channels = pl.ds(pl.multiple_of(firsts[plane], 16), piece_ref.shape[1])
+        source = w_up_ref.at[pl.ds(16 + 16 * plane, 16), channels]
+        copies.append(pltpu.make_async_copy(source, piece_ref, sems.at[plane]))
+        copies[-1].start()
+    chans, rows, cols = own_ref.shape
+    raw.wait()
+    wide_ref[...] = raw_ref[...].astype(jnp.float32).reshape(chans * rows, cols)
+    inner, outer = (1 - c) * (rows - 1), c * (rows - 1)
+    near_ref[...] = wide_ref[pl.ds(inner, chans, stride=rows), :].astype(jnp.bfloat16)
+    far_ref[...] = wide_ref[pl.ds(outer, chans, stride=rows), :].astype(jnp.bfloat16)
+    for copy in copies:
+        copy.wait()
+
+
+def call_pieces(own, w_up):
+    chans, rows, cols = own.shape
+    part, cin = w_up.shape[1:]
+    return pl.pallas_call(
+        pieces,
+        out_shape=(
+            jax.ShapeDtypeStruct((chans, cols), jnp.bfloat16),
+            jax.ShapeDtypeStruct((chans, cols), jnp.bfloat16),
+            jax.ShapeDtypeStruct((16, part // 4, cin), jnp.bfloat16),
+            jax.ShapeDtypeStruct((16, part // 2, cin), jnp.bfloat16),
+        ),
+        in_specs=[ANY, ANY],
+        out_specs=(VMEM,) * 4,
+        scratch_shapes=[
+            pltpu.VMEM((chans * rows, cols), jnp.float32),
+            pltpu.VMEM((chans, rows, cols), jnp.bfloat16),
+            pltpu.SemaphoreType.DMA((3,)),
+        ],
+        compiler_params=pltpu.CompilerParams(vmem_limit_bytes=LIMIT),
+    )(in_hbm(own), in_hbm(w_up))
+
+
+def in_hbm(operand):
+    return pltpu.with_memory_space_constraint(operand, pltpu.HBM)
+
+
+def cost(sizes):
     cin, cout, rows, cols = sizes
     flops = 2 * cout * 4 * cin * 2 * cols * (rows + 2) + 2 * 2 * cout * 9 * cout * 2 * cols * rows
-    return pl.CostEstimate(flops=flops, bytes_accessed=read, transcendentals=0)
-
-
-def call_first(body, operands, wide, sizes):
+    return pl.CostEstimate(flops=flops, bytes_accessed=8 * 2**20, transcendentals=0)
+
+
+def call_first(body, rows_in, spaces, weights, extra, sizes):
     cin, cout, rows, cols = sizes
+    w_half, b_up, w_conv = weights
     return pl.pallas_call(
         body,
         out_shape=(
@@ -220,17 +309,20 @@
             jax.ShapeDtypeStruct((2, 2 * cout, rows * cols), jnp.float32),
             jax.ShapeDtypeStruct((2 * cout, 9 * cout), jnp.bfloat16),
         ),
-        in_specs=[VMEM] * len(operands),
+        in_specs=[*spaces, ANY, VMEM, ANY],
         out_specs=(VMEM,) * 3,
         scratch_shapes=[
             pltpu.VMEM((2, 2 * cout, 9 * cout), jnp.bfloat16),
             pltpu.VMEM((cout, cout), jnp.float32),
             pltpu.VMEM((4, rows + 2, cout, cols), jnp.bfloat16),
+            pltpu.VMEM((32, cout // 2, cin), jnp.bfloat16),
+            pltpu.VMEM((27, cout, cout), jnp.bfloat16),
+            pltpu.SemaphoreType.DMA((2,)),
         ]
-        + wide,
-        cost_estimate=cost(sizes, 8 * 2**20),
+        + extra,
+        cost_estimate=cost(sizes),
         compiler_params=pltpu.CompilerParams(vmem_limit_bytes=LIMIT),
-    )(*operands)
+    )(*rows_in, in_hbm(w_half), b_up, in_hbm(w_conv))
 
 
 def call_second(paired, parts, results, biases, sizes):
@@ -238,16 +330,16 @@
     return pl.pallas_call(
         functools.partial(second, paired, len(parts)),
         out_shape=jax.ShapeDtypeStruct((cout, 2, rows, 2 * cols), jnp.bfloat16),
-        in_specs=[ANY] * len(parts) + [VMEM] * 5,
-        out_specs=VMEM,
+        in_specs=[VMEM] * (len(parts) + 5),
+        out_specs=ANY,
         scratch_shapes=[
-            pltpu.VMEM((2, 16, cout // 2, cin), jnp.bfloat16),
             pltpu.VMEM((cout, cout), jnp.float32),
             pltpu.VMEM((4, rows + 2, cout, cols), jnp.bfloat16),
             pltpu.VMEM((2, 2 * cout * rows, cols), jnp.float32),
-            pltpu.SemaphoreType.DMA((6,)),
+            pltpu.VMEM((4, cout, rows, cols), jnp.bfloat16),
+            pltpu.SemaphoreType.DMA((4,)),
         ],
-        cost_estimate=cost(sizes, 8 * 2**20),
+        cost_estimate=cost(sizes),
         compiler_params=pltpu.CompilerParams(vmem_limit_bytes=LIMIT),
     )(*parts, *results, *biases)
 
@@ -266,22 +358,27 @@
     chain = [(at(i - 1, 0), at(i, 0)) for i in range(1, spaces)]
     chain += [(at(i + 1, 1), at(i, 1)) for i in range(spaces - 1)]
 
-    peer = lax.ppermute(inputs, AXES, across)
-    w_a = lax.dynamic_slice_in_dim(w_up, 16 + 4 * lax.rem(s, 4), 4, 0)
-    w_b = lax.dynamic_slice_in_dim(w_up, 32 + 8 * lax.rem(s, 2), 8, 0)
-    w_a, w_b = lax.optimization_barrier((w_a, w_b))
+    outer = [(t, t + 1) for t in range(1, 2 * spaces - 1, 2)]
+    outer += [(j, i) for i, j in outer]
+
+    peer = lax.ppermute(inputs, AXES, across).reshape(chans, held, cols)
+    own = inputs.reshape(chans, held, cols)
+    near, far, w_a, w_b = call_pieces(own, w_up)
     w_a = lax.ppermute(w_a, AXES, across)
     w_b = lax.ppermute(w_b, AXES, across)
-
-    own, peer = inputs.reshape(chans, held, cols), peer.reshape(chans, held, cols)
-    edges = [lax.dynamic_slice_in_dim(rows, (1 - c) * (held - 1), 1, 1)[:, 0] for rows in (own, peer)]
-    halo = lax.ppermute(jnp.stack(edges), AXES, chain)
-    w_a, halo = lax.optimization_barrier((w_a, halo))
+    near = lax.ppermute(near, AXES, chain)
+    far = lax.ppermute(far, AXES, outer)
     w_ax = lax.ppermute(w_a, AXES, pairs)
     w_ac = lax.ppermute(w_a, AXES, cores)
     biases = (b_up[None], b_conv[None])
-    wide = [pltpu.VMEM((2, chans * held, cols), jnp.float32)]
-    results = call_first(paired_first, (own, peer, halo, w_up, biases[0], w_conv), wide, sizes)
+    extra = [
+        pltpu.VMEM((2, chans * held, cols), jnp.float32),
+        pltpu.VMEM((chans, held, cols), jnp.bfloat16),
+        pltpu.SemaphoreType.DMA,
+    ]
+    rows_in = (in_hbm(own), peer, near, far)
+    weights = (w_up, biases[0], w_conv)
+    results = call_first(paired_first, rows_in, (ANY, VMEM, VMEM, VMEM), weights, extra, sizes)
     w_b, w_ax, w_ac, *results = lax.optimization_barrier((w_b, w_ax, w_ac, *results))
     w_bc = lax.ppermute(w_b, AXES, cores)
     w_axc = lax.ppermute(w_ax, AXES, cores)
@@ -302,8 +399,9 @@
     share = inputs.shape[2] // chs
     rows = lax.dynamic_slice_in_dim(rows, c * share, share + 2, 0)
     biases = (b_up[None], b_conv[None])
-    results = call_first(gathered_first, (rows, w_all[:, :part], biases[0], w_conv), [], sizes)
-    return call_second(False, (w_all[:, part:],), results, biases, sizes)
+    weights = (w_all[:, :part], biases[0], w_conv)
+    results = call_first(gathered_first, (rows,), (VMEM,), weights, [], sizes)
+    return call_second(False, (w_all[:16, part:], w_all[16:, part:]), results, biases, sizes)
 
 
 def local(inputs, w_up, b_up, w_conv, b_conv):

time: 33.3 us -> 29.4 us (0.88)
  local copies, waits for them, and re-layouts: 7.36 us -> 0.01 us
  Pallas kernels: 8.77 us -> 10.5 us
  waiting for transfers between devices: 4.94 us -> 6.26 us
  starting transfers between devices: 11.8 us -> 12.4 us
    unnamed x14 -> x4, local copies, waits for them, and re-layouts: 4.38 us -> 0.01 us
    ppermute x1, waiting for transfers between devices: 1.4 us -> 4.97 us  [paired(): w_a = lax.ppermute(w_a, AXES, across)]
    dynamic_slice x4 -> x0, local copies, waits for them, and re-layouts: 2.98 us -> none  [the longest x2 1.09 us: paired(): lax.dynamic_slice_in_dim(rows, (1 - c) * (held - 1), 1, 1)[:, 0]]
    ppermute x1, starting transfers between devices: 0.3 us -> 3.27 us  [paired(): w_bc = lax.ppermute(w_b, AXES, cores)]
    ppermute x1, starting transfers between devices: 2.67 us -> 0.01 us  [paired(): w_ac = lax.ppermute(w_a, AXES, cores)]
    ppermute x2 -> x3, waiting for transfers between devices: 2.32 us -> 0.01 us  [the longest x1 0.01 us: paired(): near = lax.ppermute(near, AXES, chain)]
    pallas_call x1, Pallas kernels: 3.45 us -> 5.06 us  [call_first(): pl.pallas_call(body, out_shape=(jax.ShapeDtypeStruct((3, rows // 2 + 2, c...]
    pallas_call x0 -> x1, Pallas kernels: none -> 1.12 us  [call_pieces(): pl.pallas_call(pieces, out_shape=(jax.ShapeDtypeStruct((chans, cols), jnp...]
  transfers between devices with their start and end apart: 8 -> 9, of which waited for: 3 -> 2; matrix products, arithmetic and copies ran while one was open for 9% -> 0% of each run, Pallas kernels for 10% -> 21%
where the time goes in v6:
time: 29.4 us; the launch traced here: 29.2 us
  starting transfers between devices  12.4 us (42%)
  Pallas kernels  10.5 us (36%)
  waiting for transfers between devices  6.26 us (21%)
    pallas_call x1, Pallas kernels, call_first(): pl.pallas_call(body, out_shape=(jax.ShapeDtypeStruct((3, rows // 2 + 2, c...  5.06 us
    ppermute x1, waiting for transfers between devices, paired(): w_a = lax.ppermute(w_a, AXES, across)  4.97 us
    pallas_call x1, Pallas kernels, call_second(): pl.pallas_call(functools.partial(second, paired, len(parts)), out_shape=j...  4.3 us
    ppermute x1, starting transfers between devices, paired(): w_bc = lax.ppermute(w_b, AXES, cores)  3.27 us
    ppermute x1, starting transfers between devices, paired(): peer = lax.ppermute(inputs, AXES, across).reshape(chans, held, cols)  2.97 us
    ppermute x1, starting transfers between devices, paired(): w_ax = lax.ppermute(w_a, AXES, pairs)  2.03 us
    ppermute x1, starting transfers between devices, paired(): w_b = lax.ppermute(w_b, AXES, across)  2.01 us
    ppermute x1, starting transfers between devices, paired(): near = lax.ppermute(near, AXES, chain)  1.28 us
  transfers between devices with their start and end apart: 9, of which 2 were waited for; matrix products, arithmetic and copies ran while one was open for 0% of the time, Pallas kernels for 21%

profile of v6, /device:TPU:0, one launch (start us, length us, event | category | flops | bytes accessed | tf_op | source)
XLA Modules:
  0.0 29.2 jit_solution(13939527188423824427)
XLA Ops:
  0.0 0.0 copy-start
  0.0 3.0 %collective-permute-start.4 = (bf16[128,1,8,128]{3,2,0,1:T(8,128)(2,1)}, bf16[128,1,8,128]{3,2,0,1:T(8,128)(2,1)S(1)}, u32[]{:S(2)}, u32[]{:S(2)}) collective-permute-start(bf16[128,1,8,128]{3,2,0,1:T(8,128)(2,1)} %bitcast.9), channel_id=1, source_target_pairs={{0,1},{1,0},{2,3},{3,2},{4,5},{5,4},{6,7},{7,6},{8,9},{9,8},{10,11... | collective-permute-start | bytes 786440 | tf_op jit(solution)/shard_map/ppermute | solution.py:364
  3.0 1.1 %shard_map.55 = (bf16[128,128]{1,0:T(8,128)(2,1)S(1)}, bf16[128,128]{1,0:T(8,128)(2,1)S(1)}, bf16[16,16,256]{2,1,0:T(8,128)(2,1)S(1)}, bf16[16,32,256]{2,1,0:T(8,128)(2,1)S(1)}) custom-call(bf16[128,8,128]{2,1,0:T(8,128)(2,1)} %bitcast.10, bf16[64,64,256]{2,1,0:T(8,128)(2,1)} %refs_0_.1), custom_call_target="tpu_custom_call" | custom-call | tf_op jit(solution)/shard_map/pallas_call | solution.py:273
  4.1 0.1 collective-permute-start
  4.2 2.0 %collective-permute-start.1 = (bf16[16,32,256]{2,1,0:T(8,128)(2,1)S(1)}, bf16[16,32,256]{2,1,0:T(8,128)(2,1)S(1)}, u32[]{:S(2)}, u32[]{:S(2)}) collective-permute-start(bf16[16,32,256]{2,1,0:T(8,128)(2,1)S(1)} %get-tuple-element.19), channel_id=1, source_target_pairs={{0,1},{1,0},{2,3},{3,2},{4,5},{5,4},{6,7},{7,6},{8,9},{9,8},{10,11... | collective-permute-start | bytes 786440 | tf_op jit(solution)/shard_map/ppermute | solution.py:368
  6.2 1.3 %collective-permute-start.5 = (bf16[128,128]{1,0:T(8,128)(2,1)S(1)}, bf16[128,128]{1,0:T(8,128)(2,1)S(1)}, u32[]{:S(2)}, u32[]{:S(2)}) collective-permute-start(bf16[128,128]{1,0:T(8,128)(2,1)S(1)} %get-tuple-element.20), channel_id=1, source_target_pairs={{0,2},{2,4},{4,6},{6,8},{8,10},{10,12},{12,14},{14,16},{16,18},{18... | collective-permute-start | bytes 98312 | tf_op jit(solution)/shard_map/ppermute | solution.py:369
  7.5 0.7 %collective-permute-start.6 = (bf16[128,128]{1,0:T(8,128)(2,1)S(1)}, bf16[128,128]{1,0:T(8,128)(2,1)S(1)}, u32[]{:S(2)}, u32[]{:S(2)}) collective-permute-start(bf16[128,128]{1,0:T(8,128)(2,1)S(1)} %get-tuple-element.21), channel_id=1, source_target_pairs={{1,2},{3,4},{5,6},{7,8},{9,10},{11,12},{13,14},{15,16},{17,18},{19... | collective-permute-start | bytes 98312 | tf_op jit(solution)/shard_map/ppermute | solution.py:370
  8.1 5.0 %collective-permute-done.refs_0_ = bf16[16,16,256]{2,1,0:T(8,128)(2,1)S(1)} collective-permute-done((bf16[16,16,256]{2,1,0:T(8,128)(2,1)S(1)}, bf16[16,16,256]{2,1,0:T(8,128)(2,1)S(1)}, u32[]{:S(2)}, u32[]{:S(2)}) %collective-permute-start) | collective-permute-done | bytes 131104 | tf_op jit(solution)/shard_map/ppermute | solution.py:367
  13.1 0.0 collective-permute-start.3
  13.1 0.0 collective-permute-done.5.near_ref
  13.1 2.0 %collective-permute-start.2 = (bf16[16,16,256]{2,1,0:T(8,128)(2,1)S(1)}, bf16[16,16,256]{2,1,0:T(8,128)(2,1)S(1)}, u32[]{:S(2)}, u32[]{:S(2)}) collective-permute-start(bf16[16,16,256]{2,1,0:T(8,128)(2,1)S(1)} %collective-permute-done.refs_0_), channel_id=1, source_target_pairs={{0,4},{1,5},{2,6},{3,7},{4,0},{5,1},{6,2},{7,3},{8,12},{9,13},{10,... | collective-permute-start | bytes 393224 | tf_op jit(solution)/shard_map/ppermute | solution.py:371
  15.2 0.0 collective-permute-done.6.far_ref
  15.2 0.0 collective-permute-done.4
  15.2 0.0 copy-done
  15.2 0.0 copy-start.1
  15.2 5.1 %shard_map.56 = (bf16[3,6,256,128]{3,2,1,0:T(8,128)(2,1)S(1)}, f32[2,256,1024]{2,1,0:T(8,128)S(1)}, bf16[256,1152]{1,0:T(8,128)(2,1)S(1)}) custom-call(bf16[128,8,128]{2,1,0:T(8,128)(2,1)} %bitcast.11, bf16[128,8,128]{2,1,0:T(8,128)(2,1)S(1)} %bitcast.5, bf16[128,128]{1,0:T(8,128)(2,1)S(1)} %collective-permute-done.5.near_ref, ...), custom_call_target="tpu_custom_call" | custom-call | flops 1879048192 | bytes 8388608 | tf_op jit(solution)/shard_map/pallas_call | solution.py:305
  20.3 0.0 collective-permute-done.3.refs_1_
  20.3 0.0 collective-permute-done.2.refs_2_
  20.3 0.0 collective-permute-done.1.refs_4_
  20.3 3.3 %collective-permute-start.8 = (bf16[16,32,256]{2,1,0:T(8,128)(2,1)S(1)}, bf16[16,32,256]{2,1,0:T(8,128)(2,1)S(1)}, u32[]{:S(2)}, u32[]{:S(2)}) collective-permute-start(bf16[16,32,256]{2,1,0:T(8,128)(2,1)S(1)} %collective-permute-done.1.refs_4_), channel_id=1, source_target_pairs={{0,2},{1,3},{2,0},{3,1},{4,6},{5,7},{6,4},{7,5},{8,10},{9,11},{10,... | collective-permute-start | bytes 786440 | tf_op jit(solution)/shard_map/ppermute | solution.py:383
  23.6 0.1 collective-permute-start.7
  23.6 1.3 %collective-permute-done.7.refs_3_ = bf16[16,16,256]{2,1,0:T(8,128)(2,1)S(1)} collective-permute-done((bf16[16,16,256]{2,1,0:T(8,128)(2,1)S(1)}, bf16[16,16,256]{2,1,0:T(8,128)(2,1)S(1)}, u32[]{:S(2)}, u32[]{:S(2)}) %collective-permute-start.7) | collective-permute-done | bytes 131104 | tf_op jit(solution)/shard_map/ppermute | solution.py:384
  24.9 0.0 collective-permute-done.8.refs_5_
  24.9 0.0 copy-done.1
  24.9 4.3 %shard_map.57 = bf16[128,2,8,256]{3,2,1,0:T(8,128)(2,1)} custom-call(bf16[16,16,256]{2,1,0:T(8,128)(2,1)S(1)} %collective-permute-done.refs_0_, bf16[16,16,256]{2,1,0:T(8,128)(2,1)S(1)} %collective-permute-done.3.refs_1_, bf16[16,16,256]{2,1,0:T(8,128)(2,1)S(1)} %collective-permute-done.2.refs_2_, bf16[16,16,256]{2,1,0:T(8,128)(2,1)S(1)} %collective-permute-done.7.refs_3_, ...), custom_call_target="tpu_custom_call" | custom-call | flops 1879048192 | bytes 8388608 | tf_op jit(solution)/shard_map/pallas_call | solution.py:330
Async XLA Ops:
  0.0 15.2 %copy-start = (f32[128]{0:T(128)S(1)}, f32[128]{0:T(128)}, u32[]{:S(2)}) copy-start(f32[128]{0:T(128)} %param.7) | copy-start | bytes 1540
  0.0 15.2 %collective-permute-start.4 = (bf16[128,1,8,128]{3,2,0,1:T(8,128)(2,1)}, bf16[128,1,8,128]{3,2,0,1:T(8,128)(2,1)S(1)}, u32[]{:S(2)}, u32[]{:S(2)}) collective-permute-start(bf16[128,1,8,128]{3,2,0,1:T(8,128)(2,1)} %bitcast.9), channel_id=1, source_target_pairs={{0,1},{1,0},{2,3},{3,2},{4,5},{5,4},{6,7},{7,6},{8,9},{9,8},{10,11... | collective-permute-start | bytes 786440 | tf_op jit(solution)/shard_map/ppermute | solution.py:364
  4.1 9.0 %collective-permute-start = (bf16[16,16,256]{2,1,0:T(8,128)(2,1)S(1)}, bf16[16,16,256]{2,1,0:T(8,128)(2,1)S(1)}, u32[]{:S(2)}, u32[]{:S(2)}) collective-permute-start(bf16[16,16,256]{2,1,0:T(8,128)(2,1)S(1)} %get-tuple-element.18), channel_id=1, source_target_pairs={{0,1},{1,0},{2,3},{3,2},{4,5},{5,4},{6,7},{7,6},{8,9},{9,8},{10,11... | collective-permute-start | bytes 393224 | tf_op jit(solution)/shard_map/ppermute | solution.py:367
  4.2 16.1 %collective-permute-start.1 = (bf16[16,32,256]{2,1,0:T(8,128)(2,1)S(1)}, bf16[16,32,256]{2,1,0:T(8,128)(2,1)S(1)}, u32[]{:S(2)}, u32[]{:S(2)}) collective-permute-start(bf16[16,32,256]{2,1,0:T(8,128)(2,1)S(1)} %get-tuple-element.19), channel_id=1, source_target_pairs={{0,1},{1,0},{2,3},{3,2},{4,5},{5,4},{6,7},{7,6},{8,9},{9,8},{10,11... | collective-permute-start | bytes 786440 | tf_op jit(solution)/shard_map/ppermute | solution.py:368
  6.2 6.9 %collective-permute-start.5 = (bf16[128,128]{1,0:T(8,128)(2,1)S(1)}, bf16[128,128]{1,0:T(8,128)(2,1)S(1)}, u32[]{:S(2)}, u32[]{:S(2)}) collective-permute-start(bf16[128,128]{1,0:T(8,128)(2,1)S(1)} %get-tuple-element.20), channel_id=1, source_target_pairs={{0,2},{2,4},{4,6},{6,8},{8,10},{10,12},{12,14},{14,16},{16,18},{18... | collective-permute-start | bytes 98312 | tf_op jit(solution)/shard_map/ppermute | solution.py:369
  7.5 7.7 %collective-permute-start.6 = (bf16[128,128]{1,0:T(8,128)(2,1)S(1)}, bf16[128,128]{1,0:T(8,128)(2,1)S(1)}, u32[]{:S(2)}, u32[]{:S(2)}) collective-permute-start(bf16[128,128]{1,0:T(8,128)(2,1)S(1)} %get-tuple-element.21), channel_id=1, source_target_pairs={{1,2},{3,4},{5,6},{7,8},{9,10},{11,12},{13,14},{15,16},{17,18},{19... | collective-permute-start | bytes 98312 | tf_op jit(solution)/shard_map/ppermute | solution.py:370
  13.1 7.1 %collective-permute-start.3 = (bf16[16,16,256]{2,1,0:T(8,128)(2,1)S(1)}, bf16[16,16,256]{2,1,0:T(8,128)(2,1)S(1)}, u32[]{:S(2)}, u32[]{:S(2)}) collective-permute-start(bf16[16,16,256]{2,1,0:T(8,128)(2,1)S(1)} %collective-permute-done.refs_0_), channel_id=1, source_target_pairs={{0,2},{1,3},{2,0},{3,1},{4,6},{5,7},{6,4},{7,5},{8,10},{9,11},{10,... | collective-permute-start | bytes 393224 | tf_op jit(solution)/shard_map/ppermute | solution.py:372
  13.1 7.1 %collective-permute-start.2 = (bf16[16,16,256]{2,1,0:T(8,128)(2,1)S(1)}, bf16[16,16,256]{2,1,0:T(8,128)(2,1)S(1)}, u32[]{:S(2)}, u32[]{:S(2)}) collective-permute-start(bf16[16,16,256]{2,1,0:T(8,128)(2,1)S(1)} %collective-permute-done.refs_0_), channel_id=1, source_target_pairs={{0,4},{1,5},{2,6},{3,7},{4,0},{5,1},{6,2},{7,3},{8,12},{9,13},{10,... | collective-permute-start | bytes 393224 | tf_op jit(solution)/shard_map/ppermute | solution.py:371
  15.2 9.7 %copy-start.1 = (f32[128]{0:T(128)S(1)}, f32[128]{0:T(128)}, u32[]{:S(2)}) copy-start(f32[128]{0:T(128)} %param.9) | copy-start | bytes 1540
  20.3 4.6 %collective-permute-start.8 = (bf16[16,32,256]{2,1,0:T(8,128)(2,1)S(1)}, bf16[16,32,256]{2,1,0:T(8,128)(2,1)S(1)}, u32[]{:S(2)}, u32[]{:S(2)}) collective-permute-start(bf16[16,32,256]{2,1,0:T(8,128)(2,1)S(1)} %collective-permute-done.1.refs_4_), channel_id=1, source_target_pairs={{0,2},{1,3},{2,0},{3,1},{4,6},{5,7},{6,4},{7,5},{8,10},{9,11},{10,... | collective-permute-start | bytes 786440 | tf_op jit(solution)/shard_map/ppermute | solution.py:383
  23.6 1.3 %collective-permute-start.7 = (bf16[16,16,256]{2,1,0:T(8,128)(2,1)S(1)}, bf16[16,16,256]{2,1,0:T(8,128)(2,1)S(1)}, u32[]{:S(2)}, u32[]{:S(2)}) collective-permute-start(bf16[16,16,256]{2,1,0:T(8,128)(2,1)S(1)} %collective-permute-done.2.refs_2_), channel_id=1, source_target_pairs={{0,2},{1,3},{2,0},{3,1},{4,6},{5,7},{6,4},{7,5},{8,10},{9,11},{10,... | collective-permute-start | bytes 393224 | tf_op jit(solution)/shard_map/ppermute | solution.py:384

commit v7 on v6

--- a/solution.py
+++ b/solution.py
@@ -129,72 +129,82 @@
     return jnp.where(source == wanted, 1.0, 0.0).astype(jnp.bfloat16)
 
 
-def own_part(half, x_core, refs, results, scratch):
-    w_half_ref, b_up_ref, w_conv_ref = refs
-    x_ref, sum_ref, other_ref = results
-    halves_ref, column_ref, u_ref, w_ref, v_ref, sems = scratch
+def own_part(half, refs, results, scratch):
+    w_half_ref, kernel_ref, b_up_ref = refs
+    x_ref, sum_ref = results
+    column_ref, u_ref = scratch
+    s, c = lax.axis_index("space"), lax.axis_index("ch")
+    part, cols = w_half_ref.shape[1], u_ref.shape[3]
+
+    def tap_of(tap):
+        return jnp.concatenate([w_half_ref[tap], w_half_ref[16 + tap]], axis=0)
+
+    bias = bias_of(b_up_ref, column_ref, [(half * part, part)] * 2)
+    upsample(x_ref, tap_of, bias, u_ref, *ends(s, c))
+    kernel = kernel_ref[...]
+    for start in range(0, u_ref.shape[1] - 2, 2):
+        for col_phase in (0, 1):
+            sum_ref[col_phase, :, start * cols : (start + 2) * cols] = convolve(kernel, u_ref, start, col_phase)
+
+
+def store_rows(x_ref, wide_ref, offset):
+    c = lax.axis_index("ch")
+    share = x_ref.shape[1] - 1
+    chans = x_ref.shape[2] // 2
+    rows = wide_ref.shape[0] // chans
+    for place in range(share):
+        value = wide_ref[pl.ds(place + c * (rows - share), chans, stride=rows), :]
+        store_row(x_ref, place + 1 - c, offset, value)
+
+
+def prepare(paired, own_ref, w_half_ref, w_conv_ref, x_ref, w_ref, kernel_ref, other_ref, *scratch):
+    halves_ref, v_ref, wide_ref, raw_ref, sems = scratch
     s, c = lax.axis_index("space"), lax.axis_index("ch")
     skipped = (w_half_ref.shape[0] - 32) // 2
     copies = [
         pltpu.make_async_copy(w_conv_ref, v_ref, sems.at[0]),
-        pltpu.make_async_copy(w_half_ref.at[pl.ds(skipped, 32)], w_ref, sems.at[1]),
+        pltpu.make_async_copy(own_ref, raw_ref, sems.at[1]),
+        pltpu.make_async_copy(w_half_ref.at[pl.ds(skipped, 32)], w_ref, sems.at[2]),
     ]
     for copy in copies:
         copy.start()
-    yield
-    cout, part, cols = w_conv_ref.shape[1], w_half_ref.shape[1], u_ref.shape[3]
-
-    def tap_of(tap):
-        return jnp.concatenate([w_ref[tap], w_ref[16 + tap]], axis=0)
-
-    copies[1].wait()
-    bias = bias_of(b_up_ref, column_ref, [(half * part, part)] * 2)
-    upsample(x_ref, tap_of, bias, u_ref, *ends(s, c))
+    cout = w_conv_ref.shape[1]
+    half, x_core = (c, lax.rem(s, 4)) if paired else (0, None)
     copies[0].wait()
     split_kernels(v_ref, halves_ref)
-    matrix = arrange(x_core, part)
+    kernel_ref[...] = halves_ref[half]
+    matrix = arrange(x_core, cout // 2)
     for number in range(9):
         columns = pl.ds(number * cout, cout)
         moved = jnp.dot(halves_ref[1 - half, :, columns], matrix, preferred_element_type=jnp.float32)
         other_ref[:, columns] = moved.astype(jnp.bfloat16)
-    kernel = halves_ref[half]
-    for start in range(0, u_ref.shape[1] - 2, 2):
-        for col_phase in (0, 1):
-            sum_ref[col_phase, :, start * cols : (start + 2) * cols] = convolve(kernel, u_ref, start, col_phase)
-
-
-def paired_first(own_ref, peer_ref, near_ref, far_ref, *refs):
-    refs, results, scratch = refs[:3], refs[3:6], refs[6:]
-    *scratch, wide_ref, raw_ref, raw_sem = scratch
+    copies[1].wait()
+    if paired:
+        chans, rows, cols = own_ref.shape
+        wide_ref[...] = raw_ref[...].astype(jnp.float32).reshape(chans * rows, cols)
+        store_rows(x_ref, wide_ref, c * chans)
+    else:
+        for slot in range(own_ref.shape[0]):
+            store_row(x_ref, slot, 0, raw_ref[slot].astype(jnp.float32))
+    copies[2].wait()
+
+
+def paired_first(peer_ref, near_ref, far_ref, started_ref, *refs):
+    refs, results, scratch = refs[:3], refs[3:5], refs[5:]
+    *scratch, wide_ref = scratch
     x_ref = results[0]
-    copy = pltpu.make_async_copy(own_ref, raw_ref, raw_sem)
-    copy.start()
-    s, c = lax.axis_index("space"), lax.axis_index("ch")
-    steps = own_part(c, lax.rem(s, 4), refs, results, scratch)
-    next(steps)
-    chans, rows, cols = own_ref.shape
-    share = rows // 2 + 1
-    for number, (source, halo_ref) in enumerate(((peer_ref, far_ref), (raw_ref, near_ref))):
-        if number == 1:
-            copy.wait()
-        wide_ref[number] = source[...].astype(jnp.float32).reshape(chans * rows, cols)
-        offset = (1 - c if number == 0 else c) * chans
-        for place in range(share):
-            value = wide_ref[number, pl.ds(place + c * (rows - share), chans, stride=rows), :]
-            store_row(x_ref, place + 1 - c, offset, value)
-        store_row(x_ref, c * share, offset, halo_ref[...].astype(jnp.float32))
-    for _ in steps:
-        pass
-
-
-def gathered_first(rows_ref, *refs):
-    refs, results, scratch = refs[:3], refs[3:6], refs[6:]
-    steps = own_part(0, None, refs, results, scratch)
-    next(steps)
-    for slot in range(rows_ref.shape[0]):
-        store_row(results[0], slot, 0, rows_ref[slot].astype(jnp.float32))
-    for _ in steps:
-        pass
+    c = lax.axis_index("ch")
+    chans, rows, cols = peer_ref.shape
+    wide_ref[...] = peer_ref[...].astype(jnp.float32).reshape(chans * rows, cols)
+    store_rows(x_ref, wide_ref, (1 - c) * chans)
+    slot = c * (x_ref.shape[1] - 1)
+    store_row(x_ref, slot, c * chans, near_ref[...].astype(jnp.float32))
+    store_row(x_ref, slot, (1 - c) * chans, far_ref[...].astype(jnp.float32))
+    own_part(c, refs, results, scratch)
+
+
+def gathered_first(started_ref, *refs):
+    own_part(0, refs[:3], refs[3:5], refs[5:])
 
 
 def second(paired, count, *refs):
@@ -299,30 +309,51 @@
     return pl.CostEstimate(flops=flops, bytes_accessed=8 * 2**20, transcendentals=0)
 
 
-def call_first(body, rows_in, spaces, weights, extra, sizes):
+def call_prepare(paired, own, w_half, w_conv, sizes):
     cin, cout, rows, cols = sizes
-    w_half, b_up, w_conv = weights
+    wide = own.shape[0] * own.shape[1] if paired else 8
+    return pl.pallas_call(
+        functools.partial(prepare, paired),
+        out_shape=(
+            jax.ShapeDtypeStruct((3, rows // 2 + 2, cin, cols), jnp.bfloat16),
+            jax.ShapeDtypeStruct((32, cout // 2, cin), jnp.bfloat16),
+            jax.ShapeDtypeStruct((2 * cout, 9 * cout), jnp.bfloat16),
+            jax.ShapeDtypeStruct((2 * cout, 9 * cout), jnp.bfloat16),
+        ),
+        in_specs=[ANY] * 3,
+        out_specs=(VMEM,) * 4,
+        scratch_shapes=[
+            pltpu.VMEM((2, 2 * cout, 9 * cout), jnp.bfloat16),
+            pltpu.VMEM((27, cout, cout), jnp.bfloat16),
+            pltpu.VMEM((wide, cols), jnp.float32),
+            pltpu.VMEM(own.shape, jnp.bfloat16),
+            pltpu.SemaphoreType.DMA((3,)),
+        ],
+        cost_estimate=pl.CostEstimate(flops=2 * 18 * 256 * cout * cout, bytes_accessed=8 * 2**20, transcendentals=0),
+        compiler_params=pltpu.CompilerParams(vmem_limit_bytes=LIMIT),
+    )(in_hbm(own), in_hbm(w_half), in_hbm(w_conv))
+
+
+def call_first(body, rows_in, prepared, b_up, extra, sizes):
+    cin, cout, rows, cols = sizes
+    started, w_half, kernel = prepared
     return pl.pallas_call(
         body,
         out_shape=(
-            jax.ShapeDtypeStruct((3, rows // 2 + 2, cin, cols), jnp.bfloat16),
+            jax.ShapeDtypeStruct(started.shape, jnp.bfloat16),
             jax.ShapeDtypeStruct((2, 2 * cout, rows * cols), jnp.float32),
-            jax.ShapeDtypeStruct((2 * cout, 9 * cout), jnp.bfloat16),
         ),
-        in_specs=[*spaces, ANY, VMEM, ANY],
-        out_specs=(VMEM,) * 3,
+        in_specs=[VMEM] * (len(rows_in) + 4),
+        out_specs=(VMEM,) * 2,
         scratch_shapes=[
-            pltpu.VMEM((2, 2 * cout, 9 * cout), jnp.bfloat16),
             pltpu.VMEM((cout, cout), jnp.float32),
             pltpu.VMEM((4, rows + 2, cout, cols), jnp.bfloat16),
-            pltpu.VMEM((32, cout // 2, cin), jnp.bfloat16),
-            pltpu.VMEM((27, cout, cout), jnp.bfloat16),
-            pltpu.SemaphoreType.DMA((2,)),
         ]
         + extra,
+        input_output_aliases={len(rows_in): 0},
         cost_estimate=cost(sizes),
         compiler_params=pltpu.CompilerParams(vmem_limit_bytes=LIMIT),
-    )(*rows_in, in_hbm(w_half), b_up, in_hbm(w_conv))
+    )(*rows_in, started, w_half, kernel, b_up)
 
 
 def call_second(paired, parts, results, biases, sizes):
@@ -364,21 +395,19 @@
     peer = lax.ppermute(inputs, AXES, across).reshape(chans, held, cols)
     own = inputs.reshape(chans, held, cols)
     near, far, w_a, w_b = call_pieces(own, w_up)
+    near, far, w_conv = lax.optimization_barrier((near, far, w_conv))
+    far = lax.ppermute(far, AXES, outer)
+    near = lax.ppermute(near, AXES, chain)
+    x, w_half, kernel, other = call_prepare(True, own, w_up, w_conv, sizes)
+    near, far, w_a, w_b, kernel = lax.optimization_barrier((near, far, w_a, w_b, kernel))
     w_a = lax.ppermute(w_a, AXES, across)
     w_b = lax.ppermute(w_b, AXES, across)
-    near = lax.ppermute(near, AXES, chain)
-    far = lax.ppermute(far, AXES, outer)
     w_ax = lax.ppermute(w_a, AXES, pairs)
     w_ac = lax.ppermute(w_a, AXES, cores)
     biases = (b_up[None], b_conv[None])
-    extra = [
-        pltpu.VMEM((2, chans * held, cols), jnp.float32),
-        pltpu.VMEM((chans, held, cols), jnp.bfloat16),
-        pltpu.SemaphoreType.DMA,
-    ]
-    rows_in = (in_hbm(own), peer, near, far)
-    weights = (w_up, biases[0], w_conv)
-    results = call_first(paired_first, rows_in, (ANY, VMEM, VMEM, VMEM), weights, extra, sizes)
+    extra = [pltpu.VMEM((chans * held, cols), jnp.float32)]
+    x, total = call_first(paired_first, (peer, near, far), (x, w_half, kernel), biases[0], extra, sizes)
+    results = (x, total, other)
     w_b, w_ax, w_ac, *results = lax.optimization_barrier((w_b, w_ax, w_ac, *results))
     w_bc = lax.ppermute(w_b, AXES, cores)
     w_axc = lax.ppermute(w_ax, AXES, cores)
@@ -399,8 +428,8 @@
     share = inputs.shape[2] // chs
     rows = lax.dynamic_slice_in_dim(rows, c * share, share + 2, 0)
     biases = (b_up[None], b_conv[None])
-    weights = (w_all[:, :part], biases[0], w_conv)
-    results = call_first(gathered_first, (rows,), (VMEM,), weights, [], sizes)
+    *prepared, other = call_prepare(False, rows, w_all[:, :part], w_conv, sizes)
+    results = (*call_first(gathered_first, (), prepared, biases[0], [], sizes), other)
     return call_second(False, (w_all[:16, part:], w_all[16:, part:]), results, biases, sizes)
 
 

time: 29.4 us -> 29.8 us (1.014)
  starting transfers between devices: 12.4 us -> 13.1 us
    ppermute x1, starting transfers between devices: 0.08 us -> 4.99 us  [paired(): w_a = lax.ppermute(w_a, AXES, across)]
    ppermute x1, starting transfers between devices: 3.27 us -> 0.01 us  [paired(): w_bc = lax.ppermute(w_b, AXES, cores)]
    ppermute x1, starting transfers between devices: 2.01 us -> 0.08 us  [paired(): w_b = lax.ppermute(w_b, AXES, across)]
    ppermute x1, waiting for transfers between devices: 4.97 us -> 3.98 us  [paired(): w_a = lax.ppermute(w_a, AXES, across)]
    ppermute x1, waiting for transfers between devices: 0.01 us -> 0.78 us  [paired(): w_ax = lax.ppermute(w_a, AXES, pairs)]
    ppermute x1, starting transfers between devices: 0.08 us -> 0.5 us  [paired(): w_axc = lax.ppermute(w_ax, AXES, cores)]
    ppermute x1, starting transfers between devices: 2.03 us -> 2.43 us  [paired(): w_ax = lax.ppermute(w_a, AXES, pairs)]
    pallas_call x1 -> x2, Pallas kernels: 5.06 us -> 5.12 us  [the longest x1 2.85 us: call_first(): pl.pallas_call(body, out_shape=(jax.ShapeDtypeStruct(started.shape, jnp.b...]
  transfers between devices with their start and end apart: 9 -> 9, of which waited for: 2 -> 3; matrix products, arithmetic and copies ran while one was open for 0% -> 0% of each run, Pallas kernels for 21% -> 21%
where the time goes in v7:
time: 29.8 us; the launch traced here: 29.7 us
  starting transfers between devices  13.1 us (44%)
  Pallas kernels  10.5 us (35%)
  waiting for transfers between devices  5.99 us (20%)
    ppermute x1, starting transfers between devices, paired(): w_a = lax.ppermute(w_a, AXES, across)  4.99 us
    pallas_call x1, Pallas kernels, call_second(): pl.pallas_call(functools.partial(second, paired, len(parts)), out_shape=j...  4.24 us
    ppermute x1, waiting for transfers between devices, paired(): w_a = lax.ppermute(w_a, AXES, across)  3.98 us
    ppermute x1, starting transfers between devices, paired(): peer = lax.ppermute(inputs, AXES, across).reshape(chans, held, cols)  2.97 us
    pallas_call x1, Pallas kernels, call_first(): pl.pallas_call(body, out_shape=(jax.ShapeDtypeStruct(started.shape, jnp.b...  2.85 us
    ppermute x1, starting transfers between devices, paired(): w_ax = lax.ppermute(w_a, AXES, pairs)  2.43 us
    pallas_call x1, Pallas kernels, call_prepare(): pl.pallas_call(functools.partial(prepare, paired), out_shape=(jax.ShapeDt...  2.27 us
    ppermute x1, starting transfers between devices, paired(): near = lax.ppermute(near, AXES, chain)  1.46 us
  transfers between devices with their start and end apart: 9, of which 3 were waited for; matrix products, arithmetic and copies ran while one was open for 0% of the time, Pallas kernels for 21%

profile of v7, /device:TPU:0, one launch (start us, length us, event | category | flops | bytes accessed | tf_op | source)
XLA Modules:
  0.0 29.7 jit_solution(6950098893317993863)
XLA Ops:
  0.0 3.0 %collective-permute-start.6 = (bf16[128,1,8,128]{3,2,0,1:T(8,128)(2,1)}, bf16[128,1,8,128]{3,2,0,1:T(8,128)(2,1)S(1)}, u32[]{:S(2)}, u32[]{:S(2)}) collective-permute-start(bf16[128,1,8,128]{3,2,0,1:T(8,128)(2,1)} %bitcast.9), channel_id=1, source_target_pairs={{0,1},{1,0},{2,3},{3,2},{4,5},{5,4},{6,7},{7,6},{8,9},{9,8},{10,11... | collective-permute-start | bytes 786440 | tf_op jit(solution)/shard_map/ppermute | solution.py:395
  3.0 1.1 %shard_map.55 = (bf16[128,128]{1,0:T(8,128)(2,1)S(1)}, bf16[128,128]{1,0:T(8,128)(2,1)S(1)}, bf16[16,16,256]{2,1,0:T(8,128)(2,1)S(1)}, bf16[16,32,256]{2,1,0:T(8,128)(2,1)S(1)}) custom-call(bf16[128,8,128]{2,1,0:T(8,128)(2,1)} %bitcast.10, bf16[64,64,256]{2,1,0:T(8,128)(2,1)} %w_half_ref.1), custom_call_target="tpu_custom_call" | custom-call | tf_op jit(solution)/shard_map/pallas_call | solution.py:283
  4.1 0.0 copy-start
  4.1 1.5 %collective-permute-start = (bf16[128,128]{1,0:T(8,128)(2,1)S(1)}, bf16[128,128]{1,0:T(8,128)(2,1)S(1)}, u32[]{:S(2)}, u32[]{:S(2)}) collective-permute-start(bf16[128,128]{1,0:T(8,128)(2,1)S(1)} %get-tuple-element.31), channel_id=1, source_target_pairs={{0,2},{2,4},{4,6},{6,8},{8,10},{10,12},{12,14},{14,16},{16,18},{18... | collective-permute-start | bytes 98312 | tf_op jit(solution)/shard_map/ppermute | solution.py:400
  5.6 0.7 %collective-permute-start.1 = (bf16[128,128]{1,0:T(8,128)(2,1)S(1)}, bf16[128,128]{1,0:T(8,128)(2,1)S(1)}, u32[]{:S(2)}, u32[]{:S(2)}) collective-permute-start(bf16[128,128]{1,0:T(8,128)(2,1)S(1)} %get-tuple-element.32), channel_id=1, source_target_pairs={{1,2},{3,4},{5,6},{7,8},{9,10},{11,12},{13,14},{15,16},{17,18},{19... | collective-permute-start | bytes 98312 | tf_op jit(solution)/shard_map/ppermute | solution.py:399
  6.2 2.3 %shard_map.56 = (bf16[3,6,256,128]{3,2,1,0:T(8,128)(2,1)S(1)}, bf16[32,64,256]{2,1,0:T(8,128)(2,1)S(1)}, bf16[256,1152]{1,0:T(8,128)(2,1)S(1)}, bf16[256,1152]{1,0:T(8,128)(2,1)S(1)}) custom-call(bf16[128,8,128]{2,1,0:T(8,128)(2,1)} %bitcast.11, bf16[64,64,256]{2,1,0:T(8,128)(2,1)} %w_half_ref.1, bf16[27,128,128]{2,1,0:T(8,128)(2,1)} %w_conv_ref), custom_call_target="tpu_custom_call" | custom-call | flops 150994944 | bytes 8388608 | tf_op jit(solution)/shard_map/pallas_call | solution.py:315
  8.5 0.0 collective-permute-done.near_ref
  8.5 0.0 collective-permute-done.1.far_ref
  8.5 5.0 %collective-permute-start.2 = (bf16[16,16,256]{2,1,0:T(8,128)(2,1)S(1)}, bf16[16,16,256]{2,1,0:T(8,128)(2,1)S(1)}, u32[]{:S(2)}, u32[]{:S(2)}) collective-permute-start(bf16[16,16,256]{2,1,0:T(8,128)(2,1)S(1)} %get-tuple-element.37), channel_id=1, source_target_pairs={{0,1},{1,0},{2,3},{3,2},{4,5},{5,4},{6,7},{7,6},{8,9},{9,8},{10,11... | collective-permute-start | bytes 393224 | tf_op jit(solution)/shard_map/ppermute | solution.py:403
  13.5 0.1 collective-permute-start.3
  13.6 4.0 %collective-permute-done.2.refs_0_ = bf16[16,16,256]{2,1,0:T(8,128)(2,1)S(1)} collective-permute-done((bf16[16,16,256]{2,1,0:T(8,128)(2,1)S(1)}, bf16[16,16,256]{2,1,0:T(8,128)(2,1)S(1)}, u32[]{:S(2)}, u32[]{:S(2)}) %collective-permute-start.2) | collective-permute-done | bytes 131104 | tf_op jit(solution)/shard_map/ppermute | solution.py:403
  17.6 2.4 %collective-permute-start.4 = (bf16[16,16,256]{2,1,0:T(8,128)(2,1)S(1)}, bf16[16,16,256]{2,1,0:T(8,128)(2,1)S(1)}, u32[]{:S(2)}, u32[]{:S(2)}) collective-permute-start(bf16[16,16,256]{2,1,0:T(8,128)(2,1)S(1)} %collective-permute-done.2.refs_0_), channel_id=1, source_target_pairs={{0,4},{1,5},{2,6},{3,7},{4,0},{5,1},{6,2},{7,3},{8,12},{9,13},{10,... | collective-permute-start | bytes 393224 | tf_op jit(solution)/shard_map/ppermute | solution.py:405
  20.0 0.0 collective-permute-start.5
  20.0 0.0 collective-permute-done.6
  20.0 0.0 copy-done
  20.0 0.0 copy-start.1
  20.1 2.9 %shard_map.57 = (bf16[3,6,256,128]{3,2,1,0:T(8,128)(2,1)S(1)}, f32[2,256,1024]{2,1,0:T(8,128)S(1)}) custom-call(bf16[128,8,128]{2,1,0:T(8,128)(2,1)S(1)} %bitcast.5, bf16[128,128]{1,0:T(8,128)(2,1)S(1)} %collective-permute-done.near_ref, bf16[128,128]{1,0:T(8,128)(2,1)S(1)} %collective-permute-done.1.far_ref, ...), custom_call_target="tpu_custom_call", output_to_operand_aliasing={{0}: (3, {})} | custom-call | flops 1879048192 | bytes 8388608 | tf_op jit(solution)/shard_map/pallas_call | solution.py:340
  22.9 0.8 %collective-permute-done.4.refs_2_ = bf16[16,16,256]{2,1,0:T(8,128)(2,1)S(1)} collective-permute-done((bf16[16,16,256]{2,1,0:T(8,128)(2,1)S(1)}, bf16[16,16,256]{2,1,0:T(8,128)(2,1)S(1)}, u32[]{:S(2)}, u32[]{:S(2)}) %collective-permute-start.4) | collective-permute-done | bytes 131104 | tf_op jit(solution)/shard_map/ppermute | solution.py:405
  23.7 0.0 collective-permute-done.5.refs_1_
  23.7 0.0 collective-permute-done.3.refs_4_
  23.7 0.0 collective-permute-start.8
  23.7 0.5 %collective-permute-start.7 = (bf16[16,16,256]{2,1,0:T(8,128)(2,1)S(1)}, bf16[16,16,256]{2,1,0:T(8,128)(2,1)S(1)}, u32[]{:S(2)}, u32[]{:S(2)}) collective-permute-start(bf16[16,16,256]{2,1,0:T(8,128)(2,1)S(1)} %collective-permute-done.4.refs_2_), channel_id=1, source_target_pairs={{0,2},{1,3},{2,0},{3,1},{4,6},{5,7},{6,4},{7,5},{8,10},{9,11},{10,... | collective-permute-start | bytes 393224 | tf_op jit(solution)/shard_map/ppermute | solution.py:413
  24.2 1.2 %collective-permute-done.7.refs_3_ = bf16[16,16,256]{2,1,0:T(8,128)(2,1)S(1)} collective-permute-done((bf16[16,16,256]{2,1,0:T(8,128)(2,1)S(1)}, bf16[16,16,256]{2,1,0:T(8,128)(2,1)S(1)}, u32[]{:S(2)}, u32[]{:S(2)}) %collective-permute-start.7) | collective-permute-done | bytes 131104 | tf_op jit(solution)/shard_map/ppermute | solution.py:413
  25.4 0.0 collective-permute-done.8.refs_5_
  25.4 0.0 copy-done.1
  25.4 4.2 %shard_map.58 = bf16[128,2,8,256]{3,2,1,0:T(8,128)(2,1)} custom-call(bf16[16,16,256]{2,1,0:T(8,128)(2,1)S(1)} %collective-permute-done.2.refs_0_, bf16[16,16,256]{2,1,0:T(8,128)(2,1)S(1)} %collective-permute-done.5.refs_1_, bf16[16,16,256]{2,1,0:T(8,128)(2,1)S(1)} %collective-permute-done.4.refs_2_, bf16[16,16,256]{2,1,0:T(8,128)(2,1)S(1)} %collective-permute-done.7.refs_3_, ...), custom_call_target="tpu_custom_call" | custom-call | flops 1879048192 | bytes 8388608 | tf_op jit(solution)/shard_map/pallas_call | solution.py:361
Async XLA Ops:
  0.0 20.0 %collective-permute-start.6 = (bf16[128,1,8,128]{3,2,0,1:T(8,128)(2,1)}, bf16[128,1,8,128]{3,2,0,1:T(8,128)(2,1)S(1)}, u32[]{:S(2)}, u32[]{:S(2)}) collective-permute-start(bf16[128,1,8,128]{3,2,0,1:T(8,128)(2,1)} %bitcast.9), channel_id=1, source_target_pairs={{0,1},{1,0},{2,3},{3,2},{4,5},{5,4},{6,7},{7,6},{8,9},{9,8},{10,11... | collective-permute-start | bytes 786440 | tf_op jit(solution)/shard_map/ppermute | solution.py:395
  4.1 15.9 %copy-start = (f32[128]{0:T(128)S(1)}, f32[128]{0:T(128)}, u32[]{:S(2)}) copy-start(f32[128]{0:T(128)} %param.7) | copy-start | bytes 1540
  4.1 4.4 %collective-permute-start = (bf16[128,128]{1,0:T(8,128)(2,1)S(1)}, bf16[128,128]{1,0:T(8,128)(2,1)S(1)}, u32[]{:S(2)}, u32[]{:S(2)}) collective-permute-start(bf16[128,128]{1,0:T(8,128)(2,1)S(1)} %get-tuple-element.31), channel_id=1, source_target_pairs={{0,2},{2,4},{4,6},{6,8},{8,10},{10,12},{12,14},{14,16},{16,18},{18... | collective-permute-start | bytes 98312 | tf_op jit(solution)/shard_map/ppermute | solution.py:400
  5.6 3.0 %collective-permute-start.1 = (bf16[128,128]{1,0:T(8,128)(2,1)S(1)}, bf16[128,128]{1,0:T(8,128)(2,1)S(1)}, u32[]{:S(2)}, u32[]{:S(2)}) collective-permute-start(bf16[128,128]{1,0:T(8,128)(2,1)S(1)} %get-tuple-element.32), channel_id=1, source_target_pairs={{1,2},{3,4},{5,6},{7,8},{9,10},{11,12},{13,14},{15,16},{17,18},{19... | collective-permute-start | bytes 98312 | tf_op jit(solution)/shard_map/ppermute | solution.py:399
  8.5 9.1 %collective-permute-start.2 = (bf16[16,16,256]{2,1,0:T(8,128)(2,1)S(1)}, bf16[16,16,256]{2,1,0:T(8,128)(2,1)S(1)}, u32[]{:S(2)}, u32[]{:S(2)}) collective-permute-start(bf16[16,16,256]{2,1,0:T(8,128)(2,1)S(1)} %get-tuple-element.37), channel_id=1, source_target_pairs={{0,1},{1,0},{2,3},{3,2},{4,5},{5,4},{6,7},{7,6},{8,9},{9,8},{10,11... | collective-permute-start | bytes 393224 | tf_op jit(solution)/shard_map/ppermute | solution.py:403
  13.5 10.2 %collective-permute-start.3 = (bf16[16,32,256]{2,1,0:T(8,128)(2,1)S(1)}, bf16[16,32,256]{2,1,0:T(8,128)(2,1)S(1)}, u32[]{:S(2)}, u32[]{:S(2)}) collective-permute-start(bf16[16,32,256]{2,1,0:T(8,128)(2,1)S(1)} %get-tuple-element.38), channel_id=1, source_target_pairs={{0,1},{1,0},{2,3},{3,2},{4,5},{5,4},{6,7},{7,6},{8,9},{9,8},{10,11... | collective-permute-start | bytes 786440 | tf_op jit(solution)/shard_map/ppermute | solution.py:404
  17.6 6.1 %collective-permute-start.4 = (bf16[16,16,256]{2,1,0:T(8,128)(2,1)S(1)}, bf16[16,16,256]{2,1,0:T(8,128)(2,1)S(1)}, u32[]{:S(2)}, u32[]{:S(2)}) collective-permute-start(bf16[16,16,256]{2,1,0:T(8,128)(2,1)S(1)} %collective-permute-done.2.refs_0_), channel_id=1, source_target_pairs={{0,4},{1,5},{2,6},{3,7},{4,0},{5,1},{6,2},{7,3},{8,12},{9,13},{10,... | collective-permute-start | bytes 393224 | tf_op jit(solution)/shard_map/ppermute | solution.py:405
  20.0 3.7 %collective-permute-start.5 = (bf16[16,16,256]{2,1,0:T(8,128)(2,1)S(1)}, bf16[16,16,256]{2,1,0:T(8,128)(2,1)S(1)}, u32[]{:S(2)}, u32[]{:S(2)}) collective-permute-start(bf16[16,16,256]{2,1,0:T(8,128)(2,1)S(1)} %collective-permute-done.2.refs_0_), channel_id=1, source_target_pairs={{0,2},{1,3},{2,0},{3,1},{4,6},{5,7},{6,4},{7,5},{8,10},{9,11},{10,... | collective-permute-start | bytes 393224 | tf_op jit(solution)/shard_map/ppermute | solution.py:406
  20.0 5.4 %copy-start.1 = (f32[128]{0:T(128)S(1)}, f32[128]{0:T(128)}, u32[]{:S(2)}) copy-start(f32[128]{0:T(128)} %param.9) | copy-start | bytes 1540
  23.7 1.7 %collective-permute-start.8 = (bf16[16,32,256]{2,1,0:T(8,128)(2,1)S(1)}, bf16[16,32,256]{2,1,0:T(8,128)(2,1)S(1)}, u32[]{:S(2)}, u32[]{:S(2)}) collective-permute-start(bf16[16,32,256]{2,1,0:T(8,128)(2,1)S(1)} %collective-permute-done.3.refs_4_), channel_id=1, source_target_pairs={{0,2},{1,3},{2,0},{3,1},{4,6},{5,7},{6,4},{7,5},{8,10},{9,11},{10,... | collective-permute-start | bytes 786440 | tf_op jit(solution)/shard_map/ppermute | solution.py:412
  23.7 1.7 %collective-permute-start.7 = (bf16[16,16,256]{2,1,0:T(8,128)(2,1)S(1)}, bf16[16,16,256]{2,1,0:T(8,128)(2,1)S(1)}, u32[]{:S(2)}, u32[]{:S(2)}) collective-permute-start(bf16[16,16,256]{2,1,0:T(8,128)(2,1)S(1)} %collective-permute-done.4.refs_2_), channel_id=1, source_target_pairs={{0,2},{1,3},{2,0},{3,1},{4,6},{5,7},{6,4},{7,5},{8,10},{9,11},{10,... | collective-permute-start | bytes 393224 | tf_op jit(solution)/shard_map/ppermute | solution.py:413

commit v8 on v7

--- a/solution.py
+++ b/solution.py
@@ -147,16 +147,6 @@
             sum_ref[col_phase, :, start * cols : (start + 2) * cols] = convolve(kernel, u_ref, start, col_phase)
 
 
-def store_rows(x_ref, wide_ref, offset):
-    c = lax.axis_index("ch")
-    share = x_ref.shape[1] - 1
-    chans = x_ref.shape[2] // 2
-    rows = wide_ref.shape[0] // chans
-    for place in range(share):
-        value = wide_ref[pl.ds(place + c * (rows - share), chans, stride=rows), :]
-        store_row(x_ref, place + 1 - c, offset, value)
-
-
 def prepare(paired, own_ref, w_half_ref, w_conv_ref, x_ref, w_ref, kernel_ref, other_ref, *scratch):
     halves_ref, v_ref, wide_ref, raw_ref, sems = scratch
     s, c = lax.axis_index("space"), lax.axis_index("ch")
@@ -182,7 +172,10 @@
     if paired:
         chans, rows, cols = own_ref.shape
         wide_ref[...] = raw_ref[...].astype(jnp.float32).reshape(chans * rows, cols)
-        store_rows(x_ref, wide_ref, c * chans)
+        share = x_ref.shape[1] - 1
+        for place in range(share):
+            value = wide_ref[pl.ds(place + c * (rows - share), chans, stride=rows), :]
+            store_row(x_ref, place + 1 - c, c * chans, value)
     else:
         for slot in range(own_ref.shape[0]):
             store_row(x_ref, slot, 0, raw_ref[slot].astype(jnp.float32))
@@ -191,12 +184,11 @@
 
 def paired_first(peer_ref, near_ref, far_ref, started_ref, *refs):
     refs, results, scratch = refs[:3], refs[3:5], refs[5:]
-    *scratch, wide_ref = scratch
     x_ref = results[0]
     c = lax.axis_index("ch")
-    chans, rows, cols = peer_ref.shape
-    wide_ref[...] = peer_ref[...].astype(jnp.float32).reshape(chans * rows, cols)
-    store_rows(x_ref, wide_ref, (1 - c) * chans)
+    share, chans, _ = peer_ref.shape
+    for place in range(share):
+        store_row(x_ref, place + 1 - c, (1 - c) * chans, peer_ref[place].astype(jnp.float32))
     slot = c * (x_ref.shape[1] - 1)
     store_row(x_ref, slot, c * chans, near_ref[...].astype(jnp.float32))
     store_row(x_ref, slot, (1 - c) * chans, far_ref[...].astype(jnp.float32))
@@ -256,7 +248,7 @@
         copy.wait()
 
 
-def pieces(own_ref, w_up_ref, near_ref, far_ref, w_a_ref, w_b_ref, wide_ref, raw_ref, sems):
+def pieces(own_ref, w_up_ref, near_ref, far_ref, peer_ref, w_a_ref, w_b_ref, wide_ref, raw_ref, sems):
     s, c = lax.axis_index("space"), lax.axis_index("ch")
     raw = pltpu.make_async_copy(own_ref, raw_ref, sems.at[2])
     raw.start()
@@ -273,6 +265,10 @@
     inner, outer = (1 - c) * (rows - 1), c * (rows - 1)
     near_ref[...] = wide_ref[pl.ds(inner, chans, stride=rows), :].astype(jnp.bfloat16)
     far_ref[...] = wide_ref[pl.ds(outer, chans, stride=rows), :].astype(jnp.bfloat16)
+    share = peer_ref.shape[0]
+    for place in range(share):
+        row = wide_ref[pl.ds(place + (1 - c) * (rows - share), chans, stride=rows), :]
+        peer_ref[place] = row.astype(jnp.bfloat16)
     for copy in copies:
         copy.wait()
 
@@ -285,11 +281,12 @@
         out_shape=(
             jax.ShapeDtypeStruct((chans, cols), jnp.bfloat16),
             jax.ShapeDtypeStruct((chans, cols), jnp.bfloat16),
+            jax.ShapeDtypeStruct((rows // 2 + 1, chans, cols), jnp.bfloat16),
             jax.ShapeDtypeStruct((16, part // 4, cin), jnp.bfloat16),
             jax.ShapeDtypeStruct((16, part // 2, cin), jnp.bfloat16),
         ),
         in_specs=[ANY, ANY],
-        out_specs=(VMEM,) * 4,
+        out_specs=(VMEM,) * 5,
         scratch_shapes=[
             pltpu.VMEM((chans * rows, cols), jnp.float32),
             pltpu.VMEM((chans, rows, cols), jnp.bfloat16),
@@ -334,7 +331,7 @@
     )(in_hbm(own), in_hbm(w_half), in_hbm(w_conv))
 
 
-def call_first(body, rows_in, prepared, b_up, extra, sizes):
+def call_first(body, rows_in, prepared, b_up, sizes):
     cin, cout, rows, cols = sizes
     started, w_half, kernel = prepared
     return pl.pallas_call(
@@ -348,8 +345,7 @@
         scratch_shapes=[
             pltpu.VMEM((cout, cout), jnp.float32),
             pltpu.VMEM((4, rows + 2, cout, cols), jnp.bfloat16),
-        ]
-        + extra,
+        ],
         input_output_aliases={len(rows_in): 0},
         cost_estimate=cost(sizes),
         compiler_params=pltpu.CompilerParams(vmem_limit_bytes=LIMIT),
@@ -392,21 +388,19 @@
     outer = [(t, t + 1) for t in range(1, 2 * spaces - 1, 2)]
     outer += [(j, i) for i, j in outer]
 
-    peer = lax.ppermute(inputs, AXES, across).reshape(chans, held, cols)
     own = inputs.reshape(chans, held, cols)
-    near, far, w_a, w_b = call_pieces(own, w_up)
-    near, far, w_conv = lax.optimization_barrier((near, far, w_conv))
+    near, far, peer, w_a, w_b = call_pieces(own, w_up)
     far = lax.ppermute(far, AXES, outer)
+    far, peer, w_a, w_b, near, w_conv = lax.optimization_barrier((far, peer, w_a, w_b, near, w_conv))
+    peer = lax.ppermute(peer, AXES, across)
+    w_a = lax.ppermute(w_a, AXES, across)
+    w_b = lax.ppermute(w_b, AXES, across)
     near = lax.ppermute(near, AXES, chain)
     x, w_half, kernel, other = call_prepare(True, own, w_up, w_conv, sizes)
-    near, far, w_a, w_b, kernel = lax.optimization_barrier((near, far, w_a, w_b, kernel))
-    w_a = lax.ppermute(w_a, AXES, across)
-    w_b = lax.ppermute(w_b, AXES, across)
     w_ax = lax.ppermute(w_a, AXES, pairs)
     w_ac = lax.ppermute(w_a, AXES, cores)
     biases = (b_up[None], b_conv[None])
-    extra = [pltpu.VMEM((chans * held, cols), jnp.float32)]
-    x, total = call_first(paired_first, (peer, near, far), (x, w_half, kernel), biases[0], extra, sizes)
+    x, total = call_first(paired_first, (peer, near, far), (x, w_half, kernel), biases[0], sizes)
     results = (x, total, other)
     w_b, w_ax, w_ac, *results = lax.optimization_barrier((w_b, w_ax, w_ac, *results))
     w_bc = lax.ppermute(w_b, AXES, cores)
@@ -429,7 +423,7 @@
     rows = lax.dynamic_slice_in_dim(rows, c * share, share + 2, 0)
     biases = (b_up[None], b_conv[None])
     *prepared, other = call_prepare(False, rows, w_all[:, :part], w_conv, sizes)
-    results = (*call_first(gathered_first, (), prepared, biases[0], [], sizes), other)
+    results = (*call_first(gathered_first, (), prepared, biases[0], sizes), other)
     return call_second(False, (w_all[:16, part:], w_all[16:, part:]), results, biases, sizes)
 
 

time: 29.8 us -> 29.6 us (level); the launches traced: 29.7 us -> 29 us
  waiting for transfers between devices: 5.99 us -> 3.15 us
  starting transfers between devices: 13.1 us -> 15.4 us
    ppermute x1, starting transfers between devices: 4.99 us -> 0.03 us  [paired(): w_a = lax.ppermute(w_a, AXES, across)]
    ppermute x1, starting transfers between devices: 2.97 us -> 7.52 us  [paired(): peer = lax.ppermute(peer, AXES, across)]
    ppermute x1, waiting for transfers between devices: 3.98 us -> 1.71 us  [paired(): w_a = lax.ppermute(w_a, AXES, across)]
    ppermute x1, starting transfers between devices: 0.08 us -> 1.99 us  [paired(): w_b = lax.ppermute(w_b, AXES, across)]
    ppermute x1, waiting for transfers between devices: 0.78 us -> 0.2 us  [paired(): w_ax = lax.ppermute(w_a, AXES, pairs)]
    ppermute x1, starting transfers between devices: 2.43 us -> 2.86 us  [paired(): w_ax = lax.ppermute(w_a, AXES, pairs)]
    ppermute x1, starting transfers between devices: 0.01 us -> 0.39 us  [paired(): w_bc = lax.ppermute(w_b, AXES, cores)]
    ppermute x1, starting transfers between devices: 0.5 us -> 0.12 us  [paired(): w_axc = lax.ppermute(w_ax, AXES, cores)]
  transfers between devices with their start and end apart: 9 -> 9, of which waited for: 3 -> 3; matrix products, arithmetic and copies ran while one was open for 0% -> 0% of each run, Pallas kernels for 21% -> 17%
where the time goes in v8:
time: 29.6 us; the launch traced here: 29 us
  starting transfers between devices  15.4 us (52%)
  Pallas kernels  10.4 us (35%)
  waiting for transfers between devices  3.15 us (11%)
    ppermute x1, starting transfers between devices, paired(): peer = lax.ppermute(peer, AXES, across)  7.52 us
    pallas_call x1, Pallas kernels, call_second(): pl.pallas_call(functools.partial(second, paired, len(parts)), out_shape=j...  4.23 us
    ppermute x1, starting transfers between devices, paired(): w_ax = lax.ppermute(w_a, AXES, pairs)  2.86 us
    pallas_call x1, Pallas kernels, call_first(): pl.pallas_call(body, out_shape=(jax.ShapeDtypeStruct(started.shape, jnp.b...  2.77 us
    pallas_call x1, Pallas kernels, call_prepare(): pl.pallas_call(functools.partial(prepare, paired), out_shape=(jax.ShapeDt...  2.27 us
    ppermute x1, starting transfers between devices, paired(): w_b = lax.ppermute(w_b, AXES, across)  1.99 us
    ppermute x1, starting transfers between devices, paired(): near = lax.ppermute(near, AXES, chain)  1.8 us
    ppermute x1, waiting for transfers between devices, paired(): w_a = lax.ppermute(w_a, AXES, across)  1.71 us
  transfers between devices with their start and end apart: 9, of which 3 were waited for; matrix products, arithmetic and copies ran while one was open for 0% of the time, Pallas kernels for 17%

profile of v8, /device:TPU:0, one launch (start us, length us, event | category | flops | bytes accessed | tf_op | source)
XLA Modules:
  0.0 29.0 jit_solution(17700128645375135662)
XLA Ops:
  0.0 1.1 %shard_map.55 = (bf16[128,128]{1,0:T(8,128)(2,1)S(1)}, bf16[128,128]{1,0:T(8,128)(2,1)S(1)}, bf16[5,128,128]{2,1,0:T(8,128)(2,1)S(1)}, bf16[16,16,256]{2,1,0:T(8,128)(2,1)S(1)}, bf16[16,32,256]{2,1,0:T(8,128)(2,1)S(1)}) custom-call(bf16[128,8,128]{2,1,0:T(8,128)(2,1)} %bitcast.6, bf16[64,64,256]{2,1,0:T(8,128)(2,1)} %w_half_ref.1), custom_call_target="tpu_custom_call" | custom-call | tf_op jit(solution)/shard_map/pallas_call | solution.py:279
  1.1 0.0 copy-start
  1.1 0.7 %collective-permute-start = (bf16[128,128]{1,0:T(8,128)(2,1)S(1)}, bf16[128,128]{1,0:T(8,128)(2,1)S(1)}, u32[]{:S(2)}, u32[]{:S(2)}) collective-permute-start(bf16[128,128]{1,0:T(8,128)(2,1)S(1)} %get-tuple-element.28), channel_id=1, source_target_pairs={{1,2},{3,4},{5,6},{7,8},{9,10},{11,12},{13,14},{15,16},{17,18},{19... | collective-permute-start | bytes 98312 | tf_op jit(solution)/shard_map/ppermute | solution.py:393
  1.8 0.0 collective-permute-done.far_ref
  1.8 7.5 %collective-permute-start.5 = (bf16[5,128,128]{2,1,0:T(8,128)(2,1)S(1)}, bf16[5,128,128]{2,1,0:T(8,128)(2,1)S(1)}, u32[]{:S(2)}, u32[]{:S(2)}) collective-permute-start(bf16[5,128,128]{2,1,0:T(8,128)(2,1)S(1)} %get-tuple-element.35), channel_id=1, source_target_pairs={{0,1},{1,0},{2,3},{3,2},{4,5},{5,4},{6,7},{7,6},{8,9},{9,8},{10,11... | collective-permute-start | bytes 491528 | tf_op jit(solution)/shard_map/ppermute | solution.py:395
  9.3 0.0 collective-permute-start.1
  9.4 2.0 %collective-permute-start.2 = (bf16[16,32,256]{2,1,0:T(8,128)(2,1)S(1)}, bf16[16,32,256]{2,1,0:T(8,128)(2,1)S(1)}, u32[]{:S(2)}, u32[]{:S(2)}) collective-permute-start(bf16[16,32,256]{2,1,0:T(8,128)(2,1)S(1)} %get-tuple-element.34), channel_id=1, source_target_pairs={{0,1},{1,0},{2,3},{3,2},{4,5},{5,4},{6,7},{7,6},{8,9},{9,8},{10,11... | collective-permute-start | bytes 786440 | tf_op jit(solution)/shard_map/ppermute | solution.py:397
  11.4 1.8 %collective-permute-start.6 = (bf16[128,128]{1,0:T(8,128)(2,1)S(1)}, bf16[128,128]{1,0:T(8,128)(2,1)S(1)}, u32[]{:S(2)}, u32[]{:S(2)}) collective-permute-start(bf16[128,128]{1,0:T(8,128)(2,1)S(1)} %get-tuple-element.36), channel_id=1, source_target_pairs={{0,2},{2,4},{4,6},{6,8},{8,10},{10,12},{12,14},{14,16},{16,18},{18... | collective-permute-start | bytes 98312 | tf_op jit(solution)/shard_map/ppermute | solution.py:398
  13.2 2.3 %shard_map.56 = (bf16[3,6,256,128]{3,2,1,0:T(8,128)(2,1)S(1)}, bf16[32,64,256]{2,1,0:T(8,128)(2,1)S(1)}, bf16[256,1152]{1,0:T(8,128)(2,1)S(1)}, bf16[256,1152]{1,0:T(8,128)(2,1)S(1)}) custom-call(bf16[128,8,128]{2,1,0:T(8,128)(2,1)} %bitcast.7, bf16[64,64,256]{2,1,0:T(8,128)(2,1)} %w_half_ref.1, bf16[27,128,128]{2,1,0:T(8,128)(2,1)} %w_conv_ref), custom_call_target="tpu_custom_call" | custom-call | flops 150994944 | bytes 8388608 | tf_op jit(solution)/shard_map/pallas_call | solution.py:312
  15.4 1.7 %collective-permute-done.1.refs_0_ = bf16[16,16,256]{2,1,0:T(8,128)(2,1)S(1)} collective-permute-done((bf16[16,16,256]{2,1,0:T(8,128)(2,1)S(1)}, bf16[16,16,256]{2,1,0:T(8,128)(2,1)S(1)}, u32[]{:S(2)}, u32[]{:S(2)}) %collective-permute-start.1) | collective-permute-done | bytes 131104 | tf_op jit(solution)/shard_map/ppermute | solution.py:396
  17.2 2.9 %collective-permute-start.3 = (bf16[16,16,256]{2,1,0:T(8,128)(2,1)S(1)}, bf16[16,16,256]{2,1,0:T(8,128)(2,1)S(1)}, u32[]{:S(2)}, u32[]{:S(2)}) collective-permute-start(bf16[16,16,256]{2,1,0:T(8,128)(2,1)S(1)} %collective-permute-done.1.refs_0_), channel_id=1, source_target_pairs={{0,4},{1,5},{2,6},{3,7},{4,0},{5,1},{6,2},{7,3},{8,12},{9,13},{10,... | collective-permute-start | bytes 393224 | tf_op jit(solution)/shard_map/ppermute | solution.py:400
  20.0 0.0 collective-permute-start.4
  20.0 0.0 collective-permute-done.6.near_ref
  20.0 0.0 collective-permute-done.5.peer_ref
  20.0 0.0 copy-done
  20.0 0.0 copy-start.1
  20.0 2.8 %shard_map.57 = (bf16[3,6,256,128]{3,2,1,0:T(8,128)(2,1)S(1)}, f32[2,256,1024]{2,1,0:T(8,128)S(1)}) custom-call(bf16[5,128,128]{2,1,0:T(8,128)(2,1)S(1)} %collective-permute-done.5.peer_ref, bf16[128,128]{1,0:T(8,128)(2,1)S(1)} %collective-permute-done.6.near_ref, ...), custom_call_target="tpu_custom_call", output_to_operand_aliasing={{0}: (3, {})} | custom-call | flops 1879048192 | bytes 8388608 | tf_op jit(solution)/shard_map/pallas_call | solution.py:337
  22.8 0.2 collective-permute-done.3.refs_2_
  23.0 0.0 collective-permute-done.4.refs_1_
  23.0 0.0 collective-permute-done.2.refs_4_
  23.0 0.4 %collective-permute-start.8 = (bf16[16,32,256]{2,1,0:T(8,128)(2,1)S(1)}, bf16[16,32,256]{2,1,0:T(8,128)(2,1)S(1)}, u32[]{:S(2)}, u32[]{:S(2)}) collective-permute-start(bf16[16,32,256]{2,1,0:T(8,128)(2,1)S(1)} %collective-permute-done.2.refs_4_), channel_id=1, source_target_pairs={{0,2},{1,3},{2,0},{3,1},{4,6},{5,7},{6,4},{7,5},{8,10},{9,11},{10,... | collective-permute-start | bytes 786440 | tf_op jit(solution)/shard_map/ppermute | solution.py:406
  23.4 0.1 collective-permute-start.7
  23.5 1.2 %collective-permute-done.7.refs_3_ = bf16[16,16,256]{2,1,0:T(8,128)(2,1)S(1)} collective-permute-done((bf16[16,16,256]{2,1,0:T(8,128)(2,1)S(1)}, bf16[16,16,256]{2,1,0:T(8,128)(2,1)S(1)}, u32[]{:S(2)}, u32[]{:S(2)}) %collective-permute-start.7) | collective-permute-done | bytes 131104 | tf_op jit(solution)/shard_map/ppermute | solution.py:407
  24.8 0.0 collective-permute-done.8.refs_5_
  24.8 0.0 copy-done.1
  24.8 4.2 %shard_map.58 = bf16[128,2,8,256]{3,2,1,0:T(8,128)(2,1)} custom-call(bf16[16,16,256]{2,1,0:T(8,128)(2,1)S(1)} %collective-permute-done.1.refs_0_, bf16[16,16,256]{2,1,0:T(8,128)(2,1)S(1)} %collective-permute-done.4.refs_1_, bf16[16,16,256]{2,1,0:T(8,128)(2,1)S(1)} %collective-permute-done.3.refs_2_, bf16[16,16,256]{2,1,0:T(8,128)(2,1)S(1)} %collective-permute-done.7.refs_3_, ...), custom_call_target="tpu_custom_call" | custom-call | flops 1879048192 | bytes 8388608 | tf_op jit(solution)/shard_map/pallas_call | solution.py:357
Async XLA Ops:
  1.1 18.9 %copy-start = (f32[128]{0:T(128)S(1)}, f32[128]{0:T(128)}, u32[]{:S(2)}) copy-start(f32[128]{0:T(128)} %param.7) | copy-start | bytes 1540
  1.1 0.7 %collective-permute-start = (bf16[128,128]{1,0:T(8,128)(2,1)S(1)}, bf16[128,128]{1,0:T(8,128)(2,1)S(1)}, u32[]{:S(2)}, u32[]{:S(2)}) collective-permute-start(bf16[128,128]{1,0:T(8,128)(2,1)S(1)} %get-tuple-element.28), channel_id=1, source_target_pairs={{1,2},{3,4},{5,6},{7,8},{9,10},{11,12},{13,14},{15,16},{17,18},{19... | collective-permute-start | bytes 98312 | tf_op jit(solution)/shard_map/ppermute | solution.py:393
  1.8 18.2 %collective-permute-start.5 = (bf16[5,128,128]{2,1,0:T(8,128)(2,1)S(1)}, bf16[5,128,128]{2,1,0:T(8,128)(2,1)S(1)}, u32[]{:S(2)}, u32[]{:S(2)}) collective-permute-start(bf16[5,128,128]{2,1,0:T(8,128)(2,1)S(1)} %get-tuple-element.35), channel_id=1, source_target_pairs={{0,1},{1,0},{2,3},{3,2},{4,5},{5,4},{6,7},{7,6},{8,9},{9,8},{10,11... | collective-permute-start | bytes 491528 | tf_op jit(solution)/shard_map/ppermute | solution.py:395
  9.3 7.8 %collective-permute-start.1 = (bf16[16,16,256]{2,1,0:T(8,128)(2,1)S(1)}, bf16[16,16,256]{2,1,0:T(8,128)(2,1)S(1)}, u32[]{:S(2)}, u32[]{:S(2)}) collective-permute-start(bf16[16,16,256]{2,1,0:T(8,128)(2,1)S(1)} %get-tuple-element.33), channel_id=1, source_target_pairs={{0,1},{1,0},{2,3},{3,2},{4,5},{5,4},{6,7},{7,6},{8,9},{9,8},{10,11... | collective-permute-start | bytes 393224 | tf_op jit(solution)/shard_map/ppermute | solution.py:396
  9.4 13.7 %collective-permute-start.2 = (bf16[16,32,256]{2,1,0:T(8,128)(2,1)S(1)}, bf16[16,32,256]{2,1,0:T(8,128)(2,1)S(1)}, u32[]{:S(2)}, u32[]{:S(2)}) collective-permute-start(bf16[16,32,256]{2,1,0:T(8,128)(2,1)S(1)} %get-tuple-element.34), channel_id=1, source_target_pairs={{0,1},{1,0},{2,3},{3,2},{4,5},{5,4},{6,7},{7,6},{8,9},{9,8},{10,11... | collective-permute-start | bytes 786440 | tf_op jit(solution)/shard_map/ppermute | solution.py:397
  11.4 8.7 %collective-permute-start.6 = (bf16[128,128]{1,0:T(8,128)(2,1)S(1)}, bf16[128,128]{1,0:T(8,128)(2,1)S(1)}, u32[]{:S(2)}, u32[]{:S(2)}) collective-permute-start(bf16[128,128]{1,0:T(8,128)(2,1)S(1)} %get-tuple-element.36), channel_id=1, source_target_pairs={{0,2},{2,4},{4,6},{6,8},{8,10},{10,12},{12,14},{14,16},{16,18},{18... | collective-permute-start | bytes 98312 | tf_op jit(solution)/shard_map/ppermute | solution.py:398
  17.2 5.9 %collective-permute-start.3 = (bf16[16,16,256]{2,1,0:T(8,128)(2,1)S(1)}, bf16[16,16,256]{2,1,0:T(8,128)(2,1)S(1)}, u32[]{:S(2)}, u32[]{:S(2)}) collective-permute-start(bf16[16,16,256]{2,1,0:T(8,128)(2,1)S(1)} %collective-permute-done.1.refs_0_), channel_id=1, source_target_pairs={{0,4},{1,5},{2,6},{3,7},{4,0},{5,1},{6,2},{7,3},{8,12},{9,13},{10,... | collective-permute-start | bytes 393224 | tf_op jit(solution)/shard_map/ppermute | solution.py:400
  20.0 3.0 %collective-permute-start.4 = (bf16[16,16,256]{2,1,0:T(8,128)(2,1)S(1)}, bf16[16,16,256]{2,1,0:T(8,128)(2,1)S(1)}, u32[]{:S(2)}, u32[]{:S(2)}) collective-permute-start(bf16[16,16,256]{2,1,0:T(8,128)(2,1)S(1)} %collective-permute-done.1.refs_0_), channel_id=1, source_target_pairs={{0,2},{1,3},{2,0},{3,1},{4,6},{5,7},{6,4},{7,5},{8,10},{9,11},{10,... | collective-permute-start | bytes 393224 | tf_op jit(solution)/shard_map/ppermute | solution.py:401
  20.0 4.7 %copy-start.1 = (f32[128]{0:T(128)S(1)}, f32[128]{0:T(128)}, u32[]{:S(2)}) copy-start(f32[128]{0:T(128)} %param.9) | copy-start | bytes 1540
  23.0 1.7 %collective-permute-start.8 = (bf16[16,32,256]{2,1,0:T(8,128)(2,1)S(1)}, bf16[16,32,256]{2,1,0:T(8,128)(2,1)S(1)}, u32[]{:S(2)}, u32[]{:S(2)}) collective-permute-start(bf16[16,32,256]{2,1,0:T(8,128)(2,1)S(1)} %collective-permute-done.2.refs_4_), channel_id=1, source_target_pairs={{0,2},{1,3},{2,0},{3,1},{4,6},{5,7},{6,4},{7,5},{8,10},{9,11},{10,... | collective-permute-start | bytes 786440 | tf_op jit(solution)/shard_map/ppermute | solution.py:406
  23.4 1.3 %collective-permute-start.7 = (bf16[16,16,256]{2,1,0:T(8,128)(2,1)S(1)}, bf16[16,16,256]{2,1,0:T(8,128)(2,1)S(1)}, u32[]{:S(2)}, u32[]{:S(2)}) collective-permute-start(bf16[16,16,256]{2,1,0:T(8,128)(2,1)S(1)} %collective-permute-done.3.refs_2_), channel_id=1, source_target_pairs={{0,2},{1,3},{2,0},{3,1},{4,6},{5,7},{6,4},{7,5},{8,10},{9,11},{10,... | collective-permute-start | bytes 393224 | tf_op jit(solution)/shard_map/ppermute | solution.py:407

commit v9 on v8

--- a/solution.py
+++ b/solution.py
@@ -147,14 +147,29 @@
             sum_ref[col_phase, :, start * cols : (start + 2) * cols] = convolve(kernel, u_ref, start, col_phase)
 
 
-def prepare(paired, own_ref, w_half_ref, w_conv_ref, x_ref, w_ref, kernel_ref, other_ref, *scratch):
-    halves_ref, v_ref, wide_ref, raw_ref, sems = scratch
+def prepare_rows(paired, own_ref, x_ref, wide_ref, raw_ref, sem):
+    copy = pltpu.make_async_copy(own_ref, raw_ref, sem)
+    copy.start()
+    copy.wait()
+    if paired:
+        c = lax.axis_index("ch")
+        chans, rows, cols = own_ref.shape
+        wide_ref[...] = raw_ref[...].astype(jnp.float32).reshape(chans * rows, cols)
+        share = x_ref.shape[1] - 1
+        for place in range(share):
+            value = wide_ref[pl.ds(place + c * (rows - share), chans, stride=rows), :]
+            store_row(x_ref, place + 1 - c, c * chans, value)
+    else:
+        for slot in range(own_ref.shape[0]):
+            store_row(x_ref, slot, 0, raw_ref[slot].astype(jnp.float32))
+
+
+def prepare_kernels(paired, w_half_ref, w_conv_ref, w_ref, kernel_ref, other_ref, halves_ref, v_ref, sems):
     s, c = lax.axis_index("space"), lax.axis_index("ch")
     skipped = (w_half_ref.shape[0] - 32) // 2
     copies = [
         pltpu.make_async_copy(w_conv_ref, v_ref, sems.at[0]),
-        pltpu.make_async_copy(own_ref, raw_ref, sems.at[1]),
-        pltpu.make_async_copy(w_half_ref.at[pl.ds(skipped, 32)], w_ref, sems.at[2]),
+        pltpu.make_async_copy(w_half_ref.at[pl.ds(skipped, 32)], w_ref, sems.at[1]),
     ]
     for copy in copies:
         copy.start()
@@ -169,17 +184,6 @@
         moved = jnp.dot(halves_ref[1 - half, :, columns], matrix, preferred_element_type=jnp.float32)
         other_ref[:, columns] = moved.astype(jnp.bfloat16)
     copies[1].wait()
-    if paired:
-        chans, rows, cols = own_ref.shape
-        wide_ref[...] = raw_ref[...].astype(jnp.float32).reshape(chans * rows, cols)
-        share = x_ref.shape[1] - 1
-        for place in range(share):
-            value = wide_ref[pl.ds(place + c * (rows - share), chans, stride=rows), :]
-            store_row(x_ref, place + 1 - c, c * chans, value)
-    else:
-        for slot in range(own_ref.shape[0]):
-            store_row(x_ref, slot, 0, raw_ref[slot].astype(jnp.float32))
-    copies[2].wait()
 
 
 def paired_first(peer_ref, near_ref, far_ref, started_ref, *refs):
@@ -306,29 +310,43 @@
     return pl.CostEstimate(flops=flops, bytes_accessed=8 * 2**20, transcendentals=0)
 
 
-def call_prepare(paired, own, w_half, w_conv, sizes):
+def call_rows(paired, own, sizes):
     cin, cout, rows, cols = sizes
     wide = own.shape[0] * own.shape[1] if paired else 8
     return pl.pallas_call(
-        functools.partial(prepare, paired),
+        functools.partial(prepare_rows, paired),
+        out_shape=jax.ShapeDtypeStruct((3, rows // 2 + 2, cin, cols), jnp.bfloat16),
+        in_specs=[ANY],
+        out_specs=VMEM,
+        scratch_shapes=[
+            pltpu.VMEM((wide, cols), jnp.float32),
+            pltpu.VMEM(own.shape, jnp.bfloat16),
+            pltpu.SemaphoreType.DMA,
+        ],
+        cost_estimate=pl.CostEstimate(flops=2**20, bytes_accessed=2 * 2**20, transcendentals=0),
+        compiler_params=pltpu.CompilerParams(vmem_limit_bytes=LIMIT),
+    )(in_hbm(own))
+
+
+def call_kernels(paired, w_half, w_conv, sizes):
+    cin, cout, rows, cols = sizes
+    return pl.pallas_call(
+        functools.partial(prepare_kernels, paired),
         out_shape=(
-            jax.ShapeDtypeStruct((3, rows // 2 + 2, cin, cols), jnp.bfloat16),
             jax.ShapeDtypeStruct((32, cout // 2, cin), jnp.bfloat16),
             jax.ShapeDtypeStruct((2 * cout, 9 * cout), jnp.bfloat16),
             jax.ShapeDtypeStruct((2 * cout, 9 * cout), jnp.bfloat16),
         ),
-        in_specs=[ANY] * 3,
-        out_specs=(VMEM,) * 4,
+        in_specs=[ANY] * 2,
+        out_specs=(VMEM,) * 3,
         scratch_shapes=[
             pltpu.VMEM((2, 2 * cout, 9 * cout), jnp.bfloat16),
             pltpu.VMEM((27, cout, cout), jnp.bfloat16),
-            pltpu.VMEM((wide, cols), jnp.float32),
-            pltpu.VMEM(own.shape, jnp.bfloat16),
-            pltpu.SemaphoreType.DMA((3,)),
-        ],
-        cost_estimate=pl.CostEstimate(flops=2 * 18 * 256 * cout * cout, bytes_accessed=8 * 2**20, transcendentals=0),
+            pltpu.SemaphoreType.DMA((2,)),
+        ],
+        cost_estimate=pl.CostEstimate(flops=2 * 18 * 256 * cout * cout, bytes_accessed=6 * 2**20, transcendentals=0),
         compiler_params=pltpu.CompilerParams(vmem_limit_bytes=LIMIT),
-    )(in_hbm(own), in_hbm(w_half), in_hbm(w_conv))
+    )(in_hbm(w_half), in_hbm(w_conv))
 
 
 def call_first(body, rows_in, prepared, b_up, sizes):
@@ -390,13 +408,15 @@
 
     own = inputs.reshape(chans, held, cols)
     near, far, peer, w_a, w_b = call_pieces(own, w_up)
-    far = lax.ppermute(far, AXES, outer)
-    far, peer, w_a, w_b, near, w_conv = lax.optimization_barrier((far, peer, w_a, w_b, near, w_conv))
+    own, w_conv, peer, w_a, far, near, w_b = lax.optimization_barrier((own, w_conv, peer, w_a, far, near, w_b))
     peer = lax.ppermute(peer, AXES, across)
     w_a = lax.ppermute(w_a, AXES, across)
+    far = lax.ppermute(far, AXES, outer)
+    near = lax.ppermute(near, AXES, chain)
+    x = call_rows(True, own, sizes)
+    x, w_b, w_conv, near, far = lax.optimization_barrier((x, w_b, w_conv, near, far))
     w_b = lax.ppermute(w_b, AXES, across)
-    near = lax.ppermute(near, AXES, chain)
-    x, w_half, kernel, other = call_prepare(True, own, w_up, w_conv, sizes)
+    w_half, kernel, other = call_kernels(True, w_up, w_conv, sizes)
     w_ax = lax.ppermute(w_a, AXES, pairs)
     w_ac = lax.ppermute(w_a, AXES, cores)
     biases = (b_up[None], b_conv[None])
@@ -422,7 +442,8 @@
     share = inputs.shape[2] // chs
     rows = lax.dynamic_slice_in_dim(rows, c * share, share + 2, 0)
     biases = (b_up[None], b_conv[None])
-    *prepared, other = call_prepare(False, rows, w_all[:, :part], w_conv, sizes)
+    *prepared, other = call_kernels(False, w_all[:, :part], w_conv, sizes)
+    prepared = (call_rows(False, rows, sizes), *prepared)
     results = (*call_first(gathered_first, (), prepared, biases[0], sizes), other)
     return call_second(False, (w_all[:16, part:], w_all[16:, part:]), results, biases, sizes)
 

time: 29.6 us -> 27.8 us (0.939); the launches traced: 29 us -> 27.6 us
  waiting for transfers between devices: 3.15 us -> 1.23 us
  Pallas kernels: 10.4 us -> 11.4 us
  starting transfers between devices: 15.4 us -> 14.8 us
    ppermute x1, starting transfers between devices: 7.52 us -> 3.03 us  [paired(): peer = lax.ppermute(peer, AXES, across)]
    ppermute x1, starting transfers between devices: 1.99 us -> 5.72 us  [paired(): w_b = lax.ppermute(w_b, AXES, across)]
    ppermute x1, starting transfers between devices: 0.01 us -> 1.71 us  [paired(): w_ac = lax.ppermute(w_a, AXES, cores)]
    ppermute x1, waiting for transfers between devices: 1.71 us -> 0.01 us  [paired(): w_a = lax.ppermute(w_a, AXES, across)]
    ppermute x1, starting transfers between devices: 2.86 us -> 1.61 us  [paired(): w_ax = lax.ppermute(w_a, AXES, pairs)]
    pallas_call x1 -> x2, Pallas kernels: 2.27 us -> 3.22 us  [the longest x1 2.02 us: call_kernels(): pl.pallas_call(functools.partial(prepare_kernels, paired), out_shape=(jax...]
    ppermute x1, starting transfers between devices: 1.8 us -> 1.45 us  [paired(): near = lax.ppermute(near, AXES, chain)]
    ppermute x1, starting transfers between devices: 0.12 us -> 0.44 us  [paired(): w_axc = lax.ppermute(w_ax, AXES, cores)]
  transfers between devices with their start and end apart: 9 -> 9, of which waited for: 3 -> 1; matrix products, arithmetic and copies ran while one was open for 0% -> 0% of each run, Pallas kernels for 17% -> 22%
where the time goes in v9:
time: 27.8 us; the launch traced here: 27.6 us
  starting transfers between devices  14.8 us (53%)
  Pallas kernels  11.4 us (41%)
  waiting for transfers between devices  1.23 us (4%)
    ppermute x1, starting transfers between devices, paired(): w_b = lax.ppermute(w_b, AXES, across)  5.72 us
    pallas_call x1, Pallas kernels, call_second(): pl.pallas_call(functools.partial(second, paired, len(parts)), out_shape=j...  4.27 us
    ppermute x1, starting transfers between devices, paired(): peer = lax.ppermute(peer, AXES, across)  3.03 us
    pallas_call x1, Pallas kernels, call_first(): pl.pallas_call(body, out_shape=(jax.ShapeDtypeStruct(started.shape, jnp.b...  2.77 us
    pallas_call x1, Pallas kernels, call_kernels(): pl.pallas_call(functools.partial(prepare_kernels, paired), out_shape=(jax...  2.02 us
    ppermute x1, starting transfers between devices, paired(): w_ac = lax.ppermute(w_a, AXES, cores)  1.71 us
    ppermute x1, starting transfers between devices, paired(): w_ax = lax.ppermute(w_a, AXES, pairs)  1.61 us
    ppermute x1, starting transfers between devices, paired(): near = lax.ppermute(near, AXES, chain)  1.45 us
  transfers between devices with their start and end apart: 9, of which 1 were waited for; matrix products, arithmetic and copies ran while one was open for 0% of the time, Pallas kernels for 22%

profile of v9, /device:TPU:0, one launch (start us, length us, event | category | flops | bytes accessed | tf_op | source)
XLA Modules:
  0.0 27.6 jit_solution(10154039801104233578)
XLA Ops:
  0.0 1.1 %shard_map.55 = (bf16[128,128]{1,0:T(8,128)(2,1)S(1)}, bf16[128,128]{1,0:T(8,128)(2,1)S(1)}, bf16[5,128,128]{2,1,0:T(8,128)(2,1)S(1)}, bf16[16,16,256]{2,1,0:T(8,128)(2,1)S(1)}, bf16[16,32,256]{2,1,0:T(8,128)(2,1)S(1)}) custom-call(bf16[128,8,128]{2,1,0:T(8,128)(2,1)} %bitcast.6, bf16[64,64,256]{2,1,0:T(8,128)(2,1)} %w_half_ref.1), custom_call_target="tpu_custom_call" | custom-call | tf_op jit(solution)/shard_map/pallas_call | solution.py:283
  1.1 0.0 copy-start
  1.1 3.0 %collective-permute-start.6 = (bf16[5,128,128]{2,1,0:T(8,128)(2,1)S(1)}, bf16[5,128,128]{2,1,0:T(8,128)(2,1)S(1)}, u32[]{:S(2)}, u32[]{:S(2)}) collective-permute-start(bf16[5,128,128]{2,1,0:T(8,128)(2,1)S(1)} %get-tuple-element.45), channel_id=1, source_target_pairs={{0,1},{1,0},{2,3},{3,2},{4,5},{5,4},{6,7},{7,6},{8,9},{9,8},{10,11... | collective-permute-start | bytes 491528 | tf_op jit(solution)/shard_map/ppermute | solution.py:412
  4.2 0.1 collective-permute-start
  4.2 1.4 %collective-permute-start.1 = (bf16[128,128]{1,0:T(8,128)(2,1)S(1)}, bf16[128,128]{1,0:T(8,128)(2,1)S(1)}, u32[]{:S(2)}, u32[]{:S(2)}) collective-permute-start(bf16[128,128]{1,0:T(8,128)(2,1)S(1)} %get-tuple-element.42), channel_id=1, source_target_pairs={{0,2},{2,4},{4,6},{6,8},{8,10},{10,12},{12,14},{14,16},{16,18},{18... | collective-permute-start | bytes 98312 | tf_op jit(solution)/shard_map/ppermute | solution.py:415
  5.7 0.7 %collective-permute-start.2 = (bf16[128,128]{1,0:T(8,128)(2,1)S(1)}, bf16[128,128]{1,0:T(8,128)(2,1)S(1)}, u32[]{:S(2)}, u32[]{:S(2)}) collective-permute-start(bf16[128,128]{1,0:T(8,128)(2,1)S(1)} %get-tuple-element.43), channel_id=1, source_target_pairs={{1,2},{3,4},{5,6},{7,8},{9,10},{11,12},{13,14},{15,16},{17,18},{19... | collective-permute-start | bytes 98312 | tf_op jit(solution)/shard_map/ppermute | solution.py:414
  6.4 1.2 %shard_map.56.started_ref = bf16[3,6,256,128]{3,2,1,0:T(8,128)(2,1)S(1)} custom-call(bf16[128,8,128]{2,1,0:T(8,128)(2,1)} %bitcast.7), custom_call_target="tpu_custom_call" | custom-call | flops 1048576 | bytes 2097152 | tf_op jit(solution)/shard_map/pallas_call | solution.py:316
  7.6 0.0 collective-permute-done.1.near_ref
  7.6 0.0 collective-permute-done.2.far_ref
  7.6 5.7 %collective-permute-start.3 = (bf16[16,32,256]{2,1,0:T(8,128)(2,1)S(1)}, bf16[16,32,256]{2,1,0:T(8,128)(2,1)S(1)}, u32[]{:S(2)}, u32[]{:S(2)}) collective-permute-start(bf16[16,32,256]{2,1,0:T(8,128)(2,1)S(1)} %get-tuple-element.44), channel_id=1, source_target_pairs={{0,1},{1,0},{2,3},{3,2},{4,5},{5,4},{6,7},{7,6},{8,9},{9,8},{10,11... | collective-permute-start | bytes 786440 | tf_op jit(solution)/shard_map/ppermute | solution.py:418
  13.3 2.0 %shard_map.57 = (bf16[32,64,256]{2,1,0:T(8,128)(2,1)S(1)}, bf16[256,1152]{1,0:T(8,128)(2,1)S(1)}, bf16[256,1152]{1,0:T(8,128)(2,1)S(1)}) custom-call(bf16[64,64,256]{2,1,0:T(8,128)(2,1)} %w_half_ref.1, bf16[27,128,128]{2,1,0:T(8,128)(2,1)} %w_conv_ref), custom_call_target="tpu_custom_call" | custom-call | flops 150994944 | bytes 6291456 | tf_op jit(solution)/shard_map/pallas_call | solution.py:333
  15.4 0.0 collective-permute-done.refs_0_
  15.4 1.6 %collective-permute-start.4 = (bf16[16,16,256]{2,1,0:T(8,128)(2,1)S(1)}, bf16[16,16,256]{2,1,0:T(8,128)(2,1)S(1)}, u32[]{:S(2)}, u32[]{:S(2)}) collective-permute-start(bf16[16,16,256]{2,1,0:T(8,128)(2,1)S(1)} %collective-permute-done.refs_0_), channel_id=1, source_target_pairs={{0,4},{1,5},{2,6},{3,7},{4,0},{5,1},{6,2},{7,3},{8,12},{9,13},{10,... | collective-permute-start | bytes 393224 | tf_op jit(solution)/shard_map/ppermute | solution.py:420
  17.0 1.7 %collective-permute-start.5 = (bf16[16,16,256]{2,1,0:T(8,128)(2,1)S(1)}, bf16[16,16,256]{2,1,0:T(8,128)(2,1)S(1)}, u32[]{:S(2)}, u32[]{:S(2)}) collective-permute-start(bf16[16,16,256]{2,1,0:T(8,128)(2,1)S(1)} %collective-permute-done.refs_0_), channel_id=1, source_target_pairs={{0,2},{1,3},{2,0},{3,1},{4,6},{5,7},{6,4},{7,5},{8,10},{9,11},{10,... | collective-permute-start | bytes 393224 | tf_op jit(solution)/shard_map/ppermute | solution.py:421
  18.7 0.0 collective-permute-done.6.peer_ref
  18.7 0.0 copy-done
  18.7 0.0 copy-start.1
  18.7 2.8 %shard_map.58 = (bf16[3,6,256,128]{3,2,1,0:T(8,128)(2,1)S(1)}, f32[2,256,1024]{2,1,0:T(8,128)S(1)}) custom-call(bf16[5,128,128]{2,1,0:T(8,128)(2,1)S(1)} %collective-permute-done.6.peer_ref, bf16[128,128]{1,0:T(8,128)(2,1)S(1)} %collective-permute-done.1.near_ref, ...), custom_call_target="tpu_custom_call", output_to_operand_aliasing={{0}: (3, {})} | custom-call | flops 1879048192 | bytes 8388608 | tf_op jit(solution)/shard_map/pallas_call | solution.py:355
  21.5 0.0 collective-permute-done.4.refs_2_
  21.5 0.0 collective-permute-done.5.refs_1_
  21.5 0.0 collective-permute-done.3.refs_4_
  21.5 0.1 collective-permute-start.8
  21.6 0.4 %collective-permute-start.7 = (bf16[16,16,256]{2,1,0:T(8,128)(2,1)S(1)}, bf16[16,16,256]{2,1,0:T(8,128)(2,1)S(1)}, u32[]{:S(2)}, u32[]{:S(2)}) collective-permute-start(bf16[16,16,256]{2,1,0:T(8,128)(2,1)S(1)} %collective-permute-done.4.refs_2_), channel_id=1, source_target_pairs={{0,2},{1,3},{2,0},{3,1},{4,6},{5,7},{6,4},{7,5},{8,10},{9,11},{10,... | collective-permute-start | bytes 393224 | tf_op jit(solution)/shard_map/ppermute | solution.py:427
  22.1 1.2 %collective-permute-done.7.refs_3_ = bf16[16,16,256]{2,1,0:T(8,128)(2,1)S(1)} collective-permute-done((bf16[16,16,256]{2,1,0:T(8,128)(2,1)S(1)}, bf16[16,16,256]{2,1,0:T(8,128)(2,1)S(1)}, u32[]{:S(2)}, u32[]{:S(2)}) %collective-permute-start.7) | collective-permute-done | bytes 131104 | tf_op jit(solution)/shard_map/ppermute | solution.py:427
  23.3 0.0 collective-permute-done.8.refs_5_
  23.3 0.0 copy-done.1
  23.3 4.3 %shard_map.59 = bf16[128,2,8,256]{3,2,1,0:T(8,128)(2,1)} custom-call(bf16[16,16,256]{2,1,0:T(8,128)(2,1)S(1)} %collective-permute-done.refs_0_, bf16[16,16,256]{2,1,0:T(8,128)(2,1)S(1)} %collective-permute-done.5.refs_1_, bf16[16,16,256]{2,1,0:T(8,128)(2,1)S(1)} %collective-permute-done.4.refs_2_, bf16[16,16,256]{2,1,0:T(8,128)(2,1)S(1)} %collective-permute-done.7.refs_3_, ...), custom_call_target="tpu_custom_call" | custom-call | flops 1879048192 | bytes 8388608 | tf_op jit(solution)/shard_map/pallas_call | solution.py:375
Async XLA Ops:
  1.1 17.6 %copy-start = (f32[128]{0:T(128)S(1)}, f32[128]{0:T(128)}, u32[]{:S(2)}) copy-start(f32[128]{0:T(128)} %param.7) | copy-start | bytes 1540
  1.1 17.5 %collective-permute-start.6 = (bf16[5,128,128]{2,1,0:T(8,128)(2,1)S(1)}, bf16[5,128,128]{2,1,0:T(8,128)(2,1)S(1)}, u32[]{:S(2)}, u32[]{:S(2)}) collective-permute-start(bf16[5,128,128]{2,1,0:T(8,128)(2,1)S(1)} %get-tuple-element.45), channel_id=1, source_target_pairs={{0,1},{1,0},{2,3},{3,2},{4,5},{5,4},{6,7},{7,6},{8,9},{9,8},{10,11... | collective-permute-start | bytes 491528 | tf_op jit(solution)/shard_map/ppermute | solution.py:412
  4.2 11.2 %collective-permute-start = (bf16[16,16,256]{2,1,0:T(8,128)(2,1)S(1)}, bf16[16,16,256]{2,1,0:T(8,128)(2,1)S(1)}, u32[]{:S(2)}, u32[]{:S(2)}) collective-permute-start(bf16[16,16,256]{2,1,0:T(8,128)(2,1)S(1)} %get-tuple-element.38), channel_id=1, source_target_pairs={{0,1},{1,0},{2,3},{3,2},{4,5},{5,4},{6,7},{7,6},{8,9},{9,8},{10,11... | collective-permute-start | bytes 393224 | tf_op jit(solution)/shard_map/ppermute | solution.py:413
  4.2 3.3 %collective-permute-start.1 = (bf16[128,128]{1,0:T(8,128)(2,1)S(1)}, bf16[128,128]{1,0:T(8,128)(2,1)S(1)}, u32[]{:S(2)}, u32[]{:S(2)}) collective-permute-start(bf16[128,128]{1,0:T(8,128)(2,1)S(1)} %get-tuple-element.42), channel_id=1, source_target_pairs={{0,2},{2,4},{4,6},{6,8},{8,10},{10,12},{12,14},{14,16},{16,18},{18... | collective-permute-start | bytes 98312 | tf_op jit(solution)/shard_map/ppermute | solution.py:415
  5.7 1.9 %collective-permute-start.2 = (bf16[128,128]{1,0:T(8,128)(2,1)S(1)}, bf16[128,128]{1,0:T(8,128)(2,1)S(1)}, u32[]{:S(2)}, u32[]{:S(2)}) collective-permute-start(bf16[128,128]{1,0:T(8,128)(2,1)S(1)} %get-tuple-element.43), channel_id=1, source_target_pairs={{1,2},{3,4},{5,6},{7,8},{9,10},{11,12},{13,14},{15,16},{17,18},{19... | collective-permute-start | bytes 98312 | tf_op jit(solution)/shard_map/ppermute | solution.py:414
  7.6 13.9 %collective-permute-start.3 = (bf16[16,32,256]{2,1,0:T(8,128)(2,1)S(1)}, bf16[16,32,256]{2,1,0:T(8,128)(2,1)S(1)}, u32[]{:S(2)}, u32[]{:S(2)}) collective-permute-start(bf16[16,32,256]{2,1,0:T(8,128)(2,1)S(1)} %get-tuple-element.44), channel_id=1, source_target_pairs={{0,1},{1,0},{2,3},{3,2},{4,5},{5,4},{6,7},{7,6},{8,9},{9,8},{10,11... | collective-permute-start | bytes 786440 | tf_op jit(solution)/shard_map/ppermute | solution.py:418
  15.4 6.1 %collective-permute-start.4 = (bf16[16,16,256]{2,1,0:T(8,128)(2,1)S(1)}, bf16[16,16,256]{2,1,0:T(8,128)(2,1)S(1)}, u32[]{:S(2)}, u32[]{:S(2)}) collective-permute-start(bf16[16,16,256]{2,1,0:T(8,128)(2,1)S(1)} %collective-permute-done.refs_0_), channel_id=1, source_target_pairs={{0,4},{1,5},{2,6},{3,7},{4,0},{5,1},{6,2},{7,3},{8,12},{9,13},{10,... | collective-permute-start | bytes 393224 | tf_op jit(solution)/shard_map/ppermute | solution.py:420
  17.0 4.5 %collective-permute-start.5 = (bf16[16,16,256]{2,1,0:T(8,128)(2,1)S(1)}, bf16[16,16,256]{2,1,0:T(8,128)(2,1)S(1)}, u32[]{:S(2)}, u32[]{:S(2)}) collective-permute-start(bf16[16,16,256]{2,1,0:T(8,128)(2,1)S(1)} %collective-permute-done.refs_0_), channel_id=1, source_target_pairs={{0,2},{1,3},{2,0},{3,1},{4,6},{5,7},{6,4},{7,5},{8,10},{9,11},{10,... | collective-permute-start | bytes 393224 | tf_op jit(solution)/shard_map/ppermute | solution.py:421
  18.7 4.6 %copy-start.1 = (f32[128]{0:T(128)S(1)}, f32[128]{0:T(128)}, u32[]{:S(2)}) copy-start(f32[128]{0:T(128)} %param.9) | copy-start | bytes 1540
  21.5 1.8 %collective-permute-start.8 = (bf16[16,32,256]{2,1,0:T(8,128)(2,1)S(1)}, bf16[16,32,256]{2,1,0:T(8,128)(2,1)S(1)}, u32[]{:S(2)}, u32[]{:S(2)}) collective-permute-start(bf16[16,32,256]{2,1,0:T(8,128)(2,1)S(1)} %collective-permute-done.3.refs_4_), channel_id=1, source_target_pairs={{0,2},{1,3},{2,0},{3,1},{4,6},{5,7},{6,4},{7,5},{8,10},{9,11},{10,... | collective-permute-start | bytes 786440 | tf_op jit(solution)/shard_map/ppermute | solution.py:426
  21.6 1.7 %collective-permute-start.7 = (bf16[16,16,256]{2,1,0:T(8,128)(2,1)S(1)}, bf16[16,16,256]{2,1,0:T(8,128)(2,1)S(1)}, u32[]{:S(2)}, u32[]{:S(2)}) collective-permute-start(bf16[16,16,256]{2,1,0:T(8,128)(2,1)S(1)} %collective-permute-done.4.refs_2_), channel_id=1, source_target_pairs={{0,2},{1,3},{2,0},{3,1},{4,6},{5,7},{6,4},{7,5},{8,10},{9,11},{10,... | collective-permute-start | bytes 393224 | tf_op jit(solution)/shard_map/ppermute | solution.py:427

commit v10 on v9

--- a/solution.py
+++ b/solution.py
@@ -27,7 +27,7 @@
     return jnp.where(place == edge, 0.0, pltpu.roll(value, step % cols, 1))
 
 
-def upsample(x_ref, tap_of, bias, u_ref, first, last):
+def upsample(cell, tap_of, bias, u_ref, first, last):
     held, cols = u_ref.shape[1], u_ref.shape[3]
     for row_phase in (0, 1):
         for col_phase in (0, 1):
@@ -41,7 +41,7 @@
                 places = range(start, min(start + 2, held // 2))
                 cells = jnp.concatenate(
                     [
-                        jnp.concatenate([x_ref[copy, slot + place] for place in places], axis=1)
+                        jnp.concatenate([cell(copy, slot + place) for place in places], axis=1)
                         for _, slot, copy in taps
                     ],
                     axis=0,
@@ -106,21 +106,21 @@
     x_ref[2, slot, where] = shifted(value, 1).astype(jnp.bfloat16)
 
 
-def arrival(x_core, part):
-    if x_core is None:
+def arrival(x, part):
+    if x is None:
         return [[(0, part)], [(0, part)]]
     quarter, half = part // 4, part // 2
     return [
-        [((x_core ^ number) * quarter, quarter) for number in range(4)],
-        [((lax.rem(x_core, 2) ^ number) * half, half) for number in (0, 1)],
+        [(x * half, half), ((1 - x) * half, half)],
+        [(x * quarter, quarter), ((1 - x) * quarter, quarter), (half, half)],
     ]
 
 
-def arrange(x_core, part):
+def arrange(x, part):
     source = lax.broadcasted_iota(jnp.int32, (2 * part, 2 * part), 0)
     target = lax.broadcasted_iota(jnp.int32, (2 * part, 2 * part), 1)
     wanted = jnp.zeros_like(target)
-    for plane, blocks in enumerate(arrival(x_core, part)):
+    for plane, blocks in enumerate(arrival(x, part)):
         place = plane * part
         for first, size in blocks:
             inside = (target >= place) & (target < place + size)
@@ -140,7 +140,7 @@
         return jnp.concatenate([w_half_ref[tap], w_half_ref[16 + tap]], axis=0)
 
     bias = bias_of(b_up_ref, column_ref, [(half * part, part)] * 2)
-    upsample(x_ref, tap_of, bias, u_ref, *ends(s, c))
+    upsample(lambda copy, slot: x_ref[copy, slot], tap_of, bias, u_ref, *ends(s, c))
     kernel = kernel_ref[...]
     for start in range(0, u_ref.shape[1] - 2, 2):
         for col_phase in (0, 1):
@@ -174,11 +174,11 @@
     for copy in copies:
         copy.start()
     cout = w_conv_ref.shape[1]
-    half, x_core = (c, lax.rem(s, 4)) if paired else (0, None)
+    half, x = (c, lax.rem(s, 4) // 2) if paired else (0, None)
     copies[0].wait()
     split_kernels(v_ref, halves_ref)
     kernel_ref[...] = halves_ref[half]
-    matrix = arrange(x_core, cout // 2)
+    matrix = arrange(x, cout // 2)
     for number in range(9):
         columns = pl.ds(number * cout, cout)
         moved = jnp.dot(halves_ref[1 - half, :, columns], matrix, preferred_element_type=jnp.float32)
@@ -209,15 +209,34 @@
     s, c = lax.axis_index("space"), lax.axis_index("ch")
     cout, _, rows, _ = out_ref.shape
     part = cout // 2
-    half, x_core = (1 - c, lax.rem(s, 4)) if paired else (1, None)
+    half, x = (1 - c, lax.rem(s, 4) // 2) if paired else (1, None)
     cols = x_ref.shape[3]
-
-    def tap_of(tap):
-        return jnp.concatenate([part_ref[tap] for part_ref in parts], axis=0)
-
-    blocks = [(half * part + at, size) for plane in arrival(x_core, part) for at, size in plane]
+    if paired:
+        chans = x_ref.shape[2] // 2
+        core = lax.rem(s, 2)
+        sides = [pl.ds(pl.multiple_of(side * chans, 16), chans) for side in (core, 1 - core)]
+        big = part // 2
+
+        def tap_of(tap):
+            columns = []
+            for near_ref, far_ref, rest_ref in (parts[:3], parts[3:]):
+                rows = [near_ref[tap, :big], far_ref[tap, :big], near_ref[tap, big:], far_ref[tap, big:], rest_ref[tap]]
+                columns.append(jnp.concatenate(rows, axis=0))
+            return jnp.concatenate(columns, axis=1)
+
+        def cell(copy, slot):
+            return jnp.concatenate([x_ref[copy, slot, side] for side in sides], axis=0)
+    else:
+
+        def tap_of(tap):
+            return jnp.concatenate([part_ref[tap] for part_ref in parts], axis=0)
+
+        def cell(copy, slot):
+            return x_ref[copy, slot]
+
+    blocks = [(half * part + at, size) for plane in arrival(x, part) for at, size in plane]
     bias = bias_of(b_up_ref, column_ref, blocks)
-    upsample(x_ref, tap_of, bias, u_ref, *ends(s, c))
+    upsample(cell, tap_of, bias, u_ref, *ends(s, c))
     source = lax.broadcasted_iota(jnp.int32, (2 * cols, 2 * cols), 0)
     target = lax.broadcasted_iota(jnp.int32, (2 * cols, 2 * cols), 1)
     wanted = jnp.where(source < cols, 2 * source, 2 * (source - cols) + 1)
@@ -254,14 +273,22 @@
 
 def pieces(own_ref, w_up_ref, near_ref, far_ref, peer_ref, w_a_ref, w_b_ref, wide_ref, raw_ref, sems):
     s, c = lax.axis_index("space"), lax.axis_index("ch")
-    raw = pltpu.make_async_copy(own_ref, raw_ref, sems.at[2])
+    raw = pltpu.make_async_copy(own_ref, raw_ref, sems.at[3])
     raw.start()
-    firsts = [block[0] for plane in arrival(lax.rem(s, 4), w_up_ref.shape[1]) for block in plane[:1]]
+    me = lax.rem(s, 4)
+    part, lanes = w_up_ref.shape[1], w_a_ref.shape[2]
+    side = pl.ds(pl.multiple_of(lax.rem(me, 2) * lanes, lanes), lanes)
+    (first, big), = arrival(me // 2, part)[0][:1]
+    (second, small), _, (third, rest) = arrival(me // 2, part)[1]
+    cuts = (
+        (16, first, big, w_a_ref.at[:, pl.ds(0, big)]),
+        (32, second, small, w_a_ref.at[:, pl.ds(big, small)]),
+        (32, third, rest, w_b_ref),
+    )
     copies = []
-    for plane, piece_ref in enumerate((w_a_ref, w_b_ref)):
-        channels = pl.ds(pl.multiple_of(firsts[plane], 16), piece_ref.shape[1])
-        source = w_up_ref.at[pl.ds(16 + 16 * plane, 16), channels]
-        copies.append(pltpu.make_async_copy(source, piece_ref, sems.at[plane]))
+    for number, (tap, channel, count, place) in enumerate(cuts):
+        source = w_up_ref.at[pl.ds(tap, 16), pl.ds(pl.multiple_of(channel, 16), count), side]
+        copies.append(pltpu.make_async_copy(source, place, sems.at[number]))
         copies[-1].start()
     chans, rows, cols = own_ref.shape
     raw.wait()
@@ -286,15 +313,15 @@
             jax.ShapeDtypeStruct((chans, cols), jnp.bfloat16),
             jax.ShapeDtypeStruct((chans, cols), jnp.bfloat16),
             jax.ShapeDtypeStruct((rows // 2 + 1, chans, cols), jnp.bfloat16),
-            jax.ShapeDtypeStruct((16, part // 4, cin), jnp.bfloat16),
-            jax.ShapeDtypeStruct((16, part // 2, cin), jnp.bfloat16),
+            jax.ShapeDtypeStruct((16, 3 * part // 4, cin // 2), jnp.bfloat16),
+            jax.ShapeDtypeStruct((16, part // 2, cin // 2), jnp.bfloat16),
         ),
         in_specs=[ANY, ANY],
         out_specs=(VMEM,) * 5,
         scratch_shapes=[
             pltpu.VMEM((chans * rows, cols), jnp.float32),
             pltpu.VMEM((chans, rows, cols), jnp.bfloat16),
-            pltpu.SemaphoreType.DMA((3,)),
+            pltpu.SemaphoreType.DMA((4,)),
         ],
         compiler_params=pltpu.CompilerParams(vmem_limit_bytes=LIMIT),
     )(in_hbm(own), in_hbm(w_up))
@@ -414,7 +441,7 @@
     far = lax.ppermute(far, AXES, outer)
     near = lax.ppermute(near, AXES, chain)
     x = call_rows(True, own, sizes)
-    x, w_b, w_conv, near, far = lax.optimization_barrier((x, w_b, w_conv, near, far))
+    x, w_a, w_b, w_conv, near, far = lax.optimization_barrier((x, w_a, w_b, w_conv, near, far))
     w_b = lax.ppermute(w_b, AXES, across)
     w_half, kernel, other = call_kernels(True, w_up, w_conv, sizes)
     w_ax = lax.ppermute(w_a, AXES, pairs)
@@ -425,7 +452,7 @@
     w_b, w_ax, w_ac, *results = lax.optimization_barrier((w_b, w_ax, w_ac, *results))
     w_bc = lax.ppermute(w_b, AXES, cores)
     w_axc = lax.ppermute(w_ax, AXES, cores)
-    return call_second(True, (w_a, w_ac, w_ax, w_axc, w_b, w_bc), results, biases, sizes)
+    return call_second(True, (w_a, w_ax, w_b, w_ac, w_axc, w_bc), results, biases, sizes)
 
 
 def gathered(inputs, w_up, b_up, w_conv, b_conv, sizes):

time: 27.8 us -> 27.9 us (level)
  waiting for transfers between devices: 1.23 us -> 3.43 us
  starting transfers between devices: 14.8 us -> 12.7 us
    ppermute x1, starting transfers between devices: 5.72 us -> 2.16 us  [paired(): w_b = lax.ppermute(w_b, AXES, across)]
    ppermute x1, starting transfers between devices: 0.08 us -> 3.03 us  [paired(): w_a = lax.ppermute(w_a, AXES, across)]
    ppermute x1, starting transfers between devices: 3.03 us -> 0.08 us  [paired(): peer = lax.ppermute(peer, AXES, across)]
    ppermute x1, starting transfers between devices: 1.61 us -> 4.43 us  [paired(): w_ax = lax.ppermute(w_a, AXES, pairs)]
    ppermute x1, waiting for transfers between devices: 0.01 us -> 2.3 us  [paired(): w_a = lax.ppermute(w_a, AXES, across)]
    ppermute x1, starting transfers between devices: 1.71 us -> 0.37 us  [paired(): w_ac = lax.ppermute(w_a, AXES, cores)]
    ppermute x1, waiting for transfers between devices: 1.21 us -> 0.01 us  [paired(): w_axc = lax.ppermute(w_ax, AXES, cores)]
    ppermute x1, waiting for transfers between devices: 0.01 us -> 1.12 us  [paired(): w_bc = lax.ppermute(w_b, AXES, cores)]
  transfers between devices with their start and end apart: 9 -> 9, of which waited for: 1 -> 2; matrix products, arithmetic and copies ran while one was open for 0% -> 0% of each run, Pallas kernels for 22% -> 22%
where the time goes in v10:
time: 27.9 us; the launch traced here: 27.7 us
  starting transfers between devices  12.7 us (46%)
  Pallas kernels  11.4 us (41%)
  waiting for transfers between devices  3.43 us (12%)
    ppermute x1, starting transfers between devices, paired(): w_ax = lax.ppermute(w_a, AXES, pairs)  4.43 us
    pallas_call x1, Pallas kernels, call_second(): pl.pallas_call(functools.partial(second, paired, len(parts)), out_shape=j...  4.25 us
    ppermute x1, starting transfers between devices, paired(): w_a = lax.ppermute(w_a, AXES, across)  3.03 us
    pallas_call x1, Pallas kernels, call_first(): pl.pallas_call(body, out_shape=(jax.ShapeDtypeStruct(started.shape, jnp.b...  2.77 us
    ppermute x1, waiting for transfers between devices, paired(): w_a = lax.ppermute(w_a, AXES, across)  2.3 us
    ppermute x1, starting transfers between devices, paired(): w_b = lax.ppermute(w_b, AXES, across)  2.16 us
    pallas_call x1, Pallas kernels, call_kernels(): pl.pallas_call(functools.partial(prepare_kernels, paired), out_shape=(jax...  2.02 us
    ppermute x1, starting transfers between devices, paired(): near = lax.ppermute(near, AXES, chain)  1.45 us
  transfers between devices with their start and end apart: 9, of which 2 were waited for; matrix products, arithmetic and copies ran while one was open for 0% of the time, Pallas kernels for 22%

profile of v10, /device:TPU:0, one launch (start us, length us, event | category | flops | bytes accessed | tf_op | source)
XLA Modules:
  0.0 27.7 jit_solution(14186921054611596217)
XLA Ops:
  0.0 1.1 %shard_map.55 = (bf16[128,128]{1,0:T(8,128)(2,1)S(1)}, bf16[128,128]{1,0:T(8,128)(2,1)S(1)}, bf16[5,128,128]{2,1,0:T(8,128)(2,1)S(1)}, bf16[16,48,128]{2,1,0:T(8,128)(2,1)S(1)}, bf16[16,32,128]{2,1,0:T(8,128)(2,1)S(1)}) custom-call(bf16[128,8,128]{2,1,0:T(8,128)(2,1)} %bitcast.6, bf16[64,64,256]{2,1,0:T(8,128)(2,1)} %w_half_ref.1), custom_call_target="tpu_custom_call" | custom-call | tf_op jit(solution)/shard_map/pallas_call | solution.py:310
  1.1 0.0 copy-start
  1.1 3.0 %collective-permute-start = (bf16[16,48,128]{2,1,0:T(8,128)(2,1)S(1)}, bf16[16,48,128]{2,1,0:T(8,128)(2,1)S(1)}, u32[]{:S(2)}, u32[]{:S(2)}) collective-permute-start(bf16[16,48,128]{2,1,0:T(8,128)(2,1)S(1)} %get-tuple-element.40), channel_id=1, source_target_pairs={{0,1},{1,0},{2,3},{3,2},{4,5},{5,4},{6,7},{7,6},{8,9},{9,8},{10,11... | collective-permute-start | bytes 589832 | tf_op jit(solution)/shard_map/ppermute | solution.py:440
  4.2 0.1 collective-permute-start.6
  4.2 1.4 %collective-permute-start.1 = (bf16[128,128]{1,0:T(8,128)(2,1)S(1)}, bf16[128,128]{1,0:T(8,128)(2,1)S(1)}, u32[]{:S(2)}, u32[]{:S(2)}) collective-permute-start(bf16[128,128]{1,0:T(8,128)(2,1)S(1)} %get-tuple-element.43), channel_id=1, source_target_pairs={{0,2},{2,4},{4,6},{6,8},{8,10},{10,12},{12,14},{14,16},{16,18},{18... | collective-permute-start | bytes 98312 | tf_op jit(solution)/shard_map/ppermute | solution.py:442
  5.7 0.7 %collective-permute-start.2 = (bf16[128,128]{1,0:T(8,128)(2,1)S(1)}, bf16[128,128]{1,0:T(8,128)(2,1)S(1)}, u32[]{:S(2)}, u32[]{:S(2)}) collective-permute-start(bf16[128,128]{1,0:T(8,128)(2,1)S(1)} %get-tuple-element.44), channel_id=1, source_target_pairs={{1,2},{3,4},{5,6},{7,8},{9,10},{11,12},{13,14},{15,16},{17,18},{19... | collective-permute-start | bytes 98312 | tf_op jit(solution)/shard_map/ppermute | solution.py:441
  6.4 1.2 %shard_map.56.started_ref = bf16[3,6,256,128]{3,2,1,0:T(8,128)(2,1)S(1)} custom-call(bf16[128,8,128]{2,1,0:T(8,128)(2,1)} %bitcast.7), custom_call_target="tpu_custom_call" | custom-call | flops 1048576 | bytes 2097152 | tf_op jit(solution)/shard_map/pallas_call | solution.py:343
  7.6 0.0 collective-permute-done.1.near_ref
  7.6 0.0 collective-permute-done.2.far_ref
  7.6 2.3 %collective-permute-done.refs_0_ = bf16[16,48,128]{2,1,0:T(8,128)(2,1)S(1)} collective-permute-done((bf16[16,48,128]{2,1,0:T(8,128)(2,1)S(1)}, bf16[16,48,128]{2,1,0:T(8,128)(2,1)S(1)}, u32[]{:S(2)}, u32[]{:S(2)}) %collective-permute-start) | collective-permute-done | bytes 196640 | tf_op jit(solution)/shard_map/ppermute | solution.py:440
  9.9 4.4 %collective-permute-start.4 = (bf16[16,48,128]{2,1,0:T(8,128)(2,1)S(1)}, bf16[16,48,128]{2,1,0:T(8,128)(2,1)S(1)}, u32[]{:S(2)}, u32[]{:S(2)}) collective-permute-start(bf16[16,48,128]{2,1,0:T(8,128)(2,1)S(1)} %collective-permute-done.refs_0_), channel_id=1, source_target_pairs={{0,4},{1,5},{2,6},{3,7},{4,0},{5,1},{6,2},{7,3},{8,12},{9,13},{10,... | collective-permute-start | bytes 589832 | tf_op jit(solution)/shard_map/ppermute | solution.py:447
  14.3 0.4 %collective-permute-start.5 = (bf16[16,48,128]{2,1,0:T(8,128)(2,1)S(1)}, bf16[16,48,128]{2,1,0:T(8,128)(2,1)S(1)}, u32[]{:S(2)}, u32[]{:S(2)}) collective-permute-start(bf16[16,48,128]{2,1,0:T(8,128)(2,1)S(1)} %collective-permute-done.refs_0_), channel_id=1, source_target_pairs={{0,2},{1,3},{2,0},{3,1},{4,6},{5,7},{6,4},{7,5},{8,10},{9,11},{10,... | collective-permute-start | bytes 589832 | tf_op jit(solution)/shard_map/ppermute | solution.py:448
  14.7 2.2 %collective-permute-start.3 = (bf16[16,32,128]{2,1,0:T(8,128)(2,1)S(1)}, bf16[16,32,128]{2,1,0:T(8,128)(2,1)S(1)}, u32[]{:S(2)}, u32[]{:S(2)}) collective-permute-start(bf16[16,32,128]{2,1,0:T(8,128)(2,1)S(1)} %get-tuple-element.46), channel_id=1, source_target_pairs={{0,1},{1,0},{2,3},{3,2},{4,5},{5,4},{6,7},{7,6},{8,9},{9,8},{10,11... | collective-permute-start | bytes 393224 | tf_op jit(solution)/shard_map/ppermute | solution.py:445
  16.9 2.0 %shard_map.57 = (bf16[32,64,256]{2,1,0:T(8,128)(2,1)S(1)}, bf16[256,1152]{1,0:T(8,128)(2,1)S(1)}, bf16[256,1152]{1,0:T(8,128)(2,1)S(1)}) custom-call(bf16[64,64,256]{2,1,0:T(8,128)(2,1)} %w_half_ref.1, bf16[27,128,128]{2,1,0:T(8,128)(2,1)} %w_conv_ref), custom_call_target="tpu_custom_call" | custom-call | flops 150994944 | bytes 6291456 | tf_op jit(solution)/shard_map/pallas_call | solution.py:360
  18.9 0.0 collective-permute-done.6.peer_ref
  18.9 0.0 copy-done
  18.9 0.0 copy-start.1
  18.9 2.8 %shard_map.58 = (bf16[3,6,256,128]{3,2,1,0:T(8,128)(2,1)S(1)}, f32[2,256,1024]{2,1,0:T(8,128)S(1)}) custom-call(bf16[5,128,128]{2,1,0:T(8,128)(2,1)S(1)} %collective-permute-done.6.peer_ref, bf16[128,128]{1,0:T(8,128)(2,1)S(1)} %collective-permute-done.1.near_ref, ...), custom_call_target="tpu_custom_call", output_to_operand_aliasing={{0}: (3, {})} | custom-call | flops 1879048192 | bytes 8388608 | tf_op jit(solution)/shard_map/pallas_call | solution.py:382
  21.7 0.0 collective-permute-done.3.refs_2_
  21.7 0.0 collective-permute-done.4.refs_1_
  21.7 0.0 collective-permute-done.5.refs_3_
  21.7 0.1 collective-permute-start.7
  21.8 0.5 %collective-permute-start.8 = (bf16[16,32,128]{2,1,0:T(8,128)(2,1)S(1)}, bf16[16,32,128]{2,1,0:T(8,128)(2,1)S(1)}, u32[]{:S(2)}, u32[]{:S(2)}) collective-permute-start(bf16[16,32,128]{2,1,0:T(8,128)(2,1)S(1)} %collective-permute-done.3.refs_2_), channel_id=1, source_target_pairs={{0,2},{1,3},{2,0},{3,1},{4,6},{5,7},{6,4},{7,5},{8,10},{9,11},{10,... | collective-permute-start | bytes 393224 | tf_op jit(solution)/shard_map/ppermute | solution.py:453
  22.3 1.1 %collective-permute-done.8.refs_5_ = bf16[16,32,128]{2,1,0:T(8,128)(2,1)S(1)} collective-permute-done((bf16[16,32,128]{2,1,0:T(8,128)(2,1)S(1)}, bf16[16,32,128]{2,1,0:T(8,128)(2,1)S(1)}, u32[]{:S(2)}, u32[]{:S(2)}) %collective-permute-start.8) | collective-permute-done | bytes 131104 | tf_op jit(solution)/shard_map/ppermute | solution.py:453
  23.4 0.0 collective-permute-done.7.refs_4_
  23.4 0.0 copy-done.1
  23.4 4.3 %shard_map.59 = bf16[128,2,8,256]{3,2,1,0:T(8,128)(2,1)} custom-call(bf16[16,48,128]{2,1,0:T(8,128)(2,1)S(1)} %collective-permute-done.refs_0_, bf16[16,48,128]{2,1,0:T(8,128)(2,1)S(1)} %collective-permute-done.4.refs_1_, bf16[16,32,128]{2,1,0:T(8,128)(2,1)S(1)} %collective-permute-done.3.refs_2_, bf16[16,48,128]{2,1,0:T(8,128)(2,1)S(1)} %collective-permute-done.5.refs_3_, ...), custom_call_target="tpu_custom_call" | custom-call | flops 1879048192 | bytes 8388608 | tf_op jit(solution)/shard_map/pallas_call | solution.py:402
Async XLA Ops:
  1.1 17.8 %copy-start = (f32[128]{0:T(128)S(1)}, f32[128]{0:T(128)}, u32[]{:S(2)}) copy-start(f32[128]{0:T(128)} %param.7) | copy-start | bytes 1540
  1.1 8.8 %collective-permute-start = (bf16[16,48,128]{2,1,0:T(8,128)(2,1)S(1)}, bf16[16,48,128]{2,1,0:T(8,128)(2,1)S(1)}, u32[]{:S(2)}, u32[]{:S(2)}) collective-permute-start(bf16[16,48,128]{2,1,0:T(8,128)(2,1)S(1)} %get-tuple-element.40), channel_id=1, source_target_pairs={{0,1},{1,0},{2,3},{3,2},{4,5},{5,4},{6,7},{7,6},{8,9},{9,8},{10,11... | collective-permute-start | bytes 589832 | tf_op jit(solution)/shard_map/ppermute | solution.py:440
  4.2 14.7 %collective-permute-start.6 = (bf16[5,128,128]{2,1,0:T(8,128)(2,1)S(1)}, bf16[5,128,128]{2,1,0:T(8,128)(2,1)S(1)}, u32[]{:S(2)}, u32[]{:S(2)}) collective-permute-start(bf16[5,128,128]{2,1,0:T(8,128)(2,1)S(1)} %get-tuple-element.47), channel_id=1, source_target_pairs={{0,1},{1,0},{2,3},{3,2},{4,5},{5,4},{6,7},{7,6},{8,9},{9,8},{10,11... | collective-permute-start | bytes 491528 | tf_op jit(solution)/shard_map/ppermute | solution.py:439
  4.2 3.3 %collective-permute-start.1 = (bf16[128,128]{1,0:T(8,128)(2,1)S(1)}, bf16[128,128]{1,0:T(8,128)(2,1)S(1)}, u32[]{:S(2)}, u32[]{:S(2)}) collective-permute-start(bf16[128,128]{1,0:T(8,128)(2,1)S(1)} %get-tuple-element.43), channel_id=1, source_target_pairs={{0,2},{2,4},{4,6},{6,8},{8,10},{10,12},{12,14},{14,16},{16,18},{18... | collective-permute-start | bytes 98312 | tf_op jit(solution)/shard_map/ppermute | solution.py:442
  5.7 1.9 %collective-permute-start.2 = (bf16[128,128]{1,0:T(8,128)(2,1)S(1)}, bf16[128,128]{1,0:T(8,128)(2,1)S(1)}, u32[]{:S(2)}, u32[]{:S(2)}) collective-permute-start(bf16[128,128]{1,0:T(8,128)(2,1)S(1)} %get-tuple-element.44), channel_id=1, source_target_pairs={{1,2},{3,4},{5,6},{7,8},{9,10},{11,12},{13,14},{15,16},{17,18},{19... | collective-permute-start | bytes 98312 | tf_op jit(solution)/shard_map/ppermute | solution.py:441
  9.9 11.8 %collective-permute-start.4 = (bf16[16,48,128]{2,1,0:T(8,128)(2,1)S(1)}, bf16[16,48,128]{2,1,0:T(8,128)(2,1)S(1)}, u32[]{:S(2)}, u32[]{:S(2)}) collective-permute-start(bf16[16,48,128]{2,1,0:T(8,128)(2,1)S(1)} %collective-permute-done.refs_0_), channel_id=1, source_target_pairs={{0,4},{1,5},{2,6},{3,7},{4,0},{5,1},{6,2},{7,3},{8,12},{9,13},{10,... | collective-permute-start | bytes 589832 | tf_op jit(solution)/shard_map/ppermute | solution.py:447
  14.3 7.4 %collective-permute-start.5 = (bf16[16,48,128]{2,1,0:T(8,128)(2,1)S(1)}, bf16[16,48,128]{2,1,0:T(8,128)(2,1)S(1)}, u32[]{:S(2)}, u32[]{:S(2)}) collective-permute-start(bf16[16,48,128]{2,1,0:T(8,128)(2,1)S(1)} %collective-permute-done.refs_0_), channel_id=1, source_target_pairs={{0,2},{1,3},{2,0},{3,1},{4,6},{5,7},{6,4},{7,5},{8,10},{9,11},{10,... | collective-permute-start | bytes 589832 | tf_op jit(solution)/shard_map/ppermute | solution.py:448
  14.7 7.0 %collective-permute-start.3 = (bf16[16,32,128]{2,1,0:T(8,128)(2,1)S(1)}, bf16[16,32,128]{2,1,0:T(8,128)(2,1)S(1)}, u32[]{:S(2)}, u32[]{:S(2)}) collective-permute-start(bf16[16,32,128]{2,1,0:T(8,128)(2,1)S(1)} %get-tuple-element.46), channel_id=1, source_target_pairs={{0,1},{1,0},{2,3},{3,2},{4,5},{5,4},{6,7},{7,6},{8,9},{9,8},{10,11... | collective-permute-start | bytes 393224 | tf_op jit(solution)/shard_map/ppermute | solution.py:445
  18.9 4.5 %copy-start.1 = (f32[128]{0:T(128)S(1)}, f32[128]{0:T(128)}, u32[]{:S(2)}) copy-start(f32[128]{0:T(128)} %param.9) | copy-start | bytes 1540
  21.7 1.7 %collective-permute-start.7 = (bf16[16,48,128]{2,1,0:T(8,128)(2,1)S(1)}, bf16[16,48,128]{2,1,0:T(8,128)(2,1)S(1)}, u32[]{:S(2)}, u32[]{:S(2)}) collective-permute-start(bf16[16,48,128]{2,1,0:T(8,128)(2,1)S(1)} %collective-permute-done.4.refs_1_), channel_id=1, source_target_pairs={{0,2},{1,3},{2,0},{3,1},{4,6},{5,7},{6,4},{7,5},{8,10},{9,11},{10,... | collective-permute-start | bytes 589832 | tf_op jit(solution)/shard_map/ppermute | solution.py:454
  21.8 1.6 %collective-permute-start.8 = (bf16[16,32,128]{2,1,0:T(8,128)(2,1)S(1)}, bf16[16,32,128]{2,1,0:T(8,128)(2,1)S(1)}, u32[]{:S(2)}, u32[]{:S(2)}) collective-permute-start(bf16[16,32,128]{2,1,0:T(8,128)(2,1)S(1)} %collective-permute-done.3.refs_2_), channel_id=1, source_target_pairs={{0,2},{1,3},{2,0},{3,1},{4,6},{5,7},{6,4},{7,5},{8,10},{9,11},{10,... | collective-permute-start | bytes 393224 | tf_op jit(solution)/shard_map/ppermute | solution.py:453

commit v11 on v10

--- a/solution.py
+++ b/solution.py
@@ -147,12 +147,19 @@
             sum_ref[col_phase, :, start * cols : (start + 2) * cols] = convolve(kernel, u_ref, start, col_phase)
 
 
-def prepare_rows(paired, own_ref, x_ref, wide_ref, raw_ref, sem):
-    copy = pltpu.make_async_copy(own_ref, raw_ref, sem)
-    copy.start()
-    copy.wait()
+def prepare(paired, own_ref, w_half_ref, w_conv_ref, x_ref, w_ref, kernel_ref, other_ref, *scratch):
+    halves_ref, v_ref, wide_ref, raw_ref, sems = scratch
+    s, c = lax.axis_index("space"), lax.axis_index("ch")
+    skipped = (w_half_ref.shape[0] - 32) // 2
+    copies = [
+        pltpu.make_async_copy(own_ref, raw_ref, sems.at[0]),
+        pltpu.make_async_copy(w_conv_ref, v_ref, sems.at[1]),
+        pltpu.make_async_copy(w_half_ref.at[pl.ds(skipped, 32)], w_ref, sems.at[2]),
+    ]
+    for copy in copies:
+        copy.start()
+    copies[0].wait()
     if paired:
-        c = lax.axis_index("ch")
         chans, rows, cols = own_ref.shape
         wide_ref[...] = raw_ref[...].astype(jnp.float32).reshape(chans * rows, cols)
         share = x_ref.shape[1] - 1
@@ -162,20 +169,9 @@
     else:
         for slot in range(own_ref.shape[0]):
             store_row(x_ref, slot, 0, raw_ref[slot].astype(jnp.float32))
-
-
-def prepare_kernels(paired, w_half_ref, w_conv_ref, w_ref, kernel_ref, other_ref, halves_ref, v_ref, sems):
-    s, c = lax.axis_index("space"), lax.axis_index("ch")
-    skipped = (w_half_ref.shape[0] - 32) // 2
-    copies = [
-        pltpu.make_async_copy(w_conv_ref, v_ref, sems.at[0]),
-        pltpu.make_async_copy(w_half_ref.at[pl.ds(skipped, 32)], w_ref, sems.at[1]),
-    ]
-    for copy in copies:
-        copy.start()
     cout = w_conv_ref.shape[1]
     half, x = (c, lax.rem(s, 4) // 2) if paired else (0, None)
-    copies[0].wait()
+    copies[1].wait()
     split_kernels(v_ref, halves_ref)
     kernel_ref[...] = halves_ref[half]
     matrix = arrange(x, cout // 2)
@@ -183,7 +179,7 @@
         columns = pl.ds(number * cout, cout)
         moved = jnp.dot(halves_ref[1 - half, :, columns], matrix, preferred_element_type=jnp.float32)
         other_ref[:, columns] = moved.astype(jnp.bfloat16)
-    copies[1].wait()
+    copies[2].wait()
 
 
 def paired_first(peer_ref, near_ref, far_ref, started_ref, *refs):
@@ -337,43 +333,29 @@
     return pl.CostEstimate(flops=flops, bytes_accessed=8 * 2**20, transcendentals=0)
 
 
-def call_rows(paired, own, sizes):
+def call_prepare(paired, own, w_half, w_conv, sizes):
     cin, cout, rows, cols = sizes
     wide = own.shape[0] * own.shape[1] if paired else 8
     return pl.pallas_call(
-        functools.partial(prepare_rows, paired),
-        out_shape=jax.ShapeDtypeStruct((3, rows // 2 + 2, cin, cols), jnp.bfloat16),
-        in_specs=[ANY],
-        out_specs=VMEM,
-        scratch_shapes=[
-            pltpu.VMEM((wide, cols), jnp.float32),
-            pltpu.VMEM(own.shape, jnp.bfloat16),
-            pltpu.SemaphoreType.DMA,
-        ],
-        cost_estimate=pl.CostEstimate(flops=2**20, bytes_accessed=2 * 2**20, transcendentals=0),
-        compiler_params=pltpu.CompilerParams(vmem_limit_bytes=LIMIT),
-    )(in_hbm(own))
-
-
-def call_kernels(paired, w_half, w_conv, sizes):
-    cin, cout, rows, cols = sizes
-    return pl.pallas_call(
-        functools.partial(prepare_kernels, paired),
+        functools.partial(prepare, paired),
         out_shape=(
+            jax.ShapeDtypeStruct((3, rows // 2 + 2, cin, cols), jnp.bfloat16),
             jax.ShapeDtypeStruct((32, cout // 2, cin), jnp.bfloat16),
             jax.ShapeDtypeStruct((2 * cout, 9 * cout), jnp.bfloat16),
             jax.ShapeDtypeStruct((2 * cout, 9 * cout), jnp.bfloat16),
         ),
-        in_specs=[ANY] * 2,
-        out_specs=(VMEM,) * 3,
+        in_specs=[ANY] * 3,
+        out_specs=(VMEM,) * 4,
         scratch_shapes=[
             pltpu.VMEM((2, 2 * cout, 9 * cout), jnp.bfloat16),
             pltpu.VMEM((27, cout, cout), jnp.bfloat16),
-            pltpu.SemaphoreType.DMA((2,)),
+            pltpu.VMEM((wide, cols), jnp.float32),
+            pltpu.VMEM(own.shape, jnp.bfloat16),
+            pltpu.SemaphoreType.DMA((3,)),
         ],
-        cost_estimate=pl.CostEstimate(flops=2 * 18 * 256 * cout * cout, bytes_accessed=6 * 2**20, transcendentals=0),
+        cost_estimate=pl.CostEstimate(flops=2 * 18 * 256 * cout * cout, bytes_accessed=8 * 2**20, transcendentals=0),
         compiler_params=pltpu.CompilerParams(vmem_limit_bytes=LIMIT),
-    )(in_hbm(w_half), in_hbm(w_conv))
+    )(in_hbm(own), in_hbm(w_half), in_hbm(w_conv))
 
 
 def call_first(body, rows_in, prepared, b_up, sizes):
@@ -430,20 +412,16 @@
     chain = [(at(i - 1, 0), at(i, 0)) for i in range(1, spaces)]
     chain += [(at(i + 1, 1), at(i, 1)) for i in range(spaces - 1)]
 
-    outer = [(t, t + 1) for t in range(1, 2 * spaces - 1, 2)]
-    outer += [(j, i) for i, j in outer]
-
     own = inputs.reshape(chans, held, cols)
     near, far, peer, w_a, w_b = call_pieces(own, w_up)
-    own, w_conv, peer, w_a, far, near, w_b = lax.optimization_barrier((own, w_conv, peer, w_a, far, near, w_b))
+    far = lax.ppermute(far, AXES, across)
+    far, near, own, w_conv, w_a, peer, w_b = lax.optimization_barrier((far, near, own, w_conv, w_a, peer, w_b))
+    w_a = lax.ppermute(w_a, AXES, across)
     peer = lax.ppermute(peer, AXES, across)
-    w_a = lax.ppermute(w_a, AXES, across)
-    far = lax.ppermute(far, AXES, outer)
+    w_b = lax.ppermute(w_b, AXES, across)
     near = lax.ppermute(near, AXES, chain)
-    x = call_rows(True, own, sizes)
-    x, w_a, w_b, w_conv, near, far = lax.optimization_barrier((x, w_a, w_b, w_conv, near, far))
-    w_b = lax.ppermute(w_b, AXES, across)
-    w_half, kernel, other = call_kernels(True, w_up, w_conv, sizes)
+    far = lax.ppermute(far, AXES, chain)
+    x, w_half, kernel, other = call_prepare(True, own, w_up, w_conv, sizes)
     w_ax = lax.ppermute(w_a, AXES, pairs)
     w_ac = lax.ppermute(w_a, AXES, cores)
     biases = (b_up[None], b_conv[None])
@@ -469,8 +447,7 @@
     share = inputs.shape[2] // chs
     rows = lax.dynamic_slice_in_dim(rows, c * share, share + 2, 0)
     biases = (b_up[None], b_conv[None])
-    *prepared, other = call_kernels(False, w_all[:, :part], w_conv, sizes)
-    prepared = (call_rows(False, rows, sizes), *prepared)
+    *prepared, other = call_prepare(False, rows, w_all[:, :part], w_conv, sizes)
     results = (*call_first(gathered_first, (), prepared, biases[0], sizes), other)
     return call_second(False, (w_all[:16, part:], w_all[16:, part:]), results, biases, sizes)
 

time: 27.9 us -> 29.8 us (1.068)
  starting transfers between devices: 12.7 us -> 14.3 us
  waiting for transfers between devices: 3.43 us -> 4.96 us
  Pallas kernels: 11.4 us -> 10.3 us
    ppermute x1 -> x2, starting transfers between devices: 0.66 us -> 7.63 us  [the longest x1 4.6 us: paired(): far = lax.ppermute(far, AXES, chain)]
    ppermute x1, starting transfers between devices: 4.43 us -> 1.62 us  [paired(): w_ax = lax.ppermute(w_a, AXES, pairs)]
    ppermute x1, waiting for transfers between devices: 2.3 us -> 0.01 us  [paired(): w_a = lax.ppermute(w_a, AXES, across)]
    ppermute x1, waiting for transfers between devices: 0.01 us -> 1.93 us  [paired(): w_b = lax.ppermute(w_b, AXES, across)]
    ppermute x1 -> x2, waiting for transfers between devices: 0.01 us -> 1.9 us  [the longest x1 1.89 us: paired(): far = lax.ppermute(far, AXES, across)]
    pallas_call x2 -> x1, Pallas kernels: 3.22 us -> 2.12 us  [call_prepare(): pl.pallas_call(functools.partial(prepare, paired), out_shape=(jax.ShapeDt...]
    ppermute x1, starting transfers between devices: 3.03 us -> 2.02 us  [paired(): w_a = lax.ppermute(w_a, AXES, across)]
    ppermute x1, starting transfers between devices: 2.16 us -> 1.25 us  [paired(): w_b = lax.ppermute(w_b, AXES, across)]
  transfers between devices with their start and end apart: 9 -> 10, of which waited for: 2 -> 3; matrix products, arithmetic and copies ran while one was open for 0% -> 0% of each run, Pallas kernels for 22% -> 17%
where the time goes in v11:
time: 29.8 us; the launch traced here: 29.6 us
  starting transfers between devices  14.3 us (48%)
  Pallas kernels  10.3 us (35%)
  waiting for transfers between devices  4.96 us (17%)
    ppermute x1, starting transfers between devices, paired(): far = lax.ppermute(far, AXES, chain)  4.6 us
    pallas_call x1, Pallas kernels, call_second(): pl.pallas_call(functools.partial(second, paired, len(parts)), out_shape=j...  4.24 us
    ppermute x1, starting transfers between devices, paired(): far = lax.ppermute(far, AXES, across)  3.03 us
    pallas_call x1, Pallas kernels, call_first(): pl.pallas_call(body, out_shape=(jax.ShapeDtypeStruct(started.shape, jnp.b...  2.77 us
    pallas_call x1, Pallas kernels, call_prepare(): pl.pallas_call(functools.partial(prepare, paired), out_shape=(jax.ShapeDt...  2.12 us
    ppermute x1, starting transfers between devices, paired(): w_a = lax.ppermute(w_a, AXES, across)  2.02 us
    ppermute x1, waiting for transfers between devices, paired(): w_b = lax.ppermute(w_b, AXES, across)  1.93 us
    ppermute x1, waiting for transfers between devices, paired(): far = lax.ppermute(far, AXES, across)  1.89 us
  transfers between devices with their start and end apart: 10, of which 3 were waited for; matrix products, arithmetic and copies ran while one was open for 0% of the time, Pallas kernels for 17%

profile of v11, /device:TPU:0, one launch (start us, length us, event | category | flops | bytes accessed | tf_op | source)
XLA Modules:
  0.0 29.6 jit_solution(6160133199888777613)
XLA Ops:
  0.0 1.1 %shard_map.55 = (bf16[128,128]{1,0:T(8,128)(2,1)S(1)}, bf16[128,128]{1,0:T(8,128)(2,1)S(1)}, bf16[5,128,128]{2,1,0:T(8,128)(2,1)S(1)}, bf16[16,48,128]{2,1,0:T(8,128)(2,1)S(1)}, bf16[16,32,128]{2,1,0:T(8,128)(2,1)S(1)}) custom-call(bf16[128,8,128]{2,1,0:T(8,128)(2,1)} %bitcast.6, bf16[64,64,256]{2,1,0:T(8,128)(2,1)} %w_half_ref.1), custom_call_target="tpu_custom_call" | custom-call | tf_op jit(solution)/shard_map/pallas_call | solution.py:306
  1.1 0.0 copy-start
  1.1 3.0 %collective-permute-start = (bf16[128,128]{1,0:T(8,128)(2,1)S(1)}, bf16[128,128]{1,0:T(8,128)(2,1)S(1)}, u32[]{:S(2)}, u32[]{:S(2)}) collective-permute-start(bf16[128,128]{1,0:T(8,128)(2,1)S(1)} %get-tuple-element.29), channel_id=1, source_target_pairs={{0,1},{1,0},{2,3},{3,2},{4,5},{5,4},{6,7},{7,6},{8,9},{9,8},{10,11... | collective-permute-start | bytes 98312 | tf_op jit(solution)/shard_map/ppermute | solution.py:417
  4.2 1.9 %collective-permute-done = bf16[128,128]{1,0:T(8,128)(2,1)S(1)} collective-permute-done((bf16[128,128]{1,0:T(8,128)(2,1)S(1)}, bf16[128,128]{1,0:T(8,128)(2,1)S(1)}, u32[]{:S(2)}, u32[]{:S(2)}) %collective-permute-start) | collective-permute-done | bytes 32800 | tf_op jit(solution)/shard_map/ppermute | solution.py:417
  6.1 2.0 %collective-permute-start.1 = (bf16[16,48,128]{2,1,0:T(8,128)(2,1)S(1)}, bf16[16,48,128]{2,1,0:T(8,128)(2,1)S(1)}, u32[]{:S(2)}, u32[]{:S(2)}) collective-permute-start(bf16[16,48,128]{2,1,0:T(8,128)(2,1)S(1)} %get-tuple-element.34), channel_id=1, source_target_pairs={{0,1},{1,0},{2,3},{3,2},{4,5},{5,4},{6,7},{7,6},{8,9},{9,8},{10,11... | collective-permute-start | bytes 589832 | tf_op jit(solution)/shard_map/ppermute | solution.py:419
  8.1 0.0 collective-permute-start.5
  8.1 1.3 %collective-permute-start.6 = (bf16[128,128]{1,0:T(8,128)(2,1)S(1)}, bf16[128,128]{1,0:T(8,128)(2,1)S(1)}, u32[]{:S(2)}, u32[]{:S(2)}) collective-permute-start(bf16[128,128]{1,0:T(8,128)(2,1)S(1)} %get-tuple-element.37), channel_id=1, source_target_pairs={{0,2},{2,4},{4,6},{6,8},{8,10},{10,12},{12,14},{14,16},{16,18},{18... | collective-permute-start | bytes 98312 | tf_op jit(solution)/shard_map/ppermute | solution.py:422
  9.4 4.6 %collective-permute-start.7 = (bf16[128,128]{1,0:T(8,128)(2,1)S(1)}, bf16[128,128]{1,0:T(8,128)(2,1)S(1)}, u32[]{:S(2)}, u32[]{:S(2)}) collective-permute-start(bf16[128,128]{1,0:T(8,128)(2,1)S(1)} %collective-permute-done), channel_id=1, source_target_pairs={{0,2},{2,4},{4,6},{6,8},{8,10},{10,12},{12,14},{14,16},{16,18},{18... | collective-permute-start | bytes 98312 | tf_op jit(solution)/shard_map/ppermute | solution.py:423
  14.0 0.0 collective-permute-done.1.refs_0_
  14.0 1.6 %collective-permute-start.3 = (bf16[16,48,128]{2,1,0:T(8,128)(2,1)S(1)}, bf16[16,48,128]{2,1,0:T(8,128)(2,1)S(1)}, u32[]{:S(2)}, u32[]{:S(2)}) collective-permute-start(bf16[16,48,128]{2,1,0:T(8,128)(2,1)S(1)} %collective-permute-done.1.refs_0_), channel_id=1, source_target_pairs={{0,4},{1,5},{2,6},{3,7},{4,0},{5,1},{6,2},{7,3},{8,12},{9,13},{10,... | collective-permute-start | bytes 589832 | tf_op jit(solution)/shard_map/ppermute | solution.py:425
  15.6 0.0 collective-permute-start.4
  15.6 2.1 %shard_map.56 = (bf16[3,6,256,128]{3,2,1,0:T(8,128)(2,1)S(1)}, bf16[32,64,256]{2,1,0:T(8,128)(2,1)S(1)}, bf16[256,1152]{1,0:T(8,128)(2,1)S(1)}, bf16[256,1152]{1,0:T(8,128)(2,1)S(1)}) custom-call(bf16[128,8,128]{2,1,0:T(8,128)(2,1)} %bitcast.7, bf16[64,64,256]{2,1,0:T(8,128)(2,1)} %w_half_ref.1, bf16[27,128,128]{2,1,0:T(8,128)(2,1)} %w_conv_ref), custom_call_target="tpu_custom_call" | custom-call | flops 150994944 | bytes 8388608 | tf_op jit(solution)/shard_map/pallas_call | solution.py:339
  17.8 0.0 collective-permute-done.6.near_ref
  17.8 1.2 %collective-permute-start.2 = (bf16[16,32,128]{2,1,0:T(8,128)(2,1)S(1)}, bf16[16,32,128]{2,1,0:T(8,128)(2,1)S(1)}, u32[]{:S(2)}, u32[]{:S(2)}) collective-permute-start(bf16[16,32,128]{2,1,0:T(8,128)(2,1)S(1)} %get-tuple-element.35), channel_id=1, source_target_pairs={{0,1},{1,0},{2,3},{3,2},{4,5},{5,4},{6,7},{7,6},{8,9},{9,8},{10,11... | collective-permute-start | bytes 393224 | tf_op jit(solution)/shard_map/ppermute | solution.py:421
  19.0 0.0 collective-permute-done.7.far_ref
  19.0 0.0 collective-permute-done.5.peer_ref
  19.0 0.0 copy-done
  19.0 0.0 copy-start.1
  19.1 2.8 %shard_map.57 = (bf16[3,6,256,128]{3,2,1,0:T(8,128)(2,1)S(1)}, f32[2,256,1024]{2,1,0:T(8,128)S(1)}) custom-call(bf16[5,128,128]{2,1,0:T(8,128)(2,1)S(1)} %collective-permute-done.5.peer_ref, bf16[128,128]{1,0:T(8,128)(2,1)S(1)} %collective-permute-done.6.near_ref, ...), custom_call_target="tpu_custom_call", output_to_operand_aliasing={{0}: (3, {})} | custom-call | flops 1879048192 | bytes 8388608 | tf_op jit(solution)/shard_map/pallas_call | solution.py:364
  21.8 1.9 %collective-permute-done.2.refs_2_ = bf16[16,32,128]{2,1,0:T(8,128)(2,1)S(1)} collective-permute-done((bf16[16,32,128]{2,1,0:T(8,128)(2,1)S(1)}, bf16[16,32,128]{2,1,0:T(8,128)(2,1)S(1)}, u32[]{:S(2)}, u32[]{:S(2)}) %collective-permute-start.2) | collective-permute-done | bytes 131104 | tf_op jit(solution)/shard_map/ppermute | solution.py:421
  23.8 0.0 collective-permute-done.3.refs_1_
  23.8 0.0 collective-permute-done.4.refs_3_
  23.8 0.0 collective-permute-start.8
  23.8 0.5 %collective-permute-start.9 = (bf16[16,32,128]{2,1,0:T(8,128)(2,1)S(1)}, bf16[16,32,128]{2,1,0:T(8,128)(2,1)S(1)}, u32[]{:S(2)}, u32[]{:S(2)}) collective-permute-start(bf16[16,32,128]{2,1,0:T(8,128)(2,1)S(1)} %collective-permute-done.2.refs_2_), channel_id=1, source_target_pairs={{0,2},{1,3},{2,0},{3,1},{4,6},{5,7},{6,4},{7,5},{8,10},{9,11},{10,... | collective-permute-start | bytes 393224 | tf_op jit(solution)/shard_map/ppermute | solution.py:431
  24.3 1.1 %collective-permute-done.9.refs_5_ = bf16[16,32,128]{2,1,0:T(8,128)(2,1)S(1)} collective-permute-done((bf16[16,32,128]{2,1,0:T(8,128)(2,1)S(1)}, bf16[16,32,128]{2,1,0:T(8,128)(2,1)S(1)}, u32[]{:S(2)}, u32[]{:S(2)}) %collective-permute-start.9) | collective-permute-done | bytes 131104 | tf_op jit(solution)/shard_map/ppermute | solution.py:431
  25.4 0.0 collective-permute-done.8.refs_4_
  25.4 0.0 copy-done.1
  25.4 4.2 %shard_map.58 = bf16[128,2,8,256]{3,2,1,0:T(8,128)(2,1)} custom-call(bf16[16,48,128]{2,1,0:T(8,128)(2,1)S(1)} %collective-permute-done.1.refs_0_, bf16[16,48,128]{2,1,0:T(8,128)(2,1)S(1)} %collective-permute-done.3.refs_1_, bf16[16,32,128]{2,1,0:T(8,128)(2,1)S(1)} %collective-permute-done.2.refs_2_, bf16[16,48,128]{2,1,0:T(8,128)(2,1)S(1)} %collective-permute-done.4.refs_3_, ...), custom_call_target="tpu_custom_call" | custom-call | flops 1879048192 | bytes 8388608 | tf_op jit(solution)/shard_map/pallas_call | solution.py:384
Async XLA Ops:
  1.1 17.9 %copy-start = (f32[128]{0:T(128)S(1)}, f32[128]{0:T(128)}, u32[]{:S(2)}) copy-start(f32[128]{0:T(128)} %param.7) | copy-start | bytes 1540
  1.1 4.9 %collective-permute-start = (bf16[128,128]{1,0:T(8,128)(2,1)S(1)}, bf16[128,128]{1,0:T(8,128)(2,1)S(1)}, u32[]{:S(2)}, u32[]{:S(2)}) collective-permute-start(bf16[128,128]{1,0:T(8,128)(2,1)S(1)} %get-tuple-element.29), channel_id=1, source_target_pairs={{0,1},{1,0},{2,3},{3,2},{4,5},{5,4},{6,7},{7,6},{8,9},{9,8},{10,11... | collective-permute-start | bytes 98312 | tf_op jit(solution)/shard_map/ppermute | solution.py:417
  6.1 8.0 %collective-permute-start.1 = (bf16[16,48,128]{2,1,0:T(8,128)(2,1)S(1)}, bf16[16,48,128]{2,1,0:T(8,128)(2,1)S(1)}, u32[]{:S(2)}, u32[]{:S(2)}) collective-permute-start(bf16[16,48,128]{2,1,0:T(8,128)(2,1)S(1)} %get-tuple-element.34), channel_id=1, source_target_pairs={{0,1},{1,0},{2,3},{3,2},{4,5},{5,4},{6,7},{7,6},{8,9},{9,8},{10,11... | collective-permute-start | bytes 589832 | tf_op jit(solution)/shard_map/ppermute | solution.py:419
  8.1 11.0 %collective-permute-start.5 = (bf16[5,128,128]{2,1,0:T(8,128)(2,1)S(1)}, bf16[5,128,128]{2,1,0:T(8,128)(2,1)S(1)}, u32[]{:S(2)}, u32[]{:S(2)}) collective-permute-start(bf16[5,128,128]{2,1,0:T(8,128)(2,1)S(1)} %get-tuple-element.36), channel_id=1, source_target_pairs={{0,1},{1,0},{2,3},{3,2},{4,5},{5,4},{6,7},{7,6},{8,9},{9,8},{10,11... | collective-permute-start | bytes 491528 | tf_op jit(solution)/shard_map/ppermute | solution.py:420
  8.1 9.7 %collective-permute-start.6 = (bf16[128,128]{1,0:T(8,128)(2,1)S(1)}, bf16[128,128]{1,0:T(8,128)(2,1)S(1)}, u32[]{:S(2)}, u32[]{:S(2)}) collective-permute-start(bf16[128,128]{1,0:T(8,128)(2,1)S(1)} %get-tuple-element.37), channel_id=1, source_target_pairs={{0,2},{2,4},{4,6},{6,8},{8,10},{10,12},{12,14},{14,16},{16,18},{18... | collective-permute-start | bytes 98312 | tf_op jit(solution)/shard_map/ppermute | solution.py:422
  9.4 9.6 %collective-permute-start.7 = (bf16[128,128]{1,0:T(8,128)(2,1)S(1)}, bf16[128,128]{1,0:T(8,128)(2,1)S(1)}, u32[]{:S(2)}, u32[]{:S(2)}) collective-permute-start(bf16[128,128]{1,0:T(8,128)(2,1)S(1)} %collective-permute-done), channel_id=1, source_target_pairs={{0,2},{2,4},{4,6},{6,8},{8,10},{10,12},{12,14},{14,16},{16,18},{18... | collective-permute-start | bytes 98312 | tf_op jit(solution)/shard_map/ppermute | solution.py:423
  14.0 9.7 %collective-permute-start.3 = (bf16[16,48,128]{2,1,0:T(8,128)(2,1)S(1)}, bf16[16,48,128]{2,1,0:T(8,128)(2,1)S(1)}, u32[]{:S(2)}, u32[]{:S(2)}) collective-permute-start(bf16[16,48,128]{2,1,0:T(8,128)(2,1)S(1)} %collective-permute-done.1.refs_0_), channel_id=1, source_target_pairs={{0,4},{1,5},{2,6},{3,7},{4,0},{5,1},{6,2},{7,3},{8,12},{9,13},{10,... | collective-permute-start | bytes 589832 | tf_op jit(solution)/shard_map/ppermute | solution.py:425
  15.6 8.1 %collective-permute-start.4 = (bf16[16,48,128]{2,1,0:T(8,128)(2,1)S(1)}, bf16[16,48,128]{2,1,0:T(8,128)(2,1)S(1)}, u32[]{:S(2)}, u32[]{:S(2)}) collective-permute-start(bf16[16,48,128]{2,1,0:T(8,128)(2,1)S(1)} %collective-permute-done.1.refs_0_), channel_id=1, source_target_pairs={{0,2},{1,3},{2,0},{3,1},{4,6},{5,7},{6,4},{7,5},{8,10},{9,11},{10,... | collective-permute-start | bytes 589832 | tf_op jit(solution)/shard_map/ppermute | solution.py:426
  17.8 6.0 %collective-permute-start.2 = (bf16[16,32,128]{2,1,0:T(8,128)(2,1)S(1)}, bf16[16,32,128]{2,1,0:T(8,128)(2,1)S(1)}, u32[]{:S(2)}, u32[]{:S(2)}) collective-permute-start(bf16[16,32,128]{2,1,0:T(8,128)(2,1)S(1)} %get-tuple-element.35), channel_id=1, source_target_pairs={{0,1},{1,0},{2,3},{3,2},{4,5},{5,4},{6,7},{7,6},{8,9},{9,8},{10,11... | collective-permute-start | bytes 393224 | tf_op jit(solution)/shard_map/ppermute | solution.py:421
  19.0 6.4 %copy-start.1 = (f32[128]{0:T(128)S(1)}, f32[128]{0:T(128)}, u32[]{:S(2)}) copy-start(f32[128]{0:T(128)} %param.9) | copy-start | bytes 1540
  23.8 1.6 %collective-permute-start.8 = (bf16[16,48,128]{2,1,0:T(8,128)(2,1)S(1)}, bf16[16,48,128]{2,1,0:T(8,128)(2,1)S(1)}, u32[]{:S(2)}, u32[]{:S(2)}) collective-permute-start(bf16[16,48,128]{2,1,0:T(8,128)(2,1)S(1)} %collective-permute-done.3.refs_1_), channel_id=1, source_target_pairs={{0,2},{1,3},{2,0},{3,1},{4,6},{5,7},{6,4},{7,5},{8,10},{9,11},{10,... | collective-permute-start | bytes 589832 | tf_op jit(solution)/shard_map/ppermute | solution.py:432
  23.8 1.6 %collective-permute-start.9 = (bf16[16,32,128]{2,1,0:T(8,128)(2,1)S(1)}, bf16[16,32,128]{2,1,0:T(8,128)(2,1)S(1)}, u32[]{:S(2)}, u32[]{:S(2)}) collective-permute-start(bf16[16,32,128]{2,1,0:T(8,128)(2,1)S(1)} %collective-permute-done.2.refs_2_), channel_id=1, source_target_pairs={{0,2},{1,3},{2,0},{3,1},{4,6},{5,7},{6,4},{7,5},{8,10},{9,11},{10,... | collective-permute-start | bytes 393224 | tf_op jit(solution)/shard_map/ppermute | solution.py:431

commit v12 on v11

--- a/solution.py
+++ b/solution.py
@@ -412,16 +412,19 @@
     chain = [(at(i - 1, 0), at(i, 0)) for i in range(1, spaces)]
     chain += [(at(i + 1, 1), at(i, 1)) for i in range(spaces - 1)]
 
+    outer = [(t, t + 1) for t in range(1, 2 * spaces - 1, 2)]
+    outer += [(j, i) for i, j in outer]
+
     own = inputs.reshape(chans, held, cols)
     near, far, peer, w_a, w_b = call_pieces(own, w_up)
-    far = lax.ppermute(far, AXES, across)
-    far, near, own, w_conv, w_a, peer, w_b = lax.optimization_barrier((far, near, own, w_conv, w_a, peer, w_b))
+    own, w_conv, peer, w_a, far, near, w_b = lax.optimization_barrier((own, w_conv, peer, w_a, far, near, w_b))
+    peer = lax.ppermute(peer, AXES, across)
     w_a = lax.ppermute(w_a, AXES, across)
-    peer = lax.ppermute(peer, AXES, across)
+    far = lax.ppermute(far, AXES, outer)
+    near = lax.ppermute(near, AXES, chain)
+    x, w_half, kernel, other = call_prepare(True, own, w_up, w_conv, sizes)
+    x, w_a, w_b, near, far = lax.optimization_barrier((x, w_a, w_b, near, far))
     w_b = lax.ppermute(w_b, AXES, across)
-    near = lax.ppermute(near, AXES, chain)
-    far = lax.ppermute(far, AXES, chain)
-    x, w_half, kernel, other = call_prepare(True, own, w_up, w_conv, sizes)
     w_ax = lax.ppermute(w_a, AXES, pairs)
     w_ac = lax.ppermute(w_a, AXES, cores)
     biases = (b_up[None], b_conv[None])

time: 29.8 us -> 26.6 us (0.89)
  starting transfers between devices: 14.3 us -> 12.7 us
  waiting for transfers between devices: 4.96 us -> 3.38 us
    ppermute x2 -> x1, starting transfers between devices: 7.63 us -> 0.66 us  [paired(): far = lax.ppermute(far, AXES, outer)]
    ppermute x1, starting transfers between devices: 1.62 us -> 4.43 us  [paired(): w_ax = lax.ppermute(w_a, AXES, pairs)]
    ppermute x2 -> x1, waiting for transfers between devices: 1.9 us -> 0.01 us  [paired(): far = lax.ppermute(far, AXES, outer)]
    ppermute x1, waiting for transfers between devices: 0.01 us -> 1.37 us  [paired(): w_a = lax.ppermute(w_a, AXES, across)]
    ppermute x1, waiting for transfers between devices: 1.93 us -> 0.88 us  [paired(): w_b = lax.ppermute(w_b, AXES, across)]
    ppermute x1, starting transfers between devices: 2.02 us -> 3.03 us  [paired(): w_a = lax.ppermute(w_a, AXES, across)]
    ppermute x1, starting transfers between devices: 1.25 us -> 2.16 us  [paired(): w_b = lax.ppermute(w_b, AXES, across)]
    ppermute x1, starting transfers between devices: 0.01 us -> 0.37 us  [paired(): w_ac = lax.ppermute(w_a, AXES, cores)]
  transfers between devices with their start and end apart: 10 -> 9, of which waited for: 3 -> 3; matrix products, arithmetic and copies ran while one was open for 0% -> 0% of each run, Pallas kernels for 17% -> 19%
where the time goes in v12:
time: 26.6 us; the launch traced here: 26.4 us
  starting transfers between devices  12.7 us (48%)
  Pallas kernels  10.3 us (39%)
  waiting for transfers between devices  3.38 us (13%)
    ppermute x1, starting transfers between devices, paired(): w_ax = lax.ppermute(w_a, AXES, pairs)  4.43 us
    pallas_call x1, Pallas kernels, call_second(): pl.pallas_call(functools.partial(second, paired, len(parts)), out_shape=j...  4.24 us
    ppermute x1, starting transfers between devices, paired(): w_a = lax.ppermute(w_a, AXES, across)  3.03 us
    pallas_call x1, Pallas kernels, call_first(): pl.pallas_call(body, out_shape=(jax.ShapeDtypeStruct(started.shape, jnp.b...  2.77 us
    ppermute x1, starting transfers between devices, paired(): w_b = lax.ppermute(w_b, AXES, across)  2.16 us
    pallas_call x1, Pallas kernels, call_prepare(): pl.pallas_call(functools.partial(prepare, paired), out_shape=(jax.ShapeDt...  2.13 us
    ppermute x1, starting transfers between devices, paired(): near = lax.ppermute(near, AXES, chain)  1.45 us
    ppermute x1, waiting for transfers between devices, paired(): w_a = lax.ppermute(w_a, AXES, across)  1.37 us
  transfers between devices with their start and end apart: 9, of which 3 were waited for; matrix products, arithmetic and copies ran while one was open for 0% of the time, Pallas kernels for 19%

profile of v12, /device:TPU:0, one launch (start us, length us, event | category | flops | bytes accessed | tf_op | source)
XLA Modules:
  0.0 26.4 jit_solution(16073568048144258177)
XLA Ops:
  0.0 1.1 %shard_map.55 = (bf16[128,128]{1,0:T(8,128)(2,1)S(1)}, bf16[128,128]{1,0:T(8,128)(2,1)S(1)}, bf16[5,128,128]{2,1,0:T(8,128)(2,1)S(1)}, bf16[16,48,128]{2,1,0:T(8,128)(2,1)S(1)}, bf16[16,32,128]{2,1,0:T(8,128)(2,1)S(1)}) custom-call(bf16[128,8,128]{2,1,0:T(8,128)(2,1)} %bitcast.6, bf16[64,64,256]{2,1,0:T(8,128)(2,1)} %w_half_ref.1), custom_call_target="tpu_custom_call" | custom-call | tf_op jit(solution)/shard_map/pallas_call | solution.py:306
  1.1 0.0 copy-start
  1.1 3.0 %collective-permute-start = (bf16[16,48,128]{2,1,0:T(8,128)(2,1)S(1)}, bf16[16,48,128]{2,1,0:T(8,128)(2,1)S(1)}, u32[]{:S(2)}, u32[]{:S(2)}) collective-permute-start(bf16[16,48,128]{2,1,0:T(8,128)(2,1)S(1)} %get-tuple-element.42), channel_id=1, source_target_pairs={{0,1},{1,0},{2,3},{3,2},{4,5},{5,4},{6,7},{7,6},{8,9},{9,8},{10,11... | collective-permute-start | bytes 589832 | tf_op jit(solution)/shard_map/ppermute | solution.py:422
  4.2 0.1 collective-permute-start.6
  4.2 1.4 %collective-permute-start.1 = (bf16[128,128]{1,0:T(8,128)(2,1)S(1)}, bf16[128,128]{1,0:T(8,128)(2,1)S(1)}, u32[]{:S(2)}, u32[]{:S(2)}) collective-permute-start(bf16[128,128]{1,0:T(8,128)(2,1)S(1)} %get-tuple-element.44), channel_id=1, source_target_pairs={{0,2},{2,4},{4,6},{6,8},{8,10},{10,12},{12,14},{14,16},{16,18},{18... | collective-permute-start | bytes 98312 | tf_op jit(solution)/shard_map/ppermute | solution.py:424
  5.7 0.7 %collective-permute-start.2 = (bf16[128,128]{1,0:T(8,128)(2,1)S(1)}, bf16[128,128]{1,0:T(8,128)(2,1)S(1)}, u32[]{:S(2)}, u32[]{:S(2)}) collective-permute-start(bf16[128,128]{1,0:T(8,128)(2,1)S(1)} %get-tuple-element.45), channel_id=1, source_target_pairs={{1,2},{3,4},{5,6},{7,8},{9,10},{11,12},{13,14},{15,16},{17,18},{19... | collective-permute-start | bytes 98312 | tf_op jit(solution)/shard_map/ppermute | solution.py:423
  6.4 2.1 %shard_map.56 = (bf16[3,6,256,128]{3,2,1,0:T(8,128)(2,1)S(1)}, bf16[32,64,256]{2,1,0:T(8,128)(2,1)S(1)}, bf16[256,1152]{1,0:T(8,128)(2,1)S(1)}, bf16[256,1152]{1,0:T(8,128)(2,1)S(1)}) custom-call(bf16[128,8,128]{2,1,0:T(8,128)(2,1)} %bitcast.7, bf16[64,64,256]{2,1,0:T(8,128)(2,1)} %w_half_ref.1, bf16[27,128,128]{2,1,0:T(8,128)(2,1)} %w_conv_ref), custom_call_target="tpu_custom_call" | custom-call | flops 150994944 | bytes 8388608 | tf_op jit(solution)/shard_map/pallas_call | solution.py:339
  8.5 0.0 collective-permute-done.1.near_ref
  8.5 0.0 collective-permute-done.2.far_ref
  8.5 1.4 %collective-permute-done.refs_0_ = bf16[16,48,128]{2,1,0:T(8,128)(2,1)S(1)} collective-permute-done((bf16[16,48,128]{2,1,0:T(8,128)(2,1)S(1)}, bf16[16,48,128]{2,1,0:T(8,128)(2,1)S(1)}, u32[]{:S(2)}, u32[]{:S(2)}) %collective-permute-start) | collective-permute-done | bytes 196640 | tf_op jit(solution)/shard_map/ppermute | solution.py:422
  9.9 4.4 %collective-permute-start.4 = (bf16[16,48,128]{2,1,0:T(8,128)(2,1)S(1)}, bf16[16,48,128]{2,1,0:T(8,128)(2,1)S(1)}, u32[]{:S(2)}, u32[]{:S(2)}) collective-permute-start(bf16[16,48,128]{2,1,0:T(8,128)(2,1)S(1)} %collective-permute-done.refs_0_), channel_id=1, source_target_pairs={{0,4},{1,5},{2,6},{3,7},{4,0},{5,1},{6,2},{7,3},{8,12},{9,13},{10,... | collective-permute-start | bytes 589832 | tf_op jit(solution)/shard_map/ppermute | solution.py:428
  14.3 0.4 %collective-permute-start.5 = (bf16[16,48,128]{2,1,0:T(8,128)(2,1)S(1)}, bf16[16,48,128]{2,1,0:T(8,128)(2,1)S(1)}, u32[]{:S(2)}, u32[]{:S(2)}) collective-permute-start(bf16[16,48,128]{2,1,0:T(8,128)(2,1)S(1)} %collective-permute-done.refs_0_), channel_id=1, source_target_pairs={{0,2},{1,3},{2,0},{3,1},{4,6},{5,7},{6,4},{7,5},{8,10},{9,11},{10,... | collective-permute-start | bytes 589832 | tf_op jit(solution)/shard_map/ppermute | solution.py:429
  14.7 2.2 %collective-permute-start.3 = (bf16[16,32,128]{2,1,0:T(8,128)(2,1)S(1)}, bf16[16,32,128]{2,1,0:T(8,128)(2,1)S(1)}, u32[]{:S(2)}, u32[]{:S(2)}) collective-permute-start(bf16[16,32,128]{2,1,0:T(8,128)(2,1)S(1)} %get-tuple-element.47), channel_id=1, source_target_pairs={{0,1},{1,0},{2,3},{3,2},{4,5},{5,4},{6,7},{7,6},{8,9},{9,8},{10,11... | collective-permute-start | bytes 393224 | tf_op jit(solution)/shard_map/ppermute | solution.py:427
  16.9 0.0 collective-permute-done.6.peer_ref
  16.9 0.0 copy-done
  16.9 0.0 copy-start.1
  16.9 2.8 %shard_map.57 = (bf16[3,6,256,128]{3,2,1,0:T(8,128)(2,1)S(1)}, f32[2,256,1024]{2,1,0:T(8,128)S(1)}) custom-call(bf16[5,128,128]{2,1,0:T(8,128)(2,1)S(1)} %collective-permute-done.6.peer_ref, bf16[128,128]{1,0:T(8,128)(2,1)S(1)} %collective-permute-done.1.near_ref, ...), custom_call_target="tpu_custom_call", output_to_operand_aliasing={{0}: (3, {})} | custom-call | flops 1879048192 | bytes 8388608 | tf_op jit(solution)/shard_map/pallas_call | solution.py:364
  19.6 0.9 %collective-permute-done.3.refs_2_ = bf16[16,32,128]{2,1,0:T(8,128)(2,1)S(1)} collective-permute-done((bf16[16,32,128]{2,1,0:T(8,128)(2,1)S(1)}, bf16[16,32,128]{2,1,0:T(8,128)(2,1)S(1)}, u32[]{:S(2)}, u32[]{:S(2)}) %collective-permute-start.3) | collective-permute-done | bytes 131104 | tf_op jit(solution)/shard_map/ppermute | solution.py:427
  20.5 0.0 collective-permute-done.4.refs_1_
  20.5 0.0 collective-permute-done.5.refs_3_
  20.5 0.0 collective-permute-start.7
  20.5 0.5 %collective-permute-start.8 = (bf16[16,32,128]{2,1,0:T(8,128)(2,1)S(1)}, bf16[16,32,128]{2,1,0:T(8,128)(2,1)S(1)}, u32[]{:S(2)}, u32[]{:S(2)}) collective-permute-start(bf16[16,32,128]{2,1,0:T(8,128)(2,1)S(1)} %collective-permute-done.3.refs_2_), channel_id=1, source_target_pairs={{0,2},{1,3},{2,0},{3,1},{4,6},{5,7},{6,4},{7,5},{8,10},{9,11},{10,... | collective-permute-start | bytes 393224 | tf_op jit(solution)/shard_map/ppermute | solution.py:434
  21.0 1.1 %collective-permute-done.8.refs_5_ = bf16[16,32,128]{2,1,0:T(8,128)(2,1)S(1)} collective-permute-done((bf16[16,32,128]{2,1,0:T(8,128)(2,1)S(1)}, bf16[16,32,128]{2,1,0:T(8,128)(2,1)S(1)}, u32[]{:S(2)}, u32[]{:S(2)}) %collective-permute-start.8) | collective-permute-done | bytes 131104 | tf_op jit(solution)/shard_map/ppermute | solution.py:434
  22.2 0.0 collective-permute-done.7.refs_4_
  22.2 0.0 copy-done.1
  22.2 4.2 %shard_map.58 = bf16[128,2,8,256]{3,2,1,0:T(8,128)(2,1)} custom-call(bf16[16,48,128]{2,1,0:T(8,128)(2,1)S(1)} %collective-permute-done.refs_0_, bf16[16,48,128]{2,1,0:T(8,128)(2,1)S(1)} %collective-permute-done.4.refs_1_, bf16[16,32,128]{2,1,0:T(8,128)(2,1)S(1)} %collective-permute-done.3.refs_2_, bf16[16,48,128]{2,1,0:T(8,128)(2,1)S(1)} %collective-permute-done.5.refs_3_, ...), custom_call_target="tpu_custom_call" | custom-call | flops 1879048192 | bytes 8388608 | tf_op jit(solution)/shard_map/pallas_call | solution.py:384
Async XLA Ops:
  1.1 15.7 %copy-start = (f32[128]{0:T(128)S(1)}, f32[128]{0:T(128)}, u32[]{:S(2)}) copy-start(f32[128]{0:T(128)} %param.7) | copy-start | bytes 1540
  1.1 8.8 %collective-permute-start = (bf16[16,48,128]{2,1,0:T(8,128)(2,1)S(1)}, bf16[16,48,128]{2,1,0:T(8,128)(2,1)S(1)}, u32[]{:S(2)}, u32[]{:S(2)}) collective-permute-start(bf16[16,48,128]{2,1,0:T(8,128)(2,1)S(1)} %get-tuple-element.42), channel_id=1, source_target_pairs={{0,1},{1,0},{2,3},{3,2},{4,5},{5,4},{6,7},{7,6},{8,9},{9,8},{10,11... | collective-permute-start | bytes 589832 | tf_op jit(solution)/shard_map/ppermute | solution.py:422
  4.2 12.7 %collective-permute-start.6 = (bf16[5,128,128]{2,1,0:T(8,128)(2,1)S(1)}, bf16[5,128,128]{2,1,0:T(8,128)(2,1)S(1)}, u32[]{:S(2)}, u32[]{:S(2)}) collective-permute-start(bf16[5,128,128]{2,1,0:T(8,128)(2,1)S(1)} %get-tuple-element.48), channel_id=1, source_target_pairs={{0,1},{1,0},{2,3},{3,2},{4,5},{5,4},{6,7},{7,6},{8,9},{9,8},{10,11... | collective-permute-start | bytes 491528 | tf_op jit(solution)/shard_map/ppermute | solution.py:421
  4.2 4.3 %collective-permute-start.1 = (bf16[128,128]{1,0:T(8,128)(2,1)S(1)}, bf16[128,128]{1,0:T(8,128)(2,1)S(1)}, u32[]{:S(2)}, u32[]{:S(2)}) collective-permute-start(bf16[128,128]{1,0:T(8,128)(2,1)S(1)} %get-tuple-element.44), channel_id=1, source_target_pairs={{0,2},{2,4},{4,6},{6,8},{8,10},{10,12},{12,14},{14,16},{16,18},{18... | collective-permute-start | bytes 98312 | tf_op jit(solution)/shard_map/ppermute | solution.py:424
  5.7 2.8 %collective-permute-start.2 = (bf16[128,128]{1,0:T(8,128)(2,1)S(1)}, bf16[128,128]{1,0:T(8,128)(2,1)S(1)}, u32[]{:S(2)}, u32[]{:S(2)}) collective-permute-start(bf16[128,128]{1,0:T(8,128)(2,1)S(1)} %get-tuple-element.45), channel_id=1, source_target_pairs={{1,2},{3,4},{5,6},{7,8},{9,10},{11,12},{13,14},{15,16},{17,18},{19... | collective-permute-start | bytes 98312 | tf_op jit(solution)/shard_map/ppermute | solution.py:423
  9.9 10.6 %collective-permute-start.4 = (bf16[16,48,128]{2,1,0:T(8,128)(2,1)S(1)}, bf16[16,48,128]{2,1,0:T(8,128)(2,1)S(1)}, u32[]{:S(2)}, u32[]{:S(2)}) collective-permute-start(bf16[16,48,128]{2,1,0:T(8,128)(2,1)S(1)} %collective-permute-done.refs_0_), channel_id=1, source_target_pairs={{0,4},{1,5},{2,6},{3,7},{4,0},{5,1},{6,2},{7,3},{8,12},{9,13},{10,... | collective-permute-start | bytes 589832 | tf_op jit(solution)/shard_map/ppermute | solution.py:428
  14.3 6.2 %collective-permute-start.5 = (bf16[16,48,128]{2,1,0:T(8,128)(2,1)S(1)}, bf16[16,48,128]{2,1,0:T(8,128)(2,1)S(1)}, u32[]{:S(2)}, u32[]{:S(2)}) collective-permute-start(bf16[16,48,128]{2,1,0:T(8,128)(2,1)S(1)} %collective-permute-done.refs_0_), channel_id=1, source_target_pairs={{0,2},{1,3},{2,0},{3,1},{4,6},{5,7},{6,4},{7,5},{8,10},{9,11},{10,... | collective-permute-start | bytes 589832 | tf_op jit(solution)/shard_map/ppermute | solution.py:429
  14.7 5.8 %collective-permute-start.3 = (bf16[16,32,128]{2,1,0:T(8,128)(2,1)S(1)}, bf16[16,32,128]{2,1,0:T(8,128)(2,1)S(1)}, u32[]{:S(2)}, u32[]{:S(2)}) collective-permute-start(bf16[16,32,128]{2,1,0:T(8,128)(2,1)S(1)} %get-tuple-element.47), channel_id=1, source_target_pairs={{0,1},{1,0},{2,3},{3,2},{4,5},{5,4},{6,7},{7,6},{8,9},{9,8},{10,11... | collective-permute-start | bytes 393224 | tf_op jit(solution)/shard_map/ppermute | solution.py:427
  16.9 5.3 %copy-start.1 = (f32[128]{0:T(128)S(1)}, f32[128]{0:T(128)}, u32[]{:S(2)}) copy-start(f32[128]{0:T(128)} %param.9) | copy-start | bytes 1540
  20.5 1.6 %collective-permute-start.7 = (bf16[16,48,128]{2,1,0:T(8,128)(2,1)S(1)}, bf16[16,48,128]{2,1,0:T(8,128)(2,1)S(1)}, u32[]{:S(2)}, u32[]{:S(2)}) collective-permute-start(bf16[16,48,128]{2,1,0:T(8,128)(2,1)S(1)} %collective-permute-done.4.refs_1_), channel_id=1, source_target_pairs={{0,2},{1,3},{2,0},{3,1},{4,6},{5,7},{6,4},{7,5},{8,10},{9,11},{10,... | collective-permute-start | bytes 589832 | tf_op jit(solution)/shard_map/ppermute | solution.py:435
  20.5 1.6 %collective-permute-start.8 = (bf16[16,32,128]{2,1,0:T(8,128)(2,1)S(1)}, bf16[16,32,128]{2,1,0:T(8,128)(2,1)S(1)}, u32[]{:S(2)}, u32[]{:S(2)}) collective-permute-start(bf16[16,32,128]{2,1,0:T(8,128)(2,1)S(1)} %collective-permute-done.3.refs_2_), channel_id=1, source_target_pairs={{0,2},{1,3},{2,0},{3,1},{4,6},{5,7},{6,4},{7,5},{8,10},{9,11},{10,... | collective-permute-start | bytes 393224 | tf_op jit(solution)/shard_map/ppermute | solution.py:434

commit v13 on v12

--- a/solution.py
+++ b/solution.py
@@ -422,11 +422,11 @@
     w_a = lax.ppermute(w_a, AXES, across)
     far = lax.ppermute(far, AXES, outer)
     near = lax.ppermute(near, AXES, chain)
+    w_a, w_b, own, w_conv = lax.optimization_barrier((w_a, w_b, own, w_conv))
+    w_ax = lax.ppermute(w_a, AXES, pairs)
+    w_b = lax.ppermute(w_b, AXES, across)
+    w_ac = lax.ppermute(w_a, AXES, cores)
     x, w_half, kernel, other = call_prepare(True, own, w_up, w_conv, sizes)
-    x, w_a, w_b, near, far = lax.optimization_barrier((x, w_a, w_b, near, far))
-    w_b = lax.ppermute(w_b, AXES, across)
-    w_ax = lax.ppermute(w_a, AXES, pairs)
-    w_ac = lax.ppermute(w_a, AXES, cores)
     biases = (b_up[None], b_conv[None])
     x, total = call_first(paired_first, (peer, near, far), (x, w_half, kernel), biases[0], sizes)
     results = (x, total, other)

time: 26.6 us -> 26.1 us (0.981)
  starting transfers between devices: 12.7 us -> 9.34 us
  waiting for transfers between devices: 3.38 us -> 6.24 us
    ppermute x1, starting transfers between devices: 4.43 us -> 2.03 us  [paired(): w_ax = lax.ppermute(w_a, AXES, pairs)]
    ppermute x1, waiting for transfers between devices: 1.37 us -> 3.52 us  [paired(): w_a = lax.ppermute(w_a, AXES, across)]
    ppermute x1, waiting for transfers between devices: 0.88 us -> 1.59 us  [paired(): w_b = lax.ppermute(w_b, AXES, across)]
    ppermute x1, starting transfers between devices: 2.16 us -> 1.58 us  [paired(): w_b = lax.ppermute(w_b, AXES, across)]
    ppermute x1, starting transfers between devices: 0.37 us -> 0.01 us  [paired(): w_ac = lax.ppermute(w_a, AXES, cores)]
where the time goes in v13:
time: 26.1 us; the launch traced here: 25.9 us
  Pallas kernels  10.3 us (39%)
  starting transfers between devices  9.34 us (36%)
  waiting for transfers between devices  6.24 us (24%)
    pallas_call x1, Pallas kernels, call_second(): pl.pallas_call(functools.partial(second, paired, len(parts)), out_shape=j...  4.24 us
    ppermute x1, waiting for transfers between devices, paired(): w_a = lax.ppermute(w_a, AXES, across)  3.52 us
    ppermute x1, starting transfers between devices, paired(): w_a = lax.ppermute(w_a, AXES, across)  3.03 us
    pallas_call x1, Pallas kernels, call_first(): pl.pallas_call(body, out_shape=(jax.ShapeDtypeStruct(started.shape, jnp.b...  2.78 us
    pallas_call x1, Pallas kernels, call_prepare(): pl.pallas_call(functools.partial(prepare, paired), out_shape=(jax.ShapeDt...  2.12 us
    ppermute x1, starting transfers between devices, paired(): w_ax = lax.ppermute(w_a, AXES, pairs)  2.03 us
    ppermute x1, waiting for transfers between devices, paired(): w_b = lax.ppermute(w_b, AXES, across)  1.59 us
    ppermute x1, starting transfers between devices, paired(): w_b = lax.ppermute(w_b, AXES, across)  1.58 us
  transfers between devices with their start and end apart: 9, of which 3 were waited for; matrix products, arithmetic and copies ran while one was open for 0% of the time, Pallas kernels for 19%

profile of v13, /device:TPU:0, one launch (start us, length us, event | category | flops | bytes accessed | tf_op | source)
XLA Modules:
  0.0 25.9 jit_solution(1931686357255975322)
XLA Ops:
  0.0 1.1 %shard_map.55 = (bf16[128,128]{1,0:T(8,128)(2,1)S(1)}, bf16[128,128]{1,0:T(8,128)(2,1)S(1)}, bf16[5,128,128]{2,1,0:T(8,128)(2,1)S(1)}, bf16[16,48,128]{2,1,0:T(8,128)(2,1)S(1)}, bf16[16,32,128]{2,1,0:T(8,128)(2,1)S(1)}) custom-call(bf16[128,8,128]{2,1,0:T(8,128)(2,1)} %bitcast.6, bf16[64,64,256]{2,1,0:T(8,128)(2,1)} %w_half_ref.1), custom_call_target="tpu_custom_call" | custom-call | tf_op jit(solution)/shard_map/pallas_call | solution.py:306
  1.1 0.0 copy-start
  1.1 3.0 %collective-permute-start = (bf16[16,48,128]{2,1,0:T(8,128)(2,1)S(1)}, bf16[16,48,128]{2,1,0:T(8,128)(2,1)S(1)}, u32[]{:S(2)}, u32[]{:S(2)}) collective-permute-start(bf16[16,48,128]{2,1,0:T(8,128)(2,1)S(1)} %get-tuple-element.38), channel_id=1, source_target_pairs={{0,1},{1,0},{2,3},{3,2},{4,5},{5,4},{6,7},{7,6},{8,9},{9,8},{10,11... | collective-permute-start | bytes 589832 | tf_op jit(solution)/shard_map/ppermute | solution.py:422
  4.2 0.1 collective-permute-start.4
  4.2 1.4 %collective-permute-start.5 = (bf16[128,128]{1,0:T(8,128)(2,1)S(1)}, bf16[128,128]{1,0:T(8,128)(2,1)S(1)}, u32[]{:S(2)}, u32[]{:S(2)}) collective-permute-start(bf16[128,128]{1,0:T(8,128)(2,1)S(1)} %get-tuple-element.45), channel_id=1, source_target_pairs={{0,2},{2,4},{4,6},{6,8},{8,10},{10,12},{12,14},{14,16},{16,18},{18... | collective-permute-start | bytes 98312 | tf_op jit(solution)/shard_map/ppermute | solution.py:424
  5.7 0.7 %collective-permute-start.6 = (bf16[128,128]{1,0:T(8,128)(2,1)S(1)}, bf16[128,128]{1,0:T(8,128)(2,1)S(1)}, u32[]{:S(2)}, u32[]{:S(2)}) collective-permute-start(bf16[128,128]{1,0:T(8,128)(2,1)S(1)} %get-tuple-element.46), channel_id=1, source_target_pairs={{1,2},{3,4},{5,6},{7,8},{9,10},{11,12},{13,14},{15,16},{17,18},{19... | collective-permute-start | bytes 98312 | tf_op jit(solution)/shard_map/ppermute | solution.py:423
  6.4 3.5 %collective-permute-done.refs_0_ = bf16[16,48,128]{2,1,0:T(8,128)(2,1)S(1)} collective-permute-done((bf16[16,48,128]{2,1,0:T(8,128)(2,1)S(1)}, bf16[16,48,128]{2,1,0:T(8,128)(2,1)S(1)}, u32[]{:S(2)}, u32[]{:S(2)}) %collective-permute-start) | collective-permute-done | bytes 196640 | tf_op jit(solution)/shard_map/ppermute | solution.py:422
  9.9 2.0 %collective-permute-start.2 = (bf16[16,48,128]{2,1,0:T(8,128)(2,1)S(1)}, bf16[16,48,128]{2,1,0:T(8,128)(2,1)S(1)}, u32[]{:S(2)}, u32[]{:S(2)}) collective-permute-start(bf16[16,48,128]{2,1,0:T(8,128)(2,1)S(1)} %collective-permute-done.refs_0_), channel_id=1, source_target_pairs={{0,4},{1,5},{2,6},{3,7},{4,0},{5,1},{6,2},{7,3},{8,12},{9,13},{10,... | collective-permute-start | bytes 589832 | tf_op jit(solution)/shard_map/ppermute | solution.py:426
  11.9 0.0 collective-permute-start.3
  11.9 2.1 %shard_map.56 = (bf16[3,6,256,128]{3,2,1,0:T(8,128)(2,1)S(1)}, bf16[32,64,256]{2,1,0:T(8,128)(2,1)S(1)}, bf16[256,1152]{1,0:T(8,128)(2,1)S(1)}, bf16[256,1152]{1,0:T(8,128)(2,1)S(1)}) custom-call(bf16[128,8,128]{2,1,0:T(8,128)(2,1)} %bitcast.7, bf16[64,64,256]{2,1,0:T(8,128)(2,1)} %w_half_ref.1, bf16[27,128,128]{2,1,0:T(8,128)(2,1)} %w_conv_ref), custom_call_target="tpu_custom_call" | custom-call | flops 150994944 | bytes 8388608 | tf_op jit(solution)/shard_map/pallas_call | solution.py:339
  14.1 0.0 collective-permute-done.5.near_ref
  14.1 1.6 %collective-permute-start.1 = (bf16[16,32,128]{2,1,0:T(8,128)(2,1)S(1)}, bf16[16,32,128]{2,1,0:T(8,128)(2,1)S(1)}, u32[]{:S(2)}, u32[]{:S(2)}) collective-permute-start(bf16[16,32,128]{2,1,0:T(8,128)(2,1)S(1)} %get-tuple-element.43), channel_id=1, source_target_pairs={{0,1},{1,0},{2,3},{3,2},{4,5},{5,4},{6,7},{7,6},{8,9},{9,8},{10,11... | collective-permute-start | bytes 393224 | tf_op jit(solution)/shard_map/ppermute | solution.py:427
  15.7 0.0 collective-permute-done.6.far_ref
  15.7 0.0 collective-permute-done.4.peer_ref
  15.7 0.0 copy-done
  15.7 0.0 copy-start.1
  15.7 2.8 %shard_map.57 = (bf16[3,6,256,128]{3,2,1,0:T(8,128)(2,1)S(1)}, f32[2,256,1024]{2,1,0:T(8,128)S(1)}) custom-call(bf16[5,128,128]{2,1,0:T(8,128)(2,1)S(1)} %collective-permute-done.4.peer_ref, bf16[128,128]{1,0:T(8,128)(2,1)S(1)} %collective-permute-done.5.near_ref, ...), custom_call_target="tpu_custom_call", output_to_operand_aliasing={{0}: (3, {})} | custom-call | flops 1879048192 | bytes 8388608 | tf_op jit(solution)/shard_map/pallas_call | solution.py:364
  18.5 1.6 %collective-permute-done.1.refs_2_ = bf16[16,32,128]{2,1,0:T(8,128)(2,1)S(1)} collective-permute-done((bf16[16,32,128]{2,1,0:T(8,128)(2,1)S(1)}, bf16[16,32,128]{2,1,0:T(8,128)(2,1)S(1)}, u32[]{:S(2)}, u32[]{:S(2)}) %collective-permute-start.1) | collective-permute-done | bytes 131104 | tf_op jit(solution)/shard_map/ppermute | solution.py:427
  20.0 0.0 collective-permute-done.2.refs_1_
  20.1 0.0 collective-permute-done.3.refs_3_
  20.1 0.0 collective-permute-start.7
  20.1 0.5 %collective-permute-start.8 = (bf16[16,32,128]{2,1,0:T(8,128)(2,1)S(1)}, bf16[16,32,128]{2,1,0:T(8,128)(2,1)S(1)}, u32[]{:S(2)}, u32[]{:S(2)}) collective-permute-start(bf16[16,32,128]{2,1,0:T(8,128)(2,1)S(1)} %collective-permute-done.1.refs_2_), channel_id=1, source_target_pairs={{0,2},{1,3},{2,0},{3,1},{4,6},{5,7},{6,4},{7,5},{8,10},{9,11},{10,... | collective-permute-start | bytes 393224 | tf_op jit(solution)/shard_map/ppermute | solution.py:434
  20.6 1.1 %collective-permute-done.8.refs_5_ = bf16[16,32,128]{2,1,0:T(8,128)(2,1)S(1)} collective-permute-done((bf16[16,32,128]{2,1,0:T(8,128)(2,1)S(1)}, bf16[16,32,128]{2,1,0:T(8,128)(2,1)S(1)}, u32[]{:S(2)}, u32[]{:S(2)}) %collective-permute-start.8) | collective-permute-done | bytes 131104 | tf_op jit(solution)/shard_map/ppermute | solution.py:434
  21.7 0.0 collective-permute-done.7.refs_4_
  21.7 0.0 copy-done.1
  21.7 4.2 %shard_map.58 = bf16[128,2,8,256]{3,2,1,0:T(8,128)(2,1)} custom-call(bf16[16,48,128]{2,1,0:T(8,128)(2,1)S(1)} %collective-permute-done.refs_0_, bf16[16,48,128]{2,1,0:T(8,128)(2,1)S(1)} %collective-permute-done.2.refs_1_, bf16[16,32,128]{2,1,0:T(8,128)(2,1)S(1)} %collective-permute-done.1.refs_2_, bf16[16,48,128]{2,1,0:T(8,128)(2,1)S(1)} %collective-permute-done.3.refs_3_, ...), custom_call_target="tpu_custom_call" | custom-call | flops 1879048192 | bytes 8388608 | tf_op jit(solution)/shard_map/pallas_call | solution.py:384
Async XLA Ops:
  1.1 14.5 %copy-start = (f32[128]{0:T(128)S(1)}, f32[128]{0:T(128)}, u32[]{:S(2)}) copy-start(f32[128]{0:T(128)} %param.7) | copy-start | bytes 1540
  1.1 8.8 %collective-permute-start = (bf16[16,48,128]{2,1,0:T(8,128)(2,1)S(1)}, bf16[16,48,128]{2,1,0:T(8,128)(2,1)S(1)}, u32[]{:S(2)}, u32[]{:S(2)}) collective-permute-start(bf16[16,48,128]{2,1,0:T(8,128)(2,1)S(1)} %get-tuple-element.38), channel_id=1, source_target_pairs={{0,1},{1,0},{2,3},{3,2},{4,5},{5,4},{6,7},{7,6},{8,9},{9,8},{10,11... | collective-permute-start | bytes 589832 | tf_op jit(solution)/shard_map/ppermute | solution.py:422
  4.2 11.5 %collective-permute-start.4 = (bf16[5,128,128]{2,1,0:T(8,128)(2,1)S(1)}, bf16[5,128,128]{2,1,0:T(8,128)(2,1)S(1)}, u32[]{:S(2)}, u32[]{:S(2)}) collective-permute-start(bf16[5,128,128]{2,1,0:T(8,128)(2,1)S(1)} %get-tuple-element.44), channel_id=1, source_target_pairs={{0,1},{1,0},{2,3},{3,2},{4,5},{5,4},{6,7},{7,6},{8,9},{9,8},{10,11... | collective-permute-start | bytes 491528 | tf_op jit(solution)/shard_map/ppermute | solution.py:421
  4.2 9.8 %collective-permute-start.5 = (bf16[128,128]{1,0:T(8,128)(2,1)S(1)}, bf16[128,128]{1,0:T(8,128)(2,1)S(1)}, u32[]{:S(2)}, u32[]{:S(2)}) collective-permute-start(bf16[128,128]{1,0:T(8,128)(2,1)S(1)} %get-tuple-element.45), channel_id=1, source_target_pairs={{0,2},{2,4},{4,6},{6,8},{8,10},{10,12},{12,14},{14,16},{16,18},{18... | collective-permute-start | bytes 98312 | tf_op jit(solution)/shard_map/ppermute | solution.py:424
  5.7 10.0 %collective-permute-start.6 = (bf16[128,128]{1,0:T(8,128)(2,1)S(1)}, bf16[128,128]{1,0:T(8,128)(2,1)S(1)}, u32[]{:S(2)}, u32[]{:S(2)}) collective-permute-start(bf16[128,128]{1,0:T(8,128)(2,1)S(1)} %get-tuple-element.46), channel_id=1, source_target_pairs={{1,2},{3,4},{5,6},{7,8},{9,10},{11,12},{13,14},{15,16},{17,18},{19... | collective-permute-start | bytes 98312 | tf_op jit(solution)/shard_map/ppermute | solution.py:423
  9.9 10.1 %collective-permute-start.2 = (bf16[16,48,128]{2,1,0:T(8,128)(2,1)S(1)}, bf16[16,48,128]{2,1,0:T(8,128)(2,1)S(1)}, u32[]{:S(2)}, u32[]{:S(2)}) collective-permute-start(bf16[16,48,128]{2,1,0:T(8,128)(2,1)S(1)} %collective-permute-done.refs_0_), channel_id=1, source_target_pairs={{0,4},{1,5},{2,6},{3,7},{4,0},{5,1},{6,2},{7,3},{8,12},{9,13},{10,... | collective-permute-start | bytes 589832 | tf_op jit(solution)/shard_map/ppermute | solution.py:426
  11.9 8.1 %collective-permute-start.3 = (bf16[16,48,128]{2,1,0:T(8,128)(2,1)S(1)}, bf16[16,48,128]{2,1,0:T(8,128)(2,1)S(1)}, u32[]{:S(2)}, u32[]{:S(2)}) collective-permute-start(bf16[16,48,128]{2,1,0:T(8,128)(2,1)S(1)} %collective-permute-done.refs_0_), channel_id=1, source_target_pairs={{0,2},{1,3},{2,0},{3,1},{4,6},{5,7},{6,4},{7,5},{8,10},{9,11},{10,... | collective-permute-start | bytes 589832 | tf_op jit(solution)/shard_map/ppermute | solution.py:428
  14.1 6.0 %collective-permute-start.1 = (bf16[16,32,128]{2,1,0:T(8,128)(2,1)S(1)}, bf16[16,32,128]{2,1,0:T(8,128)(2,1)S(1)}, u32[]{:S(2)}, u32[]{:S(2)}) collective-permute-start(bf16[16,32,128]{2,1,0:T(8,128)(2,1)S(1)} %get-tuple-element.43), channel_id=1, source_target_pairs={{0,1},{1,0},{2,3},{3,2},{4,5},{5,4},{6,7},{7,6},{8,9},{9,8},{10,11... | collective-permute-start | bytes 393224 | tf_op jit(solution)/shard_map/ppermute | solution.py:427
  15.7 6.0 %copy-start.1 = (f32[128]{0:T(128)S(1)}, f32[128]{0:T(128)}, u32[]{:S(2)}) copy-start(f32[128]{0:T(128)} %param.9) | copy-start | bytes 1540
  20.1 1.6 %collective-permute-start.7 = (bf16[16,48,128]{2,1,0:T(8,128)(2,1)S(1)}, bf16[16,48,128]{2,1,0:T(8,128)(2,1)S(1)}, u32[]{:S(2)}, u32[]{:S(2)}) collective-permute-start(bf16[16,48,128]{2,1,0:T(8,128)(2,1)S(1)} %collective-permute-done.2.refs_1_), channel_id=1, source_target_pairs={{0,2},{1,3},{2,0},{3,1},{4,6},{5,7},{6,4},{7,5},{8,10},{9,11},{10,... | collective-permute-start | bytes 589832 | tf_op jit(solution)/shard_map/ppermute | solution.py:435
  20.1 1.6 %collective-permute-start.8 = (bf16[16,32,128]{2,1,0:T(8,128)(2,1)S(1)}, bf16[16,32,128]{2,1,0:T(8,128)(2,1)S(1)}, u32[]{:S(2)}, u32[]{:S(2)}) collective-permute-start(bf16[16,32,128]{2,1,0:T(8,128)(2,1)S(1)} %collective-permute-done.1.refs_2_), channel_id=1, source_target_pairs={{0,2},{1,3},{2,0},{3,1},{4,6},{5,7},{6,4},{7,5},{8,10},{9,11},{10,... | collective-permute-start | bytes 393224 | tf_op jit(solution)/shard_map/ppermute | solution.py:434

commit v14 on v13

--- a/solution.py
+++ b/solution.py
@@ -109,11 +109,8 @@
 def arrival(x, part):
     if x is None:
         return [[(0, part)], [(0, part)]]
-    quarter, half = part // 4, part // 2
-    return [
-        [(x * half, half), ((1 - x) * half, half)],
-        [(x * quarter, quarter), ((1 - x) * quarter, quarter), (half, half)],
-    ]
+    half = part // 2
+    return [[(x * half, half), ((1 - x) * half, half)]] * 2
 
 
 def arrange(x, part):
@@ -215,8 +212,8 @@
 
         def tap_of(tap):
             columns = []
-            for near_ref, far_ref, rest_ref in (parts[:3], parts[3:]):
-                rows = [near_ref[tap, :big], far_ref[tap, :big], near_ref[tap, big:], far_ref[tap, big:], rest_ref[tap]]
+            for near_ref, far_ref in (parts[:2], parts[2:]):
+                rows = [near_ref[tap, :big], far_ref[tap, :big], near_ref[tap, big:], far_ref[tap, big:]]
                 columns.append(jnp.concatenate(rows, axis=0))
             return jnp.concatenate(columns, axis=1)
 
@@ -267,20 +264,17 @@
         copy.wait()
 
 
-def pieces(own_ref, w_up_ref, near_ref, far_ref, peer_ref, w_a_ref, w_b_ref, wide_ref, raw_ref, sems):
+def pieces(own_ref, w_up_ref, near_ref, far_ref, peer_ref, w_a_ref, wide_ref, raw_ref, sems):
     s, c = lax.axis_index("space"), lax.axis_index("ch")
     raw = pltpu.make_async_copy(own_ref, raw_ref, sems.at[3])
     raw.start()
     me = lax.rem(s, 4)
     part, lanes = w_up_ref.shape[1], w_a_ref.shape[2]
     side = pl.ds(pl.multiple_of(lax.rem(me, 2) * lanes, lanes), lanes)
-    (first, big), = arrival(me // 2, part)[0][:1]
-    (second, small), _, (third, rest) = arrival(me // 2, part)[1]
-    cuts = (
-        (16, first, big, w_a_ref.at[:, pl.ds(0, big)]),
-        (32, second, small, w_a_ref.at[:, pl.ds(big, small)]),
-        (32, third, rest, w_b_ref),
-    )
+    cuts = [
+        (16 + 16 * plane, *blocks[0], w_a_ref.at[:, pl.ds(plane * blocks[0][1], blocks[0][1])])
+        for plane, blocks in enumerate(arrival(me // 2, part))
+    ]
     copies = []
     for number, (tap, channel, count, place) in enumerate(cuts):
         source = w_up_ref.at[pl.ds(tap, 16), pl.ds(pl.multiple_of(channel, 16), count), side]
@@ -309,11 +303,10 @@
             jax.ShapeDtypeStruct((chans, cols), jnp.bfloat16),
             jax.ShapeDtypeStruct((chans, cols), jnp.bfloat16),
             jax.ShapeDtypeStruct((rows // 2 + 1, chans, cols), jnp.bfloat16),
-            jax.ShapeDtypeStruct((16, 3 * part // 4, cin // 2), jnp.bfloat16),
-            jax.ShapeDtypeStruct((16, part // 2, cin // 2), jnp.bfloat16),
+            jax.ShapeDtypeStruct((16, part, cin // 2), jnp.bfloat16),
         ),
         in_specs=[ANY, ANY],
-        out_specs=(VMEM,) * 5,
+        out_specs=(VMEM,) * 4,
         scratch_shapes=[
             pltpu.VMEM((chans * rows, cols), jnp.float32),
             pltpu.VMEM((chans, rows, cols), jnp.bfloat16),
@@ -416,24 +409,22 @@
     outer += [(j, i) for i, j in outer]
 
     own = inputs.reshape(chans, held, cols)
-    near, far, peer, w_a, w_b = call_pieces(own, w_up)
-    own, w_conv, peer, w_a, far, near, w_b = lax.optimization_barrier((own, w_conv, peer, w_a, far, near, w_b))
+    near, far, peer, w_a = call_pieces(own, w_up)
+    own, w_conv, peer, w_a, far, near = lax.optimization_barrier((own, w_conv, peer, w_a, far, near))
     peer = lax.ppermute(peer, AXES, across)
     w_a = lax.ppermute(w_a, AXES, across)
     far = lax.ppermute(far, AXES, outer)
     near = lax.ppermute(near, AXES, chain)
-    w_a, w_b, own, w_conv = lax.optimization_barrier((w_a, w_b, own, w_conv))
+    w_a, own, w_conv = lax.optimization_barrier((w_a, own, w_conv))
     w_ax = lax.ppermute(w_a, AXES, pairs)
-    w_b = lax.ppermute(w_b, AXES, across)
     w_ac = lax.ppermute(w_a, AXES, cores)
     x, w_half, kernel, other = call_prepare(True, own, w_up, w_conv, sizes)
     biases = (b_up[None], b_conv[None])
     x, total = call_first(paired_first, (peer, near, far), (x, w_half, kernel), biases[0], sizes)
     results = (x, total, other)
-    w_b, w_ax, w_ac, *results = lax.optimization_barrier((w_b, w_ax, w_ac, *results))
-    w_bc = lax.ppermute(w_b, AXES, cores)
+    w_ax, w_ac, *results = lax.optimization_barrier((w_ax, w_ac, *results))
     w_axc = lax.ppermute(w_ax, AXES, cores)
-    return call_second(True, (w_a, w_ax, w_b, w_ac, w_axc, w_bc), results, biases, sizes)
+    return call_second(True, (w_a, w_ax, w_ac, w_axc), results, biases, sizes)
 
 
 def gathered(inputs, w_up, b_up, w_conv, b_conv, sizes):

time: 26.1 us -> 30.5 us (1.17)
  the two profiles are of different devices: /device:TPU:0 before, /device:TPU:25 now
where the time goes in v14:
time: 30.5 us; the launch traced here: 30.3 us
  starting transfers between devices  13 us (43%)
  Pallas kernels  10.2 us (33%)
  waiting for transfers between devices  6.88 us (23%)
    ppermute x1, waiting for transfers between devices, paired(): w_a = lax.ppermute(w_a, AXES, across)  5.71 us
    pallas_call x1, Pallas kernels, call_second(): pl.pallas_call(functools.partial(second, paired, len(parts)), out_shape=j...  4.24 us
    ppermute x1, starting transfers between devices, paired(): far = lax.ppermute(far, AXES, outer)  3.43 us
    ppermute x1, starting transfers between devices, paired(): w_ac = lax.ppermute(w_a, AXES, cores)  2.97 us
    pallas_call x1, Pallas kernels, call_first(): pl.pallas_call(body, out_shape=(jax.ShapeDtypeStruct(started.shape, jnp.b...  2.77 us
    pallas_call x1, Pallas kernels, call_prepare(): pl.pallas_call(functools.partial(prepare, paired), out_shape=(jax.ShapeDt...  2.12 us
    ppermute x1, starting transfers between devices, paired(): near = lax.ppermute(near, AXES, chain)  2.04 us
    ppermute x1, starting transfers between devices, paired(): w_axc = lax.ppermute(w_ax, AXES, cores)  1.86 us
  transfers between devices with their start and end apart: 7, of which 2 were waited for; matrix products, arithmetic and copies ran while one was open for 0% of the time, Pallas kernels for 16%

profile of v14, /device:TPU:25, one launch (start us, length us, event | category | flops | bytes accessed | tf_op | source)
XLA Modules:
  0.0 30.3 jit_solution(9898068842934590713)
XLA Ops:
  0.0 1.1 %shard_map.55 = (bf16[128,128]{1,0:T(8,128)(2,1)S(1)}, bf16[128,128]{1,0:T(8,128)(2,1)S(1)}, bf16[5,128,128]{2,1,0:T(8,128)(2,1)S(1)}, bf16[16,64,128]{2,1,0:T(8,128)(2,1)S(1)}) custom-call(bf16[128,8,128]{2,1,0:T(8,128)(2,1)} %bitcast.6, bf16[64,64,256]{2,1,0:T(8,128)(2,1)} %w_half_ref.1), custom_call_target="tpu_custom_call" | custom-call | tf_op jit(solution)/shard_map/pallas_call | solution.py:300
  1.1 0.0 copy-start
  1.1 1.3 %collective-permute-start = (bf16[16,64,128]{2,1,0:T(8,128)(2,1)S(1)}, bf16[16,64,128]{2,1,0:T(8,128)(2,1)S(1)}, u32[]{:S(2)}, u32[]{:S(2)}) collective-permute-start(bf16[16,64,128]{2,1,0:T(8,128)(2,1)S(1)} %get-tuple-element.33), channel_id=1, source_target_pairs={{0,1},{1,0},{2,3},{3,2},{4,5},{5,4},{6,7},{7,6},{8,9},{9,8},{10,11... | collective-permute-start | bytes 786440 | tf_op jit(solution)/shard_map/ppermute | solution.py:415
  2.4 0.2 collective-permute-start.3
  2.7 5.7 %collective-permute-done.refs_0_ = bf16[16,64,128]{2,1,0:T(8,128)(2,1)S(1)} collective-permute-done((bf16[16,64,128]{2,1,0:T(8,128)(2,1)S(1)}, bf16[16,64,128]{2,1,0:T(8,128)(2,1)S(1)}, u32[]{:S(2)}, u32[]{:S(2)}) %collective-permute-start) | collective-permute-done | bytes 262176 | tf_op jit(solution)/shard_map/ppermute | solution.py:415
  8.4 1.2 %collective-permute-start.1 = (bf16[16,64,128]{2,1,0:T(8,128)(2,1)S(1)}, bf16[16,64,128]{2,1,0:T(8,128)(2,1)S(1)}, u32[]{:S(2)}, u32[]{:S(2)}) collective-permute-start(bf16[16,64,128]{2,1,0:T(8,128)(2,1)S(1)} %collective-permute-done.refs_0_), channel_id=1, source_target_pairs={{0,4},{1,5},{2,6},{3,7},{4,0},{5,1},{6,2},{7,3},{8,12},{9,13},{10,... | collective-permute-start | bytes 786440 | tf_op jit(solution)/shard_map/ppermute | solution.py:419
  9.6 3.0 %collective-permute-start.2 = (bf16[16,64,128]{2,1,0:T(8,128)(2,1)S(1)}, bf16[16,64,128]{2,1,0:T(8,128)(2,1)S(1)}, u32[]{:S(2)}, u32[]{:S(2)}) collective-permute-start(bf16[16,64,128]{2,1,0:T(8,128)(2,1)S(1)} %collective-permute-done.refs_0_), channel_id=1, source_target_pairs={{0,2},{1,3},{2,0},{3,1},{4,6},{5,7},{6,4},{7,5},{8,10},{9,11},{10,... | collective-permute-start | bytes 786440 | tf_op jit(solution)/shard_map/ppermute | solution.py:420
  12.6 2.0 %collective-permute-start.4 = (bf16[128,128]{1,0:T(8,128)(2,1)S(1)}, bf16[128,128]{1,0:T(8,128)(2,1)S(1)}, u32[]{:S(2)}, u32[]{:S(2)}) collective-permute-start(bf16[128,128]{1,0:T(8,128)(2,1)S(1)} %get-tuple-element.38), channel_id=1, source_target_pairs={{0,2},{2,4},{4,6},{6,8},{8,10},{10,12},{12,14},{14,16},{16,18},{18... | collective-permute-start | bytes 98312 | tf_op jit(solution)/shard_map/ppermute | solution.py:417
  14.6 3.4 %collective-permute-start.5 = (bf16[128,128]{1,0:T(8,128)(2,1)S(1)}, bf16[128,128]{1,0:T(8,128)(2,1)S(1)}, u32[]{:S(2)}, u32[]{:S(2)}) collective-permute-start(bf16[128,128]{1,0:T(8,128)(2,1)S(1)} %get-tuple-element.39), channel_id=1, source_target_pairs={{1,2},{3,4},{5,6},{7,8},{9,10},{11,12},{13,14},{15,16},{17,18},{19... | collective-permute-start | bytes 98312 | tf_op jit(solution)/shard_map/ppermute | solution.py:416
  18.0 2.1 %shard_map.56 = (bf16[3,6,256,128]{3,2,1,0:T(8,128)(2,1)S(1)}, bf16[32,64,256]{2,1,0:T(8,128)(2,1)S(1)}, bf16[256,1152]{1,0:T(8,128)(2,1)S(1)}, bf16[256,1152]{1,0:T(8,128)(2,1)S(1)}) custom-call(bf16[128,8,128]{2,1,0:T(8,128)(2,1)} %bitcast.7, bf16[64,64,256]{2,1,0:T(8,128)(2,1)} %w_half_ref.1, bf16[27,128,128]{2,1,0:T(8,128)(2,1)} %w_conv_ref), custom_call_target="tpu_custom_call" | custom-call | flops 150994944 | bytes 8388608 | tf_op jit(solution)/shard_map/pallas_call | solution.py:332
  20.2 0.0 collective-permute-done.4.near_ref
  20.2 0.0 collective-permute-done.5.far_ref
  20.2 0.0 collective-permute-done.3.peer_ref
  20.2 0.0 copy-done
  20.2 0.0 copy-start.1
  20.2 2.8 %shard_map.57 = (bf16[3,6,256,128]{3,2,1,0:T(8,128)(2,1)S(1)}, f32[2,256,1024]{2,1,0:T(8,128)S(1)}) custom-call(bf16[5,128,128]{2,1,0:T(8,128)(2,1)S(1)} %collective-permute-done.3.peer_ref, bf16[128,128]{1,0:T(8,128)(2,1)S(1)} %collective-permute-done.4.near_ref, ...), custom_call_target="tpu_custom_call", output_to_operand_aliasing={{0}: (3, {})} | custom-call | flops 1879048192 | bytes 8388608 | tf_op jit(solution)/shard_map/pallas_call | solution.py:357
  23.0 0.0 collective-permute-done.1.refs_1_
  23.0 0.0 collective-permute-done.2.refs_2_
  23.0 1.9 %collective-permute-start.6 = (bf16[16,64,128]{2,1,0:T(8,128)(2,1)S(1)}, bf16[16,64,128]{2,1,0:T(8,128)(2,1)S(1)}, u32[]{:S(2)}, u32[]{:S(2)}) collective-permute-start(bf16[16,64,128]{2,1,0:T(8,128)(2,1)S(1)} %collective-permute-done.1.refs_1_), channel_id=1, source_target_pairs={{0,2},{1,3},{2,0},{3,1},{4,6},{5,7},{6,4},{7,5},{8,10},{9,11},{10,... | collective-permute-start | bytes 786440 | tf_op jit(solution)/shard_map/ppermute | solution.py:426
  24.9 1.2 %collective-permute-done.6.refs_3_ = bf16[16,64,128]{2,1,0:T(8,128)(2,1)S(1)} collective-permute-done((bf16[16,64,128]{2,1,0:T(8,128)(2,1)S(1)}, bf16[16,64,128]{2,1,0:T(8,128)(2,1)S(1)}, u32[]{:S(2)}, u32[]{:S(2)}) %collective-permute-start.6) | collective-permute-done | bytes 262176 | tf_op jit(solution)/shard_map/ppermute | solution.py:426
  26.0 0.0 copy-done.1
  26.1 4.2 %shard_map.58 = bf16[128,2,8,256]{3,2,1,0:T(8,128)(2,1)} custom-call(bf16[16,64,128]{2,1,0:T(8,128)(2,1)S(1)} %collective-permute-done.refs_0_, bf16[16,64,128]{2,1,0:T(8,128)(2,1)S(1)} %collective-permute-done.1.refs_1_, bf16[16,64,128]{2,1,0:T(8,128)(2,1)S(1)} %collective-permute-done.2.refs_2_, bf16[16,64,128]{2,1,0:T(8,128)(2,1)S(1)} %collective-permute-done.6.refs_3_, ...), custom_call_target="tpu_custom_call" | custom-call | flops 1879048192 | bytes 8388608 | tf_op jit(solution)/shard_map/pallas_call | solution.py:377
Async XLA Ops:
  1.1 19.1 %copy-start = (f32[128]{0:T(128)S(1)}, f32[128]{0:T(128)}, u32[]{:S(2)}) copy-start(f32[128]{0:T(128)} %param.7) | copy-start | bytes 1540
  1.1 7.2 %collective-permute-start = (bf16[16,64,128]{2,1,0:T(8,128)(2,1)S(1)}, bf16[16,64,128]{2,1,0:T(8,128)(2,1)S(1)}, u32[]{:S(2)}, u32[]{:S(2)}) collective-permute-start(bf16[16,64,128]{2,1,0:T(8,128)(2,1)S(1)} %get-tuple-element.33), channel_id=1, source_target_pairs={{0,1},{1,0},{2,3},{3,2},{4,5},{5,4},{6,7},{7,6},{8,9},{9,8},{10,11... | collective-permute-start | bytes 786440 | tf_op jit(solution)/shard_map/ppermute | solution.py:415
  2.4 17.8 %collective-permute-start.3 = (bf16[5,128,128]{2,1,0:T(8,128)(2,1)S(1)}, bf16[5,128,128]{2,1,0:T(8,128)(2,1)S(1)}, u32[]{:S(2)}, u32[]{:S(2)}) collective-permute-start(bf16[5,128,128]{2,1,0:T(8,128)(2,1)S(1)} %get-tuple-element.37), channel_id=1, source_target_pairs={{0,1},{1,0},{2,3},{3,2},{4,5},{5,4},{6,7},{7,6},{8,9},{9,8},{10,11... | collective-permute-start | bytes 491528 | tf_op jit(solution)/shard_map/ppermute | solution.py:414
  8.4 14.6 %collective-permute-start.1 = (bf16[16,64,128]{2,1,0:T(8,128)(2,1)S(1)}, bf16[16,64,128]{2,1,0:T(8,128)(2,1)S(1)}, u32[]{:S(2)}, u32[]{:S(2)}) collective-permute-start(bf16[16,64,128]{2,1,0:T(8,128)(2,1)S(1)} %collective-permute-done.refs_0_), channel_id=1, source_target_pairs={{0,4},{1,5},{2,6},{3,7},{4,0},{5,1},{6,2},{7,3},{8,12},{9,13},{10,... | collective-permute-start | bytes 786440 | tf_op jit(solution)/shard_map/ppermute | solution.py:419
  9.6 13.4 %collective-permute-start.2 = (bf16[16,64,128]{2,1,0:T(8,128)(2,1)S(1)}, bf16[16,64,128]{2,1,0:T(8,128)(2,1)S(1)}, u32[]{:S(2)}, u32[]{:S(2)}) collective-permute-start(bf16[16,64,128]{2,1,0:T(8,128)(2,1)S(1)} %collective-permute-done.refs_0_), channel_id=1, source_target_pairs={{0,2},{1,3},{2,0},{3,1},{4,6},{5,7},{6,4},{7,5},{8,10},{9,11},{10,... | collective-permute-start | bytes 786440 | tf_op jit(solution)/shard_map/ppermute | solution.py:420
  12.6 7.6 %collective-permute-start.4 = (bf16[128,128]{1,0:T(8,128)(2,1)S(1)}, bf16[128,128]{1,0:T(8,128)(2,1)S(1)}, u32[]{:S(2)}, u32[]{:S(2)}) collective-permute-start(bf16[128,128]{1,0:T(8,128)(2,1)S(1)} %get-tuple-element.38), channel_id=1, source_target_pairs={{0,2},{2,4},{4,6},{6,8},{8,10},{10,12},{12,14},{14,16},{16,18},{18... | collective-permute-start | bytes 98312 | tf_op jit(solution)/shard_map/ppermute | solution.py:417
  14.6 5.6 %collective-permute-start.5 = (bf16[128,128]{1,0:T(8,128)(2,1)S(1)}, bf16[128,128]{1,0:T(8,128)(2,1)S(1)}, u32[]{:S(2)}, u32[]{:S(2)}) collective-permute-start(bf16[128,128]{1,0:T(8,128)(2,1)S(1)} %get-tuple-element.39), channel_id=1, source_target_pairs={{1,2},{3,4},{5,6},{7,8},{9,10},{11,12},{13,14},{15,16},{17,18},{19... | collective-permute-start | bytes 98312 | tf_op jit(solution)/shard_map/ppermute | solution.py:416
  20.2 5.8 %copy-start.1 = (f32[128]{0:T(128)S(1)}, f32[128]{0:T(128)}, u32[]{:S(2)}) copy-start(f32[128]{0:T(128)} %param.9) | copy-start | bytes 1540
  23.0 3.0 %collective-permute-start.6 = (bf16[16,64,128]{2,1,0:T(8,128)(2,1)S(1)}, bf16[16,64,128]{2,1,0:T(8,128)(2,1)S(1)}, u32[]{:S(2)}, u32[]{:S(2)}) collective-permute-start(bf16[16,64,128]{2,1,0:T(8,128)(2,1)S(1)} %collective-permute-done.1.refs_1_), channel_id=1, source_target_pairs={{0,2},{1,3},{2,0},{3,1},{4,6},{5,7},{6,4},{7,5},{8,10},{9,11},{10,... | collective-permute-start | bytes 786440 | tf_op jit(solution)/shard_map/ppermute | solution.py:426

commit v15 on v13

--- a/solution.py
+++ b/solution.py
@@ -24,7 +24,7 @@
     cols = value.shape[1]
     place = lax.broadcasted_iota(jnp.int32, value.shape, 1)
     edge = 0 if step == 1 else cols - 1
-    return jnp.where(place == edge, 0.0, pltpu.roll(value, step % cols, 1))
+    return jnp.where(place == edge, jnp.zeros_like(value), pltpu.roll(value, step % cols, 1))
 
 
 def upsample(cell, tap_of, bias, u_ref, first, last):
@@ -55,9 +55,9 @@
                         value = jnp.where(first, 0.0, value)
                     if row == held - 1:
                         value = jnp.where(last, 0.0, value)
-                    u_ref[col_phase, row] = value.astype(jnp.bfloat16)
-                    moved = shifted(value, -1 if col_phase == 0 else 1)
-                    u_ref[2 + col_phase, row] = moved.astype(jnp.bfloat16)
+                    value = value.astype(jnp.bfloat16)
+                    u_ref[col_phase, row] = value
+                    u_ref[2 + col_phase, row] = shifted(value, -1 if col_phase == 0 else 1)
 
 
 def convolve(kernel, u_ref, start, col_phase):

time: 26.1 us -> 26.1 us (level)
  no operation moved by 1% of the time
where the time goes in v15:
time: 26.1 us; the launch traced here: 25.9 us
  Pallas kernels  10.3 us (39%)
  starting transfers between devices  9.34 us (36%)
  waiting for transfers between devices  6.24 us (24%)
    pallas_call x1, Pallas kernels, call_second(): pl.pallas_call(functools.partial(second, paired, len(parts)), out_shape=j...  4.24 us
    ppermute x1, waiting for transfers between devices, paired(): w_a = lax.ppermute(w_a, AXES, across)  3.52 us
    ppermute x1, starting transfers between devices, paired(): w_a = lax.ppermute(w_a, AXES, across)  3.03 us
    pallas_call x1, Pallas kernels, call_first(): pl.pallas_call(body, out_shape=(jax.ShapeDtypeStruct(started.shape, jnp.b...  2.78 us
    pallas_call x1, Pallas kernels, call_prepare(): pl.pallas_call(functools.partial(prepare, paired), out_shape=(jax.ShapeDt...  2.12 us
    ppermute x1, starting transfers between devices, paired(): w_ax = lax.ppermute(w_a, AXES, pairs)  2.03 us
    ppermute x1, starting transfers between devices, paired(): w_b = lax.ppermute(w_b, AXES, across)  1.58 us
    ppermute x1, waiting for transfers between devices, paired(): w_b = lax.ppermute(w_b, AXES, across)  1.58 us
  transfers between devices with their start and end apart: 9, of which 3 were waited for; matrix products, arithmetic and copies ran while one was open for 0% of the time, Pallas kernels for 19%

profile of v15, /device:TPU:0, one launch (start us, length us, event | category | flops | bytes accessed | tf_op | source)
XLA Modules:
  0.0 25.9 jit_solution(12580838632413579111)
XLA Ops:
  0.0 1.1 %shard_map.55 = (bf16[128,128]{1,0:T(8,128)(2,1)S(1)}, bf16[128,128]{1,0:T(8,128)(2,1)S(1)}, bf16[5,128,128]{2,1,0:T(8,128)(2,1)S(1)}, bf16[16,48,128]{2,1,0:T(8,128)(2,1)S(1)}, bf16[16,32,128]{2,1,0:T(8,128)(2,1)S(1)}) custom-call(bf16[128,8,128]{2,1,0:T(8,128)(2,1)} %bitcast.6, bf16[64,64,256]{2,1,0:T(8,128)(2,1)} %w_half_ref.1), custom_call_target="tpu_custom_call" | custom-call | tf_op jit(solution)/shard_map/pallas_call | solution.py:306
  1.1 0.0 copy-start
  1.1 3.0 %collective-permute-start = (bf16[16,48,128]{2,1,0:T(8,128)(2,1)S(1)}, bf16[16,48,128]{2,1,0:T(8,128)(2,1)S(1)}, u32[]{:S(2)}, u32[]{:S(2)}) collective-permute-start(bf16[16,48,128]{2,1,0:T(8,128)(2,1)S(1)} %get-tuple-element.38), channel_id=1, source_target_pairs={{0,1},{1,0},{2,3},{3,2},{4,5},{5,4},{6,7},{7,6},{8,9},{9,8},{10,11... | collective-permute-start | bytes 589832 | tf_op jit(solution)/shard_map/ppermute | solution.py:422
  4.2 0.1 collective-permute-start.4
  4.2 1.4 %collective-permute-start.5 = (bf16[128,128]{1,0:T(8,128)(2,1)S(1)}, bf16[128,128]{1,0:T(8,128)(2,1)S(1)}, u32[]{:S(2)}, u32[]{:S(2)}) collective-permute-start(bf16[128,128]{1,0:T(8,128)(2,1)S(1)} %get-tuple-element.45), channel_id=1, source_target_pairs={{0,2},{2,4},{4,6},{6,8},{8,10},{10,12},{12,14},{14,16},{16,18},{18... | collective-permute-start | bytes 98312 | tf_op jit(solution)/shard_map/ppermute | solution.py:424
  5.7 0.7 %collective-permute-start.6 = (bf16[128,128]{1,0:T(8,128)(2,1)S(1)}, bf16[128,128]{1,0:T(8,128)(2,1)S(1)}, u32[]{:S(2)}, u32[]{:S(2)}) collective-permute-start(bf16[128,128]{1,0:T(8,128)(2,1)S(1)} %get-tuple-element.46), channel_id=1, source_target_pairs={{1,2},{3,4},{5,6},{7,8},{9,10},{11,12},{13,14},{15,16},{17,18},{19... | collective-permute-start | bytes 98312 | tf_op jit(solution)/shard_map/ppermute | solution.py:423
  6.4 3.5 %collective-permute-done.refs_0_ = bf16[16,48,128]{2,1,0:T(8,128)(2,1)S(1)} collective-permute-done((bf16[16,48,128]{2,1,0:T(8,128)(2,1)S(1)}, bf16[16,48,128]{2,1,0:T(8,128)(2,1)S(1)}, u32[]{:S(2)}, u32[]{:S(2)}) %collective-permute-start) | collective-permute-done | bytes 196640 | tf_op jit(solution)/shard_map/ppermute | solution.py:422
  9.9 2.0 %collective-permute-start.2 = (bf16[16,48,128]{2,1,0:T(8,128)(2,1)S(1)}, bf16[16,48,128]{2,1,0:T(8,128)(2,1)S(1)}, u32[]{:S(2)}, u32[]{:S(2)}) collective-permute-start(bf16[16,48,128]{2,1,0:T(8,128)(2,1)S(1)} %collective-permute-done.refs_0_), channel_id=1, source_target_pairs={{0,4},{1,5},{2,6},{3,7},{4,0},{5,1},{6,2},{7,3},{8,12},{9,13},{10,... | collective-permute-start | bytes 589832 | tf_op jit(solution)/shard_map/ppermute | solution.py:426
  11.9 0.0 collective-permute-start.3
  11.9 2.1 %shard_map.56 = (bf16[3,6,256,128]{3,2,1,0:T(8,128)(2,1)S(1)}, bf16[32,64,256]{2,1,0:T(8,128)(2,1)S(1)}, bf16[256,1152]{1,0:T(8,128)(2,1)S(1)}, bf16[256,1152]{1,0:T(8,128)(2,1)S(1)}) custom-call(bf16[128,8,128]{2,1,0:T(8,128)(2,1)} %bitcast.7, bf16[64,64,256]{2,1,0:T(8,128)(2,1)} %w_half_ref.1, bf16[27,128,128]{2,1,0:T(8,128)(2,1)} %w_conv_ref), custom_call_target="tpu_custom_call" | custom-call | flops 150994944 | bytes 8388608 | tf_op jit(solution)/shard_map/pallas_call | solution.py:339
  14.1 0.0 collective-permute-done.5.near_ref
  14.1 1.6 %collective-permute-start.1 = (bf16[16,32,128]{2,1,0:T(8,128)(2,1)S(1)}, bf16[16,32,128]{2,1,0:T(8,128)(2,1)S(1)}, u32[]{:S(2)}, u32[]{:S(2)}) collective-permute-start(bf16[16,32,128]{2,1,0:T(8,128)(2,1)S(1)} %get-tuple-element.43), channel_id=1, source_target_pairs={{0,1},{1,0},{2,3},{3,2},{4,5},{5,4},{6,7},{7,6},{8,9},{9,8},{10,11... | collective-permute-start | bytes 393224 | tf_op jit(solution)/shard_map/ppermute | solution.py:427
  15.7 0.0 collective-permute-done.6.far_ref
  15.7 0.0 collective-permute-done.4.peer_ref
  15.7 0.0 copy-done
  15.7 0.0 copy-start.1
  15.7 2.8 %shard_map.57 = (bf16[3,6,256,128]{3,2,1,0:T(8,128)(2,1)S(1)}, f32[2,256,1024]{2,1,0:T(8,128)S(1)}) custom-call(bf16[5,128,128]{2,1,0:T(8,128)(2,1)S(1)} %collective-permute-done.4.peer_ref, bf16[128,128]{1,0:T(8,128)(2,1)S(1)} %collective-permute-done.5.near_ref, ...), custom_call_target="tpu_custom_call", output_to_operand_aliasing={{0}: (3, {})} | custom-call | flops 1879048192 | bytes 8388608 | tf_op jit(solution)/shard_map/pallas_call | solution.py:364
  18.5 1.6 %collective-permute-done.1.refs_2_ = bf16[16,32,128]{2,1,0:T(8,128)(2,1)S(1)} collective-permute-done((bf16[16,32,128]{2,1,0:T(8,128)(2,1)S(1)}, bf16[16,32,128]{2,1,0:T(8,128)(2,1)S(1)}, u32[]{:S(2)}, u32[]{:S(2)}) %collective-permute-start.1) | collective-permute-done | bytes 131104 | tf_op jit(solution)/shard_map/ppermute | solution.py:427
  20.0 0.0 collective-permute-done.2.refs_1_
  20.1 0.0 collective-permute-done.3.refs_3_
  20.1 0.0 collective-permute-start.7
  20.1 0.5 %collective-permute-start.8 = (bf16[16,32,128]{2,1,0:T(8,128)(2,1)S(1)}, bf16[16,32,128]{2,1,0:T(8,128)(2,1)S(1)}, u32[]{:S(2)}, u32[]{:S(2)}) collective-permute-start(bf16[16,32,128]{2,1,0:T(8,128)(2,1)S(1)} %collective-permute-done.1.refs_2_), channel_id=1, source_target_pairs={{0,2},{1,3},{2,0},{3,1},{4,6},{5,7},{6,4},{7,5},{8,10},{9,11},{10,... | collective-permute-start | bytes 393224 | tf_op jit(solution)/shard_map/ppermute | solution.py:434
  20.6 1.1 %collective-permute-done.8.refs_5_ = bf16[16,32,128]{2,1,0:T(8,128)(2,1)S(1)} collective-permute-done((bf16[16,32,128]{2,1,0:T(8,128)(2,1)S(1)}, bf16[16,32,128]{2,1,0:T(8,128)(2,1)S(1)}, u32[]{:S(2)}, u32[]{:S(2)}) %collective-permute-start.8) | collective-permute-done | bytes 131104 | tf_op jit(solution)/shard_map/ppermute | solution.py:434
  21.7 0.0 collective-permute-done.7.refs_4_
  21.7 0.0 copy-done.1
  21.7 4.2 %shard_map.58 = bf16[128,2,8,256]{3,2,1,0:T(8,128)(2,1)} custom-call(bf16[16,48,128]{2,1,0:T(8,128)(2,1)S(1)} %collective-permute-done.refs_0_, bf16[16,48,128]{2,1,0:T(8,128)(2,1)S(1)} %collective-permute-done.2.refs_1_, bf16[16,32,128]{2,1,0:T(8,128)(2,1)S(1)} %collective-permute-done.1.refs_2_, bf16[16,48,128]{2,1,0:T(8,128)(2,1)S(1)} %collective-permute-done.3.refs_3_, ...), custom_call_target="tpu_custom_call" | custom-call | flops 1879048192 | bytes 8388608 | tf_op jit(solution)/shard_map/pallas_call | solution.py:384
Async XLA Ops:
  1.1 14.5 %copy-start = (f32[128]{0:T(128)S(1)}, f32[128]{0:T(128)}, u32[]{:S(2)}) copy-start(f32[128]{0:T(128)} %param.7) | copy-start | bytes 1540
  1.1 8.8 %collective-permute-start = (bf16[16,48,128]{2,1,0:T(8,128)(2,1)S(1)}, bf16[16,48,128]{2,1,0:T(8,128)(2,1)S(1)}, u32[]{:S(2)}, u32[]{:S(2)}) collective-permute-start(bf16[16,48,128]{2,1,0:T(8,128)(2,1)S(1)} %get-tuple-element.38), channel_id=1, source_target_pairs={{0,1},{1,0},{2,3},{3,2},{4,5},{5,4},{6,7},{7,6},{8,9},{9,8},{10,11... | collective-permute-start | bytes 589832 | tf_op jit(solution)/shard_map/ppermute | solution.py:422
  4.2 11.5 %collective-permute-start.4 = (bf16[5,128,128]{2,1,0:T(8,128)(2,1)S(1)}, bf16[5,128,128]{2,1,0:T(8,128)(2,1)S(1)}, u32[]{:S(2)}, u32[]{:S(2)}) collective-permute-start(bf16[5,128,128]{2,1,0:T(8,128)(2,1)S(1)} %get-tuple-element.44), channel_id=1, source_target_pairs={{0,1},{1,0},{2,3},{3,2},{4,5},{5,4},{6,7},{7,6},{8,9},{9,8},{10,11... | collective-permute-start | bytes 491528 | tf_op jit(solution)/shard_map/ppermute | solution.py:421
  4.2 9.8 %collective-permute-start.5 = (bf16[128,128]{1,0:T(8,128)(2,1)S(1)}, bf16[128,128]{1,0:T(8,128)(2,1)S(1)}, u32[]{:S(2)}, u32[]{:S(2)}) collective-permute-start(bf16[128,128]{1,0:T(8,128)(2,1)S(1)} %get-tuple-element.45), channel_id=1, source_target_pairs={{0,2},{2,4},{4,6},{6,8},{8,10},{10,12},{12,14},{14,16},{16,18},{18... | collective-permute-start | bytes 98312 | tf_op jit(solution)/shard_map/ppermute | solution.py:424
  5.7 10.0 %collective-permute-start.6 = (bf16[128,128]{1,0:T(8,128)(2,1)S(1)}, bf16[128,128]{1,0:T(8,128)(2,1)S(1)}, u32[]{:S(2)}, u32[]{:S(2)}) collective-permute-start(bf16[128,128]{1,0:T(8,128)(2,1)S(1)} %get-tuple-element.46), channel_id=1, source_target_pairs={{1,2},{3,4},{5,6},{7,8},{9,10},{11,12},{13,14},{15,16},{17,18},{19... | collective-permute-start | bytes 98312 | tf_op jit(solution)/shard_map/ppermute | solution.py:423
  9.9 10.1 %collective-permute-start.2 = (bf16[16,48,128]{2,1,0:T(8,128)(2,1)S(1)}, bf16[16,48,128]{2,1,0:T(8,128)(2,1)S(1)}, u32[]{:S(2)}, u32[]{:S(2)}) collective-permute-start(bf16[16,48,128]{2,1,0:T(8,128)(2,1)S(1)} %collective-permute-done.refs_0_), channel_id=1, source_target_pairs={{0,4},{1,5},{2,6},{3,7},{4,0},{5,1},{6,2},{7,3},{8,12},{9,13},{10,... | collective-permute-start | bytes 589832 | tf_op jit(solution)/shard_map/ppermute | solution.py:426
  11.9 8.1 %collective-permute-start.3 = (bf16[16,48,128]{2,1,0:T(8,128)(2,1)S(1)}, bf16[16,48,128]{2,1,0:T(8,128)(2,1)S(1)}, u32[]{:S(2)}, u32[]{:S(2)}) collective-permute-start(bf16[16,48,128]{2,1,0:T(8,128)(2,1)S(1)} %collective-permute-done.refs_0_), channel_id=1, source_target_pairs={{0,2},{1,3},{2,0},{3,1},{4,6},{5,7},{6,4},{7,5},{8,10},{9,11},{10,... | collective-permute-start | bytes 589832 | tf_op jit(solution)/shard_map/ppermute | solution.py:428
  14.1 6.0 %collective-permute-start.1 = (bf16[16,32,128]{2,1,0:T(8,128)(2,1)S(1)}, bf16[16,32,128]{2,1,0:T(8,128)(2,1)S(1)}, u32[]{:S(2)}, u32[]{:S(2)}) collective-permute-start(bf16[16,32,128]{2,1,0:T(8,128)(2,1)S(1)} %get-tuple-element.43), channel_id=1, source_target_pairs={{0,1},{1,0},{2,3},{3,2},{4,5},{5,4},{6,7},{7,6},{8,9},{9,8},{10,11... | collective-permute-start | bytes 393224 | tf_op jit(solution)/shard_map/ppermute | solution.py:427
  15.7 6.0 %copy-start.1 = (f32[128]{0:T(128)S(1)}, f32[128]{0:T(128)}, u32[]{:S(2)}) copy-start(f32[128]{0:T(128)} %param.9) | copy-start | bytes 1540
  20.1 1.6 %collective-permute-start.7 = (bf16[16,48,128]{2,1,0:T(8,128)(2,1)S(1)}, bf16[16,48,128]{2,1,0:T(8,128)(2,1)S(1)}, u32[]{:S(2)}, u32[]{:S(2)}) collective-permute-start(bf16[16,48,128]{2,1,0:T(8,128)(2,1)S(1)} %collective-permute-done.2.refs_1_), channel_id=1, source_target_pairs={{0,2},{1,3},{2,0},{3,1},{4,6},{5,7},{6,4},{7,5},{8,10},{9,11},{10,... | collective-permute-start | bytes 589832 | tf_op jit(solution)/shard_map/ppermute | solution.py:435
  20.1 1.6 %collective-permute-start.8 = (bf16[16,32,128]{2,1,0:T(8,128)(2,1)S(1)}, bf16[16,32,128]{2,1,0:T(8,128)(2,1)S(1)}, u32[]{:S(2)}, u32[]{:S(2)}) collective-permute-start(bf16[16,32,128]{2,1,0:T(8,128)(2,1)S(1)} %collective-permute-done.1.refs_2_), channel_id=1, source_target_pairs={{0,2},{1,3},{2,0},{3,1},{4,6},{5,7},{6,4},{7,5},{8,10},{9,11},{10,... | collective-permute-start | bytes 393224 | tf_op jit(solution)/shard_map/ppermute | solution.py:434

commit v16 on v15

--- a/solution.py
+++ b/solution.py
@@ -430,9 +430,10 @@
     biases = (b_up[None], b_conv[None])
     x, total = call_first(paired_first, (peer, near, far), (x, w_half, kernel), biases[0], sizes)
     results = (x, total, other)
-    w_b, w_ax, w_ac, *results = lax.optimization_barrier((w_b, w_ax, w_ac, *results))
+    w_ax, w_ac, *results = lax.optimization_barrier((w_ax, w_ac, *results))
+    w_axc = lax.ppermute(w_ax, AXES, cores)
+    w_b, *results = lax.optimization_barrier((w_b, *results))
     w_bc = lax.ppermute(w_b, AXES, cores)
-    w_axc = lax.ppermute(w_ax, AXES, cores)
     return call_second(True, (w_a, w_ax, w_b, w_ac, w_axc, w_bc), results, biases, sizes)
 
 

time: 26.1 us -> 25.8 us (0.989)
    ppermute x1, starting transfers between devices: 0.5 us -> 0.01 us  [paired(): w_bc = lax.ppermute(w_b, AXES, cores)]
    ppermute x1, waiting for transfers between devices: 1.58 us -> 1.27 us  [paired(): w_b = lax.ppermute(w_b, AXES, across)]
    ppermute x1, starting transfers between devices: 0.01 us -> 0.29 us  [paired(): w_axc = lax.ppermute(w_ax, AXES, cores)]
where the time goes in v16:
time: 25.8 us; the launch traced here: 25.6 us
  Pallas kernels  10.3 us (40%)
  starting transfers between devices  9.13 us (35%)
  waiting for transfers between devices  6.16 us (24%)
    pallas_call x1, Pallas kernels, call_second(): pl.pallas_call(functools.partial(second, paired, len(parts)), out_shape=j...  4.24 us
    ppermute x1, waiting for transfers between devices, paired(): w_a = lax.ppermute(w_a, AXES, across)  3.52 us
    ppermute x1, starting transfers between devices, paired(): w_a = lax.ppermute(w_a, AXES, across)  3.03 us
    pallas_call x1, Pallas kernels, call_first(): pl.pallas_call(body, out_shape=(jax.ShapeDtypeStruct(started.shape, jnp.b...  2.78 us
    pallas_call x1, Pallas kernels, call_prepare(): pl.pallas_call(functools.partial(prepare, paired), out_shape=(jax.ShapeDt...  2.12 us
    ppermute x1, starting transfers between devices, paired(): w_ax = lax.ppermute(w_a, AXES, pairs)  2.03 us
    ppermute x1, starting transfers between devices, paired(): w_b = lax.ppermute(w_b, AXES, across)  1.58 us
    ppermute x1, starting transfers between devices, paired(): near = lax.ppermute(near, AXES, chain)  1.45 us
  transfers between devices with their start and end apart: 9, of which 3 were waited for; matrix products, arithmetic and copies ran while one was open for 0% of the time, Pallas kernels for 19%

profile of v16, /device:TPU:0, one launch (start us, length us, event | category | flops | bytes accessed | tf_op | source)
XLA Modules:
  0.0 25.6 jit_solution(15337145270739398198)
XLA Ops:
  0.0 1.1 %shard_map.55 = (bf16[128,128]{1,0:T(8,128)(2,1)S(1)}, bf16[128,128]{1,0:T(8,128)(2,1)S(1)}, bf16[5,128,128]{2,1,0:T(8,128)(2,1)S(1)}, bf16[16,48,128]{2,1,0:T(8,128)(2,1)S(1)}, bf16[16,32,128]{2,1,0:T(8,128)(2,1)S(1)}) custom-call(bf16[128,8,128]{2,1,0:T(8,128)(2,1)} %bitcast.6, bf16[64,64,256]{2,1,0:T(8,128)(2,1)} %w_half_ref.1), custom_call_target="tpu_custom_call" | custom-call | tf_op jit(solution)/shard_map/pallas_call | solution.py:306
  1.1 0.0 copy-start
  1.1 3.0 %collective-permute-start = (bf16[16,48,128]{2,1,0:T(8,128)(2,1)S(1)}, bf16[16,48,128]{2,1,0:T(8,128)(2,1)S(1)}, u32[]{:S(2)}, u32[]{:S(2)}) collective-permute-start(bf16[16,48,128]{2,1,0:T(8,128)(2,1)S(1)} %get-tuple-element.41), channel_id=1, source_target_pairs={{0,1},{1,0},{2,3},{3,2},{4,5},{5,4},{6,7},{7,6},{8,9},{9,8},{10,11... | collective-permute-start | bytes 589832 | tf_op jit(solution)/shard_map/ppermute | solution.py:422
  4.2 0.1 collective-permute-start.3
  4.2 1.4 %collective-permute-start.4 = (bf16[128,128]{1,0:T(8,128)(2,1)S(1)}, bf16[128,128]{1,0:T(8,128)(2,1)S(1)}, u32[]{:S(2)}, u32[]{:S(2)}) collective-permute-start(bf16[128,128]{1,0:T(8,128)(2,1)S(1)} %get-tuple-element.47), channel_id=1, source_target_pairs={{0,2},{2,4},{4,6},{6,8},{8,10},{10,12},{12,14},{14,16},{16,18},{18... | collective-permute-start | bytes 98312 | tf_op jit(solution)/shard_map/ppermute | solution.py:424
  5.7 0.7 %collective-permute-start.5 = (bf16[128,128]{1,0:T(8,128)(2,1)S(1)}, bf16[128,128]{1,0:T(8,128)(2,1)S(1)}, u32[]{:S(2)}, u32[]{:S(2)}) collective-permute-start(bf16[128,128]{1,0:T(8,128)(2,1)S(1)} %get-tuple-element.48), channel_id=1, source_target_pairs={{1,2},{3,4},{5,6},{7,8},{9,10},{11,12},{13,14},{15,16},{17,18},{19... | collective-permute-start | bytes 98312 | tf_op jit(solution)/shard_map/ppermute | solution.py:423
  6.4 3.5 %collective-permute-done.refs_0_ = bf16[16,48,128]{2,1,0:T(8,128)(2,1)S(1)} collective-permute-done((bf16[16,48,128]{2,1,0:T(8,128)(2,1)S(1)}, bf16[16,48,128]{2,1,0:T(8,128)(2,1)S(1)}, u32[]{:S(2)}, u32[]{:S(2)}) %collective-permute-start) | collective-permute-done | bytes 196640 | tf_op jit(solution)/shard_map/ppermute | solution.py:422
  9.9 2.0 %collective-permute-start.1 = (bf16[16,48,128]{2,1,0:T(8,128)(2,1)S(1)}, bf16[16,48,128]{2,1,0:T(8,128)(2,1)S(1)}, u32[]{:S(2)}, u32[]{:S(2)}) collective-permute-start(bf16[16,48,128]{2,1,0:T(8,128)(2,1)S(1)} %collective-permute-done.refs_0_), channel_id=1, source_target_pairs={{0,4},{1,5},{2,6},{3,7},{4,0},{5,1},{6,2},{7,3},{8,12},{9,13},{10,... | collective-permute-start | bytes 589832 | tf_op jit(solution)/shard_map/ppermute | solution.py:426
  11.9 0.0 collective-permute-start.2
  11.9 2.1 %shard_map.56 = (bf16[3,6,256,128]{3,2,1,0:T(8,128)(2,1)S(1)}, bf16[32,64,256]{2,1,0:T(8,128)(2,1)S(1)}, bf16[256,1152]{1,0:T(8,128)(2,1)S(1)}, bf16[256,1152]{1,0:T(8,128)(2,1)S(1)}) custom-call(bf16[128,8,128]{2,1,0:T(8,128)(2,1)} %bitcast.7, bf16[64,64,256]{2,1,0:T(8,128)(2,1)} %w_half_ref.1, bf16[27,128,128]{2,1,0:T(8,128)(2,1)} %w_conv_ref), custom_call_target="tpu_custom_call" | custom-call | flops 150994944 | bytes 8388608 | tf_op jit(solution)/shard_map/pallas_call | solution.py:339
  14.1 0.0 collective-permute-done.4.near_ref
  14.1 1.6 %collective-permute-start.6 = (bf16[16,32,128]{2,1,0:T(8,128)(2,1)S(1)}, bf16[16,32,128]{2,1,0:T(8,128)(2,1)S(1)}, u32[]{:S(2)}, u32[]{:S(2)}) collective-permute-start(bf16[16,32,128]{2,1,0:T(8,128)(2,1)S(1)} %get-tuple-element.58), channel_id=1, source_target_pairs={{0,1},{1,0},{2,3},{3,2},{4,5},{5,4},{6,7},{7,6},{8,9},{9,8},{10,11... | collective-permute-start | bytes 393224 | tf_op jit(solution)/shard_map/ppermute | solution.py:427
  15.7 0.0 collective-permute-done.5.far_ref
  15.7 0.0 collective-permute-done.3.peer_ref
  15.7 0.0 copy-done
  15.7 0.0 copy-start.1
  15.7 2.8 %shard_map.57 = (bf16[3,6,256,128]{3,2,1,0:T(8,128)(2,1)S(1)}, f32[2,256,1024]{2,1,0:T(8,128)S(1)}) custom-call(bf16[5,128,128]{2,1,0:T(8,128)(2,1)S(1)} %collective-permute-done.3.peer_ref, bf16[128,128]{1,0:T(8,128)(2,1)S(1)} %collective-permute-done.4.near_ref, ...), custom_call_target="tpu_custom_call", output_to_operand_aliasing={{0}: (3, {})} | custom-call | flops 1879048192 | bytes 8388608 | tf_op jit(solution)/shard_map/pallas_call | solution.py:364
  18.5 0.0 collective-permute-done.1.refs_1_
  18.5 0.0 collective-permute-done.2.refs_3_
  18.5 0.3 %collective-permute-start.7 = (bf16[16,48,128]{2,1,0:T(8,128)(2,1)S(1)}, bf16[16,48,128]{2,1,0:T(8,128)(2,1)S(1)}, u32[]{:S(2)}, u32[]{:S(2)}) collective-permute-start(bf16[16,48,128]{2,1,0:T(8,128)(2,1)S(1)} %collective-permute-done.1.refs_1_), channel_id=1, source_target_pairs={{0,2},{1,3},{2,0},{3,1},{4,6},{5,7},{6,4},{7,5},{8,10},{9,11},{10,... | collective-permute-start | bytes 589832 | tf_op jit(solution)/shard_map/ppermute | solution.py:434
  18.8 1.3 %collective-permute-done.6.refs_2_ = bf16[16,32,128]{2,1,0:T(8,128)(2,1)S(1)} collective-permute-done((bf16[16,32,128]{2,1,0:T(8,128)(2,1)S(1)}, bf16[16,32,128]{2,1,0:T(8,128)(2,1)S(1)}, u32[]{:S(2)}, u32[]{:S(2)}) %collective-permute-start.6) | collective-permute-done | bytes 131104 | tf_op jit(solution)/shard_map/ppermute | solution.py:427
  20.0 0.0 collective-permute-start.8
  20.1 1.3 %collective-permute-done.8.refs_5_ = bf16[16,32,128]{2,1,0:T(8,128)(2,1)S(1)} collective-permute-done((bf16[16,32,128]{2,1,0:T(8,128)(2,1)S(1)}, bf16[16,32,128]{2,1,0:T(8,128)(2,1)S(1)}, u32[]{:S(2)}, u32[]{:S(2)}) %collective-permute-start.8) | collective-permute-done | bytes 131104 | tf_op jit(solution)/shard_map/ppermute | solution.py:436
  21.4 0.0 collective-permute-done.7.refs_4_
  21.4 0.0 copy-done.1
  21.4 4.2 %shard_map.58 = bf16[128,2,8,256]{3,2,1,0:T(8,128)(2,1)} custom-call(bf16[16,48,128]{2,1,0:T(8,128)(2,1)S(1)} %collective-permute-done.refs_0_, bf16[16,48,128]{2,1,0:T(8,128)(2,1)S(1)} %collective-permute-done.1.refs_1_, bf16[16,32,128]{2,1,0:T(8,128)(2,1)S(1)} %collective-permute-done.6.refs_2_, bf16[16,48,128]{2,1,0:T(8,128)(2,1)S(1)} %collective-permute-done.2.refs_3_, ...), custom_call_target="tpu_custom_call" | custom-call | flops 1879048192 | bytes 8388608 | tf_op jit(solution)/shard_map/pallas_call | solution.py:384
Async XLA Ops:
  1.1 14.5 %copy-start = (f32[128]{0:T(128)S(1)}, f32[128]{0:T(128)}, u32[]{:S(2)}) copy-start(f32[128]{0:T(128)} %param.7) | copy-start | bytes 1540
  1.1 8.8 %collective-permute-start = (bf16[16,48,128]{2,1,0:T(8,128)(2,1)S(1)}, bf16[16,48,128]{2,1,0:T(8,128)(2,1)S(1)}, u32[]{:S(2)}, u32[]{:S(2)}) collective-permute-start(bf16[16,48,128]{2,1,0:T(8,128)(2,1)S(1)} %get-tuple-element.41), channel_id=1, source_target_pairs={{0,1},{1,0},{2,3},{3,2},{4,5},{5,4},{6,7},{7,6},{8,9},{9,8},{10,11... | collective-permute-start | bytes 589832 | tf_op jit(solution)/shard_map/ppermute | solution.py:422
  4.2 11.5 %collective-permute-start.3 = (bf16[5,128,128]{2,1,0:T(8,128)(2,1)S(1)}, bf16[5,128,128]{2,1,0:T(8,128)(2,1)S(1)}, u32[]{:S(2)}, u32[]{:S(2)}) collective-permute-start(bf16[5,128,128]{2,1,0:T(8,128)(2,1)S(1)} %get-tuple-element.46), channel_id=1, source_target_pairs={{0,1},{1,0},{2,3},{3,2},{4,5},{5,4},{6,7},{7,6},{8,9},{9,8},{10,11... | collective-permute-start | bytes 491528 | tf_op jit(solution)/shard_map/ppermute | solution.py:421
  4.2 9.8 %collective-permute-start.4 = (bf16[128,128]{1,0:T(8,128)(2,1)S(1)}, bf16[128,128]{1,0:T(8,128)(2,1)S(1)}, u32[]{:S(2)}, u32[]{:S(2)}) collective-permute-start(bf16[128,128]{1,0:T(8,128)(2,1)S(1)} %get-tuple-element.47), channel_id=1, source_target_pairs={{0,2},{2,4},{4,6},{6,8},{8,10},{10,12},{12,14},{14,16},{16,18},{18... | collective-permute-start | bytes 98312 | tf_op jit(solution)/shard_map/ppermute | solution.py:424
  5.7 10.0 %collective-permute-start.5 = (bf16[128,128]{1,0:T(8,128)(2,1)S(1)}, bf16[128,128]{1,0:T(8,128)(2,1)S(1)}, u32[]{:S(2)}, u32[]{:S(2)}) collective-permute-start(bf16[128,128]{1,0:T(8,128)(2,1)S(1)} %get-tuple-element.48), channel_id=1, source_target_pairs={{1,2},{3,4},{5,6},{7,8},{9,10},{11,12},{13,14},{15,16},{17,18},{19... | collective-permute-start | bytes 98312 | tf_op jit(solution)/shard_map/ppermute | solution.py:423
  9.9 8.6 %collective-permute-start.1 = (bf16[16,48,128]{2,1,0:T(8,128)(2,1)S(1)}, bf16[16,48,128]{2,1,0:T(8,128)(2,1)S(1)}, u32[]{:S(2)}, u32[]{:S(2)}) collective-permute-start(bf16[16,48,128]{2,1,0:T(8,128)(2,1)S(1)} %collective-permute-done.refs_0_), channel_id=1, source_target_pairs={{0,4},{1,5},{2,6},{3,7},{4,0},{5,1},{6,2},{7,3},{8,12},{9,13},{10,... | collective-permute-start | bytes 589832 | tf_op jit(solution)/shard_map/ppermute | solution.py:426
  11.9 6.5 %collective-permute-start.2 = (bf16[16,48,128]{2,1,0:T(8,128)(2,1)S(1)}, bf16[16,48,128]{2,1,0:T(8,128)(2,1)S(1)}, u32[]{:S(2)}, u32[]{:S(2)}) collective-permute-start(bf16[16,48,128]{2,1,0:T(8,128)(2,1)S(1)} %collective-permute-done.refs_0_), channel_id=1, source_target_pairs={{0,2},{1,3},{2,0},{3,1},{4,6},{5,7},{6,4},{7,5},{8,10},{9,11},{10,... | collective-permute-start | bytes 589832 | tf_op jit(solution)/shard_map/ppermute | solution.py:428
  14.1 6.0 %collective-permute-start.6 = (bf16[16,32,128]{2,1,0:T(8,128)(2,1)S(1)}, bf16[16,32,128]{2,1,0:T(8,128)(2,1)S(1)}, u32[]{:S(2)}, u32[]{:S(2)}) collective-permute-start(bf16[16,32,128]{2,1,0:T(8,128)(2,1)S(1)} %get-tuple-element.58), channel_id=1, source_target_pairs={{0,1},{1,0},{2,3},{3,2},{4,5},{5,4},{6,7},{7,6},{8,9},{9,8},{10,11... | collective-permute-start | bytes 393224 | tf_op jit(solution)/shard_map/ppermute | solution.py:427
  15.7 5.7 %copy-start.1 = (f32[128]{0:T(128)S(1)}, f32[128]{0:T(128)}, u32[]{:S(2)}) copy-start(f32[128]{0:T(128)} %param.9) | copy-start | bytes 1540
  18.5 2.9 %collective-permute-start.7 = (bf16[16,48,128]{2,1,0:T(8,128)(2,1)S(1)}, bf16[16,48,128]{2,1,0:T(8,128)(2,1)S(1)}, u32[]{:S(2)}, u32[]{:S(2)}) collective-permute-start(bf16[16,48,128]{2,1,0:T(8,128)(2,1)S(1)} %collective-permute-done.1.refs_1_), channel_id=1, source_target_pairs={{0,2},{1,3},{2,0},{3,1},{4,6},{5,7},{6,4},{7,5},{8,10},{9,11},{10,... | collective-permute-start | bytes 589832 | tf_op jit(solution)/shard_map/ppermute | solution.py:434
  20.0 1.3 %collective-permute-start.8 = (bf16[16,32,128]{2,1,0:T(8,128)(2,1)S(1)}, bf16[16,32,128]{2,1,0:T(8,128)(2,1)S(1)}, u32[]{:S(2)}, u32[]{:S(2)}) collective-permute-start(bf16[16,32,128]{2,1,0:T(8,128)(2,1)S(1)} %collective-permute-done.6.refs_2_), channel_id=1, source_target_pairs={{0,2},{1,3},{2,0},{3,1},{4,6},{5,7},{6,4},{7,5},{8,10},{9,11},{10,... | collective-permute-start | bytes 393224 | tf_op jit(solution)/shard_map/ppermute | solution.py:436

commit v17 on v16

--- a/solution.py
+++ b/solution.py
@@ -37,8 +37,7 @@
                     slot = row_shift + 1 - row_phase
                     taps.append((row_tap * 4 + col_tap, slot, col_shift % 3))
             kernel = jnp.concatenate([tap_of(tap) for tap, _, _ in taps], axis=1)
-            for start in range(0, held // 2, 2):
-                places = range(start, min(start + 2, held // 2))
+            for places in (range(held // 2),):
                 cells = jnp.concatenate(
                     [
                         jnp.concatenate([cell(copy, slot + place) for place in places], axis=1)

time: 25.8 us -> 25.8 us (level)
  no operation moved by 1% of the time
where the time goes in v17:
time: 25.8 us; the launch traced here: 25.6 us
  Pallas kernels  10.3 us (40%)
  starting transfers between devices  9.13 us (35%)
  waiting for transfers between devices  6.16 us (24%)
    pallas_call x1, Pallas kernels, call_second(): pl.pallas_call(functools.partial(second, paired, len(parts)), out_shape=j...  4.25 us
    ppermute x1, waiting for transfers between devices, paired(): w_a = lax.ppermute(w_a, AXES, across)  3.52 us
    ppermute x1, starting transfers between devices, paired(): w_a = lax.ppermute(w_a, AXES, across)  3.03 us
    pallas_call x1, Pallas kernels, call_first(): pl.pallas_call(body, out_shape=(jax.ShapeDtypeStruct(started.shape, jnp.b...  2.78 us
    pallas_call x1, Pallas kernels, call_prepare(): pl.pallas_call(functools.partial(prepare, paired), out_shape=(jax.ShapeDt...  2.12 us
    ppermute x1, starting transfers between devices, paired(): w_ax = lax.ppermute(w_a, AXES, pairs)  2.03 us
    ppermute x1, starting transfers between devices, paired(): w_b = lax.ppermute(w_b, AXES, across)  1.58 us
    ppermute x1, starting transfers between devices, paired(): near = lax.ppermute(near, AXES, chain)  1.45 us
  transfers between devices with their start and end apart: 9, of which 3 were waited for; matrix products, arithmetic and copies ran while one was open for 0% of the time, Pallas kernels for 19%

profile of v17, /device:TPU:0, one launch (start us, length us, event | category | flops | bytes accessed | tf_op | source)
XLA Modules:
  0.0 25.6 jit_solution(2277769925278753116)
XLA Ops:
  0.0 1.1 %shard_map.55 = (bf16[128,128]{1,0:T(8,128)(2,1)S(1)}, bf16[128,128]{1,0:T(8,128)(2,1)S(1)}, bf16[5,128,128]{2,1,0:T(8,128)(2,1)S(1)}, bf16[16,48,128]{2,1,0:T(8,128)(2,1)S(1)}, bf16[16,32,128]{2,1,0:T(8,128)(2,1)S(1)}) custom-call(bf16[128,8,128]{2,1,0:T(8,128)(2,1)} %bitcast.6, bf16[64,64,256]{2,1,0:T(8,128)(2,1)} %w_half_ref.1), custom_call_target="tpu_custom_call" | custom-call | tf_op jit(solution)/shard_map/pallas_call | solution.py:305
  1.1 0.0 copy-start
  1.1 3.0 %collective-permute-start = (bf16[16,48,128]{2,1,0:T(8,128)(2,1)S(1)}, bf16[16,48,128]{2,1,0:T(8,128)(2,1)S(1)}, u32[]{:S(2)}, u32[]{:S(2)}) collective-permute-start(bf16[16,48,128]{2,1,0:T(8,128)(2,1)S(1)} %get-tuple-element.41), channel_id=1, source_target_pairs={{0,1},{1,0},{2,3},{3,2},{4,5},{5,4},{6,7},{7,6},{8,9},{9,8},{10,11... | collective-permute-start | bytes 589832 | tf_op jit(solution)/shard_map/ppermute | solution.py:421
  4.2 0.1 collective-permute-start.3
  4.2 1.4 %collective-permute-start.4 = (bf16[128,128]{1,0:T(8,128)(2,1)S(1)}, bf16[128,128]{1,0:T(8,128)(2,1)S(1)}, u32[]{:S(2)}, u32[]{:S(2)}) collective-permute-start(bf16[128,128]{1,0:T(8,128)(2,1)S(1)} %get-tuple-element.47), channel_id=1, source_target_pairs={{0,2},{2,4},{4,6},{6,8},{8,10},{10,12},{12,14},{14,16},{16,18},{18... | collective-permute-start | bytes 98312 | tf_op jit(solution)/shard_map/ppermute | solution.py:423
  5.7 0.7 %collective-permute-start.5 = (bf16[128,128]{1,0:T(8,128)(2,1)S(1)}, bf16[128,128]{1,0:T(8,128)(2,1)S(1)}, u32[]{:S(2)}, u32[]{:S(2)}) collective-permute-start(bf16[128,128]{1,0:T(8,128)(2,1)S(1)} %get-tuple-element.48), channel_id=1, source_target_pairs={{1,2},{3,4},{5,6},{7,8},{9,10},{11,12},{13,14},{15,16},{17,18},{19... | collective-permute-start | bytes 98312 | tf_op jit(solution)/shard_map/ppermute | solution.py:422
  6.4 3.5 %collective-permute-done.refs_0_ = bf16[16,48,128]{2,1,0:T(8,128)(2,1)S(1)} collective-permute-done((bf16[16,48,128]{2,1,0:T(8,128)(2,1)S(1)}, bf16[16,48,128]{2,1,0:T(8,128)(2,1)S(1)}, u32[]{:S(2)}, u32[]{:S(2)}) %collective-permute-start) | collective-permute-done | bytes 196640 | tf_op jit(solution)/shard_map/ppermute | solution.py:421
  9.9 2.0 %collective-permute-start.1 = (bf16[16,48,128]{2,1,0:T(8,128)(2,1)S(1)}, bf16[16,48,128]{2,1,0:T(8,128)(2,1)S(1)}, u32[]{:S(2)}, u32[]{:S(2)}) collective-permute-start(bf16[16,48,128]{2,1,0:T(8,128)(2,1)S(1)} %collective-permute-done.refs_0_), channel_id=1, source_target_pairs={{0,4},{1,5},{2,6},{3,7},{4,0},{5,1},{6,2},{7,3},{8,12},{9,13},{10,... | collective-permute-start | bytes 589832 | tf_op jit(solution)/shard_map/ppermute | solution.py:425
  11.9 0.0 collective-permute-start.2
  11.9 2.1 %shard_map.56 = (bf16[3,6,256,128]{3,2,1,0:T(8,128)(2,1)S(1)}, bf16[32,64,256]{2,1,0:T(8,128)(2,1)S(1)}, bf16[256,1152]{1,0:T(8,128)(2,1)S(1)}, bf16[256,1152]{1,0:T(8,128)(2,1)S(1)}) custom-call(bf16[128,8,128]{2,1,0:T(8,128)(2,1)} %bitcast.7, bf16[64,64,256]{2,1,0:T(8,128)(2,1)} %w_half_ref.1, bf16[27,128,128]{2,1,0:T(8,128)(2,1)} %w_conv_ref), custom_call_target="tpu_custom_call" | custom-call | flops 150994944 | bytes 8388608 | tf_op jit(solution)/shard_map/pallas_call | solution.py:338
  14.1 0.0 collective-permute-done.4.near_ref
  14.1 1.6 %collective-permute-start.6 = (bf16[16,32,128]{2,1,0:T(8,128)(2,1)S(1)}, bf16[16,32,128]{2,1,0:T(8,128)(2,1)S(1)}, u32[]{:S(2)}, u32[]{:S(2)}) collective-permute-start(bf16[16,32,128]{2,1,0:T(8,128)(2,1)S(1)} %get-tuple-element.58), channel_id=1, source_target_pairs={{0,1},{1,0},{2,3},{3,2},{4,5},{5,4},{6,7},{7,6},{8,9},{9,8},{10,11... | collective-permute-start | bytes 393224 | tf_op jit(solution)/shard_map/ppermute | solution.py:426
  15.7 0.0 collective-permute-done.5.far_ref
  15.7 0.0 collective-permute-done.3.peer_ref
  15.7 0.0 copy-done
  15.7 0.0 copy-start.1
  15.7 2.8 %shard_map.57 = (bf16[3,6,256,128]{3,2,1,0:T(8,128)(2,1)S(1)}, f32[2,256,1024]{2,1,0:T(8,128)S(1)}) custom-call(bf16[5,128,128]{2,1,0:T(8,128)(2,1)S(1)} %collective-permute-done.3.peer_ref, bf16[128,128]{1,0:T(8,128)(2,1)S(1)} %collective-permute-done.4.near_ref, ...), custom_call_target="tpu_custom_call", output_to_operand_aliasing={{0}: (3, {})} | custom-call | flops 1879048192 | bytes 8388608 | tf_op jit(solution)/shard_map/pallas_call | solution.py:363
  18.5 0.0 collective-permute-done.1.refs_1_
  18.5 0.0 collective-permute-done.2.refs_3_
  18.5 0.3 %collective-permute-start.7 = (bf16[16,48,128]{2,1,0:T(8,128)(2,1)S(1)}, bf16[16,48,128]{2,1,0:T(8,128)(2,1)S(1)}, u32[]{:S(2)}, u32[]{:S(2)}) collective-permute-start(bf16[16,48,128]{2,1,0:T(8,128)(2,1)S(1)} %collective-permute-done.1.refs_1_), channel_id=1, source_target_pairs={{0,2},{1,3},{2,0},{3,1},{4,6},{5,7},{6,4},{7,5},{8,10},{9,11},{10,... | collective-permute-start | bytes 589832 | tf_op jit(solution)/shard_map/ppermute | solution.py:433
  18.8 1.3 %collective-permute-done.6.refs_2_ = bf16[16,32,128]{2,1,0:T(8,128)(2,1)S(1)} collective-permute-done((bf16[16,32,128]{2,1,0:T(8,128)(2,1)S(1)}, bf16[16,32,128]{2,1,0:T(8,128)(2,1)S(1)}, u32[]{:S(2)}, u32[]{:S(2)}) %collective-permute-start.6) | collective-permute-done | bytes 131104 | tf_op jit(solution)/shard_map/ppermute | solution.py:426
  20.0 0.0 collective-permute-start.8
  20.1 1.3 %collective-permute-done.8.refs_5_ = bf16[16,32,128]{2,1,0:T(8,128)(2,1)S(1)} collective-permute-done((bf16[16,32,128]{2,1,0:T(8,128)(2,1)S(1)}, bf16[16,32,128]{2,1,0:T(8,128)(2,1)S(1)}, u32[]{:S(2)}, u32[]{:S(2)}) %collective-permute-start.8) | collective-permute-done | bytes 131104 | tf_op jit(solution)/shard_map/ppermute | solution.py:435
  21.4 0.0 collective-permute-done.7.refs_4_
  21.4 0.0 copy-done.1
  21.4 4.2 %shard_map.58 = bf16[128,2,8,256]{3,2,1,0:T(8,128)(2,1)} custom-call(bf16[16,48,128]{2,1,0:T(8,128)(2,1)S(1)} %collective-permute-done.refs_0_, bf16[16,48,128]{2,1,0:T(8,128)(2,1)S(1)} %collective-permute-done.1.refs_1_, bf16[16,32,128]{2,1,0:T(8,128)(2,1)S(1)} %collective-permute-done.6.refs_2_, bf16[16,48,128]{2,1,0:T(8,128)(2,1)S(1)} %collective-permute-done.2.refs_3_, ...), custom_call_target="tpu_custom_call" | custom-call | flops 1879048192 | bytes 8388608 | tf_op jit(solution)/shard_map/pallas_call | solution.py:383
Async XLA Ops:
  1.1 14.5 %copy-start = (f32[128]{0:T(128)S(1)}, f32[128]{0:T(128)}, u32[]{:S(2)}) copy-start(f32[128]{0:T(128)} %param.7) | copy-start | bytes 1540
  1.1 8.8 %collective-permute-start = (bf16[16,48,128]{2,1,0:T(8,128)(2,1)S(1)}, bf16[16,48,128]{2,1,0:T(8,128)(2,1)S(1)}, u32[]{:S(2)}, u32[]{:S(2)}) collective-permute-start(bf16[16,48,128]{2,1,0:T(8,128)(2,1)S(1)} %get-tuple-element.41), channel_id=1, source_target_pairs={{0,1},{1,0},{2,3},{3,2},{4,5},{5,4},{6,7},{7,6},{8,9},{9,8},{10,11... | collective-permute-start | bytes 589832 | tf_op jit(solution)/shard_map/ppermute | solution.py:421
  4.2 11.5 %collective-permute-start.3 = (bf16[5,128,128]{2,1,0:T(8,128)(2,1)S(1)}, bf16[5,128,128]{2,1,0:T(8,128)(2,1)S(1)}, u32[]{:S(2)}, u32[]{:S(2)}) collective-permute-start(bf16[5,128,128]{2,1,0:T(8,128)(2,1)S(1)} %get-tuple-element.46), channel_id=1, source_target_pairs={{0,1},{1,0},{2,3},{3,2},{4,5},{5,4},{6,7},{7,6},{8,9},{9,8},{10,11... | collective-permute-start | bytes 491528 | tf_op jit(solution)/shard_map/ppermute | solution.py:420
  4.2 9.8 %collective-permute-start.4 = (bf16[128,128]{1,0:T(8,128)(2,1)S(1)}, bf16[128,128]{1,0:T(8,128)(2,1)S(1)}, u32[]{:S(2)}, u32[]{:S(2)}) collective-permute-start(bf16[128,128]{1,0:T(8,128)(2,1)S(1)} %get-tuple-element.47), channel_id=1, source_target_pairs={{0,2},{2,4},{4,6},{6,8},{8,10},{10,12},{12,14},{14,16},{16,18},{18... | collective-permute-start | bytes 98312 | tf_op jit(solution)/shard_map/ppermute | solution.py:423
  5.7 10.0 %collective-permute-start.5 = (bf16[128,128]{1,0:T(8,128)(2,1)S(1)}, bf16[128,128]{1,0:T(8,128)(2,1)S(1)}, u32[]{:S(2)}, u32[]{:S(2)}) collective-permute-start(bf16[128,128]{1,0:T(8,128)(2,1)S(1)} %get-tuple-element.48), channel_id=1, source_target_pairs={{1,2},{3,4},{5,6},{7,8},{9,10},{11,12},{13,14},{15,16},{17,18},{19... | collective-permute-start | bytes 98312 | tf_op jit(solution)/shard_map/ppermute | solution.py:422
  9.9 8.6 %collective-permute-start.1 = (bf16[16,48,128]{2,1,0:T(8,128)(2,1)S(1)}, bf16[16,48,128]{2,1,0:T(8,128)(2,1)S(1)}, u32[]{:S(2)}, u32[]{:S(2)}) collective-permute-start(bf16[16,48,128]{2,1,0:T(8,128)(2,1)S(1)} %collective-permute-done.refs_0_), channel_id=1, source_target_pairs={{0,4},{1,5},{2,6},{3,7},{4,0},{5,1},{6,2},{7,3},{8,12},{9,13},{10,... | collective-permute-start | bytes 589832 | tf_op jit(solution)/shard_map/ppermute | solution.py:425
  11.9 6.5 %collective-permute-start.2 = (bf16[16,48,128]{2,1,0:T(8,128)(2,1)S(1)}, bf16[16,48,128]{2,1,0:T(8,128)(2,1)S(1)}, u32[]{:S(2)}, u32[]{:S(2)}) collective-permute-start(bf16[16,48,128]{2,1,0:T(8,128)(2,1)S(1)} %collective-permute-done.refs_0_), channel_id=1, source_target_pairs={{0,2},{1,3},{2,0},{3,1},{4,6},{5,7},{6,4},{7,5},{8,10},{9,11},{10,... | collective-permute-start | bytes 589832 | tf_op jit(solution)/shard_map/ppermute | solution.py:427
  14.1 6.0 %collective-permute-start.6 = (bf16[16,32,128]{2,1,0:T(8,128)(2,1)S(1)}, bf16[16,32,128]{2,1,0:T(8,128)(2,1)S(1)}, u32[]{:S(2)}, u32[]{:S(2)}) collective-permute-start(bf16[16,32,128]{2,1,0:T(8,128)(2,1)S(1)} %get-tuple-element.58), channel_id=1, source_target_pairs={{0,1},{1,0},{2,3},{3,2},{4,5},{5,4},{6,7},{7,6},{8,9},{9,8},{10,11... | collective-permute-start | bytes 393224 | tf_op jit(solution)/shard_map/ppermute | solution.py:426
  15.7 5.7 %copy-start.1 = (f32[128]{0:T(128)S(1)}, f32[128]{0:T(128)}, u32[]{:S(2)}) copy-start(f32[128]{0:T(128)} %param.9) | copy-start | bytes 1540
  18.5 2.9 %collective-permute-start.7 = (bf16[16,48,128]{2,1,0:T(8,128)(2,1)S(1)}, bf16[16,48,128]{2,1,0:T(8,128)(2,1)S(1)}, u32[]{:S(2)}, u32[]{:S(2)}) collective-permute-start(bf16[16,48,128]{2,1,0:T(8,128)(2,1)S(1)} %collective-permute-done.1.refs_1_), channel_id=1, source_target_pairs={{0,2},{1,3},{2,0},{3,1},{4,6},{5,7},{6,4},{7,5},{8,10},{9,11},{10,... | collective-permute-start | bytes 589832 | tf_op jit(solution)/shard_map/ppermute | solution.py:433
  20.0 1.3 %collective-permute-start.8 = (bf16[16,32,128]{2,1,0:T(8,128)(2,1)S(1)}, bf16[16,32,128]{2,1,0:T(8,128)(2,1)S(1)}, u32[]{:S(2)}, u32[]{:S(2)}) collective-permute-start(bf16[16,32,128]{2,1,0:T(8,128)(2,1)S(1)} %collective-permute-done.6.refs_2_), channel_id=1, source_target_pairs={{0,2},{1,3},{2,0},{3,1},{4,6},{5,7},{6,4},{7,5},{8,10},{9,11},{10,... | collective-permute-start | bytes 393224 | tf_op jit(solution)/shard_map/ppermute | solution.py:435

commit v18 on v17

--- a/solution.py
+++ b/solution.py
@@ -244,11 +244,15 @@
             convolve(kernel, u_ref, start, col_phase) + sum_ref[col_phase, :, start * cols : (start + 2) * cols]
             for col_phase in (0, 1)
         ]
+        pairs = []
         for number in (0, 1):
             pair = [
                 (half[:, number * cols : (number + 1) * cols] + bias).astype(jnp.bfloat16) for half in halves
             ]
-            mixed = jnp.dot(jnp.concatenate(pair, axis=1), interleave, preferred_element_type=jnp.float32)
+            pairs.append(jnp.concatenate(pair, axis=1))
+        both = jnp.dot(jnp.concatenate(pairs, axis=0), interleave, preferred_element_type=jnp.float32)
+        for number in (0, 1):
+            mixed = both[number * 2 * cout : (number + 1) * 2 * cout]
             for side in (0, 1):
                 total_ref[side, pl.ds(start + number, 2 * cout, stride=rows), :] = mixed[
                     :, side * cols : (side + 1) * cols

time: 25.8 us -> 26 us (level)
  no operation moved by 1% of the time
where the time goes in v18:
time: 26 us; the launch traced here: 25.8 us
  Pallas kernels  10.4 us (40%)
  starting transfers between devices  9.13 us (35%)
  waiting for transfers between devices  6.16 us (24%)
    pallas_call x1, Pallas kernels, call_second(): pl.pallas_call(functools.partial(second, paired, len(parts)), out_shape=j...  4.38 us
    ppermute x1, waiting for transfers between devices, paired(): w_a = lax.ppermute(w_a, AXES, across)  3.52 us
    ppermute x1, starting transfers between devices, paired(): w_a = lax.ppermute(w_a, AXES, across)  3.03 us
    pallas_call x1, Pallas kernels, call_first(): pl.pallas_call(body, out_shape=(jax.ShapeDtypeStruct(started.shape, jnp.b...  2.78 us
    pallas_call x1, Pallas kernels, call_prepare(): pl.pallas_call(functools.partial(prepare, paired), out_shape=(jax.ShapeDt...  2.12 us
    ppermute x1, starting transfers between devices, paired(): w_ax = lax.ppermute(w_a, AXES, pairs)  2.03 us
    ppermute x1, starting transfers between devices, paired(): w_b = lax.ppermute(w_b, AXES, across)  1.58 us
    ppermute x1, starting transfers between devices, paired(): near = lax.ppermute(near, AXES, chain)  1.45 us
  transfers between devices with their start and end apart: 9, of which 3 were waited for; matrix products, arithmetic and copies ran while one was open for 0% of the time, Pallas kernels for 19%

profile of v18, /device:TPU:0, one launch (start us, length us, event | category | flops | bytes accessed | tf_op | source)
XLA Modules:
  0.0 25.8 jit_solution(16562407260737521770)
XLA Ops:
  0.0 1.1 %shard_map.55 = (bf16[128,128]{1,0:T(8,128)(2,1)S(1)}, bf16[128,128]{1,0:T(8,128)(2,1)S(1)}, bf16[5,128,128]{2,1,0:T(8,128)(2,1)S(1)}, bf16[16,48,128]{2,1,0:T(8,128)(2,1)S(1)}, bf16[16,32,128]{2,1,0:T(8,128)(2,1)S(1)}) custom-call(bf16[128,8,128]{2,1,0:T(8,128)(2,1)} %bitcast.6, bf16[64,64,256]{2,1,0:T(8,128)(2,1)} %w_half_ref.1), custom_call_target="tpu_custom_call" | custom-call | tf_op jit(solution)/shard_map/pallas_call | solution.py:309
  1.1 0.0 copy-start
  1.1 3.0 %collective-permute-start = (bf16[16,48,128]{2,1,0:T(8,128)(2,1)S(1)}, bf16[16,48,128]{2,1,0:T(8,128)(2,1)S(1)}, u32[]{:S(2)}, u32[]{:S(2)}) collective-permute-start(bf16[16,48,128]{2,1,0:T(8,128)(2,1)S(1)} %get-tuple-element.41), channel_id=1, source_target_pairs={{0,1},{1,0},{2,3},{3,2},{4,5},{5,4},{6,7},{7,6},{8,9},{9,8},{10,11... | collective-permute-start | bytes 589832 | tf_op jit(solution)/shard_map/ppermute | solution.py:425
  4.2 0.1 collective-permute-start.3
  4.2 1.4 %collective-permute-start.4 = (bf16[128,128]{1,0:T(8,128)(2,1)S(1)}, bf16[128,128]{1,0:T(8,128)(2,1)S(1)}, u32[]{:S(2)}, u32[]{:S(2)}) collective-permute-start(bf16[128,128]{1,0:T(8,128)(2,1)S(1)} %get-tuple-element.47), channel_id=1, source_target_pairs={{0,2},{2,4},{4,6},{6,8},{8,10},{10,12},{12,14},{14,16},{16,18},{18... | collective-permute-start | bytes 98312 | tf_op jit(solution)/shard_map/ppermute | solution.py:427
  5.7 0.7 %collective-permute-start.5 = (bf16[128,128]{1,0:T(8,128)(2,1)S(1)}, bf16[128,128]{1,0:T(8,128)(2,1)S(1)}, u32[]{:S(2)}, u32[]{:S(2)}) collective-permute-start(bf16[128,128]{1,0:T(8,128)(2,1)S(1)} %get-tuple-element.48), channel_id=1, source_target_pairs={{1,2},{3,4},{5,6},{7,8},{9,10},{11,12},{13,14},{15,16},{17,18},{19... | collective-permute-start | bytes 98312 | tf_op jit(solution)/shard_map/ppermute | solution.py:426
  6.4 3.5 %collective-permute-done.refs_0_ = bf16[16,48,128]{2,1,0:T(8,128)(2,1)S(1)} collective-permute-done((bf16[16,48,128]{2,1,0:T(8,128)(2,1)S(1)}, bf16[16,48,128]{2,1,0:T(8,128)(2,1)S(1)}, u32[]{:S(2)}, u32[]{:S(2)}) %collective-permute-start) | collective-permute-done | bytes 196640 | tf_op jit(solution)/shard_map/ppermute | solution.py:425
  9.9 2.0 %collective-permute-start.1 = (bf16[16,48,128]{2,1,0:T(8,128)(2,1)S(1)}, bf16[16,48,128]{2,1,0:T(8,128)(2,1)S(1)}, u32[]{:S(2)}, u32[]{:S(2)}) collective-permute-start(bf16[16,48,128]{2,1,0:T(8,128)(2,1)S(1)} %collective-permute-done.refs_0_), channel_id=1, source_target_pairs={{0,4},{1,5},{2,6},{3,7},{4,0},{5,1},{6,2},{7,3},{8,12},{9,13},{10,... | collective-permute-start | bytes 589832 | tf_op jit(solution)/shard_map/ppermute | solution.py:429
  11.9 0.0 collective-permute-start.2
  11.9 2.1 %shard_map.56 = (bf16[3,6,256,128]{3,2,1,0:T(8,128)(2,1)S(1)}, bf16[32,64,256]{2,1,0:T(8,128)(2,1)S(1)}, bf16[256,1152]{1,0:T(8,128)(2,1)S(1)}, bf16[256,1152]{1,0:T(8,128)(2,1)S(1)}) custom-call(bf16[128,8,128]{2,1,0:T(8,128)(2,1)} %bitcast.7, bf16[64,64,256]{2,1,0:T(8,128)(2,1)} %w_half_ref.1, bf16[27,128,128]{2,1,0:T(8,128)(2,1)} %w_conv_ref), custom_call_target="tpu_custom_call" | custom-call | flops 150994944 | bytes 8388608 | tf_op jit(solution)/shard_map/pallas_call | solution.py:342
  14.1 0.0 collective-permute-done.4.near_ref
  14.1 1.6 %collective-permute-start.6 = (bf16[16,32,128]{2,1,0:T(8,128)(2,1)S(1)}, bf16[16,32,128]{2,1,0:T(8,128)(2,1)S(1)}, u32[]{:S(2)}, u32[]{:S(2)}) collective-permute-start(bf16[16,32,128]{2,1,0:T(8,128)(2,1)S(1)} %get-tuple-element.58), channel_id=1, source_target_pairs={{0,1},{1,0},{2,3},{3,2},{4,5},{5,4},{6,7},{7,6},{8,9},{9,8},{10,11... | collective-permute-start | bytes 393224 | tf_op jit(solution)/shard_map/ppermute | solution.py:430
  15.7 0.0 collective-permute-done.5.far_ref
  15.7 0.0 collective-permute-done.3.peer_ref
  15.7 0.0 copy-done
  15.7 0.0 copy-start.1
  15.7 2.8 %shard_map.57 = (bf16[3,6,256,128]{3,2,1,0:T(8,128)(2,1)S(1)}, f32[2,256,1024]{2,1,0:T(8,128)S(1)}) custom-call(bf16[5,128,128]{2,1,0:T(8,128)(2,1)S(1)} %collective-permute-done.3.peer_ref, bf16[128,128]{1,0:T(8,128)(2,1)S(1)} %collective-permute-done.4.near_ref, ...), custom_call_target="tpu_custom_call", output_to_operand_aliasing={{0}: (3, {})} | custom-call | flops 1879048192 | bytes 8388608 | tf_op jit(solution)/shard_map/pallas_call | solution.py:367
  18.5 0.0 collective-permute-done.1.refs_1_
  18.5 0.0 collective-permute-done.2.refs_3_
  18.5 0.3 %collective-permute-start.7 = (bf16[16,48,128]{2,1,0:T(8,128)(2,1)S(1)}, bf16[16,48,128]{2,1,0:T(8,128)(2,1)S(1)}, u32[]{:S(2)}, u32[]{:S(2)}) collective-permute-start(bf16[16,48,128]{2,1,0:T(8,128)(2,1)S(1)} %collective-permute-done.1.refs_1_), channel_id=1, source_target_pairs={{0,2},{1,3},{2,0},{3,1},{4,6},{5,7},{6,4},{7,5},{8,10},{9,11},{10,... | collective-permute-start | bytes 589832 | tf_op jit(solution)/shard_map/ppermute | solution.py:437
  18.8 1.3 %collective-permute-done.6.refs_2_ = bf16[16,32,128]{2,1,0:T(8,128)(2,1)S(1)} collective-permute-done((bf16[16,32,128]{2,1,0:T(8,128)(2,1)S(1)}, bf16[16,32,128]{2,1,0:T(8,128)(2,1)S(1)}, u32[]{:S(2)}, u32[]{:S(2)}) %collective-permute-start.6) | collective-permute-done | bytes 131104 | tf_op jit(solution)/shard_map/ppermute | solution.py:430
  20.0 0.0 collective-permute-start.8
  20.1 1.3 %collective-permute-done.8.refs_5_ = bf16[16,32,128]{2,1,0:T(8,128)(2,1)S(1)} collective-permute-done((bf16[16,32,128]{2,1,0:T(8,128)(2,1)S(1)}, bf16[16,32,128]{2,1,0:T(8,128)(2,1)S(1)}, u32[]{:S(2)}, u32[]{:S(2)}) %collective-permute-start.8) | collective-permute-done | bytes 131104 | tf_op jit(solution)/shard_map/ppermute | solution.py:439
  21.4 0.0 collective-permute-done.7.refs_4_
  21.4 0.0 copy-done.1
  21.4 4.4 %shard_map.58 = bf16[128,2,8,256]{3,2,1,0:T(8,128)(2,1)} custom-call(bf16[16,48,128]{2,1,0:T(8,128)(2,1)S(1)} %collective-permute-done.refs_0_, bf16[16,48,128]{2,1,0:T(8,128)(2,1)S(1)} %collective-permute-done.1.refs_1_, bf16[16,32,128]{2,1,0:T(8,128)(2,1)S(1)} %collective-permute-done.6.refs_2_, bf16[16,48,128]{2,1,0:T(8,128)(2,1)S(1)} %collective-permute-done.2.refs_3_, ...), custom_call_target="tpu_custom_call" | custom-call | flops 1879048192 | bytes 8388608 | tf_op jit(solution)/shard_map/pallas_call | solution.py:387
Async XLA Ops:
  1.1 14.5 %copy-start = (f32[128]{0:T(128)S(1)}, f32[128]{0:T(128)}, u32[]{:S(2)}) copy-start(f32[128]{0:T(128)} %param.7) | copy-start | bytes 1540
  1.1 8.8 %collective-permute-start = (bf16[16,48,128]{2,1,0:T(8,128)(2,1)S(1)}, bf16[16,48,128]{2,1,0:T(8,128)(2,1)S(1)}, u32[]{:S(2)}, u32[]{:S(2)}) collective-permute-start(bf16[16,48,128]{2,1,0:T(8,128)(2,1)S(1)} %get-tuple-element.41), channel_id=1, source_target_pairs={{0,1},{1,0},{2,3},{3,2},{4,5},{5,4},{6,7},{7,6},{8,9},{9,8},{10,11... | collective-permute-start | bytes 589832 | tf_op jit(solution)/shard_map/ppermute | solution.py:425
  4.2 11.5 %collective-permute-start.3 = (bf16[5,128,128]{2,1,0:T(8,128)(2,1)S(1)}, bf16[5,128,128]{2,1,0:T(8,128)(2,1)S(1)}, u32[]{:S(2)}, u32[]{:S(2)}) collective-permute-start(bf16[5,128,128]{2,1,0:T(8,128)(2,1)S(1)} %get-tuple-element.46), channel_id=1, source_target_pairs={{0,1},{1,0},{2,3},{3,2},{4,5},{5,4},{6,7},{7,6},{8,9},{9,8},{10,11... | collective-permute-start | bytes 491528 | tf_op jit(solution)/shard_map/ppermute | solution.py:424
  4.2 9.8 %collective-permute-start.4 = (bf16[128,128]{1,0:T(8,128)(2,1)S(1)}, bf16[128,128]{1,0:T(8,128)(2,1)S(1)}, u32[]{:S(2)}, u32[]{:S(2)}) collective-permute-start(bf16[128,128]{1,0:T(8,128)(2,1)S(1)} %get-tuple-element.47), channel_id=1, source_target_pairs={{0,2},{2,4},{4,6},{6,8},{8,10},{10,12},{12,14},{14,16},{16,18},{18... | collective-permute-start | bytes 98312 | tf_op jit(solution)/shard_map/ppermute | solution.py:427
  5.7 10.0 %collective-permute-start.5 = (bf16[128,128]{1,0:T(8,128)(2,1)S(1)}, bf16[128,128]{1,0:T(8,128)(2,1)S(1)}, u32[]{:S(2)}, u32[]{:S(2)}) collective-permute-start(bf16[128,128]{1,0:T(8,128)(2,1)S(1)} %get-tuple-element.48), channel_id=1, source_target_pairs={{1,2},{3,4},{5,6},{7,8},{9,10},{11,12},{13,14},{15,16},{17,18},{19... | collective-permute-start | bytes 98312 | tf_op jit(solution)/shard_map/ppermute | solution.py:426
  9.9 8.6 %collective-permute-start.1 = (bf16[16,48,128]{2,1,0:T(8,128)(2,1)S(1)}, bf16[16,48,128]{2,1,0:T(8,128)(2,1)S(1)}, u32[]{:S(2)}, u32[]{:S(2)}) collective-permute-start(bf16[16,48,128]{2,1,0:T(8,128)(2,1)S(1)} %collective-permute-done.refs_0_), channel_id=1, source_target_pairs={{0,4},{1,5},{2,6},{3,7},{4,0},{5,1},{6,2},{7,3},{8,12},{9,13},{10,... | collective-permute-start | bytes 589832 | tf_op jit(solution)/shard_map/ppermute | solution.py:429
  11.9 6.5 %collective-permute-start.2 = (bf16[16,48,128]{2,1,0:T(8,128)(2,1)S(1)}, bf16[16,48,128]{2,1,0:T(8,128)(2,1)S(1)}, u32[]{:S(2)}, u32[]{:S(2)}) collective-permute-start(bf16[16,48,128]{2,1,0:T(8,128)(2,1)S(1)} %collective-permute-done.refs_0_), channel_id=1, source_target_pairs={{0,2},{1,3},{2,0},{3,1},{4,6},{5,7},{6,4},{7,5},{8,10},{9,11},{10,... | collective-permute-start | bytes 589832 | tf_op jit(solution)/shard_map/ppermute | solution.py:431
  14.1 6.0 %collective-permute-start.6 = (bf16[16,32,128]{2,1,0:T(8,128)(2,1)S(1)}, bf16[16,32,128]{2,1,0:T(8,128)(2,1)S(1)}, u32[]{:S(2)}, u32[]{:S(2)}) collective-permute-start(bf16[16,32,128]{2,1,0:T(8,128)(2,1)S(1)} %get-tuple-element.58), channel_id=1, source_target_pairs={{0,1},{1,0},{2,3},{3,2},{4,5},{5,4},{6,7},{7,6},{8,9},{9,8},{10,11... | collective-permute-start | bytes 393224 | tf_op jit(solution)/shard_map/ppermute | solution.py:430
  15.7 5.7 %copy-start.1 = (f32[128]{0:T(128)S(1)}, f32[128]{0:T(128)}, u32[]{:S(2)}) copy-start(f32[128]{0:T(128)} %param.9) | copy-start | bytes 1540
  18.5 2.9 %collective-permute-start.7 = (bf16[16,48,128]{2,1,0:T(8,128)(2,1)S(1)}, bf16[16,48,128]{2,1,0:T(8,128)(2,1)S(1)}, u32[]{:S(2)}, u32[]{:S(2)}) collective-permute-start(bf16[16,48,128]{2,1,0:T(8,128)(2,1)S(1)} %collective-permute-done.1.refs_1_), channel_id=1, source_target_pairs={{0,2},{1,3},{2,0},{3,1},{4,6},{5,7},{6,4},{7,5},{8,10},{9,11},{10,... | collective-permute-start | bytes 589832 | tf_op jit(solution)/shard_map/ppermute | solution.py:437
  20.0 1.3 %collective-permute-start.8 = (bf16[16,32,128]{2,1,0:T(8,128)(2,1)S(1)}, bf16[16,32,128]{2,1,0:T(8,128)(2,1)S(1)}, u32[]{:S(2)}, u32[]{:S(2)}) collective-permute-start(bf16[16,32,128]{2,1,0:T(8,128)(2,1)S(1)} %collective-permute-done.6.refs_2_), channel_id=1, source_target_pairs={{0,2},{1,3},{2,0},{3,1},{4,6},{5,7},{6,4},{7,5},{8,10},{9,11},{10,... | collective-permute-start | bytes 393224 | tf_op jit(solution)/shard_map/ppermute | solution.py:439
